TPU v7x, 32 devices: a whole 2x2x4 slice. The times are simulated.
32 devices in a mesh: dp: 16 (over z, y, core), tensor: 2 (over x).
Axes of the slice: x: 2, y: 2, z: 4, core: 2. Of those that a mesh axis runs over, the one named last changes fastest.
Arguments:
- tokens: bfloat16 [1024, 32, 1024], P('tensor', 'dp'), may hold values from -6 to 6
- d_out: bfloat16 [1024, 32, 1024], P('tensor', 'dp'), may hold values from -6 to 6
- ln1_gain: bfloat16 [1024], P('dp'), may hold values from 0.099609375 to 1.8984375
- ln1_bias: bfloat16 [1024], P('dp'), may hold values from -1.75 to 1.75
- w_qkv: bfloat16 [3, 1024, 1024], P(None, 'dp', 'tensor'), may hold values from -0.1875 to 0.1875
- w_out: bfloat16 [1024, 1024], P('tensor', 'dp'), may hold values from -3 to 3
- ln2_gain: bfloat16 [1024], P('dp'), may hold values from 0.099609375 to 1.8984375
- ln2_bias: bfloat16 [1024], P('dp'), may hold values from -1.75 to 1.75
- w_up: bfloat16 [1024, 4096], P('dp', 'tensor'), may hold values from -0.1875 to 0.1875
- w_down: bfloat16 [4096, 1024], P('tensor', 'dp'), may hold values from -0.09375 to 0.09375
Outputs:
- block_out: bfloat16 [1024, 32, 1024], P('tensor', 'dp')
- input_grad: bfloat16 [1024, 32, 1024], P('tensor', 'dp')
- grad_ln1_gain: float32 [1024], P('dp')
- grad_ln1_bias: float32 [1024], P('dp')
- grad_w_qkv: float32 [3, 1024, 1024], P(None, 'dp', 'tensor')
- grad_w_out: float32 [1024, 1024], P('tensor', 'dp')
- grad_ln2_gain: float32 [1024], P('dp')
- grad_ln2_bias: float32 [1024], P('dp')
- grad_w_up: float32 [1024, 4096], P('dp', 'tensor')
- grad_w_down: float32 [4096, 1024], P('tensor', 'dp')
All inputs are finite; a program needn't handle non-finite values.
Results may differ from a plain program's by a relative error of at most 0.023.
Values may be sent and summed in bfloat16 or wider, within the bound.
No kernel may reach another device: no remote copies, remote signals or barrier semaphores. Data moves between devices by JAX's collectives and lax.ppermute only.
A program may use at most 256 MiB of HBM per device.

v0:
```python
import jax
import jax.numpy as jnp
from jax import lax
from jax.sharding import PartitionSpec as P

HEAD_DIM = 64


EPSILON = 1e-05


def norm_rows(values, norm_gain, norm_bias):
    center = jnp.mean(values, axis=-1, keepdims=True)
    centered = values - center
    inverse = lax.rsqrt(jnp.mean(centered * centered, axis=-1, keepdims=True) + EPSILON)
    normal = centered * inverse
    return (normal * norm_gain + norm_bias, normal, inverse)


def norm_back(grad_in, normal, inverse, norm_gain):
    gain_grad = jnp.sum(grad_in * normal, axis=(0, 1))
    bias_grad = jnp.sum(grad_in, axis=(0, 1))
    scaled = grad_in * norm_gain
    first = jnp.mean(scaled, axis=-1, keepdims=True)
    second = jnp.mean(scaled * normal, axis=-1, keepdims=True)
    return (inverse * (scaled - first - normal * second), gain_grad, bias_grad)


def causal_mask(length):
    row_index = lax.broadcasted_iota(jnp.int32, (length, length), 0)
    column_index = lax.broadcasted_iota(jnp.int32, (length, length), 1)
    return column_index <= row_index


def attend_forward(triple):
    queries, key_rows, value_rows = triple
    scores = jnp.einsum(
        "qhd,khd->hqk", queries, key_rows, preferred_element_type=jnp.float32
    ) * HEAD_DIM ** (-0.5)
    scores = jnp.where(causal_mask(queries.shape[0]), scores, -1e30)
    row_max = jnp.max(scores, axis=-1, keepdims=True)
    weights = jnp.exp(scores - row_max)
    totals = jnp.sum(weights, axis=-1, keepdims=True)
    shares = (weights / totals).astype(jnp.bfloat16)
    mixed = jnp.einsum("hqk,khd->qhd", shares, value_rows, preferred_element_type=jnp.float32)
    return (mixed.astype(jnp.bfloat16), row_max + jnp.log(totals))


def attend_back(group):
    queries, key_rows, value_rows, grad_mixed, log_total = group
    factor = HEAD_DIM ** (-0.5)
    scores = (
        jnp.einsum("qhd,khd->hqk", queries, key_rows, preferred_element_type=jnp.float32) * factor
    )
    scores = jnp.where(causal_mask(queries.shape[0]), scores, -1e30)
    shares = jnp.exp(scores - log_total)
    grad_value = jnp.einsum(
        "hqk,qhd->khd", shares.astype(jnp.bfloat16), grad_mixed, preferred_element_type=jnp.float32
    )
    grad_shares = jnp.einsum(
        "qhd,khd->hqk", grad_mixed, value_rows, preferred_element_type=jnp.float32
    )
    inner = jnp.sum(shares * grad_shares, axis=-1, keepdims=True)
    grad_scores = (shares * (grad_shares - inner)).astype(jnp.bfloat16)
    grad_query = (
        jnp.einsum("hqk,khd->qhd", grad_scores, key_rows, preferred_element_type=jnp.float32)
        * factor
    )
    grad_key = (
        jnp.einsum("hqk,qhd->khd", grad_scores, queries, preferred_element_type=jnp.float32)
        * factor
    )
    return jnp.stack([grad_query, grad_key, grad_value]).astype(jnp.bfloat16)


def on_device(tokens, d_out, ln1_gain, ln1_bias, w_qkv, w_out, ln2_gain, ln2_bias, w_up, w_down):
    local_rows, seq_count, width = tokens.shape
    gathered = (
        lax.all_gather(ln1_gain, "dp", axis=0, tiled=True),
        lax.all_gather(ln1_bias, "dp", axis=0, tiled=True),
        lax.all_gather(w_qkv, "dp", axis=1, tiled=True),
        lax.all_gather(w_out, "dp", axis=1, tiled=True),
        lax.all_gather(ln2_gain, "dp", axis=0, tiled=True),
        lax.all_gather(ln2_bias, "dp", axis=0, tiled=True),
        lax.all_gather(w_up, "dp", axis=0, tiled=True),
        lax.all_gather(w_down, "dp", axis=1, tiled=True),
    )
    gain_one, bias_one, qkv_weight, out_weight, gain_two, bias_two, up_weight, down_weight = (
        gathered
    )
    residual = tokens.astype(jnp.float32)
    normed_one, normal_one, inverse_one = norm_rows(
        residual, gain_one.astype(jnp.float32), bias_one.astype(jnp.float32)
    )
    low_one = normed_one.astype(jnp.bfloat16)
    rows_one = lax.all_gather(low_one, "tensor", axis=0, tiled=True)
    full_rows = rows_one.shape[0]
    projected = jnp.einsum(
        "tgd,cde->cgte", rows_one, qkv_weight, preferred_element_type=jnp.float32
    ).astype(jnp.bfloat16)
    local_width = projected.shape[3]
    heads_local = local_width // HEAD_DIM
    split_heads = projected.reshape(3, seq_count, full_rows, heads_local, HEAD_DIM)
    mixed, log_total = lax.map(attend_forward, (split_heads[0], split_heads[1], split_heads[2]))
    mixed = mixed.reshape(seq_count, full_rows, local_width)
    piece_rows = mixed
    hidden = residual + lax.psum_scatter(
        jnp.einsum(
            "gte,ed->tgd", piece_rows, out_weight, preferred_element_type=jnp.float32
        ).astype(jnp.bfloat16),
        "tensor",
        scatter_dimension=0,
        tiled=True,
    ).astype(jnp.float32)
    normed_two, normal_two, inverse_two = norm_rows(
        hidden, gain_two.astype(jnp.float32), bias_two.astype(jnp.float32)
    )
    low_two = normed_two.astype(jnp.bfloat16)
    rows_two = lax.all_gather(low_two, "tensor", axis=0, tiled=True)
    upward = jnp.einsum("tgd,df->tgf", rows_two, up_weight, preferred_element_type=jnp.float32)
    active = jax.nn.gelu(upward, approximate=True).astype(jnp.bfloat16)
    piece_rows = active
    block_sum = lax.psum_scatter(
        jnp.einsum(
            "tgf,fd->tgd", piece_rows, down_weight, preferred_element_type=jnp.float32
        ).astype(jnp.bfloat16),
        "tensor",
        scatter_dimension=0,
        tiled=True,
    ).astype(jnp.float32)
    block_out = (hidden + block_sum).astype(jnp.bfloat16)
    grad_rows = lax.all_gather(d_out, "tensor", axis=0, tiled=True)
    grad_down = jnp.einsum("tgf,tgd->fd", active, grad_rows, preferred_element_type=jnp.float32)
    grad_active = jnp.einsum(
        "tgd,fd->tgf", grad_rows, down_weight, preferred_element_type=jnp.float32
    )
    gelu_pull = jax.vjp(lambda inner: jax.nn.gelu(inner, approximate=True), upward)[1]
    grad_upward = gelu_pull(grad_active)[0].astype(jnp.bfloat16)
    grad_up = jnp.einsum("tgd,tgf->df", rows_two, grad_upward, preferred_element_type=jnp.float32)
    piece_rows = grad_upward
    grad_normed_two = lax.psum_scatter(
        jnp.einsum("tgf,df->tgd", piece_rows, up_weight, preferred_element_type=jnp.float32).astype(
            jnp.bfloat16
        ),
        "tensor",
        scatter_dimension=0,
        tiled=True,
    ).astype(jnp.float32)
    grad_hidden_norm, gain_two_grad, bias_two_grad = norm_back(
        grad_normed_two, normal_two, inverse_two, gain_two.astype(jnp.float32)
    )
    grad_hidden = d_out.astype(jnp.float32) + grad_hidden_norm
    low_hidden = grad_hidden.astype(jnp.bfloat16)
    hidden_rows = lax.all_gather(low_hidden, "tensor", axis=0, tiled=True)
    grad_out = jnp.einsum("gte,tgd->ed", mixed, hidden_rows, preferred_element_type=jnp.float32)
    grad_mixed = jnp.einsum(
        "tgd,ed->gte", hidden_rows, out_weight, preferred_element_type=jnp.float32
    ).astype(jnp.bfloat16)
    grad_heads = lax.map(
        attend_back,
        (
            split_heads[0],
            split_heads[1],
            split_heads[2],
            grad_mixed.reshape(seq_count, full_rows, heads_local, HEAD_DIM),
            log_total,
        ),
    )
    grad_projected = grad_heads.reshape(seq_count, 3, full_rows, local_width)
    grad_qkv = jnp.einsum(
        "tgd,gcte->cde", rows_one, grad_projected, preferred_element_type=jnp.float32
    )
    piece_rows = grad_projected
    grad_normed_one = lax.psum_scatter(
        jnp.einsum(
            "gcte,cde->tgd", piece_rows, qkv_weight, preferred_element_type=jnp.float32
        ).astype(jnp.bfloat16),
        "tensor",
        scatter_dimension=0,
        tiled=True,
    ).astype(jnp.float32)
    grad_input_norm, gain_one_grad, bias_one_grad = norm_back(
        grad_normed_one, normal_one, inverse_one, gain_one.astype(jnp.float32)
    )
    input_grad = (grad_hidden + grad_input_norm).astype(jnp.bfloat16)
    owned = (
        lax.psum_scatter(
            gain_one_grad.astype(jnp.bfloat16), "dp", scatter_dimension=0, tiled=True
        ).astype(jnp.float32),
        lax.psum_scatter(
            bias_one_grad.astype(jnp.bfloat16), "dp", scatter_dimension=0, tiled=True
        ).astype(jnp.float32),
        lax.psum_scatter(
            grad_qkv.astype(jnp.bfloat16), "dp", scatter_dimension=1, tiled=True
        ).astype(jnp.float32),
        lax.psum_scatter(
            grad_out.astype(jnp.bfloat16), "dp", scatter_dimension=1, tiled=True
        ).astype(jnp.float32),
        lax.psum_scatter(
            gain_two_grad.astype(jnp.bfloat16), "dp", scatter_dimension=0, tiled=True
        ).astype(jnp.float32),
        lax.psum_scatter(
            bias_two_grad.astype(jnp.bfloat16), "dp", scatter_dimension=0, tiled=True
        ).astype(jnp.float32),
        lax.psum_scatter(
            grad_up.astype(jnp.bfloat16), "dp", scatter_dimension=0, tiled=True
        ).astype(jnp.float32),
        lax.psum_scatter(
            grad_down.astype(jnp.bfloat16), "dp", scatter_dimension=1, tiled=True
        ).astype(jnp.float32),
    )
    norm_sums = lax.psum((owned[0], owned[1], owned[4], owned[5]), "tensor")
    return (
        block_out,
        input_grad,
        norm_sums[0],
        norm_sums[1],
        owned[2],
        owned[3],
        norm_sums[2],
        norm_sums[3],
        owned[6],
        owned[7],
    )


def solution(mesh):
    placed = (
        P("tensor", "dp", None),
        P("tensor", "dp", None),
        P("dp"),
        P("dp"),
        P(None, "dp", "tensor"),
        P("tensor", "dp"),
        P("dp"),
        P("dp"),
        P("dp", "tensor"),
        P("tensor", "dp"),
    )
    return jax.shard_map(
        on_device,
        mesh=mesh,
        in_specs=placed,
        out_specs=(
            P("tensor", "dp", None),
            P("tensor", "dp", None),
            P("dp"),
            P("dp"),
            P(None, "dp", "tensor"),
            P("tensor", "dp"),
            P("dp"),
            P("dp"),
            P("dp", "tensor"),
            P("tensor", "dp"),
        ),
        check_vma=False,
    )
```

profile of v0, /device:TPU:0, one launch (start us, length us, event | category | flops | bytes accessed | tf_op | source)
XLA Modules:
  0.0 1248.3 jit_solution(5901912760766693115)
XLA Ops:
  12.7 36.0 %all-reduce.11 = (bf16[1024]{0:T(1024)(128)(2,1)}, bf16[1024]{0:T(1024)(128)(2,1)}, bf16[1024]{0:T(1024)(128)(2,1)S(1)}, bf16[1024]{0:T(1024)(128)(2,1)S(1)}) all-reduce(bf16[1024]{0:T(1024)(128)(2,1)S(1)} %dynamic-update-slice.3, bf16[1024]{0:T(1024)(128)(2,1)S(1)} %dynamic-update-slice.2, ...), channel_id=1, replica_groups=mesh['dp'=16,'tensor'=2] {'dp'}, use_global_device_ids=true, to_apply=%add.3 | all-reduce | flops 4096 | bytes 16384
  57.9 52.4 %all-gather.9.cloned.1.call-done = bf16[1024,2,1024]{2,0,1:T(8,128)(2,1)} async-done(((bf16[512,2,1024]{2,0,1:T(8,128)(2,1)}), bf16[1024,2,1024]{2,0,1:T(8,128)(2,1)}) %all-gather.9.cloned.1.call-update) | async-done | bytes 4194320 | tf_op jit(solution)/shard_map/all_gather | solution.py:96
  110.3 47.4 %all-gather.11.cloned.1.call-done = bf16[3,1024,512]{2,1,0:T(8,128)(2,1)} async-done(((bf16[3,64,512]{2,1,0:T(8,128)(2,1)}), bf16[3,1024,512]{2,1,0:T(8,128)(2,1)}) %all-gather.11.cloned.1.call-update) | async-done | bytes 3145744 | tf_op jit(solution)/shard_map/all_gather | solution.py:81
  157.7 9.6 convert_bitcast_fusion
  170.3 90.0 %while.22 = (s32[]{:T(128)}, bf16[2,1024,8,64]{1,3,2,0:T(8,128)(2,1)}, f32[2,8,1024,1]{2,1,3,0:T(8,128)S(1)}, bf16[2,1024,8,64]{1,3,2,0:T(8,128)(2,1)}, bf16[2,1...) while((s32[]{:T(128)}, bf16[2,1024,8,64]{1,3,2,0:T(8,128)(2,1)}, ...), condition=%wide.region_5.6_spmd, body=%wide.region_2.5_spmd.sunk | while | flops 2249711616 | bytes 117704816 | solution.py:104
  170.6 14.8 %fusion.145 = (f32[8,1024]{1,0:T(8,128)S(1)}, f32[8,1024,1024]{1,2,0:T(8,128)}) fusion(pred[1024,1024]{0,1:T(8,128)(4,1)S(1)} %iota_compare_fusion.4, bf16[2,1024,8,64]{1,3,2,0:T(8,128)(2,1)S(1)} %get-tuple-element.267, s32[]{:T(128)S(6)} %copy.93, bf16[2,1024,8,64]{1,3,2,0:T(8,128)(2,1)} %get-tuple-element.266), kind=kOutput, calls=%fused_computation.3.clone.1 | convolution fusion | flops 1098899456 | bytes 36733952 | tf_op jit(solution)/shard_map/while/body/eval_jaxpr/qhd,khd->hqk/dot_general | solution.py:37
  185.5 14.4 %fusion.146 = f32[8,1024]{1,0:T(8,128)S(1)} fusion(f32[8,1024,1024]{1,2,0:T(8,128)} %get-tuple-element.237, f32[8,1024]{1,0:T(8,128)S(1)} %get-tuple-element.238, pred[1024,1024]{0,1:T(8,128)(4,1)S(1)} %iota_compare_fusion.4), kind=kLoop, calls=%fused_computation.4.clone.1 | loop fusion | flops 33546240 | bytes 34668544 | tf_op jit(solution)/shard_map/while/body/eval_jaxpr/reduce_sum | solution.py:43
  199.9 15.4 %fusion.147 = bf16[2,1024,8,64]{1,3,2,0:T(8,128)(2,1)} fusion(bf16[2,1024,8,64]{1,3,2,0:T(8,128)(2,1)} %get-tuple-element.256, s32[]{:T(128)S(6)} %copy.93, f32[8,1024,1024]{1,2,0:T(8,128)} %get-tuple-element.237, f32[8,1024]{1,0:T(8,128)S(1)} %fusion.146, f32[8,1024]{1,0:T(8,128)S(1)} %get-tuple-element.238, ...), kind=kOutput, calls=%fused_computation.9.clone.1 | convolution fusion | flops 1116209152 | bytes 36766720 | tf_op jit(solution)/shard_map/while/body/eval_jaxpr/hqk,khd->qhd/dot_general | solution.py:45
  215.7 14.7 %fusion.145 = (f32[8,1024]{1,0:T(8,128)S(1)}, f32[8,1024,1024]{1,2,0:T(8,128)}) fusion(pred[1024,1024]{0,1:T(8,128)(4,1)S(1)} %iota_compare_fusion.4, bf16[2,1024,8,64]{1,3,2,0:T(8,128)(2,1)S(1)} %get-tuple-element.267, s32[]{:T(128)S(6)} %copy.93, bf16[2,1024,8,64]{1,3,2,0:T(8,128)(2,1)} %get-tuple-element.266), kind=kOutput, calls=%fused_computation.3.clone.1 | convolution fusion | flops 1098899456 | bytes 36733952 | tf_op jit(solution)/shard_map/while/body/eval_jaxpr/qhd,khd->hqk/dot_general | solution.py:37
  230.4 14.3 %fusion.146 = f32[8,1024]{1,0:T(8,128)S(1)} fusion(f32[8,1024,1024]{1,2,0:T(8,128)} %get-tuple-element.237, f32[8,1024]{1,0:T(8,128)S(1)} %get-tuple-element.238, pred[1024,1024]{0,1:T(8,128)(4,1)S(1)} %iota_compare_fusion.4), kind=kLoop, calls=%fused_computation.4.clone.1 | loop fusion | flops 33546240 | bytes 34668544 | tf_op jit(solution)/shard_map/while/body/eval_jaxpr/reduce_sum | solution.py:43
  244.8 15.4 %fusion.147 = bf16[2,1024,8,64]{1,3,2,0:T(8,128)(2,1)} fusion(bf16[2,1024,8,64]{1,3,2,0:T(8,128)(2,1)} %get-tuple-element.256, s32[]{:T(128)S(6)} %copy.93, f32[8,1024,1024]{1,2,0:T(8,128)} %get-tuple-element.237, f32[8,1024]{1,0:T(8,128)S(1)} %fusion.146, f32[8,1024]{1,0:T(8,128)S(1)} %get-tuple-element.238, ...), kind=kOutput, calls=%fused_computation.9.clone.1 | convolution fusion | flops 1116209152 | bytes 36766720 | tf_op jit(solution)/shard_map/while/body/eval_jaxpr/hqk,khd->qhd/dot_general | solution.py:45
  261.7 6.3 convert_bitcast_fusion.1
  268.8 52.6 %reduce-scatter.8.cloned.1.call-done = bf16[512,2,1024]{2,0,1:T(8,128)(2,1)} async-done(((bf16[1024,2,1024]{2,0,1:T(8,128)(2,1)}), bf16[512,2,1024]{2,0,1:T(8,128)(2,1)}) %reduce-scatter.8.cloned.1.call-update) | async-done | bytes 2097168 | tf_op jit(solution)/shard_map/reduce_scatter | solution.py:107
  331.3 42.8 %all-gather.17.cloned.1.call-done = bf16[1024,2048]{1,0:T(8,128)(2,1)} async-done(((bf16[64,2048]{1,0:T(8,128)(2,1)}), bf16[1024,2048]{1,0:T(8,128)(2,1)}) %all-gather.17.cloned.1.call-update) | async-done | bytes 4194320 | tf_op jit(solution)/shard_map/all_gather | solution.py:85
  374.2 56.7 %all-gather.15.cloned.1.call-done = bf16[1024,2,1024]{2,0,1:T(8,128)(2,1)} async-done(((bf16[512,2,1024]{2,0,1:T(8,128)(2,1)}), bf16[1024,2,1024]{2,0,1:T(8,128)(2,1)}) %all-gather.15.cloned.1.call-update) | async-done | bytes 4194320 | tf_op jit(solution)/shard_map/all_gather | solution.py:119
  430.9 15.3 %fusion.93 = f32[1024,2,2048]{2,0,1:T(8,128)} fusion(bf16[1024,2,1024]{2,0,1:T(8,128)(2,1)} %all-gather.15.cloned.1.call-done, bf16[1024,2048]{1,0:T(8,128)(2,1)} %all-gather.17.cloned.1.call-done), kind=kOutput, calls=%fused_computation.116 | convolution fusion | flops 8589934592 | bytes 25165824 | tf_op jit(solution)/shard_map/tgd,df->tgf/dot_general | solution.py:120
  446.2 43.1 %all-gather.21.cloned.1.call-done = bf16[1024,2,1024]{2,0,1:T(8,128)(2,1)} async-done(((bf16[512,2,1024]{2,0,1:T(8,128)(2,1)}), bf16[1024,2,1024]{2,0,1:T(8,128)(2,1)}) %all-gather.21.cloned.1.call-update) | async-done | bytes 4194320 | tf_op jit(solution)/shard_map/all_gather | solution.py:132
  489.3 53.0 %all-gather.19.cloned.1.call-done = bf16[2048,1024]{0,1:T(8,128)(2,1)} async-done(((bf16[2048,64]{0,1:T(8,128)(2,1)}), bf16[2048,1024]{0,1:T(8,128)(2,1)}) %all-gather.19.cloned.1.call-update) | async-done | bytes 4194320 | tf_op jit(solution)/shard_map/all_gather | solution.py:86
  542.3 22.3 %fusion.58 = bf16[1024,2,2048]{2,0,1:T(8,128)(2,1)S(1)} fusion(f32[1024,2,2048]{2,0,1:T(8,128)} %fusion.93, bf16[1024,2,1024]{2,0,1:T(8,128)(2,1)} %all-gather.21.cloned.1.call-done, bf16[2048,1024]{0,1:T(8,128)(2,1)} %all-gather.19.cloned.1.call-done), kind=kOutput, calls=%fused_computation.68 | convolution fusion | flops 8673820672 | bytes 33554432 | tf_op jit(solution)/shard_map/tgd,fd->tgf/dot_general | solution.py:134
  567.8 10.9 fusion.101
  578.8 52.9 %reduce-scatter.12.cloned.1.call-done = bf16[512,2,1024]{2,0,1:T(8,128)(2,1)} async-done(((bf16[1024,2,1024]{2,0,1:T(8,128)(2,1)}), bf16[512,2,1024]{2,0,1:T(8,128)(2,1)}) %reduce-scatter.12.cloned.1.call-update) | async-done | bytes 2097168 | tf_op jit(solution)/shard_map/reduce_scatter | solution.py:141
  639.5 16.0 %bitcast_convert_fusion = bf16[2048,1024]{0,1:T(8,128)(2,1)} fusion(bf16[1024,2,1024]{2,0,1:T(8,128)(2,1)} %all-gather.21.cloned.1.call-done, f32[1024,2,2048]{2,0,1:T(8,128)} %fusion.93), kind=kOutput, calls=%fused_computation.70 | convolution fusion | flops 8629780480 | bytes 25165824 | tf_op jit(solution)/shard_map/tgf,tgd->fd/dot_general | solution.py:133
  655.6 14.1 %bitcast_convert_fusion.1 = bf16[1024,2048]{1,0:T(8,128)(2,1)} fusion(bf16[1024,2,1024]{2,0,1:T(8,128)(2,1)} %all-gather.15.cloned.1.call-done, bf16[1024,2,2048]{2,0,1:T(8,128)(2,1)} %copy-done.32), kind=kOutput, calls=%fused_computation.71 | convolution fusion | flops 8592031744 | bytes 16777216 | tf_op jit(solution)/shard_map/tgd,tgf->df/dot_general | solution.py:139
  669.8 26.6 %all-gather.23.cloned.1.call-done = bf16[1024,2,1024]{2,0,1:T(8,128)(2,1)} async-done(((bf16[512,2,1024]{2,0,1:T(8,128)(2,1)}), bf16[1024,2,1024]{2,0,1:T(8,128)(2,1)}) %all-gather.23.cloned.1.call-update) | async-done | bytes 4194320 | tf_op jit(solution)/shard_map/all_gather | solution.py:154
  696.4 5.9 convolution_convert_fusion
  702.3 220.0 %while.23 = (s32[]{:T(128)}, bf16[2,3,1024,8,64]{2,4,3,1,0:T(8,128)(2,1)}, bf16[2,1024,8,64]{1,3,2,0:T(8,128)(2,1)S(1)}, bf16[2,1024,8,64]{1,3,2,0:T(8,128)(2,1)...) while((s32[]{:T(128)}, ...), condition=%wide.region_15.16_spmd, body=%wide.region_13.15_spmd.sunk | while | flops 5507637248 | bytes 272861280 | solution.py:159
  703.1 16.0 %fusion.156 = f32[8,1024,1024]{1,2,0:T(8,128)} fusion(bf16[2,1024,8,64]{1,3,2,0:T(8,128)(2,1)} %get-tuple-element.288, s32[]{:T(128)S(6)} %copy.101, bf16[2,1024,8,64]{1,3,2,0:T(8,128)(2,1)S(1)} %get-tuple-element.287), kind=kOutput, calls=%fused_computation.41.clone.1 | convolution fusion | flops 1073741824 | bytes 35652608 | tf_op jit(solution)/shard_map/while/body/eval_jaxpr/qhd,khd->hqk/dot_general | solution.py:53
  719.1 16.4 %fusion.157 = bf16[1,1,1024,8,64]{2,4,3,1,0:T(8,128)(2,1)} fusion(f32[8,1024,1024]{1,2,0:T(8,128)} %fusion.156, f32[8,1024]{1,0:T(8,128)S(1)} %dynamic-slice_bitcast_fusion.2, pred[1024,1024]{0,1:T(8,128)(4,1)S(1)} %iota_compare_fusion.5, bf16[2,1024,8,64]{1,3,2,0:T(8,128)(2,1)} %get-tuple-element.290, s32[]{:T(128)S(6)} %copy.101), kind=kOutput, calls=%fused_computation.35.clone.1 | convolution fusion | flops 1107820544 | bytes 36732932 | tf_op jit(solution)/shard_map/while/body/eval_jaxpr/hqk,qhd->khd/dot_general | solution.py:57
  735.5 24.0 %multiply_reduce_fusion.3 = (f32[8,1024]{1,0:T(8,128)S(1)}, f32[8,1024,1024]{1,2,0:T(8,128)}) fusion(f32[8,1024,1024]{1,2,0:T(8,128)} %fusion.156, f32[8,1024]{1,0:T(8,128)S(1)} %dynamic-slice_bitcast_fusion.2, pred[1024,1024]{0,1:T(8,128)(4,1)S(1)} %iota_compare_fusion.5, bf16[2,1024,8,64]{1,3,2,0:T(8,128)(2,1)} %get-tuple-element.291, ...), kind=kOutput, calls=%fused_computation.23.clone.1 | convolution fusion | flops 1115676672 | bytes 70321152 | tf_op jit(solution)/shard_map/while/body/eval_jaxpr/qhd,khd->hqk/dot_general | solution.py:60
  759.5 29.1 %multiply_convert_fusion.7 = bf16[8,1024,1024]{1,2,0:T(8,128)(2,1)} fusion(f32[8,1024,1024]{1,2,0:T(8,128)} %get-tuple-element.246, f32[8,1024,1024]{1,2,0:T(8,128)} %fusion.156, f32[8,1024]{1,0:T(8,128)S(1)} %get-tuple-element.247, f32[8,1024]{1,0:T(8,128)S(1)} %dynamic-slice_bitcast_fusion.2, pred[1024,1024]{0,1:T(8,128)(4,1)S(1)} %iota_compare_fusion.5), kind=kLoop, calls=%fused_computation.22.clone.1 | loop fusion | flops 50331648 | bytes 85000192 | tf_op jit(solution)/shard_map/while/body/eval_jaxpr/convert_element_type | solution.py:64
  788.6 9.6 fusion.159
  798.2 12.3 fusion.158
  814.4 14.6 %fusion.156 = f32[8,1024,1024]{1,2,0:T(8,128)} fusion(bf16[2,1024,8,64]{1,3,2,0:T(8,128)(2,1)} %get-tuple-element.288, s32[]{:T(128)S(6)} %copy.101, bf16[2,1024,8,64]{1,3,2,0:T(8,128)(2,1)S(1)} %get-tuple-element.287), kind=kOutput, calls=%fused_computation.41.clone.1 | convolution fusion | flops 1073741824 | bytes 35652608 | tf_op jit(solution)/shard_map/while/body/eval_jaxpr/qhd,khd->hqk/dot_general | solution.py:53
  829.0 16.2 %fusion.157 = bf16[1,1,1024,8,64]{2,4,3,1,0:T(8,128)(2,1)} fusion(f32[8,1024,1024]{1,2,0:T(8,128)} %fusion.156, f32[8,1024]{1,0:T(8,128)S(1)} %dynamic-slice_bitcast_fusion.2, pred[1024,1024]{0,1:T(8,128)(4,1)S(1)} %iota_compare_fusion.5, bf16[2,1024,8,64]{1,3,2,0:T(8,128)(2,1)} %get-tuple-element.290, s32[]{:T(128)S(6)} %copy.101), kind=kOutput, calls=%fused_computation.35.clone.1 | convolution fusion | flops 1107820544 | bytes 36732932 | tf_op jit(solution)/shard_map/while/body/eval_jaxpr/hqk,qhd->khd/dot_general | solution.py:57
  845.2 23.8 %multiply_reduce_fusion.3 = (f32[8,1024]{1,0:T(8,128)S(1)}, f32[8,1024,1024]{1,2,0:T(8,128)}) fusion(f32[8,1024,1024]{1,2,0:T(8,128)} %fusion.156, f32[8,1024]{1,0:T(8,128)S(1)} %dynamic-slice_bitcast_fusion.2, pred[1024,1024]{0,1:T(8,128)(4,1)S(1)} %iota_compare_fusion.5, bf16[2,1024,8,64]{1,3,2,0:T(8,128)(2,1)} %get-tuple-element.291, ...), kind=kOutput, calls=%fused_computation.23.clone.1 | convolution fusion | flops 1115676672 | bytes 70321152 | tf_op jit(solution)/shard_map/while/body/eval_jaxpr/qhd,khd->hqk/dot_general | solution.py:60
  869.0 28.5 %multiply_convert_fusion.7 = bf16[8,1024,1024]{1,2,0:T(8,128)(2,1)} fusion(f32[8,1024,1024]{1,2,0:T(8,128)} %get-tuple-element.246, f32[8,1024,1024]{1,2,0:T(8,128)} %fusion.156, f32[8,1024]{1,0:T(8,128)S(1)} %get-tuple-element.247, f32[8,1024]{1,0:T(8,128)S(1)} %dynamic-slice_bitcast_fusion.2, pred[1024,1024]{0,1:T(8,128)(4,1)S(1)} %iota_compare_fusion.5), kind=kLoop, calls=%fused_computation.22.clone.1 | loop fusion | flops 50331648 | bytes 85000192 | tf_op jit(solution)/shard_map/while/body/eval_jaxpr/convert_element_type | solution.py:64
  897.5 8.8 fusion.159
  906.3 12.3 fusion.158
  922.3 10.0 fusion.98
  938.2 6.3 bitcast_convert_fusion.4
  944.6 11.2 fusion.83
  955.9 16.6 %fusion.104 = bf16[1024,2,1024]{2,0,1:T(8,128)(2,1)} fusion(bf16[2048,1024]{0,1:T(8,128)(2,1)} %all-gather.19.cloned.1.call-done, f32[1024,2,2048]{2,0,1:T(8,128)} %fusion.93), kind=kOutput, calls=%fused_computation.128 | convolution fusion | flops 8629780480 | bytes 25165824 | tf_op jit(solution)/shard_map/tgf,fd->tgd/dot_general | solution.py:124
  978.9 70.7 %all-reduce.14.cloned.1.call-done = bf16[3,1024,512]{2,0,1:T(4,128)(2,1)} async-done(((bf16[3,1024,512]{2,0,1:T(4,128)(2,1)}), bf16[3,1024,512]{2,0,1:T(4,128)(2,1)}) %all-reduce.14.cloned.1.call-update) | async-done | bytes 3145744
  1051.5 59.0 %reduce-scatter.16.cloned.1.call-done = bf16[512,64]{0,1:T(8,128)(2,1)} async-done(((bf16[512,1024]{0,1:T(8,128)(2,1)}), bf16[512,64]{0,1:T(8,128)(2,1)}) %reduce-scatter.16.cloned.1.call-update) | async-done | bytes 65552 | tf_op jit(solution)/shard_map/reduce_scatter | solution.py:196
  1111.9 54.0 %reduce-scatter.14.cloned.1.call-done = bf16[512,2,1024]{2,0,1:T(8,128)(2,1)} async-done(((bf16[1024,2,1024]{2,0,1:T(8,128)(2,1)}), bf16[512,2,1024]{2,0,1:T(8,128)(2,1)}) %reduce-scatter.14.cloned.1.call-update) | async-done | bytes 2097168 | tf_op jit(solution)/shard_map/reduce_scatter | solution.py:174
  1171.5 33.9 %all-reduce.10 = (bf16[1024]{0:T(1024)(128)(2,1)S(1)}, bf16[1024]{0:T(1024)(128)(2,1)S(1)}, bf16[1024]{0:T(1024)(128)(2,1)S(1)}, bf16[1024]{0:T(1024)(128)(2,1)S(1)}) all-reduce(bf16[1024]{0:T(1024)(128)(2,1)S(1)} %get-tuple-element.105, bf16[1024]{0:T(1024)(128)(2,1)S(1)} %reduce_sum.141, ...), channel_id=6, replica_groups=mesh['dp'=16,'tensor'=2] {'dp'}, use_global_device_ids=true, to_apply=%region_20.21.clone | all-reduce | flops 4096 | bytes 16384
  1205.7 16.8 %reduce-scatter.10.cloned.1.call-done = bf16[512,2,1024]{2,0,1:T(8,128)(2,1)} async-done(((bf16[1024,2,1024]{2,0,1:T(8,128)(2,1)}), bf16[512,2,1024]{2,0,1:T(8,128)(2,1)}) %reduce-scatter.10.cloned.1.call-update) | async-done | bytes 2097168 | tf_op jit(solution)/shard_map/reduce_scatter | solution.py:123
  1222.5 6.6 fusion.74
  (162 shorter events, 81.6 us)
Async XLA Ops:
  7.2 46.7 %copy-start = (bf16[512,2,1024]{2,1,0:T(2,128)(2,1)S(1)}, bf16[512,2,1024]{2,1,0:T(2,128)(2,1)}, u32[]{:S(2)}) copy-start(bf16[512,2,1024]{2,1,0:T(2,128)(2,1)} %param.14) | copy-start | bytes 6291460
  7.2 103.1 %all-gather.9.cloned.1.call-start = ((), (), s32[]{:S(2)}) async-start(), calls=%async_computation.7 | async-start | bytes 6291456 | tf_op jit(solution)/shard_map/all_gather | solution.py:96
  48.7 4.7 copy-start.18
  50.9 2.4 copy-start.16
  56.1 101.6 %all-gather.11.cloned.1.call-start = ((), (), s32[]{:S(2)}) async-start(), calls=%async_computation.8 | async-start | bytes 3342336 | tf_op jit(solution)/shard_map/all_gather | solution.py:81
  56.9 203.5 %all-gather.13.cloned.1.call-start = ((), (), s32[]{:S(2)}) async-start(), calls=%async_computation.9 | async-start | bytes 1114112 | tf_op jit(solution)/shard_map/all_gather | solution.py:82
  57.6 263.7 %reduce-scatter.8.cloned.1.call-start = ((), (), s32[]{:S(2)}) async-start(), calls=%async_computation.10 | async-start | bytes 6291456 | tf_op jit(solution)/shard_map/reduce_scatter | solution.py:107
  185.5 14.4 %copy-start.8 = (bf16[2,1024,8,64]{1,3,2,0:T(8,128)(2,1)S(1)}, bf16[2,1024,8,64]{1,3,2,0:T(8,128)(2,1)}, u32[]{:S(2)}) copy-start(bf16[2,1024,8,64]{1,3,2,0:T(8,128)(2,1)} %get-tuple-element.265) | copy-start | bytes 6291460 | tf_op jit(solution)/shard_map/while
  230.4 14.4 %copy-start.8 = (bf16[2,1024,8,64]{1,3,2,0:T(8,128)(2,1)S(1)}, bf16[2,1024,8,64]{1,3,2,0:T(8,128)(2,1)}, u32[]{:S(2)}) copy-start(bf16[2,1024,8,64]{1,3,2,0:T(8,128)(2,1)} %get-tuple-element.265) | copy-start | bytes 6291460 | tf_op jit(solution)/shard_map/while
  260.4 1.3 copy-start.3
  268.1 0.7 copy-start.27
  268.1 53.3 %copy-start.1 = (bf16[512,2,1024]{2,1,0:T(2,128)(2,1)S(1)}, bf16[512,2,1024]{2,1,0:T(2,128)(2,1)}, u32[]{:S(2)}) copy-start(bf16[512,2,1024]{2,1,0:T(2,128)(2,1)} %param.14) | copy-start | bytes 6291460
  268.1 106.1 %all-gather.17.cloned.1.call-start = ((), (), s32[]{:S(2)}) async-start(), calls=%async_computation.12 | async-start | bytes 4456448 | tf_op jit(solution)/shard_map/all_gather | solution.py:85
  268.7 162.2 %all-gather.15.cloned.1.call-start = ((), (), s32[]{:S(2)}) async-start(), calls=%async_computation.11 | async-start | bytes 6291456 | tf_op jit(solution)/shard_map/all_gather | solution.py:119
  268.8 367.8 %copy-start.12 = (f32[1024]{0:T(1024)}, f32[1024]{0:T(1024)S(1)}, u32[]{:S(2)}) copy-start(f32[1024]{0:T(1024)S(1)} %convert_element_type.162) | copy-start | bytes 12292
  321.3 2.5 copy-start.5
  323.8 312.7 %copy-start.10 = (f32[512,2]{0,1:T(2,128)}, f32[512,2]{0,1:T(2,128)S(1)}, u32[]{:S(2)}) copy-start(f32[512,2]{0,1:T(2,128)S(1)} %broadcast_multiply_fusion.4) | copy-start | bytes 12292
  324.8 311.8 %copy-start.14 = (f32[512,2]{0,1:T(2,128)}, f32[512,2]{0,1:T(2,128)S(1)}, u32[]{:S(2)}) copy-start(f32[512,2]{0,1:T(2,128)S(1)} %add_rsqrt_fusion) | copy-start | bytes 12292
  326.9 162.4 %all-gather.21.cloned.1.call-start = ((), (), s32[]{:S(2)}) async-start(), calls=%async_computation.15 | async-start | bytes 6291456 | tf_op jit(solution)/shard_map/all_gather | solution.py:132
  330.5 211.8 %all-gather.19.cloned.1.call-start = ((), (), s32[]{:S(2)}) async-start(), calls=%async_computation.13 | async-start | bytes 4456448 | tf_op jit(solution)/shard_map/all_gather | solution.py:86
  331.3 300.4 %reduce-scatter.12.cloned.1.call-start = ((), (), s32[]{:S(2)}) async-start(), calls=%async_computation.16 | async-start | bytes 6291456 | tf_op jit(solution)/shard_map/reduce_scatter | solution.py:141
  542.3 25.5 %copy-start.29 = (bf16[1024,2048]{1,0:T(8,128)(2,1)S(1)}, bf16[1024,2048]{1,0:T(8,128)(2,1)}, u32[]{:S(2)}) copy-start(bf16[1024,2048]{1,0:T(8,128)(2,1)} %all-gather.17.cloned.1.call-done) | copy-start | bytes 12582916
  564.6 3.2 copy-start.32
  578.8 117.6 %all-gather.23.cloned.1.call-start = ((), (), s32[]{:S(2)}) async-start(), calls=%async_computation.17 | async-start | bytes 6291456 | tf_op jit(solution)/shard_map/all_gather | solution.py:154
  631.7 4.9 copy-start.6
  631.7 4.9 copy-start.7
  631.7 4.9 copy-start.9
  636.5 2.9 copy-start.22
  636.5 2.9 copy-start.24
  639.5 333.9 %reduce-scatter.20.cloned.1.call-start = ((), (), s32[]{:S(2)}) async-start(), calls=%async_computation.21 | async-start | bytes 4456448 | tf_op jit(solution)/shard_map/reduce_scatter | solution.py:208
  655.6 319.6 %reduce-scatter.18.cloned.1.call-start = ((), (), s32[]{:S(2)}) async-start(), calls=%async_computation.20 | async-start | bytes 4456448 | tf_op jit(solution)/shard_map/reduce_scatter | solution.py:205
  669.7 26.7 %copy-start.31 = (bf16[512,1024]{0,1:T(8,128)(2,1)S(1)}, bf16[512,1024]{0,1:T(8,128)(2,1)}, u32[]{:S(2)}) copy-start(bf16[512,1024]{0,1:T(8,128)(2,1)} %all-gather.13.cloned.1.call-done) | copy-start | bytes 3145732
  669.7 32.6 %copy-start.4 = (bf16[2,1024,8,64]{1,3,2,0:T(8,128)(2,1)S(1)}, bf16[2,1024,8,64]{1,3,2,0:T(8,128)(2,1)}, u32[]{:S(2)}) copy-start(bf16[2,1024,8,64]{1,3,2,0:T(8,128)(2,1)} %copy-done.3) | copy-start | bytes 6291460
  669.7 379.9 %all-reduce.14.cloned.1.call-start = ((), (), s32[]{:S(2)}) async-start(), calls=%async_computation.22 | async-start | bytes 8388608
  938.2 6.5 copy-start.30
  938.2 172.3 %reduce-scatter.16.cloned.1.call-start = ((), (), s32[]{:S(2)}) async-start(), calls=%async_computation.19 | async-start | bytes 1114112 | tf_op jit(solution)/shard_map/reduce_scatter | solution.py:196
  944.6 221.4 %reduce-scatter.14.cloned.1.call-start = ((), (), s32[]{:S(2)}) async-start(), calls=%async_computation.18 | async-start | bytes 6291456 | tf_op jit(solution)/shard_map/reduce_scatter | solution.py:174
  955.8 266.7 %reduce-scatter.10.cloned.1.call-start = ((), (), s32[]{:S(2)}) async-start(), calls=%async_computation.14 | async-start | bytes 6291456 | tf_op jit(solution)/shard_map/reduce_scatter | solution.py:123
  972.5 195.4 %copy-start.2 = (bf16[512,2,1024]{2,1,0:T(2,128)(2,1)S(1)}, bf16[512,2,1024]{2,1,0:T(2,128)(2,1)}, u32[]{:S(2)}) copy-start(bf16[512,2,1024]{2,1,0:T(2,128)(2,1)} %param.14) | copy-start | bytes 6291460
  972.5 195.4 %copy-start.17 = (f32[512,2]{0,1:T(2,128)S(1)}, f32[512,2]{0,1:T(2,128)}, u32[]{:S(2)}) copy-start(f32[512,2]{0,1:T(2,128)} %copy-done.16) | copy-start | bytes 12292
  972.5 195.4 %copy-start.19 = (f32[1024]{0:T(1024)S(1)}, f32[1024]{0:T(1024)}, u32[]{:S(2)}) copy-start(f32[1024]{0:T(1024)} %copy-done.18) | copy-start | bytes 12292
  972.5 195.4 %copy-start.21 = (f32[512,2]{0,1:T(2,128)S(1)}, f32[512,2]{0,1:T(2,128)}, u32[]{:S(2)}) copy-start(f32[512,2]{0,1:T(2,128)} %copy-done.20) | copy-start | bytes 12292
  978.9 192.6 %copy-start.26 = (bf16[1024]{0:T(1024)(128)(2,1)S(1)}, bf16[1024]{0:T(1024)(128)(2,1)}, u32[]{:S(2)}) copy-start(bf16[1024]{0:T(1024)(128)(2,1)} %get-tuple-element.103) | copy-start | bytes 6148
  978.9 243.6 %copy-start.11 = (f32[512,2]{0,1:T(2,128)S(1)}, f32[512,2]{0,1:T(2,128)}, u32[]{:S(2)}) copy-start(f32[512,2]{0,1:T(2,128)} %copy-done.10) | copy-start | bytes 12292
  978.9 243.6 %copy-start.13 = (f32[1024]{0:T(1024)S(1)}, f32[1024]{0:T(1024)}, u32[]{:S(2)}) copy-start(f32[1024]{0:T(1024)} %copy-done.12) | copy-start | bytes 12292
  978.9 243.6 %copy-start.15 = (f32[512,2]{0,1:T(2,128)S(1)}, f32[512,2]{0,1:T(2,128)}, u32[]{:S(2)}) copy-start(f32[512,2]{0,1:T(2,128)} %copy-done.14) | copy-start | bytes 12292
  978.9 243.6 %copy-start.23 = (f32[512,2]{0,1:T(2,128)S(1)}, f32[512,2]{0,1:T(2,128)}, u32[]{:S(2)}) copy-start(f32[512,2]{0,1:T(2,128)} %copy-done.22) | copy-start | bytes 12292
  978.9 243.6 %copy-start.25 = (f32[512,2]{0,1:T(2,128)S(1)}, f32[512,2]{0,1:T(2,128)}, u32[]{:S(2)}) copy-start(f32[512,2]{0,1:T(2,128)} %copy-done.24) | copy-start | bytes 12292
  (2 other events, 1.3 us)
Sparse Core Ops, SparseCore 0:
  56.3 53.9 all-gather.8
  112.5 45.2 all-gather.10
  159.9 36.7 all-gather.12
  268.2 53.0 reduce-scatter.7
  323.6 50.5 all-gather.16
  375.6 55.2 all-gather.14
  432.5 56.7 all-gather.20
  491.7 50.5 all-gather.18
  578.9 52.7 reduce-scatter.11
  639.6 56.7 all-gather.22
  700.3 72.4 reduce-scatter.19
  777.0 71.4 reduce-scatter.17
  938.3 111.2 all-reduce.13
  1054.1 56.2 reduce-scatter.15
  1112.6 53.3 reduce-scatter.13
  1168.2 54.2 reduce-scatter.9
where the time goes:
time: 1250 us
  waiting for transfers between devices  631 us (50%)
  matrix products  359 us (29%)
  other arithmetic  135 us (11%)
  blocking collectives  75.3 us (6%)
  local copies, waits for them, and re-layouts  30.2 us (2%)
  between operations  16.1 us (1%)
    unnamed x17, waiting for transfers between devices  73.5 us
    unnamed x2, blocking collectives  69.9 us
    reduce_scatter x1, waiting for transfers between devices, on_device(): lax.psum_scatter(grad_out.astype(jnp.bfloat16), 'dp', scatter_dimension=1...  59 us
    convert_element_type x2, other arithmetic, attend_back(): grad_scores = (shares * (grad_shares - inner)).astype(jnp.bfloat16)  57.6 us
    all_gather x1, waiting for transfers between devices, on_device(): rows_two = lax.all_gather(low_two, 'tensor', axis=0, tiled=True)  56.7 us
    reduce_scatter x1, waiting for transfers between devices, on_device(): lax.psum_scatter(jnp.einsum('gcte,cde->tgd', piece_rows, qkv_weight, pref...  54 us
    all_gather x1, waiting for transfers between devices, on_device(): lax.all_gather(w_down, 'dp', axis=1, tiled=True)  53 us
    reduce_scatter x1, waiting for transfers between devices, on_device(): lax.psum_scatter(jnp.einsum('tgf,df->tgd', piece_rows, up_weight, preferr...  52.9 us
  transfers between devices with their start and end apart: 16, of which 13 were waited for; matrix products, arithmetic and copies ran while one was open for 36% of the time, Pallas kernels for 0%

commit v1 on v0

--- a/solution.py
+++ b/solution.py
@@ -1,6 +1,11 @@
+import functools
+import math
+
 import jax
 import jax.numpy as jnp
 from jax import lax
+from jax.experimental import pallas as pl
+from jax.experimental.pallas import tpu as pltpu
 from jax.sharding import PartitionSpec as P
 
 HEAD_DIM = 64
@@ -73,7 +78,7 @@
     return jnp.stack([grad_query, grad_key, grad_value]).astype(jnp.bfloat16)
 
 
-def on_device(tokens, d_out, ln1_gain, ln1_bias, w_qkv, w_out, ln2_gain, ln2_bias, w_up, w_down):
+def on_device_shared(tokens, d_out, ln1_gain, ln1_bias, w_qkv, w_out, ln2_gain, ln2_bias, w_up, w_down):
     local_rows, seq_count, width = tokens.shape
     gathered = (
         lax.all_gather(ln1_gain, "dp", axis=0, tiled=True),
@@ -224,7 +229,392 @@
     )
 
 
+LOG2E = 1.4426950408889634
+BLOCK = 256
+NT = (((1,), (1,)), ((), ()))
+TN = (((0,), (0,)), ((), ()))
+NN = (((1,), (0,)), ((), ()))
+
+
+def mul(left, right, dims=NN):
+    return lax.dot_general(left, right, dims, preferred_element_type=jnp.float32)
+
+
+def fwd_kernel(q_ref, k_ref, v_ref, o_ref, lse_ref):
+    length = q_ref.shape[0]
+    scale = LOG2E * HEAD_DIM**-0.5
+    block = min(BLOCK, length)
+    keep = lax.broadcasted_iota(jnp.int32, (block, block), 1) <= lax.broadcasted_iota(
+        jnp.int32, (block, block), 0
+    )
+    heads = q_ref.shape[1] // HEAD_DIM
+    for i in range(length // block):
+        rows = slice(i * block, (i + 1) * block)
+        outs = []
+        for h in range(heads):
+            cols = slice(h * HEAD_DIM, (h + 1) * HEAD_DIM)
+            q = q_ref[rows, cols]
+            diag = jnp.where(keep, mul(q, k_ref[rows, cols], NT), -1e30)
+            top = jnp.max(diag, axis=1, keepdims=True)
+            if i > 0:
+                past = mul(q, k_ref[: i * block, cols], NT)
+                top = jnp.maximum(top, jnp.max(past, axis=1, keepdims=True))
+            shift = top * scale
+            w = jnp.exp2(diag * scale - shift)
+            total = jnp.sum(w, axis=1, keepdims=True)
+            out = mul(w.astype(jnp.bfloat16), v_ref[rows, cols])
+            if i > 0:
+                w = jnp.exp2(past * scale - shift)
+                total = total + jnp.sum(w, axis=1, keepdims=True)
+                out = out + mul(w.astype(jnp.bfloat16), v_ref[: i * block, cols])
+            outs.append(out / total)
+            lse = shift + jnp.log2(total)
+            lse_ref[0, h : h + 1, rows] = jnp.broadcast_to(lse, (block, 128)).T[:1]
+        o_ref[rows, :] = jnp.concatenate(outs, axis=1).astype(jnp.bfloat16)
+
+
+def attend(qkv):
+    length, width3 = qkv.shape
+    width = width3 // 3
+    pairs = width // 128
+    return pl.pallas_call(
+        fwd_kernel,
+        grid=(pairs,),
+        in_specs=[
+            pl.BlockSpec((length, 128), lambda j: (0, j)),
+            pl.BlockSpec((length, 128), lambda j: (0, pairs + j)),
+            pl.BlockSpec((length, 128), lambda j: (0, 2 * pairs + j)),
+        ],
+        out_specs=[
+            pl.BlockSpec((length, 128), lambda j: (0, j)),
+            pl.BlockSpec((1, 8, length), lambda j: (j, 0, 0)),
+        ],
+        out_shape=[
+            jax.ShapeDtypeStruct((length, width), jnp.bfloat16),
+            jax.ShapeDtypeStruct((pairs, 8, length), jnp.float32),
+        ],
+        compiler_params=pltpu.CompilerParams(vmem_limit_bytes=40 * 2**20),
+        cost_estimate=pl.CostEstimate(
+            flops=8 * length * length * width, bytes_accessed=8 * length * width, transcendentals=0
+        ),
+    )(qkv, qkv, qkv)
+
+
+def back_kernel(q_ref, k_ref, v_ref, do_ref, o_ref, lse_ref, dqkv_ref):
+    length = q_ref.shape[0]
+    width = dqkv_ref.shape[1] // 3
+    factor = HEAD_DIM**-0.5
+    scale = LOG2E * factor
+    block = min(BLOCK, length)
+    keep = lax.broadcasted_iota(jnp.int32, (block, block), 0) <= lax.broadcasted_iota(
+        jnp.int32, (block, block), 1
+    )
+    count = length // block
+    heads = q_ref.shape[1] // HEAD_DIM
+    col = pl.program_id(0) * 128
+    both = do_ref[...].astype(jnp.float32) * o_ref[...].astype(jnp.float32)
+    both = both.T
+    deltas = [
+        jnp.sum(both[h * HEAD_DIM : (h + 1) * HEAD_DIM], axis=0, keepdims=True)
+        for h in range(heads)
+    ]
+    dqs = [[None] * count for _ in range(heads)]
+    for j in range(count):
+        rows = slice(j * block, (j + 1) * block)
+        dks, dvs = [], []
+        for h in range(heads):
+            cols = slice(h * HEAD_DIM, (h + 1) * HEAD_DIM)
+            k, v = k_ref[rows, cols], v_ref[rows, cols]
+            q, do = q_ref[j * block :, cols], do_ref[j * block :, cols]
+            lse = lse_ref[0, h : h + 1, j * block :]
+            w = jnp.exp2(mul(k, q, NT) * scale - lse)
+            if j + 1 < count:
+                w = jnp.concatenate([jnp.where(keep, w[:, :block], 0.0), w[:, block:]], axis=1)
+            else:
+                w = jnp.where(keep, w, 0.0)
+            ds = (w * (mul(v, do, NT) - deltas[h][:, j * block :])).astype(jnp.bfloat16)
+            dvs.append(mul(w.astype(jnp.bfloat16), do))
+            dks.append(mul(ds, q) * factor)
+            dq = mul(ds, k, TN)
+            for i in range(j, count):
+                part = dq[(i - j) * block : (i - j + 1) * block]
+                dqs[h][i] = part if dqs[h][i] is None else dqs[h][i] + part
+        dqkv_ref[rows, pl.ds(pl.multiple_of(width + col, 128), 128)] = jnp.concatenate(
+            dks, axis=1
+        ).astype(jnp.bfloat16)
+        dqkv_ref[rows, pl.ds(pl.multiple_of(2 * width + col, 128), 128)] = jnp.concatenate(
+            dvs, axis=1
+        ).astype(jnp.bfloat16)
+        dqkv_ref[rows, pl.ds(pl.multiple_of(col, 128), 128)] = (
+            jnp.concatenate([dqs[h][j] for h in range(heads)], axis=1) * factor
+        ).astype(jnp.bfloat16)
+
+
+def attend_grad(qkv, grad_mixed, mixed, lse):
+    length, width3 = qkv.shape
+    width = width3 // 3
+    pairs = width // 128
+    return pl.pallas_call(
+        back_kernel,
+        grid=(pairs,),
+        in_specs=[
+            pl.BlockSpec((length, 128), lambda j: (0, j)),
+            pl.BlockSpec((length, 128), lambda j: (0, pairs + j)),
+            pl.BlockSpec((length, 128), lambda j: (0, 2 * pairs + j)),
+            pl.BlockSpec((length, 128), lambda j: (0, j)),
+            pl.BlockSpec((length, 128), lambda j: (0, j)),
+            pl.BlockSpec((1, 8, length), lambda j: (j, 0, 0)),
+        ],
+        out_specs=pl.BlockSpec((length, width3), lambda j: (0, 0)),
+        out_shape=jax.ShapeDtypeStruct((length, width3), jnp.bfloat16),
+        compiler_params=pltpu.CompilerParams(vmem_limit_bytes=40 * 2**20),
+        cost_estimate=pl.CostEstimate(
+            flops=20 * length * length * width, bytes_accessed=16 * length * width, transcendentals=0
+        ),
+    )(qkv, qkv, qkv, grad_mixed, mixed, lse)
+
+
+def swap_dp(array, size, mask):
+    return lax.ppermute(array, "dp", [(i, i ^ mask) for i in range(size)])
+
+
+def swap_tensor(array):
+    return lax.ppermute(array, "tensor", [(0, 1), (1, 0)])
+
+
+def gather_pair(shard, size, tensor_first, axis=0):
+    def grow(array, mask):
+        return jnp.concatenate([array, swap_dp(array, size, mask)], axis=axis)
+
+    mask = size // 2
+    own = shard
+    while mask >= 4:
+        own = grow(own, mask)
+        mask //= 2
+    if tensor_first:
+        other = swap_tensor(own)
+        own, other = grow(own, 2), grow(other, 2)
+    else:
+        own = grow(own, 2)
+        other = swap_tensor(own)
+    return grow(own, 1), grow(other, 1)
+
+
+def add_low(left, right):
+    return (left.astype(jnp.float32) + right.astype(jnp.float32)).astype(jnp.bfloat16)
+
+
+def scatter_pair(rows, own, other, size, tensor_first):
+    half = rows.shape[1] // 2
+
+    def core_sum(columns):
+        away = mul(rows[:, half:], columns, TN).astype(jnp.bfloat16)
+        arrived = swap_dp(away, size, 1)
+        return (mul(rows[:, :half], columns, TN) + arrived.astype(jnp.float32)).astype(jnp.bfloat16)
+
+    def fold(array, mask):
+        middle = array.shape[0] // 2
+        return array[:middle], swap_dp(array[middle:], size, mask)
+
+    own, other = core_sum(own), core_sum(other)
+    if tensor_first:
+        own = add_low(own, swap_tensor(other))
+        own = add_low(*fold(own, 2))
+    else:
+        own, other = add_low(*fold(own, 2)), add_low(*fold(other, 2))
+        own = add_low(own, swap_tensor(other))
+    mask = 4
+    while mask < size:
+        kept, arrived = fold(own, mask)
+        mask *= 2
+        if mask < size:
+            own = add_low(kept, arrived)
+        else:
+            own = kept.astype(jnp.float32) + arrived.astype(jnp.float32)
+    return own
+
+
+def norm_rows_grad(grad_in, normal, inverse, norm_gain):
+    gain_grad = jnp.sum(grad_in * normal, axis=0, keepdims=True)
+    bias_grad = jnp.sum(grad_in, axis=0, keepdims=True)
+    scaled = grad_in * norm_gain
+    first = jnp.mean(scaled, axis=-1, keepdims=True)
+    second = jnp.mean(scaled * normal, axis=-1, keepdims=True)
+    return (inverse * (scaled - first - normal * second), gain_grad, bias_grad)
+
+
+def block_order(size, width):
+    block = width // size
+    here = lax.axis_index("dp")
+    column = lax.broadcasted_iota(jnp.int32, (width, width), 1)
+    place, inside = column // block, column % block
+    source = here
+    bit, value = size // 2, 1
+    while bit >= 1:
+        source = source ^ jnp.where((place // bit) % 2 == 1, value, 0)
+        bit //= 2
+        value *= 2
+    row = lax.broadcasted_iota(jnp.int32, (width, width), 0)
+    return (row == source * block + inside).astype(jnp.bfloat16)
+
+
+def gelu_both(u):
+    inner = math.sqrt(2 / math.pi)
+    t = jnp.tanh(inner * (u + 0.044715 * u * u * u))
+    slope = 0.5 * (1.0 + t) + 0.5 * u * (1.0 - t * t) * inner * (1.0 + 3 * 0.044715 * u * u)
+    return 0.5 * u * (1.0 + t), slope
+
+
+def on_device_whole(
+    size, tokens, d_out, ln1_gain, ln1_bias, w_qkv, w_out, ln2_gain, ln2_bias, w_up, w_down
+):
+    half_rows, _, width = tokens.shape
+    me = lax.axis_index("tensor")
+    first = me == 0
+    order = block_order(size, width)
+
+    def assemble(array):
+        ours = jnp.where(first, array[:, 0], array[:, 1])
+        away = jnp.where(first, array[:, 1], array[:, 0])
+        arrived = swap_tensor(away)
+        rows = jnp.concatenate(
+            [jnp.where(first, ours, arrived), jnp.where(first, arrived, ours)], axis=0
+        )
+        return mul(rows, order).astype(jnp.bfloat16)
+
+    def disperse(rows):
+        rows = mul(rows, order, NT).astype(jnp.bfloat16)
+        ours = jnp.where(first, rows[:half_rows], rows[half_rows:])
+        away = jnp.where(first, rows[half_rows:], rows[:half_rows])
+        arrived = swap_tensor(away)
+        return jnp.stack(
+            [jnp.where(first, ours, arrived), jnp.where(first, arrived, ours)], axis=1
+        )
+
+    local_width = w_qkv.shape[2]
+    pieces = local_width // 256
+    step = local_width // pieces
+    row_count = w_qkv.shape[1]
+    qkv_shards = [
+        w_qkv[:, :, p * step : (p + 1) * step].transpose(1, 0, 2).reshape(row_count, 3 * step)
+        for p in range(pieces)
+    ]
+    params = jnp.stack([ln1_gain, ln1_bias, ln2_gain, ln2_bias])
+    x16 = assemble(tokens)
+    mask = size // 2
+    while mask >= 1:
+        params = jnp.concatenate([params, swap_dp(params, size, mask)], axis=1)
+        mask //= 2
+    gain_one, bias_one, gain_two, bias_two = (
+        params[i : i + 1].astype(jnp.float32) for i in range(4)
+    )
+    qkv_w = [gather_pair(s, size, p % 2 == 0) for p, s in enumerate(qkv_shards)]
+    out_w = gather_pair(w_out.T, size, True)
+    hidden_step = w_up.shape[1] // 2
+    up_w = [
+        gather_pair(w_up[:, p * hidden_step : (p + 1) * hidden_step], size, p == 0)
+        for p in range(2)
+    ]
+    down_t = w_down.T
+    down_w = [
+        gather_pair(down_t[:, p * hidden_step : (p + 1) * hidden_step], size, p == 0)
+        for p in range(2)
+    ]
+    dy16 = assemble(d_out)
+
+    x = x16.astype(jnp.float32)
+    normed_one, normal_one, inverse_one = norm_rows(x, gain_one, bias_one)
+    normed_one = normed_one.astype(jnp.bfloat16)
+    attended = []
+    for side in range(2):
+        for p in range(pieces):
+            qkv = mul(normed_one, qkv_w[p][side]).astype(jnp.bfloat16)
+            attended.append((qkv,) + tuple(attend(qkv)))
+    mixed = jnp.concatenate([a[1] for a in attended], axis=1)
+    out_all = jnp.concatenate([out_w[0], out_w[1]], axis=1)
+    hidden = x + mul(mixed, out_all, NT)
+    normed_two, normal_two, inverse_two = norm_rows(hidden, gain_two, bias_two)
+    normed_two = normed_two.astype(jnp.bfloat16)
+    up_all = [up_w[p][side] for side in range(2) for p in range(2)]
+    down_all = [down_w[p][side] for side in range(2) for p in range(2)]
+    actives, slopes = [], []
+    for w in up_all:
+        active, slope = gelu_both(mul(normed_two, w))
+        actives.append(active.astype(jnp.bfloat16))
+        slopes.append(slope.astype(jnp.bfloat16))
+
+    grad_down = [
+        scatter_pair(dy16, actives[p], actives[2 + p], size, p == 0) for p in range(2)
+    ]
+    grad_upward = [
+        (mul(dy16, w) * slope.astype(jnp.float32)).astype(jnp.bfloat16)
+        for w, slope in zip(down_all, slopes)
+    ]
+    grad_up = [
+        scatter_pair(normed_two, grad_upward[p], grad_upward[2 + p], size, p == 0)
+        for p in range(2)
+    ]
+    down_cat = jnp.concatenate(down_all, axis=1)
+    up_cat = jnp.concatenate(up_all, axis=1)
+    block_out = (hidden + mul(jnp.concatenate(actives, axis=1), down_cat, NT)).astype(jnp.bfloat16)
+    grad_normed_two = mul(jnp.concatenate(grad_upward, axis=1), up_cat, NT)
+    grad_norm, gain_two_grad, bias_two_grad = norm_rows_grad(
+        grad_normed_two, normal_two, inverse_two, gain_two
+    )
+    grad_hidden = dy16.astype(jnp.float32) + grad_norm
+    low_hidden = grad_hidden.astype(jnp.bfloat16)
+
+    grad_out = scatter_pair(
+        low_hidden, mixed[:, :local_width], mixed[:, local_width:], size, True
+    )
+    grad_mixed = mul(low_hidden, out_all).astype(jnp.bfloat16)
+    grad_qkv16 = []
+    for n, (qkv, mixed_n, lse) in enumerate(attended):
+        grad_qkv16.append(
+            attend_grad(qkv, grad_mixed[:, n * step : (n + 1) * step], mixed_n, lse)
+        )
+    grad_qkv = [
+        scatter_pair(normed_one, grad_qkv16[p], grad_qkv16[pieces + p], size, p % 2 == 0)
+        for p in range(pieces)
+    ]
+    qkv_cat = jnp.concatenate([qkv_w[p][side] for side in range(2) for p in range(pieces)], axis=1)
+    grad_normed_one = mul(jnp.concatenate(grad_qkv16, axis=1), qkv_cat, NT)
+    grad_norm, gain_one_grad, bias_one_grad = norm_rows_grad(
+        grad_normed_one, normal_one, inverse_one, gain_one
+    )
+    input_grad = (grad_hidden + grad_norm).astype(jnp.bfloat16)
+
+    sums = jnp.concatenate([gain_one_grad, bias_one_grad, gain_two_grad, bias_two_grad], axis=0)
+    mask = 1
+    while mask < size:
+        middle = sums.shape[1] // 2
+        sums = sums[:, :middle] + swap_dp(sums[:, middle:], size, mask)
+        mask *= 2
+    sums = sums + swap_tensor(sums)
+
+    return (
+        disperse(block_out),
+        disperse(input_grad),
+        sums[0],
+        sums[1],
+        jnp.concatenate(
+            [g.reshape(row_count, 3, step).transpose(1, 0, 2) for g in grad_qkv], axis=2
+        ),
+        grad_out.T,
+        sums[2],
+        sums[3],
+        jnp.concatenate(grad_up, axis=1),
+        jnp.concatenate(grad_down, axis=1).T,
+    )
+
+
 def solution(mesh):
+    sizes = dict(mesh.shape)
+    dp_size, tensor_size = sizes["dp"], sizes["tensor"]
+    if tensor_size == 2 and dp_size >= 4 and dp_size & (dp_size - 1) == 0:
+        body = functools.partial(on_device_whole, dp_size)
+    else:
+        body = on_device_shared
     placed = (
         P("tensor", "dp", None),
         P("tensor", "dp", None),
@@ -238,7 +628,7 @@
         P("tensor", "dp"),
     )
     return jax.shard_map(
-        on_device,
+        body,
         mesh=mesh,
         in_specs=placed,
         out_specs=(

time: 1250 us -> 718 us (0.57)
  waiting for transfers between devices: 631 us -> 248 us
  matrix products: 359 us -> 180 us
  other arithmetic: 135 us -> 42.1 us
  starting transfers between devices: 0.82 us -> 91.7 us
  blocking collectives: 75.3 us -> 0 us
  Pallas kernels: 0 us -> 66 us
  local copies, waits for them, and re-layouts: 30.2 us -> 83.1 us
  between operations: 16.1 us -> 3.38 us
    all_gather x8 -> x0, waiting for transfers between devices: 322 us -> none  [the longest x1 56.7 us: on_device(): rows_two = lax.all_gather(low_two, 'tensor', axis=0, tiled=True)]
    ppermute x0 -> x104, waiting for transfers between devices: none -> 248 us  [the longest x85 155 us: swap_dp(): return lax.ppermute(array, 'dp', [(i, i ^ mask) for i in range(size)])]
    reduce_scatter x7 -> x0, waiting for transfers between devices: 235 us -> none  [the longest x1 59 us: on_device(): lax.psum_scatter(grad_out.astype(jnp.bfloat16), 'dp', scatter_dimension=1...]
    dot_general x26 -> x49, matrix products: 359 us -> 180 us  [mul(): lax.dot_general(left, right, dims, preferred_element_type=jnp.float32)]
    ppermute x0 -> x104, starting transfers between devices: none -> 91.7 us  [the longest x85 68.6 us: swap_dp(): return lax.ppermute(array, 'dp', [(i, i ^ mask) for i in range(size)])]
    unnamed x17 -> x0, waiting for transfers between devices: 73.5 us -> none
    unnamed x2 -> x0, blocking collectives: 69.9 us -> none
    pallas_call x0 -> x8, Pallas kernels: none -> 66 us  [the longest x4 35.3 us: attend_grad(): pl.pallas_call(back_kernel, grid=(pairs,), in_specs=[pl.BlockSpec((length...]
  transfers between devices with their start and end apart: 16 -> 104, of which waited for: 13 -> 40; matrix products, arithmetic and copies ran while one was open for 36% -> 40% of each run, Pallas kernels for 0% -> 9%
where the time goes in v1:
time: 718 us; the launch traced here: 715 us
  waiting for transfers between devices  248 us (35%)
  matrix products  180 us (25%)
  starting transfers between devices  91.7 us (13%)
  local copies, waits for them, and re-layouts  83.1 us (12%)
  Pallas kernels  66 us (9%)
  other arithmetic  42.1 us (6%)
    dot_general x49, matrix products, mul(): lax.dot_general(left, right, dims, preferred_element_type=jnp.float32)  180 us
    ppermute x85, waiting for transfers between devices, swap_dp(): return lax.ppermute(array, 'dp', [(i, i ^ mask) for i in range(size)])  155 us
    ppermute x19, waiting for transfers between devices, swap_tensor(): return lax.ppermute(array, 'tensor', [(0, 1), (1, 0)])  93.2 us
    ppermute x85, starting transfers between devices, swap_dp(): return lax.ppermute(array, 'dp', [(i, i ^ mask) for i in range(size)])  68.6 us
    unnamed x303, local copies, waits for them, and re-layouts  47.7 us
    pallas_call x4, Pallas kernels, attend_grad(): pl.pallas_call(back_kernel, grid=(pairs,), in_specs=[pl.BlockSpec((length...  35.3 us
    pallas_call x4, Pallas kernels, attend(): pl.pallas_call(fwd_kernel, grid=(pairs,), in_specs=[pl.BlockSpec((length,...  30.7 us
    ppermute x19, starting transfers between devices, swap_tensor(): return lax.ppermute(array, 'tensor', [(0, 1), (1, 0)])  23.1 us
  transfers between devices with their start and end apart: 104, of which 40 were waited for; matrix products, arithmetic and copies ran while one was open for 40% of the time, Pallas kernels for 9%

profile of v1, /device:TPU:0, one launch (start us, length us, event | category | flops | bytes accessed | tf_op | source)
XLA Modules:
  0.0 714.7 jit_solution(3673862975526352481)
XLA Ops:
  1.4 4.1 collective-permute-start.1
  16.3 6.9 fusion.218
  23.3 4.3 fusion.217
  28.4 4.0 select_bitcast_fusion.5
  50.5 8.5 %collective-permute-done.25 = bf16[64,1024]{1,0:T(8,128)(2,1)S(1)} collective-permute-done((bf16[64,1024]{1,0:T(8,128)(2,1)S(1)}, bf16[64,1024]{1,0:T(8,128)(2,1)S(1)}, u32[]{:S(2)}, u32[]{:S(2)}) %collective-permute-start.25) | collective-permute-done | bytes 131104 | tf_op jit(solution)/shard_map/ppermute | solution.py:378
  73.9 4.1 collective-permute-done.30
  85.1 9.6 %collective-permute-done.39 = bf16[128,1024]{1,0:T(8,128)(2,1)S(1)} collective-permute-done((bf16[128,1024]{1,0:T(8,128)(2,1)S(1)}, bf16[128,1024]{1,0:T(8,128)(2,1)S(1)}, u32[]{:S(2)}, u32[]{:S(2)}) %collective-permute-start.39) | collective-permute-done | bytes 262176 | tf_op jit(solution)/shard_map/ppermute | solution.py:378
  100.7 6.0 collective-permute-done.7
  108.9 6.3 collective-permute-done.11
  118.1 13.9 %collective-permute-done.23 = bf16[256,512]{1,0:T(8,128)(2,1)S(1)} collective-permute-done((bf16[256,512]{1,0:T(8,128)(2,1)S(1)}, bf16[256,512]{1,0:T(8,128)(2,1)S(1)}, u32[]{:S(2)}, u32[]{:S(2)}) %collective-permute-start.23) | collective-permute-done | bytes 262176 | tf_op jit(solution)/shard_map/ppermute | solution.py:378
  138.7 4.5 collective-permute-done.27
  144.1 10.4 %collective-permute-done.44 = bf16[256,1024]{1,0:T(8,128)(2,1)S(1)} collective-permute-done((bf16[256,1024]{1,0:T(8,128)(2,1)S(1)}, bf16[256,1024]{1,0:T(8,128)(2,1)S(1)}, u32[]{:S(2)}, u32[]{:S(2)}) %collective-permute-start.44) | collective-permute-done | bytes 524320 | tf_op jit(solution)/shard_map/ppermute | solution.py:378
  156.9 7.9 %collective-permute-done.40 = bf16[256,1024]{1,0:T(8,128)(2,1)S(1)} collective-permute-done((bf16[256,1024]{1,0:T(8,128)(2,1)S(1)}, bf16[256,1024]{1,0:T(8,128)(2,1)S(1)}, u32[]{:S(2)}, u32[]{:S(2)}) %collective-permute-start.40) | collective-permute-done | bytes 524320 | tf_op jit(solution)/shard_map/ppermute | solution.py:378
  172.0 10.9 %collective-permute-done.52 = bf16[512,1024]{1,0:T(8,128)(2,1)S(1)} collective-permute-done((bf16[512,1024]{1,0:T(8,128)(2,1)S(1)}, bf16[512,1024]{1,0:T(8,128)(2,1)S(1)}, u32[]{:S(2)}, u32[]{:S(2)}) %collective-permute-start.52) | collective-permute-done | bytes 1048608 | tf_op jit(solution)/shard_map/ppermute | solution.py:382
  190.6 9.3 %collective-permute-done.47 = bf16[256,1024]{1,0:T(8,128)(2,1)S(1)} collective-permute-done((bf16[256,1024]{1,0:T(8,128)(2,1)S(1)}, bf16[256,1024]{1,0:T(8,128)(2,1)S(1)}, u32[]{:S(2)}, u32[]{:S(2)}) %collective-permute-start.47) | collective-permute-done | bytes 524320 | tf_op jit(solution)/shard_map/ppermute | solution.py:378
  206.8 7.5 %shard_map.177 = (bf16[1024,256]{1,0:T(8,128)(2,1)S(1)}, f32[2,8,1024]{2,1,0:T(8,128)S(1)}) custom-call(bf16[1024,768]{1,0:T(8,128)(2,1)S(1)} %convolution_convert_fusion.4.q_ref.k_ref.v_ref, bf16[1024,768]{1,0:T(8,128)(2,1)S(1)} %convolution_convert_fusion.4.q_ref.k_ref.v_ref, bf16[1024,768]{1,0:T(8,128)(2,1)S(1)} %convolution_convert_fusion.4.q_ref.k_ref.v_ref), custom_call_target="tpu_custom_call" | custom-call | flops 2147483648 | bytes 2097152 | tf_op jit(solution)/shard_map/pallas_call | solution.py:280
  219.0 7.7 %shard_map.178 = (bf16[1024,256]{1,0:T(8,128)(2,1)S(1)}, f32[2,8,1024]{2,1,0:T(8,128)S(1)}) custom-call(bf16[1024,768]{1,0:T(8,128)(2,1)S(1)} %convolution_convert_fusion.3.q_ref.k_ref.v_ref, bf16[1024,768]{1,0:T(8,128)(2,1)S(1)} %convolution_convert_fusion.3.q_ref.k_ref.v_ref, bf16[1024,768]{1,0:T(8,128)(2,1)S(1)} %convolution_convert_fusion.3.q_ref.k_ref.v_ref), custom_call_target="tpu_custom_call" | custom-call | flops 2147483648 | bytes 2097152 | tf_op jit(solution)/shard_map/pallas_call | solution.py:280
  231.6 7.5 %shard_map.179 = (bf16[1024,256]{1,0:T(8,128)(2,1)S(1)}, f32[2,8,1024]{2,1,0:T(8,128)S(1)}) custom-call(bf16[1024,768]{1,0:T(8,128)(2,1)S(1)} %convolution_convert_fusion.2.q_ref.k_ref.v_ref, bf16[1024,768]{1,0:T(8,128)(2,1)S(1)} %convolution_convert_fusion.2.q_ref.k_ref.v_ref, bf16[1024,768]{1,0:T(8,128)(2,1)S(1)} %convolution_convert_fusion.2.q_ref.k_ref.v_ref), custom_call_target="tpu_custom_call" | custom-call | flops 2147483648 | bytes 2097152 | tf_op jit(solution)/shard_map/pallas_call | solution.py:280
  250.8 7.9 %shard_map.180 = (bf16[1024,256]{1,0:T(8,128)(2,1)S(1)}, f32[2,8,1024]{2,1,0:T(8,128)S(1)}) custom-call(bf16[1024,768]{1,0:T(8,128)(2,1)S(1)} %convolution_convert_fusion.1.q_ref.k_ref.v_ref, bf16[1024,768]{1,0:T(8,128)(2,1)S(1)} %convolution_convert_fusion.1.q_ref.k_ref.v_ref, bf16[1024,768]{1,0:T(8,128)(2,1)S(1)} %convolution_convert_fusion.1.q_ref.k_ref.v_ref), custom_call_target="tpu_custom_call" | custom-call | flops 2147483648 | bytes 2097152 | tf_op jit(solution)/shard_map/pallas_call | solution.py:280
  268.8 4.9 multiply_convert_fusion.3
  284.6 4.9 multiply_convert_fusion.2
  302.2 6.7 multiply_convert_fusion.1
  315.3 5.4 multiply_convert_fusion.4
  323.9 16.8 %fusion = f32[1024,1024]{0,1:T(8,128)} fusion(bf16[1024,1024]{1,0:T(8,128)(2,1)} %constant_dynamic-update-slice_fusion.40, bf16[1024,1024]{1,0:T(8,128)(2,1)} %constant_dynamic-update-slice_fusion.37, bf16[1024,1024]{1,0:T(8,128)(2,1)} %copy-done.83, bf16[1024,1024]{1,0:T(8,128)(2,1)} %copy-done.89, bf16[1024,1024]{0,1:T(8,128)(2,1)} %copy-done.116, ...), kind=kOutput, calls=%fused_computation.4 | convolution fusion | flops 8657043456 | bytes 20971520 | tf_op jit(solution)/shard_map/dot_general | solution.py:240
  340.7 8.3 %multiply_convert_fusion = bf16[1024,1024]{0,1:T(8,128)(2,1)S(1)} fusion(bf16[1024,1024]{0,1:T(8,128)(2,1)} %copy-done.37, bf16[1024,1024]{1,0:T(8,128)(2,1)} %constant_dynamic-update-slice_fusion.40, f32[1024,1024]{0,1:T(8,128)} %get-tuple-element.105), kind=kOutput, calls=%fused_computation.137 | convolution fusion | flops 2169503744 | bytes 10485760 | tf_op jit(solution)/shard_map/dot_general | solution.py:240
  352.6 25.5 %fusion.220 = (f32[1024]{0:T(1024)S(1)}, f32[1024,1024]{1,0:T(8,128)}) fusion(bf16[1024,1024]{1,0:T(8,128)(2,1)} %copy-done.49, bf16[1024,1024]{1,0:T(8,128)(2,1)} %copy-done.65, bf16[1024,1024]{1,0:T(8,128)(2,1)} %copy-done.80, bf16[1024,1024]{1,0:T(8,128)(2,1)} %copy-done.86, bf16[1024,1024]{0,1:T(8,128)(2,1)} %copy-done.118, ...), kind=kOutput, calls=%fused_computation.442 | convolution fusion | flops 8658091008 | bytes 20975616 | tf_op jit(solution)/shard_map/dot_general | solution.py:240
  378.1 5.3 copy.40
  383.4 4.9 multiply_reduce_fusion
  398.5 9.1 %shard_map.181 = bf16[1024,768]{1,0:T(8,128)(2,1)S(1)} custom-call(bf16[1024,768]{1,0:T(8,128)(2,1)S(1)} %copy-done.10, bf16[1024,768]{1,0:T(8,128)(2,1)S(1)} %copy-done.10, bf16[1024,768]{1,0:T(8,128)(2,1)S(1)} %copy-done.10, bf16[1024,256]{1,0:T(8,128)(2,1)S(1)} %get-tuple-element.60.do_ref, bf16[1024,256]{1,0:T(8,128)(2,1)S(1)} %get-tuple-element.18.o_ref, ...), custom_call_target="tpu_custom_call" | custom-call | flops 5368709120 | bytes 4194304 | tf_op jit(solution)/shard_map/pallas_call | solution.py:357
  412.3 3.9 fusion.137
  416.2 8.9 %shard_map.184 = bf16[1024,768]{1,0:T(8,128)(2,1)S(1)} custom-call(bf16[1024,768]{1,0:T(8,128)(2,1)S(1)} %copy-done.14, bf16[1024,768]{1,0:T(8,128)(2,1)S(1)} %copy-done.14, bf16[1024,768]{1,0:T(8,128)(2,1)S(1)} %copy-done.14, bf16[1024,256]{1,0:T(8,128)(2,1)S(1)} %get-tuple-element.61.do_ref, bf16[1024,256]{1,0:T(8,128)(2,1)S(1)} %get-tuple-element.21.o_ref, ...), custom_call_target="tpu_custom_call" | custom-call | flops 5368709120 | bytes 4194304 | tf_op jit(solution)/shard_map/pallas_call | solution.py:357
  427.0 8.7 %shard_map.183 = bf16[1024,768]{1,0:T(8,128)(2,1)S(1)} custom-call(bf16[1024,768]{1,0:T(8,128)(2,1)S(1)} %copy-done.12, bf16[1024,768]{1,0:T(8,128)(2,1)S(1)} %copy-done.12, bf16[1024,768]{1,0:T(8,128)(2,1)S(1)} %copy-done.12, bf16[1024,256]{1,0:T(8,128)(2,1)S(1)} %get-tuple-element.62.do_ref, bf16[1024,256]{1,0:T(8,128)(2,1)S(1)} %copy-done.3, ...), custom_call_target="tpu_custom_call" | custom-call | flops 5368709120 | bytes 4194304 | tf_op jit(solution)/shard_map/pallas_call | solution.py:357
  437.6 8.7 %shard_map.182 = bf16[1024,768]{1,0:T(8,128)(2,1)S(1)} custom-call(bf16[1024,768]{1,0:T(8,128)(2,1)S(1)} %copy-done.8, bf16[1024,768]{1,0:T(8,128)(2,1)S(1)} %copy-done.8, bf16[1024,768]{1,0:T(8,128)(2,1)S(1)} %copy-done.8, bf16[1024,256]{1,0:T(8,128)(2,1)S(1)} %get-tuple-element.63.do_ref, bf16[1024,256]{1,0:T(8,128)(2,1)S(1)} %copy-done.1, ...), custom_call_target="tpu_custom_call" | custom-call | flops 5368709120 | bytes 4194304 | tf_op jit(solution)/shard_map/pallas_call | solution.py:357
  447.5 12.4 %fusion.221 = (f32[1024]{0:T(1024)S(1)}, f32[1024,1024]{1,0:T(8,128)}) fusion(bf16[1024,768]{1,0:T(8,128)(2,1)} %copy-done.52, bf16[1024,768]{1,0:T(8,128)(2,1)} %constant_dynamic-update-slice_fusion.17, bf16[1024,768]{1,0:T(8,128)(2,1)} %constant_dynamic-update-slice_fusion.12, bf16[1024,768]{1,0:T(8,128)(2,1)} %copy-done.92, ...), kind=kOutput, calls=%fused_computation.443 | convolution fusion | flops 6493830144 | bytes 16781312 | tf_op jit(solution)/shard_map/dot_general | solution.py:240
  459.9 5.4 copy.41
  465.3 4.2 fusion.58
  470.0 9.0 %fusion.134 = bf16[1024,1024]{1,0:T(8,128)(2,1)S(1)} fusion(bf16[1024,1024]{0,1:T(8,128)(2,1)S(1)} %copy-done.20, f32[1024,1024]{0,1:T(8,128)} %copy.41, f32[1024]{0:T(1024)S(1)} %broadcast_multiply_fusion, f32[1024]{0:T(1024)S(1)} %broadcast_multiply_fusion.1, f32[1024]{0:T(1024)S(1)} %bitcast.129, f32[1024]{0:T(1024)S(1)} %copy-done.70, ...), kind=kOutput, calls=%fused_computation.192 | convolution fusion | flops 2261778432 | bytes 18933764 | tf_op jit(solution)/shard_map/dot_general | solution.py:240
  487.7 4.3 collective-permute-done.57
  516.4 31.5 %collective-permute-done.74 = bf16[512,512]{1,0:T(8,128)(2,1)S(1)} collective-permute-done((bf16[512,512]{1,0:T(8,128)(2,1)S(1)}, bf16[512,512]{1,0:T(8,128)(2,1)S(1)}, u32[]{:S(2)}, u32[]{:S(2)}) %collective-permute-start.74) | collective-permute-done | bytes 524320 | tf_op jit(solution)/shard_map/ppermute | solution.py:382
  553.9 20.2 %collective-permute-done.53 = bf16[512,1024]{1,0:T(8,128)(2,1)S(1)} collective-permute-done((bf16[512,1024]{1,0:T(8,128)(2,1)S(1)}, bf16[512,1024]{1,0:T(8,128)(2,1)S(1)}, u32[]{:S(2)}, u32[]{:S(2)}) %collective-permute-start.53) | collective-permute-done | bytes 1048608 | tf_op jit(solution)/shard_map/ppermute | solution.py:382
  574.8 6.8 collective-permute-done.75
  585.6 3.7 copy.45
  599.8 11.1 %collective-permute-done.100 = bf16[256,1024]{1,0:T(8,128)(2,1)S(1)} collective-permute-done((bf16[256,1024]{1,0:T(8,128)(2,1)S(1)}, bf16[256,1024]{1,0:T(8,128)(2,1)S(1)}, u32[]{:S(2)}, u32[]{:S(2)}) %collective-permute-start.100) | collective-permute-done | bytes 524320 | tf_op jit(solution)/shard_map/ppermute | solution.py:378
  619.3 24.6 %collective-permute-done.69 = bf16[256,768]{1,0:T(8,128)(2,1)S(1)} collective-permute-done((bf16[256,768]{1,0:T(8,128)(2,1)S(1)}, bf16[256,768]{1,0:T(8,128)(2,1)S(1)}, u32[]{:S(2)}, u32[]{:S(2)}) %collective-permute-start.69) | collective-permute-done | bytes 393248 | tf_op jit(solution)/shard_map/ppermute | solution.py:382
  648.2 3.6 collective-permute-done.70
  653.4 5.4 collective-permute-done.87
  688.3 6.9 collective-permute-done.64
  707.2 5.1 collective-permute-done.96
  (669 shorter events, 293.8 us)
Async XLA Ops:
  1.4 33.4 %collective-permute-start.1 = (bf16[4,64]{1,0:T(4,128)(2,1)S(1)}, bf16[4,64]{1,0:T(4,128)(2,1)S(1)}, u32[]{:S(2)}, u32[]{:S(2)}) collective-permute-start(bf16[4,64]{1,0:T(4,128)(2,1)S(1)} %pad_maximum_fusion.30), channel_id=1, source_target_pairs={{0,16},{2,18},{4,20},{6,22},{8,24},{10,26},{12,28},{14,30},{16,0},... | collective-permute-start | bytes 1544 | tf_op jit(solution)/shard_map/ppermute | solution.py:378
  5.5 38.1 %collective-permute-start.18 = (bf16[64,512]{1,0:T(8,128)(2,1)}, bf16[64,512]{1,0:T(8,128)(2,1)S(1)}, u32[]{:S(2)}, u32[]{:S(2)}) collective-permute-start(bf16[64,512]{1,0:T(8,128)(2,1)} %bitcast.118), channel_id=1, source_target_pairs={{0,16},{2,18},{4,20},{6,22},{8,24},{10,26},{12,28},{14,30},{16,0},... | collective-permute-start | bytes 196616 | tf_op jit(solution)/shard_map/ppermute | solution.py:378
  6.5 40.7 %collective-permute-start.9 = (bf16[64,768]{1,0:T(8,128)(2,1)S(1)}, bf16[64,768]{1,0:T(8,128)(2,1)S(1)}, u32[]{:S(2)}, u32[]{:S(2)}) collective-permute-start(bf16[64,768]{1,0:T(8,128)(2,1)S(1)} %bitcast.112), channel_id=1, source_target_pairs={{0,16},{2,18},{4,20},{6,22},{8,24},{10,26},{12,28},{14,30},{16,0},... | collective-permute-start | bytes 294920 | tf_op jit(solution)/shard_map/ppermute | solution.py:378
  9.4 37.7 %collective-permute-start.5 = (bf16[64,768]{1,0:T(8,128)(2,1)S(1)}, bf16[64,768]{1,0:T(8,128)(2,1)S(1)}, u32[]{:S(2)}, u32[]{:S(2)}) collective-permute-start(bf16[64,768]{1,0:T(8,128)(2,1)S(1)} %bitcast.108), channel_id=1, source_target_pairs={{0,16},{2,18},{4,20},{6,22},{8,24},{10,26},{12,28},{14,30},{16,0},... | collective-permute-start | bytes 294920 | tf_op jit(solution)/shard_map/ppermute | solution.py:378
  11.3 48.4 %collective-permute-start.29 = (bf16[64,1024]{1,0:T(8,128)(2,1)S(1)}, bf16[64,1024]{1,0:T(8,128)(2,1)S(1)}, u32[]{:S(2)}, u32[]{:S(2)}) collective-permute-start(bf16[64,1024]{1,0:T(8,128)(2,1)S(1)} %get-tuple-element.72), channel_id=1, source_target_pairs={{0,16},{2,18},{4,20},{6,22},{8,24},{10,26},{12,28},{14,30},{16,0},... | collective-permute-start | bytes 393224 | tf_op jit(solution)/shard_map/ppermute | solution.py:378
  67.4 28.9 %collective-permute-start.43 = (bf16[128,1024]{1,0:T(8,128)(2,1)S(1)}, bf16[128,1024]{1,0:T(8,128)(2,1)S(1)}, u32[]{:S(2)}, u32[]{:S(2)}) collective-permute-start(bf16[128,1024]{1,0:T(8,128)(2,1)S(1)} %pad_maximum_fusion.21), channel_id=1, source_target_pairs={{0,8},{2,10},{4,12},{6,14},{8,0},{10,2},{12,4},{14,6},{16,24},{18,... | collective-permute-start | bytes 786440 | tf_op jit(solution)/shard_map/ppermute | solution.py:378
  68.1 26.6 %collective-permute-start.39 = (bf16[128,1024]{1,0:T(8,128)(2,1)S(1)}, bf16[128,1024]{1,0:T(8,128)(2,1)S(1)}, u32[]{:S(2)}, u32[]{:S(2)}) collective-permute-start(bf16[128,1024]{1,0:T(8,128)(2,1)S(1)} %pad_maximum_fusion.20), channel_id=1, source_target_pairs={{0,8},{2,10},{4,12},{6,14},{8,0},{10,2},{12,4},{14,6},{16,24},{18,... | collective-permute-start | bytes 786440 | tf_op jit(solution)/shard_map/ppermute | solution.py:378
  72.4 35.9 %collective-permute-start.22 = (bf16[256,512]{1,0:T(8,128)(2,1)S(1)}, bf16[256,512]{1,0:T(8,128)(2,1)S(1)}, u32[]{:S(2)}, u32[]{:S(2)}) collective-permute-start(bf16[256,512]{1,0:T(8,128)(2,1)S(1)} %pad_maximum_fusion.19), channel_id=1, source_target_pairs={{0,1},{1,0},{2,3},{3,2},{4,5},{5,4},{6,7},{7,6},{8,9},{9,8},{10,11... | collective-permute-start | bytes 786440 | tf_op jit(solution)/shard_map/ppermute | solution.py:382
  83.6 33.9 %collective-permute-start.13 = (bf16[256,768]{1,0:T(8,128)(2,1)S(1)}, bf16[256,768]{1,0:T(8,128)(2,1)S(1)}, u32[]{:S(2)}, u32[]{:S(2)}) collective-permute-start(bf16[256,768]{1,0:T(8,128)(2,1)S(1)} %get-tuple-element.79), channel_id=1, source_target_pairs={{0,1},{1,0},{2,3},{3,2},{4,5},{5,4},{6,7},{7,6},{8,9},{9,8},{10,11... | collective-permute-start | bytes 1179656 | tf_op jit(solution)/shard_map/ppermute | solution.py:382
  99.1 38.2 %collective-permute-start.31 = (bf16[256,1024]{1,0:T(8,128)(2,1)S(1)}, bf16[256,1024]{1,0:T(8,128)(2,1)S(1)}, u32[]{:S(2)}, u32[]{:S(2)}) collective-permute-start(bf16[256,1024]{1,0:T(8,128)(2,1)S(1)} %pad_maximum_fusion.15), channel_id=1, source_target_pairs={{0,4},{2,6},{4,0},{6,2},{8,12},{10,14},{12,8},{14,10},{16,20},{18,... | collective-permute-start | bytes 1572872 | tf_op jit(solution)/shard_map/ppermute | solution.py:378
  106.7 27.7 %collective-permute-start.33 = (bf16[256,1024]{1,0:T(8,128)(2,1)S(1)}, bf16[256,1024]{1,0:T(8,128)(2,1)S(1)}, u32[]{:S(2)}, u32[]{:S(2)}) collective-permute-start(bf16[256,1024]{1,0:T(8,128)(2,1)S(1)} %pad_maximum_fusion.14), channel_id=1, source_target_pairs={{0,1},{1,0},{2,3},{3,2},{4,5},{5,4},{6,7},{7,6},{8,9},{9,8},{10,11... | collective-permute-start | bytes 1572872 | tf_op jit(solution)/shard_map/ppermute | solution.py:382
  108.3 27.6 %collective-permute-start.46 = (bf16[256,1024]{1,0:T(8,128)(2,1)S(1)}, bf16[256,1024]{1,0:T(8,128)(2,1)S(1)}, u32[]{:S(2)}, u32[]{:S(2)}) collective-permute-start(bf16[256,1024]{1,0:T(8,128)(2,1)S(1)} %pad_maximum_fusion.12), channel_id=1, source_target_pairs={{0,1},{1,0},{2,3},{3,2},{4,5},{5,4},{6,7},{7,6},{8,9},{9,8},{10,11... | collective-permute-start | bytes 1572872 | tf_op jit(solution)/shard_map/ppermute | solution.py:382
  117.5 25.7 %collective-permute-start.27 = (bf16[256,1024]{1,0:T(8,128)(2,1)S(1)}, bf16[256,1024]{1,0:T(8,128)(2,1)S(1)}, u32[]{:S(2)}, u32[]{:S(2)}) collective-permute-start(bf16[256,1024]{1,0:T(8,128)(2,1)S(1)} %pad_maximum_fusion.14), channel_id=1, source_target_pairs={{0,4},{2,6},{4,0},{6,2},{8,12},{10,14},{12,8},{14,10},{16,20},{18,... | collective-permute-start | bytes 1572872 | tf_op jit(solution)/shard_map/ppermute | solution.py:378
  134.4 33.1 %collective-permute-start = (bf16[512,1024]{1,0:T(8,128)(2,1)S(1)}, bf16[512,1024]{1,0:T(8,128)(2,1)S(1)}, u32[]{:S(2)}, u32[]{:S(2)}) collective-permute-start(bf16[512,1024]{1,0:T(8,128)(2,1)S(1)} %copy-done.47), channel_id=1, source_target_pairs={{0,1},{1,0},{2,3},{3,2},{4,5},{5,4},{6,7},{7,6},{8,9},{9,8},{10,11... | collective-permute-start | bytes 3145736 | tf_op jit(solution)/shard_map/ppermute | solution.py:382
  135.9 28.8 %collective-permute-start.40 = (bf16[256,1024]{1,0:T(8,128)(2,1)S(1)}, bf16[256,1024]{1,0:T(8,128)(2,1)S(1)}, u32[]{:S(2)}, u32[]{:S(2)}) collective-permute-start(bf16[256,1024]{1,0:T(8,128)(2,1)S(1)} %pad_maximum_fusion.12), channel_id=1, source_target_pairs={{0,4},{2,6},{4,0},{6,2},{8,12},{10,14},{12,8},{14,10},{16,20},{18,... | collective-permute-start | bytes 1572872 | tf_op jit(solution)/shard_map/ppermute | solution.py:378
  137.3 45.6 %collective-permute-start.52 = (bf16[512,1024]{1,0:T(8,128)(2,1)S(1)}, bf16[512,1024]{1,0:T(8,128)(2,1)S(1)}, u32[]{:S(2)}, u32[]{:S(2)}) collective-permute-start(bf16[512,1024]{1,0:T(8,128)(2,1)S(1)} %copy-done.46), channel_id=1, source_target_pairs={{0,1},{1,0},{2,3},{3,2},{4,5},{5,4},{6,7},{7,6},{8,9},{9,8},{10,11... | collective-permute-start | bytes 3145736 | tf_op jit(solution)/shard_map/ppermute | solution.py:382
  143.2 22.6 %collective-permute-start.21 = (bf16[512,512]{1,0:T(8,128)(2,1)S(1)}, bf16[512,512]{1,0:T(8,128)(2,1)S(1)}, u32[]{:S(2)}, u32[]{:S(2)}) collective-permute-start(bf16[512,512]{1,0:T(8,128)(2,1)S(1)} %pad_maximum_fusion.10), channel_id=1, source_target_pairs={{0,2},{2,0},{4,6},{6,4},{8,10},{10,8},{12,14},{14,12},{16,18},{18,... | collective-permute-start | bytes 1572872 | tf_op jit(solution)/shard_map/ppermute | solution.py:378
  154.5 46.5 %collective-permute-start.16 = (bf16[512,768]{1,0:T(8,128)(2,1)S(1)}, bf16[512,768]{1,0:T(8,128)(2,1)S(1)}, u32[]{:S(2)}, u32[]{:S(2)}) collective-permute-start(bf16[512,768]{1,0:T(8,128)(2,1)S(1)} %get-tuple-element.69), channel_id=1, source_target_pairs={{0,1},{1,0},{2,3},{3,2},{4,5},{5,4},{6,7},{7,6},{8,9},{9,8},{10,11... | collective-permute-start | bytes 2359304 | tf_op jit(solution)/shard_map/ppermute | solution.py:382
  164.8 49.6 %collective-permute-start.12 = (bf16[512,768]{1,0:T(8,128)(2,1)S(1)}, bf16[512,768]{1,0:T(8,128)(2,1)S(1)}, u32[]{:S(2)}, u32[]{:S(2)}) collective-permute-start(bf16[512,768]{1,0:T(8,128)(2,1)S(1)} %get-tuple-element.69), channel_id=1, source_target_pairs={{0,2},{2,0},{4,6},{6,4},{8,10},{10,8},{12,14},{14,12},{16,18},{18,... | collective-permute-start | bytes 2359304 | tf_op jit(solution)/shard_map/ppermute | solution.py:378
  189.1 39.0 %collective-permute-start.36 = (bf16[512,1024]{1,0:T(8,128)(2,1)S(1)}, bf16[512,1024]{1,0:T(8,128)(2,1)S(1)}, u32[]{:S(2)}, u32[]{:S(2)}) collective-permute-start(bf16[512,1024]{1,0:T(8,128)(2,1)S(1)} %pad_maximum_fusion.6), channel_id=1, source_target_pairs={{0,1},{1,0},{2,3},{3,2},{4,5},{5,4},{6,7},{7,6},{8,9},{9,8},{10,11... | collective-permute-start | bytes 3145736 | tf_op jit(solution)/shard_map/ppermute | solution.py:382
  199.9 44.5 %collective-permute-start.32 = (bf16[512,1024]{1,0:T(8,128)(2,1)S(1)}, bf16[512,1024]{1,0:T(8,128)(2,1)S(1)}, u32[]{:S(2)}, u32[]{:S(2)}) collective-permute-start(bf16[512,1024]{1,0:T(8,128)(2,1)S(1)} %pad_maximum_fusion.6), channel_id=1, source_target_pairs={{0,2},{2,0},{4,6},{6,4},{8,10},{10,8},{12,14},{14,12},{16,18},{18,... | collective-permute-start | bytes 3145736 | tf_op jit(solution)/shard_map/ppermute | solution.py:378
  200.9 40.7 %collective-permute-start.49 = (bf16[512,1024]{1,0:T(8,128)(2,1)S(1)}, bf16[512,1024]{1,0:T(8,128)(2,1)S(1)}, u32[]{:S(2)}, u32[]{:S(2)}) collective-permute-start(bf16[512,1024]{1,0:T(8,128)(2,1)S(1)} %pad_maximum_fusion.3), channel_id=1, source_target_pairs={{0,1},{1,0},{2,3},{3,2},{4,5},{5,4},{6,7},{7,6},{8,9},{9,8},{10,11... | collective-permute-start | bytes 3145736 | tf_op jit(solution)/shard_map/ppermute | solution.py:382
  203.5 41.8 %collective-permute-start.45 = (bf16[512,1024]{1,0:T(8,128)(2,1)S(1)}, bf16[512,1024]{1,0:T(8,128)(2,1)S(1)}, u32[]{:S(2)}, u32[]{:S(2)}) collective-permute-start(bf16[512,1024]{1,0:T(8,128)(2,1)S(1)} %pad_maximum_fusion.3), channel_id=1, source_target_pairs={{0,2},{2,0},{4,6},{6,4},{8,10},{10,8},{12,14},{14,12},{16,18},{18,... | collective-permute-start | bytes 3145736 | tf_op jit(solution)/shard_map/ppermute | solution.py:378
  244.4 52.4 %collective-permute-start.35 = (bf16[512,1024]{1,0:T(8,128)(2,1)S(1)}, bf16[512,1024]{1,0:T(8,128)(2,1)S(1)}, u32[]{:S(2)}, u32[]{:S(2)}) collective-permute-start(bf16[512,1024]{1,0:T(8,128)(2,1)S(1)} %pad_maximum_fusion.7), channel_id=1, source_target_pairs={{0,2},{2,0},{4,6},{6,4},{8,10},{10,8},{12,14},{14,12},{16,18},{18,... | collective-permute-start | bytes 3145736 | tf_op jit(solution)/shard_map/ppermute | solution.py:378
  244.6 56.3 %collective-permute-start.48 = (bf16[512,1024]{1,0:T(8,128)(2,1)S(1)}, bf16[512,1024]{1,0:T(8,128)(2,1)S(1)}, u32[]{:S(2)}, u32[]{:S(2)}) collective-permute-start(bf16[512,1024]{1,0:T(8,128)(2,1)S(1)} %pad_maximum_fusion.4), channel_id=1, source_target_pairs={{0,2},{2,0},{4,6},{6,4},{8,10},{10,8},{12,14},{14,12},{16,18},{18,... | collective-permute-start | bytes 3145736 | tf_op jit(solution)/shard_map/ppermute | solution.py:378
  245.2 69.6 %collective-permute-start.37 = (bf16[512,1024]{1,0:T(8,128)(2,1)S(1)}, bf16[512,1024]{1,0:T(8,128)(2,1)S(1)}, u32[]{:S(2)}, u32[]{:S(2)}) collective-permute-start(bf16[512,1024]{1,0:T(8,128)(2,1)S(1)} %collective-permute-done.36), channel_id=1, source_target_pairs={{0,2},{2,0},{4,6},{6,4},{8,10},{10,8},{12,14},{14,12},{16,18},{18,... | collective-permute-start | bytes 3145736 | tf_op jit(solution)/shard_map/ppermute | solution.py:378
  245.4 77.4 %collective-permute-start.50 = (bf16[512,1024]{1,0:T(8,128)(2,1)S(1)}, bf16[512,1024]{1,0:T(8,128)(2,1)S(1)}, u32[]{:S(2)}, u32[]{:S(2)}) collective-permute-start(bf16[512,1024]{1,0:T(8,128)(2,1)S(1)} %collective-permute-done.49), channel_id=1, source_target_pairs={{0,2},{2,0},{4,6},{6,4},{8,10},{10,8},{12,14},{14,12},{16,18},{18,... | collective-permute-start | bytes 3145736 | tf_op jit(solution)/shard_map/ppermute | solution.py:378
  296.7 199.4 %collective-permute-start.97 = (bf16[512,1024]{1,0:T(8,128)(2,1)}, bf16[512,1024]{1,0:T(8,128)(2,1)}, u32[]{:S(2)}, u32[]{:S(2)}) collective-permute-start(bf16[512,1024]{1,0:T(8,128)(2,1)} %convolution_convert_fusion.6), channel_id=1, source_target_pairs={{0,2},{2,0},{4,6},{6,4},{8,10},{10,8},{12,14},{14,12},{16,18},{18,... | collective-permute-start | bytes 3145736 | tf_op jit(solution)/shard_map/ppermute | solution.py:378
  296.8 203.6 %collective-permute-start.84 = (bf16[512,1024]{1,0:T(8,128)(2,1)}, bf16[512,1024]{1,0:T(8,128)(2,1)}, u32[]{:S(2)}, u32[]{:S(2)}) collective-permute-start(bf16[512,1024]{1,0:T(8,128)(2,1)} %convolution_convert_fusion.10), channel_id=1, source_target_pairs={{0,2},{2,0},{4,6},{6,4},{8,10},{10,8},{12,14},{14,12},{16,18},{18,... | collective-permute-start | bytes 3145736 | tf_op jit(solution)/shard_map/ppermute | solution.py:378
  300.9 297.3 %collective-permute-start.91 = (bf16[512,1024]{1,0:T(8,128)(2,1)}, bf16[512,1024]{1,0:T(8,128)(2,1)}, u32[]{:S(2)}, u32[]{:S(2)}) collective-permute-start(bf16[512,1024]{1,0:T(8,128)(2,1)} %convolution_convert_fusion.8), channel_id=1, source_target_pairs={{0,2},{2,0},{4,6},{6,4},{8,10},{10,8},{12,14},{14,12},{16,18},{18,... | collective-permute-start | bytes 3145736 | tf_op jit(solution)/shard_map/ppermute | solution.py:378
  314.8 189.4 %collective-permute-start.92 = (bf16[512,1024]{1,0:T(8,128)(2,1)}, bf16[512,1024]{1,0:T(8,128)(2,1)}, u32[]{:S(2)}, u32[]{:S(2)}) collective-permute-start(bf16[512,1024]{1,0:T(8,128)(2,1)} %convolution_convert_fusion.7), channel_id=1, source_target_pairs={{0,2},{2,0},{4,6},{6,4},{8,10},{10,8},{12,14},{14,12},{16,18},{18,... | collective-permute-start | bytes 3145736 | tf_op jit(solution)/shard_map/ppermute | solution.py:378
  496.2 53.9 %collective-permute-start.99 = (bf16[512,1024]{1,0:T(8,128)(2,1)S(1)}, bf16[512,1024]{1,0:T(8,128)(2,1)S(1)}, u32[]{:S(2)}, u32[]{:S(2)}) collective-permute-start(bf16[512,1024]{1,0:T(8,128)(2,1)S(1)} %copy-done.110), channel_id=1, source_target_pairs={{0,2},{2,0},{4,6},{6,4},{8,10},{10,8},{12,14},{14,12},{16,18},{18,... | collective-permute-start | bytes 3145736 | tf_op jit(solution)/shard_map/ppermute | solution.py:378
  511.1 37.0 %collective-permute-start.51 = (bf16[512,1024]{1,0:T(8,128)(2,1)S(1)}, bf16[512,1024]{1,0:T(8,128)(2,1)S(1)}, u32[]{:S(2)}, u32[]{:S(2)}) collective-permute-start(bf16[512,1024]{1,0:T(8,128)(2,1)S(1)} %broadcast_select_fusion.4), channel_id=1, source_target_pairs={{0,1},{1,0},{2,3},{3,2},{4,5},{5,4},{6,7},{7,6},{8,9},{9,8},{10,11... | collective-permute-start | bytes 3145736 | tf_op jit(solution)/shard_map/ppermute | solution.py:382
  513.7 34.2 %collective-permute-start.74 = (bf16[512,512]{1,0:T(8,128)(2,1)S(1)}, bf16[512,512]{1,0:T(8,128)(2,1)S(1)}, u32[]{:S(2)}, u32[]{:S(2)}) collective-permute-start(bf16[512,512]{1,0:T(8,128)(2,1)S(1)} %add_convert_fusion.29), channel_id=1, source_target_pairs={{0,1},{1,0},{2,3},{3,2},{4,5},{5,4},{6,7},{7,6},{8,9},{9,8},{10,11... | collective-permute-start | bytes 1572872 | tf_op jit(solution)/shard_map/ppermute | solution.py:382
  515.3 36.6 %collective-permute-start.86 = (bf16[512,1024]{1,0:T(8,128)(2,1)S(1)}, bf16[512,1024]{1,0:T(8,128)(2,1)S(1)}, u32[]{:S(2)}, u32[]{:S(2)}) collective-permute-start(bf16[512,1024]{1,0:T(8,128)(2,1)S(1)} %copy-done.111), channel_id=1, source_target_pairs={{0,2},{2,0},{4,6},{6,4},{8,10},{10,8},{12,14},{14,12},{16,18},{18,... | collective-permute-start | bytes 3145736 | tf_op jit(solution)/shard_map/ppermute | solution.py:378
  547.9 49.4 %collective-permute-start.59 = (bf16[512,768]{1,0:T(8,128)(2,1)S(1)}, bf16[512,768]{1,0:T(8,128)(2,1)S(1)}, u32[]{:S(2)}, u32[]{:S(2)}) collective-permute-start(bf16[512,768]{1,0:T(8,128)(2,1)S(1)} %copy-done.113), channel_id=1, source_target_pairs={{0,2},{2,0},{4,6},{6,4},{8,10},{10,8},{12,14},{14,12},{16,18},{18,... | collective-permute-start | bytes 2359304 | tf_op jit(solution)/shard_map/ppermute | solution.py:378
  548.1 26.0 %collective-permute-start.53 = (bf16[512,1024]{1,0:T(8,128)(2,1)S(1)}, bf16[512,1024]{1,0:T(8,128)(2,1)S(1)}, u32[]{:S(2)}, u32[]{:S(2)}) collective-permute-start(bf16[512,1024]{1,0:T(8,128)(2,1)S(1)} %broadcast_select_fusion.2), channel_id=1, source_target_pairs={{0,1},{1,0},{2,3},{3,2},{4,5},{5,4},{6,7},{7,6},{8,9},{9,8},{10,11... | collective-permute-start | bytes 3145736 | tf_op jit(solution)/shard_map/ppermute | solution.py:382
  550.1 47.2 %collective-permute-start.61 = (bf16[512,768]{1,0:T(8,128)(2,1)S(1)}, bf16[512,768]{1,0:T(8,128)(2,1)S(1)}, u32[]{:S(2)}, u32[]{:S(2)}) collective-permute-start(bf16[512,768]{1,0:T(8,128)(2,1)S(1)} %add_convert_fusion.18), channel_id=1, source_target_pairs={{0,1},{1,0},{2,3},{3,2},{4,5},{5,4},{6,7},{7,6},{8,9},{9,8},{10,11... | collective-permute-start | bytes 2359304 | tf_op jit(solution)/shard_map/ppermute | solution.py:382
  552.0 38.9 %collective-permute-start.68 = (bf16[256,768]{1,0:T(8,128)(2,1)S(1)}, bf16[256,768]{1,0:T(8,128)(2,1)S(1)}, u32[]{:S(2)}, u32[]{:S(2)}) collective-permute-start(bf16[256,768]{1,0:T(8,128)(2,1)S(1)} %slice.423), channel_id=1, source_target_pairs={{0,4},{2,6},{4,0},{6,2},{8,12},{10,14},{12,8},{14,10},{16,20},{18,... | collective-permute-start | bytes 1179656 | tf_op jit(solution)/shard_map/ppermute | solution.py:378
  589.3 26.1 %collective-permute-start.93 = (bf16[512,1024]{1,0:T(8,128)(2,1)S(1)}, bf16[512,1024]{1,0:T(8,128)(2,1)S(1)}, u32[]{:S(2)}, u32[]{:S(2)}) collective-permute-start(bf16[512,1024]{1,0:T(8,128)(2,1)S(1)} %add_convert_fusion.6), channel_id=1, source_target_pairs={{0,1},{1,0},{2,3},{3,2},{4,5},{5,4},{6,7},{7,6},{8,9},{9,8},{10,11... | collective-permute-start | bytes 3145736 | tf_op jit(solution)/shard_map/ppermute | solution.py:382
  597.3 47.3 %collective-permute-start.78 = (bf16[512,1024]{1,0:T(8,128)(2,1)S(1)}, bf16[512,1024]{1,0:T(8,128)(2,1)S(1)}, u32[]{:S(2)}, u32[]{:S(2)}) collective-permute-start(bf16[512,1024]{1,0:T(8,128)(2,1)S(1)} %copy-done.109), channel_id=1, source_target_pairs={{0,2},{2,0},{4,6},{6,4},{8,10},{10,8},{12,14},{14,12},{16,18},{18,... | collective-permute-start | bytes 3145736 | tf_op jit(solution)/shard_map/ppermute | solution.py:378
  597.3 48.9 %collective-permute-start.80 = (bf16[512,1024]{1,0:T(8,128)(2,1)S(1)}, bf16[512,1024]{1,0:T(8,128)(2,1)S(1)}, u32[]{:S(2)}, u32[]{:S(2)}) collective-permute-start(bf16[512,1024]{1,0:T(8,128)(2,1)S(1)} %add_convert_fusion.11), channel_id=1, source_target_pairs={{0,1},{1,0},{2,3},{3,2},{4,5},{5,4},{6,7},{7,6},{8,9},{9,8},{10,11... | collective-permute-start | bytes 3145736 | tf_op jit(solution)/shard_map/ppermute | solution.py:382
  610.9 33.0 %collective-permute-start.69 = (bf16[256,768]{1,0:T(8,128)(2,1)S(1)}, bf16[256,768]{1,0:T(8,128)(2,1)S(1)}, u32[]{:S(2)}, u32[]{:S(2)}) collective-permute-start(bf16[256,768]{1,0:T(8,128)(2,1)S(1)} %add_convert_fusion.32), channel_id=1, source_target_pairs={{0,1},{1,0},{2,3},{3,2},{4,5},{5,4},{6,7},{7,6},{8,9},{9,8},{10,11... | collective-permute-start | bytes 1179656 | tf_op jit(solution)/shard_map/ppermute | solution.py:382
  615.4 53.3 %collective-permute-start.98 = (bf16[256,1024]{1,0:T(8,128)(2,1)}, bf16[256,1024]{1,0:T(8,128)(2,1)}, u32[]{:S(2)}, u32[]{:S(2)}) collective-permute-start(bf16[256,1024]{1,0:T(8,128)(2,1)} %slice.461), channel_id=1, source_target_pairs={{0,4},{2,6},{4,0},{6,2},{8,12},{10,14},{12,8},{14,10},{16,20},{18,... | collective-permute-start | bytes 1572872 | tf_op jit(solution)/shard_map/ppermute | solution.py:378
  617.7 55.4 %collective-permute-start.85 = (bf16[256,1024]{1,0:T(8,128)(2,1)}, bf16[256,1024]{1,0:T(8,128)(2,1)}, u32[]{:S(2)}, u32[]{:S(2)}) collective-permute-start(bf16[256,1024]{1,0:T(8,128)(2,1)} %slice.445), channel_id=1, source_target_pairs={{0,4},{2,6},{4,0},{6,2},{8,12},{10,14},{12,8},{14,10},{16,20},{18,... | collective-permute-start | bytes 1572872 | tf_op jit(solution)/shard_map/ppermute | solution.py:378
  644.6 25.7 %collective-permute-start.101 = (bf16[256,1024]{1,0:T(8,128)(2,1)}, bf16[256,1024]{1,0:T(8,128)(2,1)}, u32[]{:S(2)}, u32[]{:S(2)}) collective-permute-start(bf16[256,1024]{1,0:T(8,128)(2,1)} %add_convert_fusion.21), channel_id=1, source_target_pairs={{0,1},{1,0},{2,3},{3,2},{4,5},{5,4},{6,7},{7,6},{8,9},{9,8},{10,11... | collective-permute-start | bytes 1572872 | tf_op jit(solution)/shard_map/ppermute | solution.py:382
  673.2 23.1 %collective-permute-start.102 = (bf16[128,1024]{1,0:T(8,128)(2,1)}, bf16[128,1024]{1,0:T(8,128)(2,1)}, u32[]{:S(2)}, u32[]{:S(2)}) collective-permute-start(bf16[128,1024]{1,0:T(8,128)(2,1)} %slice.465), channel_id=1, source_target_pairs={{0,8},{2,10},{4,12},{6,14},{8,0},{10,2},{12,4},{14,6},{16,24},{18,... | collective-permute-start | bytes 786440 | tf_op jit(solution)/shard_map/ppermute | solution.py:378
  677.1 23.7 %collective-permute-start.89 = (bf16[128,1024]{1,0:T(8,128)(2,1)}, bf16[128,1024]{1,0:T(8,128)(2,1)}, u32[]{:S(2)}, u32[]{:S(2)}) collective-permute-start(bf16[128,1024]{1,0:T(8,128)(2,1)} %slice.449), channel_id=1, source_target_pairs={{0,8},{2,10},{4,12},{6,14},{8,0},{10,2},{12,4},{14,6},{16,24},{18,... | collective-permute-start | bytes 786440 | tf_op jit(solution)/shard_map/ppermute | solution.py:378
  (187 other events, 2980.2 us)

commit v2 on v1

--- a/solution.py
+++ b/solution.py
@@ -382,56 +382,81 @@
     return lax.ppermute(array, "tensor", [(0, 1), (1, 0)])
 
 
-def gather_pair(shard, size, tensor_first, axis=0):
-    def grow(array, mask):
-        return jnp.concatenate([array, swap_dp(array, size, mask)], axis=axis)
-
-    mask = size // 2
-    own = shard
-    while mask >= 4:
-        own = grow(own, mask)
-        mask //= 2
-    if tensor_first:
-        other = swap_tensor(own)
-        own, other = grow(own, 2), grow(other, 2)
-    else:
-        own = grow(own, 2)
-        other = swap_tensor(own)
-    return grow(own, 1), grow(other, 1)
-
-
 def add_low(left, right):
     return (left.astype(jnp.float32) + right.astype(jnp.float32)).astype(jnp.bfloat16)
 
 
-def scatter_pair(rows, own, other, size, tensor_first):
+def sum_kernel(count, *refs):
+    total = mul(refs[0][...], refs[count][...], NT)
+    for i in range(1, count):
+        total = total + mul(refs[i][...], refs[count + i][...], NT)
+    refs[2 * count][...] = total
+
+
+def sum_products(lefts, rights):
+    rows, columns = lefts[0].shape[0], rights[0].shape[0]
+    block = min(256, rows)
+    depth = sum(left.shape[1] for left in lefts)
+    return pl.pallas_call(
+        functools.partial(sum_kernel, len(lefts)),
+        grid=(rows // block,),
+        in_specs=[pl.BlockSpec((block, left.shape[1]), lambda i: (i, 0)) for left in lefts]
+        + [pl.BlockSpec(right.shape, lambda i: (0, 0)) for right in rights],
+        out_specs=pl.BlockSpec((block, columns), lambda i: (i, 0)),
+        out_shape=jax.ShapeDtypeStruct((rows, columns), jnp.float32),
+        compiler_params=pltpu.CompilerParams(vmem_limit_bytes=40 * 2**20),
+        cost_estimate=pl.CostEstimate(
+            flops=2 * rows * columns * depth,
+            bytes_accessed=2 * (rows + columns) * depth + 4 * rows * columns,
+            transcendentals=0,
+        ),
+    )(*lefts, *rights)
+
+
+def stack_rows(array, arrived):
+    return jnp.concatenate([array, arrived], axis=0)
+
+
+def low_half(array):
+    return array[: array.shape[0] // 2]
+
+
+def high_half(array):
+    return array[array.shape[0] // 2 :]
+
+
+def away_rows(rows, columns):
     half = rows.shape[1] // 2
-
-    def core_sum(columns):
-        away = mul(rows[:, half:], columns, TN).astype(jnp.bfloat16)
-        arrived = swap_dp(away, size, 1)
-        return (mul(rows[:, :half], columns, TN) + arrived.astype(jnp.float32)).astype(jnp.bfloat16)
-
-    def fold(array, mask):
-        middle = array.shape[0] // 2
-        return array[:middle], swap_dp(array[middle:], size, mask)
-
-    own, other = core_sum(own), core_sum(other)
-    if tensor_first:
-        own = add_low(own, swap_tensor(other))
-        own = add_low(*fold(own, 2))
-    else:
-        own, other = add_low(*fold(own, 2)), add_low(*fold(other, 2))
-        own = add_low(own, swap_tensor(other))
-    mask = 4
-    while mask < size:
-        kept, arrived = fold(own, mask)
-        mask *= 2
-        if mask < size:
-            own = add_low(kept, arrived)
-        else:
-            own = kept.astype(jnp.float32) + arrived.astype(jnp.float32)
-    return own
+    return mul(rows[:, half:], columns, TN).astype(jnp.bfloat16)
+
+
+def kept_rows(rows, columns, arrived):
+    half = rows.shape[1] // 2
+    return (mul(rows[:, :half], columns, TN) + arrived.astype(jnp.float32)).astype(jnp.bfloat16)
+
+
+def fold_dp(array, size, mask):
+    return add_low(low_half(array), swap_dp(high_half(array), size, mask))
+
+
+class Steps:
+    def __init__(self):
+        self.live = {}
+
+    def __getattr__(self, name):
+        return self.live[name]
+
+    def put(self, **arrays):
+        self.live.update(arrays)
+
+    def drop(self, *names):
+        for name in names:
+            del self.live[name]
+
+    def cut(self):
+        names = list(self.live)
+        arrays = lax.optimization_barrier(tuple(self.live[name] for name in names))
+        self.live = dict(zip(names, arrays))
 
 
 def norm_rows_grad(grad_in, normal, inverse, norm_gain):
@@ -469,122 +494,242 @@
     size, tokens, d_out, ln1_gain, ln1_bias, w_qkv, w_out, ln2_gain, ln2_bias, w_up, w_down
 ):
     half_rows, _, width = tokens.shape
-    me = lax.axis_index("tensor")
-    first = me == 0
-    order = block_order(size, width)
-
-    def assemble(array):
-        ours = jnp.where(first, array[:, 0], array[:, 1])
-        away = jnp.where(first, array[:, 1], array[:, 0])
-        arrived = swap_tensor(away)
+    first = lax.axis_index("tensor") == 0
+    far, near = size // 2, size // 4
+
+    def split(array):
+        return (
+            jnp.where(first, array[:, 0], array[:, 1]),
+            jnp.where(first, array[:, 1], array[:, 0]),
+        )
+
+    def join(ours, arrived, order):
         rows = jnp.concatenate(
             [jnp.where(first, ours, arrived), jnp.where(first, arrived, ours)], axis=0
         )
         return mul(rows, order).astype(jnp.bfloat16)
 
-    def disperse(rows):
-        rows = mul(rows, order, NT).astype(jnp.bfloat16)
-        ours = jnp.where(first, rows[:half_rows], rows[half_rows:])
-        away = jnp.where(first, rows[half_rows:], rows[:half_rows])
-        arrived = swap_tensor(away)
+    def reorder(rows, order):
+        return mul(rows, order, NT).astype(jnp.bfloat16)
+
+    def part(rows):
+        low, high = rows[:half_rows], rows[half_rows:]
+        return jnp.where(first, low, high), jnp.where(first, high, low)
+
+    def place(ours, arrived):
         return jnp.stack(
             [jnp.where(first, ours, arrived), jnp.where(first, arrived, ours)], axis=1
         )
 
-    local_width = w_qkv.shape[2]
-    pieces = local_width // 256
-    step = local_width // pieces
-    row_count = w_qkv.shape[1]
-    qkv_shards = [
+    def grow(array, mask):
+        return stack_rows(array, swap_dp(array, size, mask))
+
+    def grow_params(array, mask):
+        return jnp.concatenate([array, swap_dp(array, size, mask)], axis=1)
+
+    row_count, local_width = w_qkv.shape[1:]
+    step = local_width // 2
+    qkv_a, qkv_b = (
         w_qkv[:, :, p * step : (p + 1) * step].transpose(1, 0, 2).reshape(row_count, 3 * step)
-        for p in range(pieces)
-    ]
-    params = jnp.stack([ln1_gain, ln1_bias, ln2_gain, ln2_bias])
-    x16 = assemble(tokens)
-    mask = size // 2
-    while mask >= 1:
-        params = jnp.concatenate([params, swap_dp(params, size, mask)], axis=1)
-        mask //= 2
+        for p in range(2)
+    )
+    s = Steps()
+
+    ours, away = split(tokens)
+    arriving = swap_tensor(away)
+    s.put(a=grow(qkv_a, far), b=grow(qkv_b, far))
+    s.put(par=grow_params(jnp.stack([ln1_gain, ln1_bias, ln2_gain, ln2_bias]), far))
+    s.put(o=w_out.T, u=w_up, d=w_down.T, ours=ours, order=block_order(size, width), d_out=d_out)
+    s.cut()
+    s.put(a=grow(s.a, near), b=grow(s.b, near), o=grow(s.o, far), par=grow_params(s.par, near))
+    s.put(arrived=arriving)
+    s.cut()
+    s.put(ax=swap_tensor(s.a), a=grow(s.a, 2), o=grow(s.o, near), par=grow_params(s.par, 2))
+    arriving = grow(s.u, far)
+    s.put(x16=join(s.ours, s.arrived, s.order))
+    s.drop("ours", "arrived")
+    s.cut()
+    s.put(a_own=grow(s.a, 1), b=grow(s.b, 2), ox=swap_tensor(s.o), par=grow_params(s.par, 1))
+    s.put(u=arriving)
     gain_one, bias_one, gain_two, bias_two = (
-        params[i : i + 1].astype(jnp.float32) for i in range(4)
-    )
-    qkv_w = [gather_pair(s, size, p % 2 == 0) for p, s in enumerate(qkv_shards)]
-    out_w = gather_pair(w_out.T, size, True)
-    hidden_step = w_up.shape[1] // 2
-    up_w = [
-        gather_pair(w_up[:, p * hidden_step : (p + 1) * hidden_step], size, p == 0)
-        for p in range(2)
-    ]
-    down_t = w_down.T
-    down_w = [
-        gather_pair(down_t[:, p * hidden_step : (p + 1) * hidden_step], size, p == 0)
-        for p in range(2)
-    ]
-    dy16 = assemble(d_out)
-
-    x = x16.astype(jnp.float32)
-    normed_one, normal_one, inverse_one = norm_rows(x, gain_one, bias_one)
-    normed_one = normed_one.astype(jnp.bfloat16)
-    attended = []
-    for side in range(2):
-        for p in range(pieces):
-            qkv = mul(normed_one, qkv_w[p][side]).astype(jnp.bfloat16)
-            attended.append((qkv,) + tuple(attend(qkv)))
-    mixed = jnp.concatenate([a[1] for a in attended], axis=1)
-    out_all = jnp.concatenate([out_w[0], out_w[1]], axis=1)
-    hidden = x + mul(mixed, out_all, NT)
-    normed_two, normal_two, inverse_two = norm_rows(hidden, gain_two, bias_two)
-    normed_two = normed_two.astype(jnp.bfloat16)
-    up_all = [up_w[p][side] for side in range(2) for p in range(2)]
-    down_all = [down_w[p][side] for side in range(2) for p in range(2)]
-    actives, slopes = [], []
-    for w in up_all:
-        active, slope = gelu_both(mul(normed_two, w))
-        actives.append(active.astype(jnp.bfloat16))
-        slopes.append(slope.astype(jnp.bfloat16))
-
-    grad_down = [
-        scatter_pair(dy16, actives[p], actives[2 + p], size, p == 0) for p in range(2)
-    ]
-    grad_upward = [
-        (mul(dy16, w) * slope.astype(jnp.float32)).astype(jnp.bfloat16)
-        for w, slope in zip(down_all, slopes)
-    ]
-    grad_up = [
-        scatter_pair(normed_two, grad_upward[p], grad_upward[2 + p], size, p == 0)
-        for p in range(2)
-    ]
-    down_cat = jnp.concatenate(down_all, axis=1)
-    up_cat = jnp.concatenate(up_all, axis=1)
-    block_out = (hidden + mul(jnp.concatenate(actives, axis=1), down_cat, NT)).astype(jnp.bfloat16)
-    grad_normed_two = mul(jnp.concatenate(grad_upward, axis=1), up_cat, NT)
+        s.par[i : i + 1].astype(jnp.float32) for i in range(4)
+    )
+    normed, normal, inverse = norm_rows(s.x16.astype(jnp.float32), gain_one, bias_one)
+    s.put(n1=normed.astype(jnp.bfloat16), normal1=normal, inverse1=inverse)
+    s.put(gain_one=gain_one, gain_two=gain_two, bias_two=bias_two)
+    s.drop("a", "par")
+    s.cut()
+    b_arriving = swap_tensor(s.b)
+    arriving = grow(s.u, near)
+    s.put(b_own=grow(s.b, 1), ax=grow(s.ax, 2))
+    qkv = mul(s.n1, s.a_own).astype(jnp.bfloat16)
+    mixed, lse = attend(qkv)
+    s.put(qkv0=qkv, mixed0=mixed, lse0=lse)
+    s.drop("b")
+    s.cut()
+    s.put(a_oth=grow(s.ax, 1), o=grow(s.o, 2), ox=grow(s.ox, 2))
+    qkv = mul(s.n1, s.b_own).astype(jnp.bfloat16)
+    mixed, lse = attend(qkv)
+    s.put(qkv1=qkv, mixed1=mixed, lse1=lse, bx=b_arriving, u=arriving)
+    s.drop("ax")
+    s.cut()
+    x_arriving = swap_tensor(s.u)
+    y_arriving = grow(s.u, 2)
+    s.put(b_oth=grow(s.bx, 1), o=grow(s.o, 1), ox=grow(s.ox, 1), d=grow(s.d, far))
+    qkv = mul(s.n1, s.a_oth).astype(jnp.bfloat16)
+    mixed, lse = attend(qkv)
+    s.put(qkv2=qkv, mixed2=mixed, lse2=lse)
+    s.drop("bx")
+    s.cut()
+    s.put(d=grow(s.d, near))
+    qkv = mul(s.n1, s.b_oth).astype(jnp.bfloat16)
+    mixed, lse = attend(qkv)
+    s.put(qkv3=qkv, mixed3=mixed, lse3=lse, ux=x_arriving, u=y_arriving)
+    s.cut()
+    y_arriving = grow(s.ux, 2)
+    ours, away = split(s.d_out)
+    x_arriving = swap_tensor(away)
+    s.put(u_own=grow(s.u, 1))
+    mixed = jnp.concatenate([s.mixed0, s.mixed1, s.mixed2, s.mixed3], axis=1)
+    out_all = jnp.concatenate([s.o, s.ox], axis=1)
+    hidden = s.x16.astype(jnp.float32) + mul(mixed, out_all, NT)
+    normed, normal, inverse = norm_rows(hidden, s.gain_two, s.bias_two)
+    s.put(mixed=mixed, out_all=out_all, hidden=hidden, n2=normed.astype(jnp.bfloat16))
+    s.put(normal2=normal, inverse2=inverse, ours=ours)
+    s.drop("u", "o", "ox", "x16", "d_out", "bias_two")
+    s.cut()
+    active, slope = gelu_both(mul(s.n2, s.u_own))
+    s.put(active0=active.astype(jnp.bfloat16), slope0=slope.astype(jnp.bfloat16))
+    s.put(ux=y_arriving, arrived=x_arriving)
+    s.cut()
+    s.put(u_oth=grow(s.ux, 1))
+    x_arriving = swap_tensor(s.d)
+    y_arriving = grow(s.d, 2)
+    dy16 = join(s.ours, s.arrived, s.order)
+    away0 = away_rows(dy16, s.active0)
+    s.put(dy16=dy16, down0=swap_dp(away0, size, 1))
+    s.drop("ux", "ours", "arrived")
+    s.cut()
+    active, slope = gelu_both(mul(s.n2, s.u_oth))
+    s.put(active1=active.astype(jnp.bfloat16), slope1=slope.astype(jnp.bfloat16))
+    s.put(dx=x_arriving, d=y_arriving)
+    s.cut()
+    y_arriving = grow(s.dx, 2)
+    s.put(d_own=grow(s.d, 1))
+    away1 = away_rows(s.dy16, s.active1)
+    s.put(down1=swap_dp(away1, size, 1), down0=kept_rows(s.dy16, s.active0, s.down0))
+    s.drop("d")
+    s.cut()
+    grad = mul(s.dy16, s.d_own) * s.slope0.astype(jnp.float32)
+    s.put(up_grad0=grad.astype(jnp.bfloat16), down1=kept_rows(s.dy16, s.active1, s.down1))
+    s.put(dx=y_arriving)
+    s.drop("slope0")
+    s.cut()
+    down_arriving = swap_tensor(s.down1)
+    s.put(d_oth=grow(s.dx, 1))
+    s.put(up0=swap_dp(away_rows(s.n2, s.up_grad0), size, 1))
+    s.drop("dx", "down1")
+    s.cut()
+    grad = mul(s.dy16, s.d_oth) * s.slope1.astype(jnp.float32)
+    grad = grad.astype(jnp.bfloat16)
+    s.put(up_grad1=grad, up1=swap_dp(away_rows(s.n2, grad), size, 1))
+    s.put(up0=kept_rows(s.n2, s.up_grad0, s.up0))
+    s.drop("slope1")
+    s.cut()
+    total = sum_products([s.active0, s.active1], [s.d_own, s.d_oth])
+    rows = reorder((s.hidden + total).astype(jnp.bfloat16), s.order)
+    ours, away = part(rows)
+    s.put(ours=ours, away=away, up1=kept_rows(s.n2, s.up_grad1, s.up1))
+    s.drop("active0", "active1", "d_own", "d_oth", "hidden", "n2")
+    s.cut()
+    s.put(down0=add_low(s.down0, down_arriving))
+    s.cut()
+    x_arriving = swap_tensor(s.away)
+    s.put(down0=fold_dp(s.down0, size, 2))
+    s.put(grad_n2=sum_products([s.up_grad0, s.up_grad1], [s.u_own, s.u_oth]))
+    s.drop("away", "up_grad0", "up_grad1", "u_own", "u_oth")
+    s.cut()
+    up0_arriving = fold_dp(s.up0, size, 2)
+    up1_arriving = fold_dp(s.up1, size, 2)
+    s.put(down0=fold_dp(s.down0, size, near))
     grad_norm, gain_two_grad, bias_two_grad = norm_rows_grad(
-        grad_normed_two, normal_two, inverse_two, gain_two
-    )
-    grad_hidden = dy16.astype(jnp.float32) + grad_norm
+        s.grad_n2, s.normal2, s.inverse2, s.gain_two
+    )
+    grad_hidden = s.dy16.astype(jnp.float32) + grad_norm
     low_hidden = grad_hidden.astype(jnp.bfloat16)
-
-    grad_out = scatter_pair(
-        low_hidden, mixed[:, :local_width], mixed[:, local_width:], size, True
-    )
-    grad_mixed = mul(low_hidden, out_all).astype(jnp.bfloat16)
-    grad_qkv16 = []
-    for n, (qkv, mixed_n, lse) in enumerate(attended):
-        grad_qkv16.append(
-            attend_grad(qkv, grad_mixed[:, n * step : (n + 1) * step], mixed_n, lse)
+    s.put(gain_two_grad=gain_two_grad, bias_two_grad=bias_two_grad, grad_hidden=grad_hidden)
+    s.put(low_hidden=low_hidden, grad_mixed=mul(low_hidden, s.out_all).astype(jnp.bfloat16))
+    s.put(out0=swap_dp(away_rows(low_hidden, s.mixed[:, :local_width]), size, 1))
+    s.put(out1=swap_dp(away_rows(low_hidden, s.mixed[:, local_width:]), size, 1))
+    s.drop("grad_n2", "normal2", "inverse2", "gain_two", "out_all", "dy16", "up0", "up1")
+    s.cut()
+    down_grad = swap_dp(high_half(s.down0), size, far).astype(jnp.float32)
+    s.put(down=low_half(s.down0).astype(jnp.float32) + down_grad)
+    s.put(out0=kept_rows(s.low_hidden, s.mixed[:, :local_width], s.out0))
+    s.put(out1=kept_rows(s.low_hidden, s.mixed[:, local_width:], s.out1))
+    s.put(dqkv0=attend_grad(s.qkv0, s.grad_mixed[:, :step], s.mixed0, s.lse0))
+    s.drop("low_hidden", "mixed", "qkv0", "mixed0", "lse0", "down0")
+    s.cut()
+    s.put(out0=add_low(s.out0, swap_tensor(s.out1)), block_away=x_arriving)
+    s.put(dqkv2=attend_grad(s.qkv2, s.grad_mixed[:, 2 * step : 3 * step], s.mixed2, s.lse2))
+    s.drop("out1", "qkv2", "mixed2", "lse2")
+    s.cut()
+    s.put(a0=swap_dp(away_rows(s.n1, s.dqkv0), size, 1))
+    s.put(a1=swap_dp(away_rows(s.n1, s.dqkv2), size, 1))
+    s.put(dqkv1=attend_grad(s.qkv1, s.grad_mixed[:, step : 2 * step], s.mixed1, s.lse1))
+    s.put(up0=up0_arriving, up1=up1_arriving)
+    s.drop("qkv1", "mixed1", "lse1")
+    s.cut()
+    arriving = swap_tensor(s.up1)
+    s.put(out0=fold_dp(s.out0, size, 2))
+    s.put(a0=kept_rows(s.n1, s.dqkv0, s.a0), a1=kept_rows(s.n1, s.dqkv2, s.a1))
+    s.put(dqkv3=attend_grad(s.qkv3, s.grad_mixed[:, 3 * step :], s.mixed3, s.lse3))
+    s.drop("up1", "qkv3", "mixed3", "lse3", "grad_mixed")
+    s.cut()
+    a0, a1 = fold_dp(s.a0, size, 2), fold_dp(s.a1, size, 2)
+    s.put(b0=swap_dp(away_rows(s.n1, s.dqkv1), size, 1))
+    s.put(b1=swap_dp(away_rows(s.n1, s.dqkv3), size, 1))
+    s.put(out0=fold_dp(s.out0, size, near))
+    s.put(
+        grad_n1=sum_products(
+            [s.dqkv0, s.dqkv1, s.dqkv2, s.dqkv3], [s.a_own, s.b_own, s.a_oth, s.b_oth]
         )
-    grad_qkv = [
-        scatter_pair(normed_one, grad_qkv16[p], grad_qkv16[pieces + p], size, p % 2 == 0)
-        for p in range(pieces)
-    ]
-    qkv_cat = jnp.concatenate([qkv_w[p][side] for side in range(2) for p in range(pieces)], axis=1)
-    grad_normed_one = mul(jnp.concatenate(grad_qkv16, axis=1), qkv_cat, NT)
+    )
+    s.put(up0=add_low(s.up0, arriving), a0=a0, a1=a1)
+    s.drop("dqkv0", "dqkv2", "a_own", "b_own", "a_oth", "b_oth")
+    s.cut()
+    s.put(up0=fold_dp(s.up0, size, near))
+    s.put(b0=kept_rows(s.n1, s.dqkv1, s.b0), b1=kept_rows(s.n1, s.dqkv3, s.b1))
     grad_norm, gain_one_grad, bias_one_grad = norm_rows_grad(
-        grad_normed_one, normal_one, inverse_one, gain_one
-    )
-    input_grad = (grad_hidden + grad_norm).astype(jnp.bfloat16)
-
-    sums = jnp.concatenate([gain_one_grad, bias_one_grad, gain_two_grad, bias_two_grad], axis=0)
+        s.grad_n1, s.normal1, s.inverse1, s.gain_one
+    )
+    rows = reorder((s.grad_hidden + grad_norm).astype(jnp.bfloat16), s.order)
+    ours, away = part(rows)
+    s.put(input_ours=ours, input_away=away)
+    s.put(
+        sums=jnp.concatenate(
+            [gain_one_grad, bias_one_grad, s.gain_two_grad, s.bias_two_grad], axis=0
+        )
+    )
+    s.cut()
+    input_grad = place(s.input_ours, swap_tensor(s.input_away))
+    block_out = place(s.ours, s.block_away)
+
+    def last_folds(array):
+        array = fold_dp(array, size, near)
+        arrived = swap_dp(high_half(array), size, far)
+        return low_half(array).astype(jnp.float32) + arrived.astype(jnp.float32)
+
+    def last_fold(array):
+        arrived = swap_dp(high_half(array), size, far)
+        return low_half(array).astype(jnp.float32) + arrived.astype(jnp.float32)
+
+    grad_a = last_folds(add_low(s.a0, swap_tensor(s.a1)))
+    b0, b1 = fold_dp(s.b0, size, 2), fold_dp(s.b1, size, 2)
+    grad_b = last_folds(add_low(b0, swap_tensor(b1)))
+    grad_up = last_fold(s.up0)
+    grad_out = last_fold(s.out0)
+    sums = s.sums
     mask = 1
     while mask < size:
         middle = sums.shape[1] // 2
@@ -593,25 +738,25 @@
     sums = sums + swap_tensor(sums)
 
     return (
-        disperse(block_out),
-        disperse(input_grad),
+        block_out,
+        input_grad,
         sums[0],
         sums[1],
         jnp.concatenate(
-            [g.reshape(row_count, 3, step).transpose(1, 0, 2) for g in grad_qkv], axis=2
+            [g.reshape(row_count, 3, step).transpose(1, 0, 2) for g in (grad_a, grad_b)], axis=2
         ),
         grad_out.T,
         sums[2],
         sums[3],
-        jnp.concatenate(grad_up, axis=1),
-        jnp.concatenate(grad_down, axis=1).T,
+        grad_up,
+        s.down.T,
     )
 
 
 def solution(mesh):
     sizes = dict(mesh.shape)
     dp_size, tensor_size = sizes["dp"], sizes["tensor"]
-    if tensor_size == 2 and dp_size >= 4 and dp_size & (dp_size - 1) == 0:
+    if tensor_size == 2 and dp_size == 16:
         body = functools.partial(on_device_whole, dp_size)
     else:
         body = on_device_shared

time: 718 us -> 564 us (0.79)
  matrix products: 180 us -> 105 us
  local copies, waits for them, and re-layouts: 83.1 us -> 31.5 us
  starting transfers between devices: 91.7 us -> 54.6 us
  Pallas kernels: 66 us -> 101 us
  waiting for transfers between devices: 248 us -> 214 us
    dot_general x49 -> x34, matrix products: 180 us -> 105 us  [mul(): lax.dot_general(left, right, dims, preferred_element_type=jnp.float32)]
    ppermute x19 -> x15, waiting for transfers between devices: 93.2 us -> 49.1 us  [swap_tensor(): return lax.ppermute(array, 'tensor', [(0, 1), (1, 0)])]
    pallas_call x0 -> x3, Pallas kernels: none -> 34.7 us  [sum_products(): pl.pallas_call(functools.partial(sum_kernel, len(lefts)), grid=(rows // b...]
    unnamed x303 -> x137, local copies, waits for them, and re-layouts: 47.7 us -> 20.4 us
    ppermute x85 -> x65, starting transfers between devices: 68.6 us -> 42.2 us  [swap_dp(): return lax.ppermute(array, 'dp', [(i, i ^ mask) for i in range(size)])]
    dot_general x2 -> x0, local copies, waits for them, and re-layouts: 10.7 us -> none  [mul(): lax.dot_general(left, right, dims, preferred_element_type=jnp.float32)]
    ppermute x19 -> x15, starting transfers between devices: 23.1 us -> 12.4 us  [swap_tensor(): return lax.ppermute(array, 'tensor', [(0, 1), (1, 0)])]
    slice x27 -> x23, local copies, waits for them, and re-layouts: 18.9 us -> 9.44 us  [the longest x1 6.57 us: split(): array[:, 0]]
  transfers between devices with their start and end apart: 104 -> 80, of which waited for: 40 -> 33; matrix products, arithmetic and copies ran while one was open for 40% -> 26% of each run, Pallas kernels for 9% -> 18%
where the time goes in v2:
time: 564 us; the launch traced here: 557 us
  waiting for transfers between devices  214 us (38%)
  matrix products  105 us (19%)
  Pallas kernels  101 us (18%)
  starting transfers between devices  54.6 us (10%)
  other arithmetic  47.9 us (8%)
  local copies, waits for them, and re-layouts  31.5 us (6%)
    ppermute x65, waiting for transfers between devices, swap_dp(): return lax.ppermute(array, 'dp', [(i, i ^ mask) for i in range(size)])  164 us
    dot_general x34, matrix products, mul(): lax.dot_general(left, right, dims, preferred_element_type=jnp.float32)  105 us
    ppermute x15, waiting for transfers between devices, swap_tensor(): return lax.ppermute(array, 'tensor', [(0, 1), (1, 0)])  49.1 us
    ppermute x65, starting transfers between devices, swap_dp(): return lax.ppermute(array, 'dp', [(i, i ^ mask) for i in range(size)])  42.2 us
    pallas_call x4, Pallas kernels, attend_grad(): pl.pallas_call(back_kernel, grid=(pairs,), in_specs=[pl.BlockSpec((length...  35.2 us
    pallas_call x3, Pallas kernels, sum_products(): pl.pallas_call(functools.partial(sum_kernel, len(lefts)), grid=(rows // b...  34.7 us
    pallas_call x4, Pallas kernels, attend(): pl.pallas_call(fwd_kernel, grid=(pairs,), in_specs=[pl.BlockSpec((length,...  30.8 us
    unnamed x137, local copies, waits for them, and re-layouts  20.4 us
  transfers between devices with their start and end apart: 80, of which 33 were waited for; matrix products, arithmetic and copies ran while one was open for 26% of the time, Pallas kernels for 18%

profile of v2, /device:TPU:0, one launch (start us, length us, event | category | flops | bytes accessed | tf_op | source)
XLA Modules:
  0.0 556.9 jit_solution(11834733640827397216)
XLA Ops:
  1.9 4.0 collective-permute-start.2
  10.0 6.6 %fusion.92 = (bf16[512,1,1024]{2,1,0:T(2,128)(2,1)S(1)}, bf16[512,1,1024]{2,1,0:T(2,128)(2,1)}) fusion(bf16[512,2,1024]{2,1,0:T(2,128)(2,1)} %param.10), kind=kLoop, calls=%fused_computation.271 | loop fusion | bytes 4194304 | tf_op jit(solution)/shard_map/slice | solution.py:502
  16.6 3.2 select_bitcast_fusion.6
  26.9 3.8 collective-permute-done.6
  35.5 8.6 %collective-permute-done.7 = bf16[512,1024]{1,0:T(8,128)(2,1)S(1)} collective-permute-done((bf16[512,1024]{1,0:T(8,128)(2,1)}, bf16[512,1024]{1,0:T(8,128)(2,1)S(1)}, u32[]{:S(2)}, u32[]{:S(2)}) %collective-permute-start.7) | collective-permute-done | bytes 1048608 | tf_op jit(solution)/shard_map/ppermute | solution.py:382
  54.4 6.5 %collective-permute-done.13 = bf16[64,2048]{1,0:T(8,128)(2,1)S(1)} collective-permute-done((bf16[64,2048]{1,0:T(8,128)(2,1)}, bf16[64,2048]{1,0:T(8,128)(2,1)S(1)}, u32[]{:S(2)}, u32[]{:S(2)}) %collective-permute-start.13) | collective-permute-done | bytes 262176 | tf_op jit(solution)/shard_map/ppermute | solution.py:378
  68.3 6.7 %collective-permute-done.12 = bf16[256,768]{1,0:T(8,128)(2,1)S(1)} collective-permute-done((bf16[256,768]{1,0:T(8,128)(2,1)S(1)}, bf16[256,768]{1,0:T(8,128)(2,1)S(1)}, u32[]{:S(2)}, u32[]{:S(2)}) %collective-permute-start.12) | collective-permute-done | bytes 393248 | tf_op jit(solution)/shard_map/ppermute | solution.py:378
  81.2 8.0 %shard_map.177 = (bf16[1024,256]{1,0:T(8,128)(2,1)S(1)}, f32[2,8,1024]{2,1,0:T(8,128)S(1)}) custom-call(bf16[1024,768]{1,0:T(8,128)(2,1)S(1)} %convolution_convert_fusion.8.q_ref.k_ref.v_ref, bf16[1024,768]{1,0:T(8,128)(2,1)S(1)} %convolution_convert_fusion.8.q_ref.k_ref.v_ref, bf16[1024,768]{1,0:T(8,128)(2,1)S(1)} %convolution_convert_fusion.8.q_ref.k_ref.v_ref), custom_call_target="tpu_custom_call" | custom-call | flops 2147483648 | bytes 2097152 | tf_op jit(solution)/shard_map/pallas_call | solution.py:280
  97.6 7.5 %shard_map.178 = (bf16[1024,256]{1,0:T(8,128)(2,1)S(1)}, f32[2,8,1024]{2,1,0:T(8,128)S(1)}) custom-call(bf16[1024,768]{1,0:T(8,128)(2,1)S(1)} %convolution_convert_fusion.7.q_ref.k_ref.v_ref, bf16[1024,768]{1,0:T(8,128)(2,1)S(1)} %convolution_convert_fusion.7.q_ref.k_ref.v_ref, bf16[1024,768]{1,0:T(8,128)(2,1)S(1)} %convolution_convert_fusion.7.q_ref.k_ref.v_ref), custom_call_target="tpu_custom_call" | custom-call | flops 2147483648 | bytes 2097152 | tf_op jit(solution)/shard_map/pallas_call | solution.py:280
  110.8 7.7 %shard_map.179 = (bf16[1024,256]{1,0:T(8,128)(2,1)S(1)}, f32[2,8,1024]{2,1,0:T(8,128)S(1)}) custom-call(bf16[1024,768]{1,0:T(8,128)(2,1)S(1)} %convolution_convert_fusion.6.q_ref.k_ref.v_ref, bf16[1024,768]{1,0:T(8,128)(2,1)S(1)} %convolution_convert_fusion.6.q_ref.k_ref.v_ref, bf16[1024,768]{1,0:T(8,128)(2,1)S(1)} %convolution_convert_fusion.6.q_ref.k_ref.v_ref), custom_call_target="tpu_custom_call" | custom-call | flops 2147483648 | bytes 2097152 | tf_op jit(solution)/shard_map/pallas_call | solution.py:280
  125.1 7.7 %shard_map.180 = (bf16[1024,256]{1,0:T(8,128)(2,1)S(1)}, f32[2,8,1024]{2,1,0:T(8,128)S(1)}) custom-call(bf16[1024,768]{1,0:T(8,128)(2,1)S(1)} %convolution_convert_fusion.5.q_ref.k_ref.v_ref, bf16[1024,768]{1,0:T(8,128)(2,1)S(1)} %convolution_convert_fusion.5.q_ref.k_ref.v_ref, bf16[1024,768]{1,0:T(8,128)(2,1)S(1)} %convolution_convert_fusion.5.q_ref.k_ref.v_ref), custom_call_target="tpu_custom_call" | custom-call | flops 2147483648 | bytes 2097152 | tf_op jit(solution)/shard_map/pallas_call | solution.py:280
  132.8 13.5 %collective-permute-done.28 = bf16[256,2048]{1,0:T(8,128)(2,1)S(1)} collective-permute-done((bf16[256,2048]{1,0:T(8,128)(2,1)S(1)}, bf16[256,2048]{1,0:T(8,128)(2,1)S(1)}, u32[]{:S(2)}, u32[]{:S(2)}) %collective-permute-start.28) | collective-permute-done | bytes 1048608 | tf_op jit(solution)/shard_map/ppermute | solution.py:378
  156.0 15.0 %collective-permute-done.32 = bf16[256,2048]{1,0:T(8,128)(2,1)S(1)} collective-permute-done((bf16[256,2048]{1,0:T(8,128)(2,1)S(1)}, bf16[256,2048]{1,0:T(8,128)(2,1)S(1)}, u32[]{:S(2)}, u32[]{:S(2)}) %collective-permute-start.32) | collective-permute-done | bytes 1048608 | tf_op jit(solution)/shard_map/ppermute | solution.py:378
  171.9 10.7 %fusion.5 = (bf16[1024,2048]{1,0:T(8,128)(2,1)}, bf16[1024,2048]{1,0:T(8,128)(2,1)S(1)}) fusion(bf16[1024,1024]{1,0:T(8,128)(2,1)S(1)} %get-tuple-element.1155, bf16[1024,2048]{1,0:T(8,128)(2,1)S(1)} %pad_maximum_fusion.refs_2_), kind=kOutput, calls=%fused_computation.13 | convolution fusion | flops 4336910336 | bytes 14680064 | tf_op jit(solution)/shard_map/dot_general | solution.py:240
  189.2 24.1 %collective-permute-done.34 = bf16[256,2048]{1,0:T(8,128)(2,1)S(1)} collective-permute-done((bf16[256,2048]{1,0:T(8,128)(2,1)S(1)}, bf16[256,2048]{1,0:T(8,128)(2,1)S(1)}, u32[]{:S(2)}, u32[]{:S(2)}) %collective-permute-start.34) | collective-permute-done | bytes 1048608 | tf_op jit(solution)/shard_map/ppermute | solution.py:378
  214.2 10.9 %fusion.11 = (bf16[1024,2048]{1,0:T(8,128)(2,1)}, bf16[1024,2048]{1,0:T(8,128)(2,1)S(1)}) fusion(bf16[1024,1024]{1,0:T(8,128)(2,1)S(1)} %get-tuple-element.1155, bf16[1024,2048]{1,0:T(8,128)(2,1)S(1)} %pad_maximum_fusion.1.refs_3_), kind=kOutput, calls=%fused_computation.19 | convolution fusion | flops 4336910336 | bytes 14680064 | tf_op jit(solution)/shard_map/dot_general | solution.py:240
  225.2 3.7 convolution_convert_fusion.2
  229.9 3.7 add_convert_fusion.6
  233.6 20.8 %collective-permute-done.40 = bf16[256,2048]{1,0:T(8,128)(2,1)S(1)} collective-permute-done((bf16[256,2048]{1,0:T(8,128)(2,1)S(1)}, bf16[256,2048]{1,0:T(8,128)(2,1)S(1)}, u32[]{:S(2)}, u32[]{:S(2)}) %collective-permute-start.40) | collective-permute-done | bytes 1048608 | tf_op jit(solution)/shard_map/ppermute | solution.py:378
  255.3 3.7 add_convert_fusion.5
  259.8 4.7 multiply_convert_fusion.1.refs_0_
  264.6 3.7 convolution_convert_fusion.1
  269.4 3.5 collective-permute-done.42
  273.0 6.4 %multiply_convert_fusion.refs_1_ = bf16[1024,2048]{1,0:T(8,128)(2,1)S(1)} fusion(bf16[1024,2048]{1,0:T(8,128)(2,1)} %get-tuple-element.1121, bf16[1024,1024]{1,0:T(8,128)(2,1)S(1)} %fusion.48, bf16[1024,2048]{1,0:T(8,128)(2,1)S(1)} %pad_maximum_fusion.3.refs_3_), kind=kOutput, calls=%fused_computation.20 | convolution fusion | flops 4301258752 | bytes 14680064 | tf_op jit(solution)/shard_map/dot_general | solution.py:240
  282.8 5.3 add_convert_fusion.4
  288.1 13.1 %shard_map.181 = f32[1024,1024]{1,0:T(8,128)S(1)} custom-call(bf16[1024,2048]{1,0:T(8,128)(2,1)S(1)} %get-tuple-element.1158.refs_0_, bf16[1024,2048]{1,0:T(8,128)(2,1)S(1)} %get-tuple-element.1159.refs_1_, bf16[1024,2048]{1,0:T(8,128)(2,1)} %copy-done.33, bf16[1024,2048]{1,0:T(8,128)(2,1)} %copy-done.34), custom_call_target="tpu_custom_call" | custom-call | flops 8589934592 | bytes 20971520 | tf_op jit(solution)/shard_map/pallas_call | solution.py:400
  301.2 5.2 fusion.55
  308.5 4.1 add_convert_fusion.3
  312.6 17.6 %collective-permute-done.44 = bf16[512,2048]{1,0:T(8,128)(2,1)} collective-permute-done((bf16[512,2048]{1,0:T(8,128)(2,1)}, bf16[512,2048]{1,0:T(8,128)(2,1)}, u32[]{:S(2)}, u32[]{:S(2)}) %collective-permute-start.44) | collective-permute-done | bytes 2097184 | tf_op jit(solution)/shard_map/ppermute | solution.py:382
  334.9 13.1 %shard_map.182 = f32[1024,1024]{1,0:T(8,128)S(1)} custom-call(bf16[1024,2048]{1,0:T(8,128)(2,1)S(1)} %multiply_convert_fusion.1.refs_0_, bf16[1024,2048]{1,0:T(8,128)(2,1)S(1)} %multiply_convert_fusion.refs_1_, bf16[1024,2048]{1,0:T(8,128)(2,1)} %copy-done.31, bf16[1024,2048]{1,0:T(8,128)(2,1)} %copy-done.32), custom_call_target="tpu_custom_call" | custom-call | flops 8589934592 | bytes 20971520 | tf_op jit(solution)/shard_map/pallas_call | solution.py:400
  348.0 10.6 %collective-permute-done.45 = bf16[256,2048]{1,0:T(8,128)(2,1)} collective-permute-done((bf16[256,2048]{1,0:T(8,128)(2,1)}, bf16[256,2048]{1,0:T(8,128)(2,1)}, u32[]{:S(2)}, u32[]{:S(2)}) %collective-permute-start.45) | collective-permute-done | bytes 1048608 | tf_op jit(solution)/shard_map/ppermute | solution.py:378
  369.8 7.4 %collective-permute-done.46 = bf16[128,2048]{1,0:T(8,128)(2,1)S(1)} collective-permute-done((bf16[128,2048]{1,0:T(8,128)(2,1)S(1)}, bf16[128,2048]{1,0:T(8,128)(2,1)S(1)}, u32[]{:S(2)}, u32[]{:S(2)}) %collective-permute-start.46) | collective-permute-done | bytes 524320 | tf_op jit(solution)/shard_map/ppermute | solution.py:378
  380.2 8.7 %shard_map.183.refs_0_ = bf16[1024,768]{1,0:T(8,128)(2,1)S(1)} custom-call(bf16[1024,768]{1,0:T(8,128)(2,1)S(1)} %copy-done.19, bf16[1024,768]{1,0:T(8,128)(2,1)S(1)} %copy-done.19, bf16[1024,768]{1,0:T(8,128)(2,1)S(1)} %copy-done.19, bf16[1024,256]{1,0:T(8,128)(2,1)S(1)} %slice.294.do_ref, bf16[1024,256]{1,0:T(8,128)(2,1)S(1)} %copy-done.11, ...), custom_call_target="tpu_custom_call" | custom-call | flops 5368709120 | bytes 4194304 | tf_op jit(solution)/shard_map/pallas_call | solution.py:357
  392.8 8.8 %shard_map.184.refs_2_ = bf16[1024,768]{1,0:T(8,128)(2,1)S(1)} custom-call(bf16[1024,768]{1,0:T(8,128)(2,1)S(1)} %copy-done.23, bf16[1024,768]{1,0:T(8,128)(2,1)S(1)} %copy-done.23, bf16[1024,768]{1,0:T(8,128)(2,1)S(1)} %copy-done.23, bf16[1024,256]{1,0:T(8,128)(2,1)S(1)} %slice.295.do_ref, bf16[1024,256]{1,0:T(8,128)(2,1)S(1)} %copy-done.15, ...), custom_call_target="tpu_custom_call" | custom-call | flops 5368709120 | bytes 4194304 | tf_op jit(solution)/shard_map/pallas_call | solution.py:357
  409.4 7.3 %collective-permute-done.54 = bf16[256,2048]{1,0:T(8,128)(2,1)S(1)} collective-permute-done((bf16[256,2048]{1,0:T(8,128)(2,1)}, bf16[256,2048]{1,0:T(8,128)(2,1)S(1)}, u32[]{:S(2)}, u32[]{:S(2)}) %collective-permute-start.54) | collective-permute-done | bytes 1048608 | tf_op jit(solution)/shard_map/ppermute | solution.py:378
  417.2 8.9 %shard_map.185.refs_1_ = bf16[1024,768]{1,0:T(8,128)(2,1)S(1)} custom-call(bf16[1024,768]{1,0:T(8,128)(2,1)S(1)} %copy-done.17, bf16[1024,768]{1,0:T(8,128)(2,1)S(1)} %copy-done.17, bf16[1024,768]{1,0:T(8,128)(2,1)S(1)} %copy-done.17, bf16[1024,256]{1,0:T(8,128)(2,1)S(1)} %slice.297.do_ref, bf16[1024,256]{1,0:T(8,128)(2,1)S(1)} %copy-done.9, ...), custom_call_target="tpu_custom_call" | custom-call | flops 5368709120 | bytes 4194304 | tf_op jit(solution)/shard_map/pallas_call | solution.py:357
  429.7 8.7 %shard_map.186.refs_3_ = bf16[1024,768]{1,0:T(8,128)(2,1)S(1)} custom-call(bf16[1024,768]{1,0:T(8,128)(2,1)S(1)} %copy-done.21, bf16[1024,768]{1,0:T(8,128)(2,1)S(1)} %copy-done.21, bf16[1024,768]{1,0:T(8,128)(2,1)S(1)} %copy-done.21, bf16[1024,256]{1,0:T(8,128)(2,1)S(1)} %slice.305.do_ref, bf16[1024,256]{1,0:T(8,128)(2,1)S(1)} %copy-done.13, ...), custom_call_target="tpu_custom_call" | custom-call | flops 5368709120 | bytes 4194304 | tf_op jit(solution)/shard_map/pallas_call | solution.py:357
  448.7 8.5 %shard_map.187 = f32[1024,1024]{1,0:T(8,128)} custom-call(bf16[1024,768]{1,0:T(8,128)(2,1)S(1)} %shard_map.183.refs_0_, bf16[1024,768]{1,0:T(8,128)(2,1)S(1)} %shard_map.185.refs_1_, bf16[1024,768]{1,0:T(8,128)(2,1)S(1)} %shard_map.184.refs_2_, bf16[1024,768]{1,0:T(8,128)(2,1)S(1)} %shard_map.186.refs_3_, bf16[1024,768]{1,0:T(8,128)(2,1)S(1)} %copy-done.1, ...), custom_call_target="tpu_custom_call" | custom-call | flops 6442450944 | bytes 16777216 | tf_op jit(solution)/shard_map/pallas_call | solution.py:400
  462.6 3.8 multiply_reduce_fusion
  475.7 4.8 collective-permute-done.63
  486.9 3.3 collective-permute-done.67
  496.5 3.5 copy.38
  506.2 3.0 collective-permute-done.78
  510.4 3.8 collective-permute-done.74
  518.5 4.5 collective-permute-done.71
  523.2 19.2 %collective-permute-done.75 = bf16[256,768]{1,0:T(8,128)(2,1)S(1)} collective-permute-done((bf16[256,768]{1,0:T(8,128)(2,1)S(1)}, bf16[256,768]{1,0:T(8,128)(2,1)S(1)}, u32[]{:S(2)}, u32[]{:S(2)}) %collective-permute-start.75) | collective-permute-done | bytes 393248 | tf_op jit(solution)/shard_map/ppermute | solution.py:382
  543.1 6.2 %collective-permute-done.76 = bf16[128,768]{1,0:T(8,128)(2,1)S(1)} collective-permute-done((bf16[128,768]{1,0:T(8,128)(2,1)S(1)}, bf16[128,768]{1,0:T(8,128)(2,1)S(1)}, u32[]{:S(2)}, u32[]{:S(2)}) %collective-permute-start.76) | collective-permute-done | bytes 196640 | tf_op jit(solution)/shard_map/ppermute | solution.py:378
  551.0 3.5 copy.39
  (423 shorter events, 175.7 us)
Async XLA Ops:
  1.9 20.1 %collective-permute-start.2 = (bf16[4,64]{1,0:T(4,128)(2,1)}, bf16[4,64]{1,0:T(4,128)(2,1)}, u32[]{:S(2)}, u32[]{:S(2)}) collective-permute-start(bf16[4,64]{1,0:T(4,128)(2,1)} %pad_maximum_fusion.35), channel_id=1, source_target_pairs={{0,16},{2,18},{4,20},{6,22},{8,24},{10,26},{12,28},{14,30},{16,0},... | collective-permute-start | bytes 1544 | tf_op jit(solution)/shard_map/ppermute | solution.py:378
  6.9 15.9 %collective-permute-start = (bf16[64,768]{1,0:T(8,128)(2,1)S(1)}, bf16[64,768]{1,0:T(8,128)(2,1)S(1)}, u32[]{:S(2)}, u32[]{:S(2)}) collective-permute-start(bf16[64,768]{1,0:T(8,128)(2,1)S(1)} %bitcast.100), channel_id=1, source_target_pairs={{0,16},{2,18},{4,20},{6,22},{8,24},{10,26},{12,28},{14,30},{16,0},... | collective-permute-start | bytes 294920 | tf_op jit(solution)/shard_map/ppermute | solution.py:378
  7.0 15.8 %collective-permute-start.1 = (bf16[64,768]{1,0:T(8,128)(2,1)S(1)}, bf16[64,768]{1,0:T(8,128)(2,1)S(1)}, u32[]{:S(2)}, u32[]{:S(2)}) collective-permute-start(bf16[64,768]{1,0:T(8,128)(2,1)S(1)} %bitcast.102), channel_id=1, source_target_pairs={{0,16},{2,18},{4,20},{6,22},{8,24},{10,26},{12,28},{14,30},{16,0},... | collective-permute-start | bytes 294920 | tf_op jit(solution)/shard_map/ppermute | solution.py:378
  19.8 24.3 %collective-permute-start.7 = (bf16[512,1024]{1,0:T(8,128)(2,1)}, bf16[512,1024]{1,0:T(8,128)(2,1)S(1)}, u32[]{:S(2)}, u32[]{:S(2)}) collective-permute-start(bf16[512,1024]{1,0:T(8,128)(2,1)} %get-tuple-element.1470), channel_id=1, source_target_pairs={{0,1},{1,0},{2,3},{3,2},{4,5},{5,4},{6,7},{7,6},{8,9},{9,8},{10,11... | collective-permute-start | bytes 3145736 | tf_op jit(solution)/shard_map/ppermute | solution.py:382
  44.1 17.9 %collective-permute-start.11 = (bf16[256,768]{1,0:T(8,128)(2,1)S(1)}, bf16[256,768]{1,0:T(8,128)(2,1)S(1)}, u32[]{:S(2)}, u32[]{:S(2)}) collective-permute-start(bf16[256,768]{1,0:T(8,128)(2,1)S(1)} %pad_maximum_fusion.26), channel_id=1, source_target_pairs={{0,1},{1,0},{2,3},{3,2},{4,5},{5,4},{6,7},{7,6},{8,9},{9,8},{10,11... | collective-permute-start | bytes 1179656 | tf_op jit(solution)/shard_map/ppermute | solution.py:382
  45.6 16.4 %collective-permute-start.8 = (bf16[256,768]{1,0:T(8,128)(2,1)S(1)}, bf16[256,768]{1,0:T(8,128)(2,1)S(1)}, u32[]{:S(2)}, u32[]{:S(2)}) collective-permute-start(bf16[256,768]{1,0:T(8,128)(2,1)S(1)} %pad_maximum_fusion.26), channel_id=1, source_target_pairs={{0,4},{2,6},{4,0},{6,2},{8,12},{10,14},{12,8},{14,10},{16,20},{18,... | collective-permute-start | bytes 1179656 | tf_op jit(solution)/shard_map/ppermute | solution.py:378
  75.1 30.8 %collective-permute-start.23 = (bf16[512,768]{1,0:T(8,128)(2,1)S(1)}, bf16[512,768]{1,0:T(8,128)(2,1)S(1)}, u32[]{:S(2)}, u32[]{:S(2)}) collective-permute-start(bf16[512,768]{1,0:T(8,128)(2,1)S(1)} %pad_maximum_fusion.19), channel_id=1, source_target_pairs={{0,1},{1,0},{2,3},{3,2},{4,5},{5,4},{6,7},{7,6},{8,9},{9,8},{10,11... | collective-permute-start | bytes 2359304 | tf_op jit(solution)/shard_map/ppermute | solution.py:382
  76.7 15.7 %collective-permute-start.18 = (bf16[512,768]{1,0:T(8,128)(2,1)S(1)}, bf16[512,768]{1,0:T(8,128)(2,1)S(1)}, u32[]{:S(2)}, u32[]{:S(2)}) collective-permute-start(bf16[512,768]{1,0:T(8,128)(2,1)S(1)} %pad_maximum_fusion.19), channel_id=1, source_target_pairs={{0,2},{2,0},{4,6},{6,4},{8,10},{10,8},{12,14},{14,12},{16,18},{18,... | collective-permute-start | bytes 2359304 | tf_op jit(solution)/shard_map/ppermute | solution.py:378
  78.2 14.1 %collective-permute-start.20 = (bf16[128,2048]{1,0:T(8,128)(2,1)S(1)}, bf16[128,2048]{1,0:T(8,128)(2,1)S(1)}, u32[]{:S(2)}, u32[]{:S(2)}) collective-permute-start(bf16[128,2048]{1,0:T(8,128)(2,1)S(1)} %pad_maximum_fusion.21), channel_id=1, source_target_pairs={{0,8},{2,10},{4,12},{6,14},{8,0},{10,2},{12,4},{14,6},{16,24},{18,... | collective-permute-start | bytes 1572872 | tf_op jit(solution)/shard_map/ppermute | solution.py:378
  106.2 15.0 %collective-permute-start.25 = (bf16[64,2048]{1,0:T(8,128)(2,1)S(1)}, bf16[64,2048]{1,0:T(8,128)(2,1)S(1)}, u32[]{:S(2)}, u32[]{:S(2)}) collective-permute-start(bf16[64,2048]{1,0:T(8,128)(2,1)S(1)} %bitcast.104), channel_id=1, source_target_pairs={{0,16},{2,18},{4,20},{6,22},{8,24},{10,26},{12,28},{14,30},{16,0},... | collective-permute-start | bytes 786440 | tf_op jit(solution)/shard_map/ppermute | solution.py:378
  106.2 15.5 %collective-permute-start.24 = (bf16[512,512]{1,0:T(8,128)(2,1)S(1)}, bf16[512,512]{1,0:T(8,128)(2,1)S(1)}, u32[]{:S(2)}, u32[]{:S(2)}) collective-permute-start(bf16[512,512]{1,0:T(8,128)(2,1)S(1)} %pad_maximum_fusion.22), channel_id=1, source_target_pairs={{0,2},{2,0},{4,6},{6,4},{8,10},{10,8},{12,14},{14,12},{16,18},{18,... | collective-permute-start | bytes 1572872 | tf_op jit(solution)/shard_map/ppermute | solution.py:378
  106.7 15.1 %collective-permute-start.26 = (bf16[512,512]{1,0:T(8,128)(2,1)S(1)}, bf16[512,512]{1,0:T(8,128)(2,1)S(1)}, u32[]{:S(2)}, u32[]{:S(2)}) collective-permute-start(bf16[512,512]{1,0:T(8,128)(2,1)S(1)} %pad_maximum_fusion.23), channel_id=1, source_target_pairs={{0,2},{2,0},{4,6},{6,4},{8,10},{10,8},{12,14},{14,12},{16,18},{18,... | collective-permute-start | bytes 1572872 | tf_op jit(solution)/shard_map/ppermute | solution.py:378
  106.7 15.2 %collective-permute-start.27 = (bf16[512,768]{1,0:T(8,128)(2,1)S(1)}, bf16[512,768]{1,0:T(8,128)(2,1)S(1)}, u32[]{:S(2)}, u32[]{:S(2)}) collective-permute-start(bf16[512,768]{1,0:T(8,128)(2,1)S(1)} %collective-permute-done.23), channel_id=1, source_target_pairs={{0,2},{2,0},{4,6},{6,4},{8,10},{10,8},{12,14},{14,12},{16,18},{18,... | collective-permute-start | bytes 2359304 | tf_op jit(solution)/shard_map/ppermute | solution.py:378
  107.3 39.4 %collective-permute-start.30 = (bf16[256,2048]{1,0:T(8,128)(2,1)S(1)}, bf16[256,2048]{1,0:T(8,128)(2,1)S(1)}, u32[]{:S(2)}, u32[]{:S(2)}) collective-permute-start(bf16[256,2048]{1,0:T(8,128)(2,1)S(1)} %pad_maximum_fusion.14), channel_id=1, source_target_pairs={{0,1},{1,0},{2,3},{3,2},{4,5},{5,4},{6,7},{7,6},{8,9},{9,8},{10,11... | collective-permute-start | bytes 3145736 | tf_op jit(solution)/shard_map/ppermute | solution.py:382
  121.2 25.1 %collective-permute-start.28 = (bf16[256,2048]{1,0:T(8,128)(2,1)S(1)}, bf16[256,2048]{1,0:T(8,128)(2,1)S(1)}, u32[]{:S(2)}, u32[]{:S(2)}) collective-permute-start(bf16[256,2048]{1,0:T(8,128)(2,1)S(1)} %pad_maximum_fusion.14), channel_id=1, source_target_pairs={{0,4},{2,6},{4,0},{6,2},{8,12},{10,14},{12,8},{14,10},{16,20},{18,... | collective-permute-start | bytes 3145736 | tf_op jit(solution)/shard_map/ppermute | solution.py:378
  122.0 24.5 %collective-permute-start.29 = (bf16[128,2048]{1,0:T(8,128)(2,1)S(1)}, bf16[128,2048]{1,0:T(8,128)(2,1)S(1)}, u32[]{:S(2)}, u32[]{:S(2)}) collective-permute-start(bf16[128,2048]{1,0:T(8,128)(2,1)S(1)} %pad_maximum_fusion.24), channel_id=1, source_target_pairs={{0,8},{2,10},{4,12},{6,14},{8,0},{10,2},{12,4},{14,6},{16,24},{18,... | collective-permute-start | bytes 1572872 | tf_op jit(solution)/shard_map/ppermute | solution.py:378
  146.7 24.4 %collective-permute-start.32 = (bf16[256,2048]{1,0:T(8,128)(2,1)S(1)}, bf16[256,2048]{1,0:T(8,128)(2,1)S(1)}, u32[]{:S(2)}, u32[]{:S(2)}) collective-permute-start(bf16[256,2048]{1,0:T(8,128)(2,1)S(1)} %collective-permute-done.30), channel_id=1, source_target_pairs={{0,4},{2,6},{4,0},{6,2},{8,12},{10,14},{12,8},{14,10},{16,20},{18,... | collective-permute-start | bytes 3145736 | tf_op jit(solution)/shard_map/ppermute | solution.py:378
  148.9 33.7 %collective-permute-start.33 = (bf16[512,1024]{1,0:T(8,128)(2,1)S(1)}, bf16[512,1024]{1,0:T(8,128)(2,1)S(1)}, u32[]{:S(2)}, u32[]{:S(2)}) collective-permute-start(bf16[512,1024]{1,0:T(8,128)(2,1)S(1)} %get-tuple-element.1484), channel_id=1, source_target_pairs={{0,1},{1,0},{2,3},{3,2},{4,5},{5,4},{6,7},{7,6},{8,9},{9,8},{10,11... | collective-permute-start | bytes 3145736 | tf_op jit(solution)/shard_map/ppermute | solution.py:382
  149.6 21.7 %collective-permute-start.31 = (bf16[512,2048]{1,0:T(8,128)(2,1)S(1)}, bf16[512,2048]{1,0:T(8,128)(2,1)S(1)}, u32[]{:S(2)}, u32[]{:S(2)}) collective-permute-start(bf16[512,2048]{1,0:T(8,128)(2,1)S(1)} %pad_maximum_fusion.4), channel_id=1, source_target_pairs={{0,2},{2,0},{4,6},{6,4},{8,10},{10,8},{12,14},{14,12},{16,18},{18,... | collective-permute-start | bytes 6291464 | tf_op jit(solution)/shard_map/ppermute | solution.py:378
  182.7 30.9 %collective-permute-start.35 = (bf16[512,2048]{1,0:T(8,128)(2,1)S(1)}, bf16[512,2048]{1,0:T(8,128)(2,1)S(1)}, u32[]{:S(2)}, u32[]{:S(2)}) collective-permute-start(bf16[512,2048]{1,0:T(8,128)(2,1)S(1)} %pad_maximum_fusion.5), channel_id=1, source_target_pairs={{0,2},{2,0},{4,6},{6,4},{8,10},{10,8},{12,14},{14,12},{16,18},{18,... | collective-permute-start | bytes 6291464 | tf_op jit(solution)/shard_map/ppermute | solution.py:378
  187.6 26.6 %collective-permute-start.36 = (bf16[512,2048]{1,0:T(8,128)(2,1)S(1)}, bf16[512,2048]{1,0:T(8,128)(2,1)S(1)}, u32[]{:S(2)}, u32[]{:S(2)}) collective-permute-start(bf16[512,2048]{1,0:T(8,128)(2,1)S(1)} %convolution_convert_fusion.3), channel_id=1, source_target_pairs={{0,2},{2,0},{4,6},{6,4},{8,10},{10,8},{12,14},{14,12},{16,18},{18,... | collective-permute-start | bytes 6291464 | tf_op jit(solution)/shard_map/ppermute | solution.py:378
  188.2 25.1 %collective-permute-start.34 = (bf16[256,2048]{1,0:T(8,128)(2,1)S(1)}, bf16[256,2048]{1,0:T(8,128)(2,1)S(1)}, u32[]{:S(2)}, u32[]{:S(2)}) collective-permute-start(bf16[256,2048]{1,0:T(8,128)(2,1)S(1)} %pad_maximum_fusion.17), channel_id=1, source_target_pairs={{0,4},{2,6},{4,0},{6,2},{8,12},{10,14},{12,8},{14,10},{16,20},{18,... | collective-permute-start | bytes 3145736 | tf_op jit(solution)/shard_map/ppermute | solution.py:378
  188.7 36.4 %collective-permute-start.37 = (bf16[256,2048]{1,0:T(8,128)(2,1)S(1)}, bf16[256,2048]{1,0:T(8,128)(2,1)S(1)}, u32[]{:S(2)}, u32[]{:S(2)}) collective-permute-start(bf16[256,2048]{1,0:T(8,128)(2,1)S(1)} %pad_maximum_fusion.17), channel_id=1, source_target_pairs={{0,1},{1,0},{2,3},{3,2},{4,5},{5,4},{6,7},{7,6},{8,9},{9,8},{10,11... | collective-permute-start | bytes 3145736 | tf_op jit(solution)/shard_map/ppermute | solution.py:382
  225.1 29.6 %collective-permute-start.38 = (bf16[512,2048]{1,0:T(8,128)(2,1)S(1)}, bf16[512,2048]{1,0:T(8,128)(2,1)S(1)}, u32[]{:S(2)}, u32[]{:S(2)}) collective-permute-start(bf16[512,2048]{1,0:T(8,128)(2,1)S(1)} %pad_maximum_fusion.6), channel_id=1, source_target_pairs={{0,2},{2,0},{4,6},{6,4},{8,10},{10,8},{12,14},{14,12},{16,18},{18,... | collective-permute-start | bytes 6291464 | tf_op jit(solution)/shard_map/ppermute | solution.py:378
  228.9 26.4 %collective-permute-start.39 = (bf16[512,2048]{1,0:T(8,128)(2,1)}, bf16[512,2048]{1,0:T(8,128)(2,1)S(1)}, u32[]{:S(2)}, u32[]{:S(2)}) collective-permute-start(bf16[512,2048]{1,0:T(8,128)(2,1)} %convolution_convert_fusion.2), channel_id=1, source_target_pairs={{0,2},{2,0},{4,6},{6,4},{8,10},{10,8},{12,14},{14,12},{16,18},{18,... | collective-permute-start | bytes 6291464 | tf_op jit(solution)/shard_map/ppermute | solution.py:378
  229.4 25.1 %collective-permute-start.40 = (bf16[256,2048]{1,0:T(8,128)(2,1)S(1)}, bf16[256,2048]{1,0:T(8,128)(2,1)S(1)}, u32[]{:S(2)}, u32[]{:S(2)}) collective-permute-start(bf16[256,2048]{1,0:T(8,128)(2,1)S(1)} %collective-permute-done.37), channel_id=1, source_target_pairs={{0,4},{2,6},{4,0},{6,2},{8,12},{10,14},{12,8},{14,10},{16,20},{18,... | collective-permute-start | bytes 3145736 | tf_op jit(solution)/shard_map/ppermute | solution.py:378
  282.2 48.0 %collective-permute-start.44 = (bf16[512,2048]{1,0:T(8,128)(2,1)}, bf16[512,2048]{1,0:T(8,128)(2,1)}, u32[]{:S(2)}, u32[]{:S(2)}) collective-permute-start(bf16[512,2048]{1,0:T(8,128)(2,1)} %add_convert_fusion.5), channel_id=1, source_target_pairs={{0,1},{1,0},{2,3},{3,2},{4,5},{5,4},{6,7},{7,6},{8,9},{9,8},{10,11... | collective-permute-start | bytes 6291464 | tf_op jit(solution)/shard_map/ppermute | solution.py:382
  333.8 24.7 %collective-permute-start.45 = (bf16[256,2048]{1,0:T(8,128)(2,1)}, bf16[256,2048]{1,0:T(8,128)(2,1)}, u32[]{:S(2)}, u32[]{:S(2)}) collective-permute-start(bf16[256,2048]{1,0:T(8,128)(2,1)} %slice.283), channel_id=1, source_target_pairs={{0,4},{2,6},{4,0},{6,2},{8,12},{10,14},{12,8},{14,10},{16,20},{18,... | collective-permute-start | bytes 3145736 | tf_op jit(solution)/shard_map/ppermute | solution.py:378
  334.3 70.7 %collective-permute-start.51 = (bf16[512,1024]{1,0:T(8,128)(2,1)}, bf16[512,1024]{1,0:T(8,128)(2,1)}, u32[]{:S(2)}, u32[]{:S(2)}) collective-permute-start(bf16[512,1024]{1,0:T(8,128)(2,1)} %get-tuple-element.1319), channel_id=1, source_target_pairs={{0,1},{1,0},{2,3},{3,2},{4,5},{5,4},{6,7},{7,6},{8,9},{9,8},{10,11... | collective-permute-start | bytes 3145736 | tf_op jit(solution)/shard_map/ppermute | solution.py:382
  365.0 12.8 %collective-permute-start.47 = (bf16[512,512]{1,0:T(8,128)(2,1)S(1)}, bf16[512,512]{1,0:T(8,128)(2,1)S(1)}, u32[]{:S(2)}, u32[]{:S(2)}) collective-permute-start(bf16[512,512]{1,0:T(8,128)(2,1)S(1)} %convolution_convert_fusion.14), channel_id=1, source_target_pairs={{0,2},{2,0},{4,6},{6,4},{8,10},{10,8},{12,14},{14,12},{16,18},{18,... | collective-permute-start | bytes 1572872 | tf_op jit(solution)/shard_map/ppermute | solution.py:378
  365.0 12.8 %collective-permute-start.48 = (bf16[512,512]{1,0:T(8,128)(2,1)S(1)}, bf16[512,512]{1,0:T(8,128)(2,1)S(1)}, u32[]{:S(2)}, u32[]{:S(2)}) collective-permute-start(bf16[512,512]{1,0:T(8,128)(2,1)S(1)} %convolution_convert_fusion.13), channel_id=1, source_target_pairs={{0,2},{2,0},{4,6},{6,4},{8,10},{10,8},{12,14},{14,12},{16,18},{18,... | collective-permute-start | bytes 1572872 | tf_op jit(solution)/shard_map/ppermute | solution.py:378
  369.2 32.5 %collective-permute-start.55 = (bf16[256,2048]{1,0:T(8,128)(2,1)S(1)}, bf16[256,2048]{1,0:T(8,128)(2,1)}, u32[]{:S(2)}, u32[]{:S(2)}) collective-permute-start(bf16[256,2048]{1,0:T(8,128)(2,1)S(1)} %slice.301), channel_id=1, source_target_pairs={{0,4},{2,6},{4,0},{6,2},{8,12},{10,14},{12,8},{14,10},{16,20},{18,... | collective-permute-start | bytes 3145736 | tf_op jit(solution)/shard_map/ppermute | solution.py:378
  377.2 39.6 %collective-permute-start.54 = (bf16[256,2048]{1,0:T(8,128)(2,1)}, bf16[256,2048]{1,0:T(8,128)(2,1)S(1)}, u32[]{:S(2)}, u32[]{:S(2)}) collective-permute-start(bf16[256,2048]{1,0:T(8,128)(2,1)} %slice.299), channel_id=1, source_target_pairs={{0,4},{2,6},{4,0},{6,2},{8,12},{10,14},{12,8},{14,10},{16,20},{18,... | collective-permute-start | bytes 3145736 | tf_op jit(solution)/shard_map/ppermute | solution.py:378
  392.0 12.9 %collective-permute-start.50 = (bf16[512,512]{1,0:T(8,128)(2,1)S(1)}, bf16[512,512]{1,0:T(8,128)(2,1)S(1)}, u32[]{:S(2)}, u32[]{:S(2)}) collective-permute-start(bf16[512,512]{1,0:T(8,128)(2,1)S(1)} %fusion.57), channel_id=1, source_target_pairs={{0,1},{1,0},{2,3},{3,2},{4,5},{5,4},{6,7},{7,6},{8,9},{9,8},{10,11... | collective-permute-start | bytes 1572872 | tf_op jit(solution)/shard_map/ppermute | solution.py:382
  407.0 19.2 %collective-permute-start.53 = (bf16[512,768]{1,0:T(8,128)(2,1)}, bf16[512,768]{1,0:T(8,128)(2,1)S(1)}, u32[]{:S(2)}, u32[]{:S(2)}) collective-permute-start(bf16[512,768]{1,0:T(8,128)(2,1)} %convolution_convert_fusion.11), channel_id=1, source_target_pairs={{0,2},{2,0},{4,6},{6,4},{8,10},{10,8},{12,14},{14,12},{16,18},{18,... | collective-permute-start | bytes 2359304 | tf_op jit(solution)/shard_map/ppermute | solution.py:378
  408.9 17.3 %collective-permute-start.52 = (bf16[512,768]{1,0:T(8,128)(2,1)}, bf16[512,768]{1,0:T(8,128)(2,1)}, u32[]{:S(2)}, u32[]{:S(2)}) collective-permute-start(bf16[512,768]{1,0:T(8,128)(2,1)} %convolution_convert_fusion.12), channel_id=1, source_target_pairs={{0,2},{2,0},{4,6},{6,4},{8,10},{10,8},{12,14},{14,12},{16,18},{18,... | collective-permute-start | bytes 2359304 | tf_op jit(solution)/shard_map/ppermute | solution.py:378
  426.2 13.2 %collective-permute-start.56 = (bf16[256,512]{1,0:T(8,128)(2,1)S(1)}, bf16[256,512]{1,0:T(8,128)(2,1)S(1)}, u32[]{:S(2)}, u32[]{:S(2)}) collective-permute-start(bf16[256,512]{1,0:T(8,128)(2,1)S(1)} %slice.303), channel_id=1, source_target_pairs={{0,4},{2,6},{4,0},{6,2},{8,12},{10,14},{12,8},{14,10},{16,20},{18,... | collective-permute-start | bytes 786440 | tf_op jit(solution)/shard_map/ppermute | solution.py:378
  426.9 34.0 %collective-permute-start.60 = (bf16[256,2048]{1,0:T(8,128)(2,1)S(1)}, bf16[256,2048]{1,0:T(8,128)(2,1)}, u32[]{:S(2)}, u32[]{:S(2)}) collective-permute-start(bf16[256,2048]{1,0:T(8,128)(2,1)S(1)} %add_convert_fusion.12), channel_id=1, source_target_pairs={{0,1},{1,0},{2,3},{3,2},{4,5},{5,4},{6,7},{7,6},{8,9},{9,8},{10,11... | collective-permute-start | bytes 3145736 | tf_op jit(solution)/shard_map/ppermute | solution.py:382
  439.6 17.6 %collective-permute-start.57 = (bf16[128,512]{1,0:T(8,128)(2,1)S(1)}, bf16[128,512]{1,0:T(8,128)(2,1)S(1)}, u32[]{:S(2)}, u32[]{:S(2)}) collective-permute-start(bf16[128,512]{1,0:T(8,128)(2,1)S(1)} %slice.307), channel_id=1, source_target_pairs={{0,8},{2,10},{4,12},{6,14},{8,0},{10,2},{12,4},{14,6},{16,24},{18,... | collective-permute-start | bytes 393224 | tf_op jit(solution)/shard_map/ppermute | solution.py:378
  441.6 15.8 %collective-permute-start.59 = (bf16[256,768]{1,0:T(8,128)(2,1)S(1)}, bf16[256,768]{1,0:T(8,128)(2,1)}, u32[]{:S(2)}, u32[]{:S(2)}) collective-permute-start(bf16[256,768]{1,0:T(8,128)(2,1)S(1)} %slice.311), channel_id=1, source_target_pairs={{0,4},{2,6},{4,0},{6,2},{8,12},{10,14},{12,8},{14,10},{16,20},{18,... | collective-permute-start | bytes 1179656 | tf_op jit(solution)/shard_map/ppermute | solution.py:378
  443.2 16.5 %collective-permute-start.58 = (bf16[256,768]{1,0:T(8,128)(2,1)S(1)}, bf16[256,768]{1,0:T(8,128)(2,1)}, u32[]{:S(2)}, u32[]{:S(2)}) collective-permute-start(bf16[256,768]{1,0:T(8,128)(2,1)S(1)} %slice.309), channel_id=1, source_target_pairs={{0,4},{2,6},{4,0},{6,2},{8,12},{10,14},{12,8},{14,10},{16,20},{18,... | collective-permute-start | bytes 1179656 | tf_op jit(solution)/shard_map/ppermute | solution.py:378
  447.5 15.0 %collective-permute-start.61 = (bf16[512,768]{1,0:T(8,128)(2,1)}, bf16[512,768]{1,0:T(8,128)(2,1)}, u32[]{:S(2)}, u32[]{:S(2)}) collective-permute-start(bf16[512,768]{1,0:T(8,128)(2,1)} %convolution_convert_fusion.10), channel_id=1, source_target_pairs={{0,2},{2,0},{4,6},{6,4},{8,10},{10,8},{12,14},{14,12},{16,18},{18,... | collective-permute-start | bytes 2359304 | tf_op jit(solution)/shard_map/ppermute | solution.py:378
  466.5 14.1 %collective-permute-start.63 = (bf16[128,2048]{1,0:T(8,128)(2,1)S(1)}, bf16[128,2048]{1,0:T(8,128)(2,1)}, u32[]{:S(2)}, u32[]{:S(2)}) collective-permute-start(bf16[128,2048]{1,0:T(8,128)(2,1)S(1)} %slice.314), channel_id=1, source_target_pairs={{0,8},{2,10},{4,12},{6,14},{8,0},{10,2},{12,4},{14,6},{16,24},{18,... | collective-permute-start | bytes 1572872 | tf_op jit(solution)/shard_map/ppermute | solution.py:378
  500.0 17.7 %collective-permute-start.79 = (bf16[64,2048]{1,0:T(8,128)(2,1)S(1)}, bf16[64,2048]{1,0:T(8,128)(2,1)S(1)}, u32[]{:S(2)}, u32[]{:S(2)}) collective-permute-start(bf16[64,2048]{1,0:T(8,128)(2,1)S(1)} %slice.345), channel_id=1, source_target_pairs={{0,16},{2,18},{4,20},{6,22},{8,24},{10,26},{12,28},{14,30},{16,0},... | collective-permute-start | bytes 786440 | tf_op jit(solution)/shard_map/ppermute | solution.py:378
  504.6 18.6 %collective-permute-start.73 = (bf16[256,768]{1,0:T(8,128)(2,1)S(1)}, bf16[256,768]{1,0:T(8,128)(2,1)S(1)}, u32[]{:S(2)}, u32[]{:S(2)}) collective-permute-start(bf16[256,768]{1,0:T(8,128)(2,1)S(1)} %slice.333), channel_id=1, source_target_pairs={{0,4},{2,6},{4,0},{6,2},{8,12},{10,14},{12,8},{14,10},{16,20},{18,... | collective-permute-start | bytes 1179656 | tf_op jit(solution)/shard_map/ppermute | solution.py:378
  509.2 40.2 %collective-permute-start.64 = (bf16[512,1024]{1,0:T(8,128)(2,1)}, bf16[512,1024]{1,0:T(8,128)(2,1)}, u32[]{:S(2)}, u32[]{:S(2)}) collective-permute-start(bf16[512,1024]{1,0:T(8,128)(2,1)} %get-tuple-element.1423), channel_id=1, source_target_pairs={{0,1},{1,0},{2,3},{3,2},{4,5},{5,4},{6,7},{7,6},{8,9},{9,8},{10,11... | collective-permute-start | bytes 3145736 | tf_op jit(solution)/shard_map/ppermute | solution.py:382
  514.3 28.1 %collective-permute-start.75 = (bf16[256,768]{1,0:T(8,128)(2,1)S(1)}, bf16[256,768]{1,0:T(8,128)(2,1)S(1)}, u32[]{:S(2)}, u32[]{:S(2)}) collective-permute-start(bf16[256,768]{1,0:T(8,128)(2,1)S(1)} %add_convert_fusion.27), channel_id=1, source_target_pairs={{0,1},{1,0},{2,3},{3,2},{4,5},{5,4},{6,7},{7,6},{8,9},{9,8},{10,11... | collective-permute-start | bytes 1179656 | tf_op jit(solution)/shard_map/ppermute | solution.py:382
  523.1 19.8 %collective-permute-start.72 = (bf16[64,768]{1,0:T(8,128)(2,1)S(1)}, bf16[64,768]{1,0:T(8,128)(2,1)S(1)}, u32[]{:S(2)}, u32[]{:S(2)}) collective-permute-start(bf16[64,768]{1,0:T(8,128)(2,1)S(1)} %slice.365), channel_id=1, source_target_pairs={{0,16},{2,18},{4,20},{6,22},{8,24},{10,26},{12,28},{14,30},{16,0},... | collective-permute-start | bytes 294920 | tf_op jit(solution)/shard_map/ppermute | solution.py:378
  (96 other events, 1039.4 us)

commit v3 on v2

--- a/solution.py
+++ b/solution.py
@@ -484,10 +484,12 @@
 
 
 def gelu_both(u):
-    inner = math.sqrt(2 / math.pi)
-    t = jnp.tanh(inner * (u + 0.044715 * u * u * u))
-    slope = 0.5 * (1.0 + t) + 0.5 * u * (1.0 - t * t) * inner * (1.0 + 3 * 0.044715 * u * u)
-    return 0.5 * u * (1.0 + t), slope
+    first = math.sqrt(2 / math.pi)
+    third = 0.044715 * first
+    square = u * u
+    h = 0.5 * jnp.tanh(u * (first + third * square)) + 0.5
+    slope = h + (h - h * h) * (u * (2 * first + 6 * third * square))
+    return u * h, slope
 
 
 def on_device_whole(
@@ -498,9 +500,10 @@
     far, near = size // 2, size // 4
 
     def split(array):
+        me = lax.axis_index("tensor")
         return (
-            jnp.where(first, array[:, 0], array[:, 1]),
-            jnp.where(first, array[:, 1], array[:, 0]),
+            lax.dynamic_index_in_dim(array, me, 1, keepdims=False),
+            lax.dynamic_index_in_dim(array, 1 - me, 1, keepdims=False),
         )
 
     def join(ours, arrived, order):
@@ -536,21 +539,22 @@
     s = Steps()
 
     ours, away = split(tokens)
-    arriving = swap_tensor(away)
+    tokens_arriving = swap_tensor(away)
     s.put(a=grow(qkv_a, far), b=grow(qkv_b, far))
     s.put(par=grow_params(jnp.stack([ln1_gain, ln1_bias, ln2_gain, ln2_bias]), far))
     s.put(o=w_out.T, u=w_up, d=w_down.T, ours=ours, order=block_order(size, width), d_out=d_out)
     s.cut()
+    u_arriving = grow(s.u, far)
     s.put(a=grow(s.a, near), b=grow(s.b, near), o=grow(s.o, far), par=grow_params(s.par, near))
-    s.put(arrived=arriving)
+    s.put(arrived=tokens_arriving)
     s.cut()
     s.put(ax=swap_tensor(s.a), a=grow(s.a, 2), o=grow(s.o, near), par=grow_params(s.par, 2))
-    arriving = grow(s.u, far)
-    s.put(x16=join(s.ours, s.arrived, s.order))
+    s.put(x16=join(s.ours, s.arrived, s.order), u=u_arriving)
     s.drop("ours", "arrived")
     s.cut()
+    u_arriving = grow(s.u, near)
+    d_arriving = grow(s.d, far)
     s.put(a_own=grow(s.a, 1), b=grow(s.b, 2), ox=swap_tensor(s.o), par=grow_params(s.par, 1))
-    s.put(u=arriving)
     gain_one, bias_one, gain_two, bias_two = (
         s.par[i : i + 1].astype(jnp.float32) for i in range(4)
     )
@@ -560,98 +564,88 @@
     s.drop("a", "par")
     s.cut()
     b_arriving = swap_tensor(s.b)
-    arriving = grow(s.u, near)
     s.put(b_own=grow(s.b, 1), ax=grow(s.ax, 2))
     qkv = mul(s.n1, s.a_own).astype(jnp.bfloat16)
     mixed, lse = attend(qkv)
-    s.put(qkv0=qkv, mixed0=mixed, lse0=lse)
+    s.put(qkv0=qkv, mixed0=mixed, lse0=lse, u=u_arriving)
     s.drop("b")
     s.cut()
+    ux_arriving = swap_tensor(s.u)
     s.put(a_oth=grow(s.ax, 1), o=grow(s.o, 2), ox=grow(s.ox, 2))
+    u_arriving = grow(s.u, 2)
     qkv = mul(s.n1, s.b_own).astype(jnp.bfloat16)
     mixed, lse = attend(qkv)
-    s.put(qkv1=qkv, mixed1=mixed, lse1=lse, bx=b_arriving, u=arriving)
+    s.put(qkv1=qkv, mixed1=mixed, lse1=lse, bx=b_arriving, d=d_arriving)
     s.drop("ax")
     s.cut()
-    x_arriving = swap_tensor(s.u)
-    y_arriving = grow(s.u, 2)
-    s.put(b_oth=grow(s.bx, 1), o=grow(s.o, 1), ox=grow(s.ox, 1), d=grow(s.d, far))
+    d_arriving = grow(s.d, near)
+    s.put(b_oth=grow(s.bx, 1), o=grow(s.o, 1), ox=grow(s.ox, 1))
     qkv = mul(s.n1, s.a_oth).astype(jnp.bfloat16)
     mixed, lse = attend(qkv)
-    s.put(qkv2=qkv, mixed2=mixed, lse2=lse)
+    s.put(qkv2=qkv, mixed2=mixed, lse2=lse, ux=ux_arriving, u=u_arriving, d=d_arriving)
     s.drop("bx")
     s.cut()
-    s.put(d=grow(s.d, near))
+    ux_arriving = grow(s.ux, 2)
+    dx_arriving = swap_tensor(s.d)
+    s.put(u_own=grow(s.u, 1))
     qkv = mul(s.n1, s.b_oth).astype(jnp.bfloat16)
     mixed, lse = attend(qkv)
-    s.put(qkv3=qkv, mixed3=mixed, lse3=lse, ux=x_arriving, u=y_arriving)
-    s.cut()
-    y_arriving = grow(s.ux, 2)
-    ours, away = split(s.d_out)
-    x_arriving = swap_tensor(away)
-    s.put(u_own=grow(s.u, 1))
+    s.put(qkv3=qkv, mixed3=mixed, lse3=lse)
+    s.drop("u")
+    s.cut()
     mixed = jnp.concatenate([s.mixed0, s.mixed1, s.mixed2, s.mixed3], axis=1)
     out_all = jnp.concatenate([s.o, s.ox], axis=1)
     hidden = s.x16.astype(jnp.float32) + mul(mixed, out_all, NT)
     normed, normal, inverse = norm_rows(hidden, s.gain_two, s.bias_two)
     s.put(mixed=mixed, out_all=out_all, hidden=hidden, n2=normed.astype(jnp.bfloat16))
-    s.put(normal2=normal, inverse2=inverse, ours=ours)
-    s.drop("u", "o", "ox", "x16", "d_out", "bias_two")
-    s.cut()
+    s.put(normal2=normal, inverse2=inverse, ux=ux_arriving, dx=dx_arriving)
+    s.drop("o", "ox", "x16", "bias_two")
+    s.cut()
+    ours, away = split(s.d_out)
+    cot_arriving = swap_tensor(away)
+    d_arriving = grow(s.d, 2)
+    s.put(u_oth=grow(s.ux, 1), ours=ours)
     active, slope = gelu_both(mul(s.n2, s.u_own))
     s.put(active0=active.astype(jnp.bfloat16), slope0=slope.astype(jnp.bfloat16))
-    s.put(ux=y_arriving, arrived=x_arriving)
-    s.cut()
-    s.put(u_oth=grow(s.ux, 1))
-    x_arriving = swap_tensor(s.d)
-    y_arriving = grow(s.d, 2)
-    dy16 = join(s.ours, s.arrived, s.order)
-    away0 = away_rows(dy16, s.active0)
-    s.put(dy16=dy16, down0=swap_dp(away0, size, 1))
-    s.drop("ux", "ours", "arrived")
+    s.drop("d_out", "ux")
     s.cut()
     active, slope = gelu_both(mul(s.n2, s.u_oth))
     s.put(active1=active.astype(jnp.bfloat16), slope1=slope.astype(jnp.bfloat16))
-    s.put(dx=x_arriving, d=y_arriving)
-    s.cut()
-    y_arriving = grow(s.dx, 2)
+    s.put(arrived=cot_arriving, d=d_arriving)
+    s.cut()
+    dx_arriving = grow(s.dx, 2)
     s.put(d_own=grow(s.d, 1))
-    away1 = away_rows(s.dy16, s.active1)
-    s.put(down1=swap_dp(away1, size, 1), down0=kept_rows(s.dy16, s.active0, s.down0))
-    s.drop("d")
+    dy16 = join(s.ours, s.arrived, s.order)
+    s.put(dy16=dy16, down0=swap_dp(away_rows(dy16, s.active0), size, 1))
+    s.put(down1=swap_dp(away_rows(dy16, s.active1), size, 1))
+    s.drop("d", "ours", "arrived")
     s.cut()
     grad = mul(s.dy16, s.d_own) * s.slope0.astype(jnp.float32)
-    s.put(up_grad0=grad.astype(jnp.bfloat16), down1=kept_rows(s.dy16, s.active1, s.down1))
-    s.put(dx=y_arriving)
+    s.put(up_grad0=grad.astype(jnp.bfloat16), dx=dx_arriving)
+    s.put(down0=kept_rows(s.dy16, s.active0, s.down0), down1=kept_rows(s.dy16, s.active1, s.down1))
     s.drop("slope0")
     s.cut()
     down_arriving = swap_tensor(s.down1)
-    s.put(d_oth=grow(s.dx, 1))
-    s.put(up0=swap_dp(away_rows(s.n2, s.up_grad0), size, 1))
-    s.drop("dx", "down1")
-    s.cut()
-    grad = mul(s.dy16, s.d_oth) * s.slope1.astype(jnp.float32)
-    grad = grad.astype(jnp.bfloat16)
-    s.put(up_grad1=grad, up1=swap_dp(away_rows(s.n2, grad), size, 1))
-    s.put(up0=kept_rows(s.n2, s.up_grad0, s.up0))
-    s.drop("slope1")
-    s.cut()
+    d_oth = grow(s.dx, 1)
+    up0 = swap_dp(away_rows(s.n2, s.up_grad0), size, 1)
+    grad = (mul(s.dy16, d_oth) * s.slope1.astype(jnp.float32)).astype(jnp.bfloat16)
+    s.put(d_oth=d_oth, up_grad1=grad, up1=swap_dp(away_rows(s.n2, grad), size, 1))
+    s.put(up0=kept_rows(s.n2, s.up_grad0, up0))
+    s.drop("dx", "down1", "slope1")
+    s.cut()
+    up0_arriving = fold_dp(s.up0, size, 2)
     total = sum_products([s.active0, s.active1], [s.d_own, s.d_oth])
     rows = reorder((s.hidden + total).astype(jnp.bfloat16), s.order)
     ours, away = part(rows)
     s.put(ours=ours, away=away, up1=kept_rows(s.n2, s.up_grad1, s.up1))
-    s.drop("active0", "active1", "d_own", "d_oth", "hidden", "n2")
-    s.cut()
+    s.drop("active0", "active1", "d_own", "d_oth", "hidden", "n2", "up0")
+    s.cut()
+    up1_arriving = fold_dp(s.up1, size, 2)
+    s.put(grad_n2=sum_products([s.up_grad0, s.up_grad1], [s.u_own, s.u_oth]))
     s.put(down0=add_low(s.down0, down_arriving))
-    s.cut()
-    x_arriving = swap_tensor(s.away)
-    s.put(down0=fold_dp(s.down0, size, 2))
-    s.put(grad_n2=sum_products([s.up_grad0, s.up_grad1], [s.u_own, s.u_oth]))
-    s.drop("away", "up_grad0", "up_grad1", "u_own", "u_oth")
-    s.cut()
-    up0_arriving = fold_dp(s.up0, size, 2)
-    up1_arriving = fold_dp(s.up1, size, 2)
-    s.put(down0=fold_dp(s.down0, size, near))
+    s.drop("up_grad0", "up_grad1", "u_own", "u_oth", "up1")
+    s.cut()
+    block_arriving = swap_tensor(s.away)
     grad_norm, gain_two_grad, bias_two_grad = norm_rows_grad(
         s.grad_n2, s.normal2, s.inverse2, s.gain_two
     )
@@ -661,45 +655,55 @@
     s.put(low_hidden=low_hidden, grad_mixed=mul(low_hidden, s.out_all).astype(jnp.bfloat16))
     s.put(out0=swap_dp(away_rows(low_hidden, s.mixed[:, :local_width]), size, 1))
     s.put(out1=swap_dp(away_rows(low_hidden, s.mixed[:, local_width:]), size, 1))
-    s.drop("grad_n2", "normal2", "inverse2", "gain_two", "out_all", "dy16", "up0", "up1")
-    s.cut()
-    down_grad = swap_dp(high_half(s.down0), size, far).astype(jnp.float32)
-    s.put(down=low_half(s.down0).astype(jnp.float32) + down_grad)
+    s.drop("grad_n2", "normal2", "inverse2", "gain_two", "out_all", "dy16", "away")
+    s.cut()
     s.put(out0=kept_rows(s.low_hidden, s.mixed[:, :local_width], s.out0))
     s.put(out1=kept_rows(s.low_hidden, s.mixed[:, local_width:], s.out1))
     s.put(dqkv0=attend_grad(s.qkv0, s.grad_mixed[:, :step], s.mixed0, s.lse0))
-    s.drop("low_hidden", "mixed", "qkv0", "mixed0", "lse0", "down0")
-    s.cut()
-    s.put(out0=add_low(s.out0, swap_tensor(s.out1)), block_away=x_arriving)
+    s.put(up0=up0_arriving, up1=up1_arriving)
+    s.drop("low_hidden", "mixed", "qkv0", "mixed0", "lse0")
+    s.cut()
+    down_arriving = fold_dp(s.down0, size, 2)
+    out_arriving = swap_tensor(s.out1)
     s.put(dqkv2=attend_grad(s.qkv2, s.grad_mixed[:, 2 * step : 3 * step], s.mixed2, s.lse2))
-    s.drop("out1", "qkv2", "mixed2", "lse2")
-    s.cut()
+    s.put(block_arrived=block_arriving)
+    s.drop("out1", "qkv2", "mixed2", "lse2", "down0")
+    s.cut()
+    up_arriving = swap_tensor(s.up1)
     s.put(a0=swap_dp(away_rows(s.n1, s.dqkv0), size, 1))
     s.put(a1=swap_dp(away_rows(s.n1, s.dqkv2), size, 1))
     s.put(dqkv1=attend_grad(s.qkv1, s.grad_mixed[:, step : 2 * step], s.mixed1, s.lse1))
-    s.put(up0=up0_arriving, up1=up1_arriving)
-    s.drop("qkv1", "mixed1", "lse1")
-    s.cut()
-    arriving = swap_tensor(s.up1)
-    s.put(out0=fold_dp(s.out0, size, 2))
+    s.put(down0=down_arriving, out0=add_low(s.out0, out_arriving))
+    s.drop("qkv1", "mixed1", "lse1", "up1")
+    s.cut()
+    s.put(down0=fold_dp(s.down0, size, near), out0=fold_dp(s.out0, size, 2))
     s.put(a0=kept_rows(s.n1, s.dqkv0, s.a0), a1=kept_rows(s.n1, s.dqkv2, s.a1))
     s.put(dqkv3=attend_grad(s.qkv3, s.grad_mixed[:, 3 * step :], s.mixed3, s.lse3))
-    s.drop("up1", "qkv3", "mixed3", "lse3", "grad_mixed")
-    s.cut()
-    a0, a1 = fold_dp(s.a0, size, 2), fold_dp(s.a1, size, 2)
+    s.put(up0=add_low(s.up0, up_arriving))
+    s.drop("qkv3", "mixed3", "lse3", "grad_mixed")
+    s.cut()
+
+    def last_fold(array):
+        arrived = swap_dp(high_half(array), size, far)
+        return low_half(array).astype(jnp.float32) + arrived.astype(jnp.float32)
+
+    a_arriving = swap_tensor(s.a1)
     s.put(b0=swap_dp(away_rows(s.n1, s.dqkv1), size, 1))
     s.put(b1=swap_dp(away_rows(s.n1, s.dqkv3), size, 1))
-    s.put(out0=fold_dp(s.out0, size, near))
+    s.put(up0=fold_dp(s.up0, size, near), out0=fold_dp(s.out0, size, near))
+    s.put(grad_down=last_fold(s.down0))
     s.put(
         grad_n1=sum_products(
             [s.dqkv0, s.dqkv1, s.dqkv2, s.dqkv3], [s.a_own, s.b_own, s.a_oth, s.b_oth]
         )
     )
-    s.put(up0=add_low(s.up0, arriving), a0=a0, a1=a1)
-    s.drop("dqkv0", "dqkv2", "a_own", "b_own", "a_oth", "b_oth")
-    s.cut()
-    s.put(up0=fold_dp(s.up0, size, near))
-    s.put(b0=kept_rows(s.n1, s.dqkv1, s.b0), b1=kept_rows(s.n1, s.dqkv3, s.b1))
+    s.drop("dqkv0", "dqkv2", "a_own", "b_own", "a_oth", "b_oth", "a1", "down0")
+    s.cut()
+    b1 = kept_rows(s.n1, s.dqkv3, s.b1)
+    b_arriving = swap_tensor(b1)
+    s.put(a0=add_low(s.a0, a_arriving))
+    s.put(b0=kept_rows(s.n1, s.dqkv1, s.b0))
+    s.put(grad_up=last_fold(s.up0), grad_out=last_fold(s.out0))
     grad_norm, gain_one_grad, bias_one_grad = norm_rows_grad(
         s.grad_n1, s.normal1, s.inverse1, s.gain_one
     )
@@ -711,24 +715,12 @@
             [gain_one_grad, bias_one_grad, s.gain_two_grad, s.bias_two_grad], axis=0
         )
     )
+    s.put(block_out=place(s.ours, s.block_arrived), grad_down=s.grad_down.T)
+    s.drop("ours", "block_arrived", "b1", "up0", "out0", "dqkv1", "dqkv3", "n1", "grad_n1")
     s.cut()
     input_grad = place(s.input_ours, swap_tensor(s.input_away))
-    block_out = place(s.ours, s.block_away)
-
-    def last_folds(array):
-        array = fold_dp(array, size, near)
-        arrived = swap_dp(high_half(array), size, far)
-        return low_half(array).astype(jnp.float32) + arrived.astype(jnp.float32)
-
-    def last_fold(array):
-        arrived = swap_dp(high_half(array), size, far)
-        return low_half(array).astype(jnp.float32) + arrived.astype(jnp.float32)
-
-    grad_a = last_folds(add_low(s.a0, swap_tensor(s.a1)))
-    b0, b1 = fold_dp(s.b0, size, 2), fold_dp(s.b1, size, 2)
-    grad_b = last_folds(add_low(b0, swap_tensor(b1)))
-    grad_up = last_fold(s.up0)
-    grad_out = last_fold(s.out0)
+    grad_a = last_fold(fold_dp(fold_dp(s.a0, size, 2), size, near))
+    grad_b = last_fold(fold_dp(fold_dp(add_low(s.b0, b_arriving), size, 2), size, near))
     sums = s.sums
     mask = 1
     while mask < size:
@@ -738,18 +730,18 @@
     sums = sums + swap_tensor(sums)
 
     return (
-        block_out,
+        s.block_out,
         input_grad,
         sums[0],
         sums[1],
         jnp.concatenate(
             [g.reshape(row_count, 3, step).transpose(1, 0, 2) for g in (grad_a, grad_b)], axis=2
         ),
-        grad_out.T,
+        s.grad_out.T,
         sums[2],
         sums[3],
-        grad_up,
-        s.down.T,
+        s.grad_up,
+        s.grad_down,
     )
 
 

time: 564 us -> 532 us (0.943)
  waiting for transfers between devices: 214 us -> 156 us
  starting transfers between devices: 54.6 us -> 81.5 us
  other arithmetic: 47.9 us -> 40.2 us
  local copies, waits for them, and re-layouts: 31.5 us -> 38.6 us
    ppermute x15, waiting for transfers between devices: 49.1 us -> 18.9 us  [swap_tensor(): return lax.ppermute(array, 'tensor', [(0, 1), (1, 0)])]
    ppermute x65 -> x63, waiting for transfers between devices: 164 us -> 137 us  [swap_dp(): return lax.ppermute(array, 'dp', [(i, i ^ mask) for i in range(size)])]
    ppermute x65 -> x63, starting transfers between devices: 42.2 us -> 63.5 us  [swap_dp(): return lax.ppermute(array, 'dp', [(i, i ^ mask) for i in range(size)])]
    slice x1 -> x0, local copies, waits for them, and re-layouts: 6.57 us -> none  [split(): array[:, 0]]
    dynamic_slice x0 -> x1, local copies, waits for them, and re-layouts: none -> 6.54 us  [split(): lax.dynamic_index_in_dim(array, 1 - me, 1, keepdims=False)]
    unnamed x137 -> x140, local copies, waits for them, and re-layouts: 20.4 us -> 24.3 us
    convert_element_type x17 -> x16, other arithmetic: 13.1 us -> 9.32 us  [add_low(): (left.astype(jnp.float32) + right.astype(jnp.float32)).astype(jnp.bfloat16)]
  transfers between devices with their start and end apart: 80 -> 78, of which waited for: 33 -> 31; matrix products, arithmetic and copies ran while one was open for 26% -> 28% of each run, Pallas kernels for 18% -> 19%
where the time goes in v3:
time: 532 us; the launch traced here: 527 us
  waiting for transfers between devices  156 us (29%)
  matrix products  108 us (20%)
  Pallas kernels  101 us (19%)
  starting transfers between devices  81.5 us (15%)
  other arithmetic  40.2 us (8%)
  local copies, waits for them, and re-layouts  38.6 us (7%)
    ppermute x63, waiting for transfers between devices, swap_dp(): return lax.ppermute(array, 'dp', [(i, i ^ mask) for i in range(size)])  137 us
    dot_general x34, matrix products, mul(): lax.dot_general(left, right, dims, preferred_element_type=jnp.float32)  108 us
    ppermute x63, starting transfers between devices, swap_dp(): return lax.ppermute(array, 'dp', [(i, i ^ mask) for i in range(size)])  63.5 us
    pallas_call x4, Pallas kernels, attend_grad(): pl.pallas_call(back_kernel, grid=(pairs,), in_specs=[pl.BlockSpec((length...  35.1 us
    pallas_call x3, Pallas kernels, sum_products(): pl.pallas_call(functools.partial(sum_kernel, len(lefts)), grid=(rows // b...  34.9 us
    pallas_call x4, Pallas kernels, attend(): pl.pallas_call(fwd_kernel, grid=(pairs,), in_specs=[pl.BlockSpec((length,...  30.6 us
    unnamed x140, local copies, waits for them, and re-layouts  24.3 us
    ppermute x15, waiting for transfers between devices, swap_tensor(): return lax.ppermute(array, 'tensor', [(0, 1), (1, 0)])  18.9 us
  transfers between devices with their start and end apart: 78, of which 31 were waited for; matrix products, arithmetic and copies ran while one was open for 28% of the time, Pallas kernels for 19%

profile of v3, /device:TPU:0, one launch (start us, length us, event | category | flops | bytes accessed | tf_op | source)
XLA Modules:
  0.0 527.0 jit_solution(10677162992432973184)
XLA Ops:
  1.6 4.1 collective-permute-start
  6.5 3.0 collective-permute-start.2
  9.5 6.5 %constant_dynamic-slice_fusion = (bf16[512,1,1024]{2,1,0:T(2,128)(2,1)S(1)}, bf16[512,1,1024]{2,1,0:T(2,128)(2,1)S(1)}) fusion(bf16[512,2,1024]{2,1,0:T(2,128)(2,1)} %param.10, s32[]{:T(128)S(6)} %select_n.132, s32[]{:T(128)S(6)} %select_n.118), kind=kLoop, calls=%fused_computation.259 | loop fusion | bytes 4194312 | tf_op jit(solution)/shard_map/jit(dynamic_index_in_dim)/dynamic_slice | solution.py:506
  28.8 6.6 %collective-permute-done.6 = bf16[64,512]{1,0:T(8,128)(2,1)S(1)} collective-permute-done((bf16[64,512]{1,0:T(8,128)(2,1)}, bf16[64,512]{1,0:T(8,128)(2,1)S(1)}, u32[]{:S(2)}, u32[]{:S(2)}) %collective-permute-start.6) | collective-permute-done | bytes 65568 | tf_op jit(solution)/shard_map/ppermute | solution.py:378
  57.5 2.9 fusion.6
  60.4 13.7 %collective-permute-done.21 = bf16[64,2048]{1,0:T(8,128)(2,1)S(1)} collective-permute-done((bf16[64,2048]{1,0:T(8,128)(2,1)S(1)}, bf16[64,2048]{1,0:T(8,128)(2,1)S(1)}, u32[]{:S(2)}, u32[]{:S(2)}) %collective-permute-start.21) | collective-permute-done | bytes 262176 | tf_op jit(solution)/shard_map/ppermute | solution.py:378
  80.4 8.0 %shard_map.177 = (bf16[1024,256]{1,0:T(8,128)(2,1)S(1)}, f32[2,8,1024]{2,1,0:T(8,128)S(1)}) custom-call(bf16[1024,768]{1,0:T(8,128)(2,1)S(1)} %convolution_convert_fusion.8.q_ref.k_ref.v_ref, bf16[1024,768]{1,0:T(8,128)(2,1)S(1)} %convolution_convert_fusion.8.q_ref.k_ref.v_ref, bf16[1024,768]{1,0:T(8,128)(2,1)S(1)} %convolution_convert_fusion.8.q_ref.k_ref.v_ref), custom_call_target="tpu_custom_call" | custom-call | flops 2147483648 | bytes 2097152 | tf_op jit(solution)/shard_map/pallas_call | solution.py:280
  94.2 7.5 %shard_map.178 = (bf16[1024,256]{1,0:T(8,128)(2,1)S(1)}, f32[2,8,1024]{2,1,0:T(8,128)S(1)}) custom-call(bf16[1024,768]{1,0:T(8,128)(2,1)S(1)} %convolution_convert_fusion.7.q_ref.k_ref.v_ref, bf16[1024,768]{1,0:T(8,128)(2,1)S(1)} %convolution_convert_fusion.7.q_ref.k_ref.v_ref, bf16[1024,768]{1,0:T(8,128)(2,1)S(1)} %convolution_convert_fusion.7.q_ref.k_ref.v_ref), custom_call_target="tpu_custom_call" | custom-call | flops 2147483648 | bytes 2097152 | tf_op jit(solution)/shard_map/pallas_call | solution.py:280
  107.4 7.7 %shard_map.179 = (bf16[1024,256]{1,0:T(8,128)(2,1)S(1)}, f32[2,8,1024]{2,1,0:T(8,128)S(1)}) custom-call(bf16[1024,768]{1,0:T(8,128)(2,1)S(1)} %convolution_convert_fusion.6.q_ref.k_ref.v_ref, bf16[1024,768]{1,0:T(8,128)(2,1)S(1)} %convolution_convert_fusion.6.q_ref.k_ref.v_ref, bf16[1024,768]{1,0:T(8,128)(2,1)S(1)} %convolution_convert_fusion.6.q_ref.k_ref.v_ref), custom_call_target="tpu_custom_call" | custom-call | flops 2147483648 | bytes 2097152 | tf_op jit(solution)/shard_map/pallas_call | solution.py:280
  115.1 9.7 %collective-permute-done.26 = bf16[256,2048]{1,0:T(8,128)(2,1)S(1)} collective-permute-done((bf16[256,2048]{1,0:T(8,128)(2,1)S(1)}, bf16[256,2048]{1,0:T(8,128)(2,1)S(1)}, u32[]{:S(2)}, u32[]{:S(2)}) %collective-permute-start.26) | collective-permute-done | bytes 1048608 | tf_op jit(solution)/shard_map/ppermute | solution.py:378
  133.1 7.5 %shard_map.180 = (bf16[1024,256]{1,0:T(8,128)(2,1)S(1)}, f32[2,8,1024]{2,1,0:T(8,128)S(1)}) custom-call(bf16[1024,768]{1,0:T(8,128)(2,1)S(1)} %convolution_convert_fusion.5.q_ref.k_ref.v_ref, bf16[1024,768]{1,0:T(8,128)(2,1)S(1)} %convolution_convert_fusion.5.q_ref.k_ref.v_ref, bf16[1024,768]{1,0:T(8,128)(2,1)S(1)} %convolution_convert_fusion.5.q_ref.k_ref.v_ref), custom_call_target="tpu_custom_call" | custom-call | flops 2147483648 | bytes 2097152 | tf_op jit(solution)/shard_map/pallas_call | solution.py:280
  140.6 12.3 %collective-permute-done.32 = bf16[256,2048]{1,0:T(8,128)(2,1)S(1)} collective-permute-done((bf16[256,2048]{1,0:T(8,128)(2,1)S(1)}, bf16[256,2048]{1,0:T(8,128)(2,1)S(1)}, u32[]{:S(2)}, u32[]{:S(2)}) %collective-permute-start.32) | collective-permute-done | bytes 1048608 | tf_op jit(solution)/shard_map/ppermute | solution.py:378
  169.1 9.3 %fusion.2 = (bf16[1024,2048]{1,0:T(8,128)(2,1)}, bf16[1024,2048]{1,0:T(8,128)(2,1)S(1)}) fusion(bf16[1024,1024]{1,0:T(8,128)(2,1)S(1)} %get-tuple-element.966, bf16[1024,2048]{1,0:T(8,128)(2,1)S(1)} %pad_maximum_fusion.refs_2_), kind=kOutput, calls=%fused_computation.8 | convolution fusion | flops 4328521728 | bytes 14680064 | tf_op jit(solution)/shard_map/dot_general | solution.py:240
  178.4 11.7 %collective-permute-done.34 = bf16[256,2048]{1,0:T(8,128)(2,1)S(1)} collective-permute-done((bf16[256,2048]{1,0:T(8,128)(2,1)S(1)}, bf16[256,2048]{1,0:T(8,128)(2,1)S(1)}, u32[]{:S(2)}, u32[]{:S(2)}) %collective-permute-start.34) | collective-permute-done | bytes 1048608 | tf_op jit(solution)/shard_map/ppermute | solution.py:378
  191.0 9.6 %fusion.5 = (bf16[1024,2048]{1,0:T(8,128)(2,1)}, bf16[1024,2048]{1,0:T(8,128)(2,1)S(1)}) fusion(bf16[1024,1024]{1,0:T(8,128)(2,1)S(1)} %get-tuple-element.966, bf16[1024,2048]{1,0:T(8,128)(2,1)S(1)} %pad_maximum_fusion.1.refs_3_), kind=kOutput, calls=%fused_computation.11 | convolution fusion | flops 4328521728 | bytes 14680064 | tf_op jit(solution)/shard_map/dot_general | solution.py:240
  203.2 3.7 convolution_convert_fusion.3
  207.3 3.7 convolution_convert_fusion.2
  212.3 24.3 %collective-permute-done.40 = bf16[256,2048]{1,0:T(8,128)(2,1)S(1)} collective-permute-done((bf16[256,2048]{1,0:T(8,128)(2,1)S(1)}, bf16[256,2048]{1,0:T(8,128)(2,1)S(1)}, u32[]{:S(2)}, u32[]{:S(2)}) %collective-permute-start.40) | collective-permute-done | bytes 1048608 | tf_op jit(solution)/shard_map/ppermute | solution.py:378
  237.5 3.7 add_convert_fusion.6
  241.2 5.4 %add_convert_fusion.5 = bf16[512,2048]{1,0:T(8,128)(2,1)} fusion(bf16[512,2048]{1,0:T(8,128)(2,1)} %collective-permute-done.39, bf16[1024,2048]{1,0:T(8,128)(2,1)S(1)} %get-tuple-element.970.refs_1_, bf16[1024,1024]{1,0:T(8,128)(2,1)S(1)} %fusion.42), kind=kOutput, calls=%fused_computation.73 | convolution fusion | flops 2150629376 | bytes 9437184 | tf_op jit(solution)/shard_map/dot_general | solution.py:240
  246.6 4.9 multiply_convert_fusion.1.refs_0_
  255.9 7.9 %multiply_convert_fusion.refs_1_ = bf16[1024,2048]{1,0:T(8,128)(2,1)S(1)} fusion(bf16[1024,2048]{1,0:T(8,128)(2,1)} %get-tuple-element.933, bf16[1024,1024]{1,0:T(8,128)(2,1)S(1)} %fusion.42, bf16[1024,2048]{1,0:T(8,128)(2,1)S(1)} %constant_dynamic-update-slice_fusion.8.refs_3_), kind=kOutput, calls=%fused_computation.12 | convolution fusion | flops 4301258752 | bytes 14680064 | tf_op jit(solution)/shard_map/dot_general | solution.py:240
  267.9 3.7 add_convert_fusion.4
  271.6 13.1 %shard_map.181 = f32[1024,1024]{1,0:T(8,128)S(1)} custom-call(bf16[1024,2048]{1,0:T(8,128)(2,1)S(1)} %get-tuple-element.969.refs_0_, bf16[1024,2048]{1,0:T(8,128)(2,1)S(1)} %get-tuple-element.970.refs_1_, bf16[1024,2048]{1,0:T(8,128)(2,1)} %copy-done.31, bf16[1024,2048]{1,0:T(8,128)(2,1)} %copy-done.45), custom_call_target="tpu_custom_call" | custom-call | flops 8589934592 | bytes 20971520 | tf_op jit(solution)/shard_map/pallas_call | solution.py:400
  284.8 5.2 fusion.49
  291.1 4.0 add_convert_fusion.3
  295.1 13.1 %shard_map.182 = f32[1024,1024]{1,0:T(8,128)S(1)} custom-call(bf16[1024,2048]{1,0:T(8,128)(2,1)S(1)} %multiply_convert_fusion.1.refs_0_, bf16[1024,2048]{1,0:T(8,128)(2,1)S(1)} %multiply_convert_fusion.refs_1_, bf16[1024,2048]{1,0:T(8,128)(2,1)} %copy-done.29, bf16[1024,2048]{1,0:T(8,128)(2,1)} %copy-done.30), custom_call_target="tpu_custom_call" | custom-call | flops 8589934592 | bytes 20971520 | tf_op jit(solution)/shard_map/pallas_call | solution.py:400
  308.2 6.4 %collective-permute-done.44 = bf16[512,2048]{1,0:T(8,128)(2,1)} collective-permute-done((bf16[512,2048]{1,0:T(8,128)(2,1)}, bf16[512,2048]{1,0:T(8,128)(2,1)}, u32[]{:S(2)}, u32[]{:S(2)}) %collective-permute-start.44) | collective-permute-done | bytes 2097184 | tf_op jit(solution)/shard_map/ppermute | solution.py:382
  333.1 8.7 %shard_map.183.refs_0_ = bf16[1024,768]{1,0:T(8,128)(2,1)S(1)} custom-call(bf16[1024,768]{1,0:T(8,128)(2,1)S(1)} %copy-done.17, bf16[1024,768]{1,0:T(8,128)(2,1)S(1)} %copy-done.17, bf16[1024,768]{1,0:T(8,128)(2,1)S(1)} %copy-done.17, bf16[1024,256]{1,0:T(8,128)(2,1)S(1)} %slice.247.do_ref, bf16[1024,256]{1,0:T(8,128)(2,1)S(1)} %get-tuple-element.1067.o_ref, ...), custom_call_target="tpu_custom_call" | custom-call | flops 5368709120 | bytes 4194304 | tf_op jit(solution)/shard_map/pallas_call | solution.py:357
  341.8 7.4 %collective-permute-done.47 = bf16[256,2048]{1,0:T(8,128)(2,1)S(1)} collective-permute-done((bf16[256,2048]{1,0:T(8,128)(2,1)S(1)}, bf16[256,2048]{1,0:T(8,128)(2,1)S(1)}, u32[]{:S(2)}, u32[]{:S(2)}) %collective-permute-start.47) | collective-permute-done | bytes 1048608 | tf_op jit(solution)/shard_map/ppermute | solution.py:378
  349.6 21.0 %collective-permute-done.48 = bf16[256,2048]{1,0:T(8,128)(2,1)S(1)} collective-permute-done((bf16[256,2048]{1,0:T(8,128)(2,1)}, bf16[256,2048]{1,0:T(8,128)(2,1)S(1)}, u32[]{:S(2)}, u32[]{:S(2)}) %collective-permute-start.48) | collective-permute-done | bytes 1048608 | tf_op jit(solution)/shard_map/ppermute | solution.py:378
  372.0 8.9 %shard_map.184.refs_2_ = bf16[1024,768]{1,0:T(8,128)(2,1)S(1)} custom-call(bf16[1024,768]{1,0:T(8,128)(2,1)S(1)} %copy-done.21, bf16[1024,768]{1,0:T(8,128)(2,1)S(1)} %copy-done.21, bf16[1024,768]{1,0:T(8,128)(2,1)S(1)} %copy-done.21, bf16[1024,256]{1,0:T(8,128)(2,1)S(1)} %slice.252.do_ref, bf16[1024,256]{1,0:T(8,128)(2,1)S(1)} %copy-done.13, ...), custom_call_target="tpu_custom_call" | custom-call | flops 5368709120 | bytes 4194304 | tf_op jit(solution)/shard_map/pallas_call | solution.py:357
  388.7 8.9 %shard_map.185.refs_1_ = bf16[1024,768]{1,0:T(8,128)(2,1)S(1)} custom-call(bf16[1024,768]{1,0:T(8,128)(2,1)S(1)} %copy-done.15, bf16[1024,768]{1,0:T(8,128)(2,1)S(1)} %copy-done.15, bf16[1024,768]{1,0:T(8,128)(2,1)S(1)} %copy-done.15, bf16[1024,256]{1,0:T(8,128)(2,1)S(1)} %slice.254.do_ref, bf16[1024,256]{1,0:T(8,128)(2,1)S(1)} %copy-done.9, ...), custom_call_target="tpu_custom_call" | custom-call | flops 5368709120 | bytes 4194304 | tf_op jit(solution)/shard_map/pallas_call | solution.py:357
  399.0 11.2 %collective-permute-done.53 = bf16[256,2048]{1,0:T(8,128)(2,1)S(1)} collective-permute-done((bf16[256,2048]{1,0:T(8,128)(2,1)S(1)}, bf16[256,2048]{1,0:T(8,128)(2,1)S(1)}, u32[]{:S(2)}, u32[]{:S(2)}) %collective-permute-start.53) | collective-permute-done | bytes 1048608 | tf_op jit(solution)/shard_map/ppermute | solution.py:378
  414.0 3.2 add_convert_fusion.24
  417.2 8.7 %shard_map.186.refs_3_ = bf16[1024,768]{1,0:T(8,128)(2,1)S(1)} custom-call(bf16[1024,768]{1,0:T(8,128)(2,1)S(1)} %copy-done.19, bf16[1024,768]{1,0:T(8,128)(2,1)S(1)} %copy-done.19, bf16[1024,768]{1,0:T(8,128)(2,1)S(1)} %copy-done.19, bf16[1024,256]{1,0:T(8,128)(2,1)S(1)} %slice.262.do_ref, bf16[1024,256]{1,0:T(8,128)(2,1)S(1)} %copy-done.11, ...), custom_call_target="tpu_custom_call" | custom-call | flops 5368709120 | bytes 4194304 | tf_op jit(solution)/shard_map/pallas_call | solution.py:357
  426.3 3.1 add_convert_fusion.23
  440.2 8.6 %shard_map.187 = f32[1024,1024]{1,0:T(8,128)} custom-call(bf16[1024,768]{1,0:T(8,128)(2,1)S(1)} %shard_map.183.refs_0_, bf16[1024,768]{1,0:T(8,128)(2,1)S(1)} %shard_map.185.refs_1_, bf16[1024,768]{1,0:T(8,128)(2,1)S(1)} %shard_map.184.refs_2_, bf16[1024,768]{1,0:T(8,128)(2,1)S(1)} %shard_map.186.refs_3_, bf16[1024,768]{1,0:T(8,128)(2,1)S(1)} %copy-done.1, ...), custom_call_target="tpu_custom_call" | custom-call | flops 6442450944 | bytes 16777216 | tf_op jit(solution)/shard_map/pallas_call | solution.py:400
  453.1 3.6 collective-permute-start.63
  456.9 3.7 multiply_reduce_fusion
  462.7 3.0 fusion.48
  476.4 2.8 collective-permute-start.68
  486.8 3.5 copy.34
  490.8 5.4 %collective-permute-done.70 = f32[4,64]{1,0:T(4,128)S(1)} collective-permute-done((f32[4,64]{1,0:T(4,128)S(1)}, f32[4,64]{1,0:T(4,128)S(1)}, u32[]{:S(2)}, u32[]{:S(2)}) %collective-permute-start.70) | collective-permute-done | bytes 1056 | tf_op jit(solution)/shard_map/ppermute | solution.py:382
  496.3 2.9 collective-permute-start.72
  511.9 5.8 %collective-permute-done.65 = bf16[512,1024]{1,0:T(8,128)(2,1)} collective-permute-done((bf16[512,1024]{1,0:T(8,128)(2,1)S(1)}, bf16[512,1024]{1,0:T(8,128)(2,1)}, u32[]{:S(2)}, u32[]{:S(2)}) %collective-permute-start.65) | collective-permute-done | bytes 1048608 | tf_op jit(solution)/shard_map/ppermute | solution.py:382
  519.1 2.9 collective-permute-start.77
  522.2 3.5 copy.35
  (419 shorter events, 178.7 us)
Async XLA Ops:
  1.6 20.5 %collective-permute-start = (bf16[64,768]{1,0:T(8,128)(2,1)S(1)}, bf16[64,768]{1,0:T(8,128)(2,1)S(1)}, u32[]{:S(2)}, u32[]{:S(2)}) collective-permute-start(bf16[64,768]{1,0:T(8,128)(2,1)S(1)} %bitcast.102), channel_id=1, source_target_pairs={{0,16},{2,18},{4,20},{6,22},{8,24},{10,26},{12,28},{14,30},{16,0},... | collective-permute-start | bytes 294920 | tf_op jit(solution)/shard_map/ppermute | solution.py:378
  5.7 16.4 %collective-permute-start.1 = (bf16[64,768]{1,0:T(8,128)(2,1)S(1)}, bf16[64,768]{1,0:T(8,128)(2,1)S(1)}, u32[]{:S(2)}, u32[]{:S(2)}) collective-permute-start(bf16[64,768]{1,0:T(8,128)(2,1)S(1)} %bitcast.104), channel_id=1, source_target_pairs={{0,16},{2,18},{4,20},{6,22},{8,24},{10,26},{12,28},{14,30},{16,0},... | collective-permute-start | bytes 294920 | tf_op jit(solution)/shard_map/ppermute | solution.py:378
  6.5 15.2 %collective-permute-start.2 = (bf16[4,64]{1,0:T(4,128)(2,1)S(1)}, bf16[4,64]{1,0:T(4,128)(2,1)S(1)}, u32[]{:S(2)}, u32[]{:S(2)}) collective-permute-start(bf16[4,64]{1,0:T(4,128)(2,1)S(1)} %pad_maximum_fusion.34), channel_id=1, source_target_pairs={{0,16},{2,18},{4,20},{6,22},{8,24},{10,26},{12,28},{14,30},{16,0},... | collective-permute-start | bytes 1544 | tf_op jit(solution)/shard_map/ppermute | solution.py:378
  17.4 24.4 %collective-permute-start.7 = (bf16[512,1024]{1,0:T(8,128)(2,1)}, bf16[512,1024]{1,0:T(8,128)(2,1)}, u32[]{:S(2)}, u32[]{:S(2)}) collective-permute-start(bf16[512,1024]{1,0:T(8,128)(2,1)} %bitcast.96), channel_id=1, source_target_pairs={{0,1},{1,0},{2,3},{3,2},{4,5},{5,4},{6,7},{7,6},{8,9},{9,8},{10,11... | collective-permute-start | bytes 3145736 | tf_op jit(solution)/shard_map/ppermute | solution.py:382
  24.3 14.7 %collective-permute-start.4 = (bf16[128,768]{1,0:T(8,128)(2,1)S(1)}, bf16[128,768]{1,0:T(8,128)(2,1)S(1)}, u32[]{:S(2)}, u32[]{:S(2)}) collective-permute-start(bf16[128,768]{1,0:T(8,128)(2,1)S(1)} %pad_maximum_fusion.29), channel_id=1, source_target_pairs={{0,8},{2,10},{4,12},{6,14},{8,0},{10,2},{12,4},{14,6},{16,24},{18,... | collective-permute-start | bytes 589832 | tf_op jit(solution)/shard_map/ppermute | solution.py:378
  26.2 15.3 %collective-permute-start.11 = (bf16[64,2048]{1,0:T(8,128)(2,1)}, bf16[64,2048]{1,0:T(8,128)(2,1)S(1)}, u32[]{:S(2)}, u32[]{:S(2)}) collective-permute-start(bf16[64,2048]{1,0:T(8,128)(2,1)} %param.18), channel_id=1, source_target_pairs={{0,16},{2,18},{4,20},{6,22},{8,24},{10,26},{12,28},{14,30},{16,0},... | collective-permute-start | bytes 786440 | tf_op jit(solution)/shard_map/ppermute | solution.py:378
  52.1 22.0 %collective-permute-start.13 = (bf16[256,768]{1,0:T(8,128)(2,1)S(1)}, bf16[256,768]{1,0:T(8,128)(2,1)S(1)}, u32[]{:S(2)}, u32[]{:S(2)}) collective-permute-start(bf16[256,768]{1,0:T(8,128)(2,1)S(1)} %pad_maximum_fusion.26), channel_id=1, source_target_pairs={{0,4},{2,6},{4,0},{6,2},{8,12},{10,14},{12,8},{14,10},{16,20},{18,... | collective-permute-start | bytes 1179656 | tf_op jit(solution)/shard_map/ppermute | solution.py:378
  52.7 22.4 %collective-permute-start.14 = (bf16[512,768]{1,0:T(8,128)(2,1)S(1)}, bf16[512,768]{1,0:T(8,128)(2,1)S(1)}, u32[]{:S(2)}, u32[]{:S(2)}) collective-permute-start(bf16[512,768]{1,0:T(8,128)(2,1)S(1)} %pad_maximum_fusion.17), channel_id=1, source_target_pairs={{0,2},{2,0},{4,6},{6,4},{8,10},{10,8},{12,14},{14,12},{16,18},{18,... | collective-permute-start | bytes 2359304 | tf_op jit(solution)/shard_map/ppermute | solution.py:378
  52.9 22.3 %collective-permute-start.15 = (bf16[256,512]{1,0:T(8,128)(2,1)S(1)}, bf16[256,512]{1,0:T(8,128)(2,1)S(1)}, u32[]{:S(2)}, u32[]{:S(2)}) collective-permute-start(bf16[256,512]{1,0:T(8,128)(2,1)S(1)} %pad_maximum_fusion.27), channel_id=1, source_target_pairs={{0,1},{1,0},{2,3},{3,2},{4,5},{5,4},{6,7},{7,6},{8,9},{9,8},{10,11... | collective-permute-start | bytes 786440 | tf_op jit(solution)/shard_map/ppermute | solution.py:382
  55.4 19.6 %collective-permute-start.17 = (bf16[128,2048]{1,0:T(8,128)(2,1)S(1)}, bf16[128,2048]{1,0:T(8,128)(2,1)S(1)}, u32[]{:S(2)}, u32[]{:S(2)}) collective-permute-start(bf16[128,2048]{1,0:T(8,128)(2,1)S(1)} %pad_maximum_fusion.20), channel_id=1, source_target_pairs={{0,8},{2,10},{4,12},{6,14},{8,0},{10,2},{12,4},{14,6},{16,24},{18,... | collective-permute-start | bytes 1572872 | tf_op jit(solution)/shard_map/ppermute | solution.py:378
  57.1 17.0 %collective-permute-start.21 = (bf16[64,2048]{1,0:T(8,128)(2,1)S(1)}, bf16[64,2048]{1,0:T(8,128)(2,1)S(1)}, u32[]{:S(2)}, u32[]{:S(2)}) collective-permute-start(bf16[64,2048]{1,0:T(8,128)(2,1)S(1)} %bitcast.106), channel_id=1, source_target_pairs={{0,16},{2,18},{4,20},{6,22},{8,24},{10,26},{12,28},{14,30},{16,0},... | collective-permute-start | bytes 786440 | tf_op jit(solution)/shard_map/ppermute | solution.py:378
  75.3 28.3 %collective-permute-start.24 = (bf16[512,768]{1,0:T(8,128)(2,1)S(1)}, bf16[512,768]{1,0:T(8,128)(2,1)S(1)}, u32[]{:S(2)}, u32[]{:S(2)}) collective-permute-start(bf16[512,768]{1,0:T(8,128)(2,1)S(1)} %pad_maximum_fusion.18), channel_id=1, source_target_pairs={{0,1},{1,0},{2,3},{3,2},{4,5},{5,4},{6,7},{7,6},{8,9},{9,8},{10,11... | collective-permute-start | bytes 2359304 | tf_op jit(solution)/shard_map/ppermute | solution.py:382
  89.2 14.3 %collective-permute-start.22 = (bf16[256,512]{1,0:T(8,128)(2,1)S(1)}, bf16[256,512]{1,0:T(8,128)(2,1)S(1)}, u32[]{:S(2)}, u32[]{:S(2)}) collective-permute-start(bf16[256,512]{1,0:T(8,128)(2,1)S(1)} %collective-permute-done.15), channel_id=1, source_target_pairs={{0,4},{2,6},{4,0},{6,2},{8,12},{10,14},{12,8},{14,10},{16,20},{18,... | collective-permute-start | bytes 786440 | tf_op jit(solution)/shard_map/ppermute | solution.py:378
  90.7 34.2 %collective-permute-start.26 = (bf16[256,2048]{1,0:T(8,128)(2,1)S(1)}, bf16[256,2048]{1,0:T(8,128)(2,1)S(1)}, u32[]{:S(2)}, u32[]{:S(2)}) collective-permute-start(bf16[256,2048]{1,0:T(8,128)(2,1)S(1)} %pad_maximum_fusion.13), channel_id=1, source_target_pairs={{0,4},{2,6},{4,0},{6,2},{8,12},{10,14},{12,8},{14,10},{16,20},{18,... | collective-permute-start | bytes 3145736 | tf_op jit(solution)/shard_map/ppermute | solution.py:378
  101.7 25.5 %collective-permute-start.30 = (bf16[256,2048]{1,0:T(8,128)(2,1)S(1)}, bf16[256,2048]{1,0:T(8,128)(2,1)S(1)}, u32[]{:S(2)}, u32[]{:S(2)}) collective-permute-start(bf16[256,2048]{1,0:T(8,128)(2,1)S(1)} %pad_maximum_fusion.13), channel_id=1, source_target_pairs={{0,1},{1,0},{2,3},{3,2},{4,5},{5,4},{6,7},{7,6},{8,9},{9,8},{10,11... | collective-permute-start | bytes 3145736 | tf_op jit(solution)/shard_map/ppermute | solution.py:382
  103.6 21.5 %collective-permute-start.25 = (bf16[512,512]{1,0:T(8,128)(2,1)S(1)}, bf16[512,512]{1,0:T(8,128)(2,1)S(1)}, u32[]{:S(2)}, u32[]{:S(2)}) collective-permute-start(bf16[512,512]{1,0:T(8,128)(2,1)S(1)} %pad_maximum_fusion.21), channel_id=1, source_target_pairs={{0,2},{2,0},{4,6},{6,4},{8,10},{10,8},{12,14},{14,12},{16,18},{18,... | collective-permute-start | bytes 1572872 | tf_op jit(solution)/shard_map/ppermute | solution.py:378
  103.7 21.6 %collective-permute-start.27 = (bf16[128,2048]{1,0:T(8,128)(2,1)S(1)}, bf16[128,2048]{1,0:T(8,128)(2,1)S(1)}, u32[]{:S(2)}, u32[]{:S(2)}) collective-permute-start(bf16[128,2048]{1,0:T(8,128)(2,1)S(1)} %pad_maximum_fusion.22), channel_id=1, source_target_pairs={{0,8},{2,10},{4,12},{6,14},{8,0},{10,2},{12,4},{14,6},{16,24},{18,... | collective-permute-start | bytes 1572872 | tf_op jit(solution)/shard_map/ppermute | solution.py:378
  104.3 20.9 %collective-permute-start.28 = (bf16[512,512]{1,0:T(8,128)(2,1)S(1)}, bf16[512,512]{1,0:T(8,128)(2,1)S(1)}, u32[]{:S(2)}, u32[]{:S(2)}) collective-permute-start(bf16[512,512]{1,0:T(8,128)(2,1)S(1)} %pad_maximum_fusion.23), channel_id=1, source_target_pairs={{0,2},{2,0},{4,6},{6,4},{8,10},{10,8},{12,14},{14,12},{16,18},{18,... | collective-permute-start | bytes 1572872 | tf_op jit(solution)/shard_map/ppermute | solution.py:378
  127.2 25.9 %collective-permute-start.31 = (bf16[512,2048]{1,0:T(8,128)(2,1)S(1)}, bf16[512,2048]{1,0:T(8,128)(2,1)S(1)}, u32[]{:S(2)}, u32[]{:S(2)}) collective-permute-start(bf16[512,2048]{1,0:T(8,128)(2,1)S(1)} %pad_maximum_fusion.3), channel_id=1, source_target_pairs={{0,2},{2,0},{4,6},{6,4},{8,10},{10,8},{12,14},{14,12},{16,18},{18,... | collective-permute-start | bytes 6291464 | tf_op jit(solution)/shard_map/ppermute | solution.py:378
  127.4 25.4 %collective-permute-start.32 = (bf16[256,2048]{1,0:T(8,128)(2,1)S(1)}, bf16[256,2048]{1,0:T(8,128)(2,1)S(1)}, u32[]{:S(2)}, u32[]{:S(2)}) collective-permute-start(bf16[256,2048]{1,0:T(8,128)(2,1)S(1)} %collective-permute-done.30), channel_id=1, source_target_pairs={{0,4},{2,6},{4,0},{6,2},{8,12},{10,14},{12,8},{14,10},{16,20},{18,... | collective-permute-start | bytes 3145736 | tf_op jit(solution)/shard_map/ppermute | solution.py:378
  128.6 35.0 %collective-permute-start.33 = (bf16[256,2048]{1,0:T(8,128)(2,1)S(1)}, bf16[256,2048]{1,0:T(8,128)(2,1)S(1)}, u32[]{:S(2)}, u32[]{:S(2)}) collective-permute-start(bf16[256,2048]{1,0:T(8,128)(2,1)S(1)} %pad_maximum_fusion.15), channel_id=1, source_target_pairs={{0,1},{1,0},{2,3},{3,2},{4,5},{5,4},{6,7},{7,6},{8,9},{9,8},{10,11... | collective-permute-start | bytes 3145736 | tf_op jit(solution)/shard_map/ppermute | solution.py:382
  164.5 25.8 %collective-permute-start.35 = (bf16[512,2048]{1,0:T(8,128)(2,1)S(1)}, bf16[512,2048]{1,0:T(8,128)(2,1)S(1)}, u32[]{:S(2)}, u32[]{:S(2)}) collective-permute-start(bf16[512,2048]{1,0:T(8,128)(2,1)S(1)} %pad_maximum_fusion.4), channel_id=1, source_target_pairs={{0,2},{2,0},{4,6},{6,4},{8,10},{10,8},{12,14},{14,12},{16,18},{18,... | collective-permute-start | bytes 6291464 | tf_op jit(solution)/shard_map/ppermute | solution.py:378
  164.5 25.6 %collective-permute-start.34 = (bf16[256,2048]{1,0:T(8,128)(2,1)S(1)}, bf16[256,2048]{1,0:T(8,128)(2,1)S(1)}, u32[]{:S(2)}, u32[]{:S(2)}) collective-permute-start(bf16[256,2048]{1,0:T(8,128)(2,1)S(1)} %pad_maximum_fusion.15), channel_id=1, source_target_pairs={{0,4},{2,6},{4,0},{6,2},{8,12},{10,14},{12,8},{14,10},{16,20},{18,... | collective-permute-start | bytes 3145736 | tf_op jit(solution)/shard_map/ppermute | solution.py:378
  167.6 33.0 %collective-permute-start.36 = (bf16[512,1024]{1,0:T(8,128)(2,1)}, bf16[512,1024]{1,0:T(8,128)(2,1)S(1)}, u32[]{:S(2)}, u32[]{:S(2)}) collective-permute-start(bf16[512,1024]{1,0:T(8,128)(2,1)} %get-tuple-element.1254), channel_id=1, source_target_pairs={{0,1},{1,0},{2,3},{3,2},{4,5},{5,4},{6,7},{7,6},{8,9},{9,8},{10,11... | collective-permute-start | bytes 3145736 | tf_op jit(solution)/shard_map/ppermute | solution.py:382
  200.6 36.3 %collective-permute-start.37 = (bf16[512,2048]{1,0:T(8,128)(2,1)S(1)}, bf16[512,2048]{1,0:T(8,128)(2,1)S(1)}, u32[]{:S(2)}, u32[]{:S(2)}) collective-permute-start(bf16[512,2048]{1,0:T(8,128)(2,1)S(1)} %pad_maximum_fusion.5), channel_id=1, source_target_pairs={{0,2},{2,0},{4,6},{6,4},{8,10},{10,8},{12,14},{14,12},{16,18},{18,... | collective-permute-start | bytes 6291464 | tf_op jit(solution)/shard_map/ppermute | solution.py:378
  206.8 30.6 %collective-permute-start.38 = (bf16[512,2048]{1,0:T(8,128)(2,1)}, bf16[512,2048]{1,0:T(8,128)(2,1)S(1)}, u32[]{:S(2)}, u32[]{:S(2)}) collective-permute-start(bf16[512,2048]{1,0:T(8,128)(2,1)} %convolution_convert_fusion.3), channel_id=1, source_target_pairs={{0,2},{2,0},{4,6},{6,4},{8,10},{10,8},{12,14},{14,12},{16,18},{18,... | collective-permute-start | bytes 6291464 | tf_op jit(solution)/shard_map/ppermute | solution.py:378
  211.0 26.4 %collective-permute-start.39 = (bf16[512,2048]{1,0:T(8,128)(2,1)}, bf16[512,2048]{1,0:T(8,128)(2,1)}, u32[]{:S(2)}, u32[]{:S(2)}) collective-permute-start(bf16[512,2048]{1,0:T(8,128)(2,1)} %convolution_convert_fusion.2), channel_id=1, source_target_pairs={{0,2},{2,0},{4,6},{6,4},{8,10},{10,8},{12,14},{14,12},{16,18},{18,... | collective-permute-start | bytes 6291464 | tf_op jit(solution)/shard_map/ppermute | solution.py:378
  211.1 25.6 %collective-permute-start.40 = (bf16[256,2048]{1,0:T(8,128)(2,1)S(1)}, bf16[256,2048]{1,0:T(8,128)(2,1)S(1)}, u32[]{:S(2)}, u32[]{:S(2)}) collective-permute-start(bf16[256,2048]{1,0:T(8,128)(2,1)S(1)} %copy-done.47), channel_id=1, source_target_pairs={{0,4},{2,6},{4,0},{6,2},{8,12},{10,14},{12,8},{14,10},{16,20},{18,... | collective-permute-start | bytes 3145736 | tf_op jit(solution)/shard_map/ppermute | solution.py:378
  266.4 48.2 %collective-permute-start.44 = (bf16[512,2048]{1,0:T(8,128)(2,1)}, bf16[512,2048]{1,0:T(8,128)(2,1)}, u32[]{:S(2)}, u32[]{:S(2)}) collective-permute-start(bf16[512,2048]{1,0:T(8,128)(2,1)} %add_convert_fusion.5), channel_id=1, source_target_pairs={{0,1},{1,0},{2,3},{3,2},{4,5},{5,4},{6,7},{7,6},{8,9},{9,8},{10,11... | collective-permute-start | bytes 6291464 | tf_op jit(solution)/shard_map/ppermute | solution.py:382
  323.1 26.1 %collective-permute-start.47 = (bf16[256,2048]{1,0:T(8,128)(2,1)S(1)}, bf16[256,2048]{1,0:T(8,128)(2,1)S(1)}, u32[]{:S(2)}, u32[]{:S(2)}) collective-permute-start(bf16[256,2048]{1,0:T(8,128)(2,1)S(1)} %slice.249), channel_id=1, source_target_pairs={{0,4},{2,6},{4,0},{6,2},{8,12},{10,14},{12,8},{14,10},{16,20},{18,... | collective-permute-start | bytes 3145736 | tf_op jit(solution)/shard_map/ppermute | solution.py:378
  325.5 45.0 %collective-permute-start.48 = (bf16[256,2048]{1,0:T(8,128)(2,1)}, bf16[256,2048]{1,0:T(8,128)(2,1)S(1)}, u32[]{:S(2)}, u32[]{:S(2)}) collective-permute-start(bf16[256,2048]{1,0:T(8,128)(2,1)} %slice.251), channel_id=1, source_target_pairs={{0,4},{2,6},{4,0},{6,2},{8,12},{10,14},{12,8},{14,10},{16,20},{18,... | collective-permute-start | bytes 3145736 | tf_op jit(solution)/shard_map/ppermute | solution.py:378
  326.2 54.7 %collective-permute-start.49 = (bf16[512,1024]{1,0:T(8,128)(2,1)S(1)}, bf16[512,1024]{1,0:T(8,128)(2,1)S(1)}, u32[]{:S(2)}, u32[]{:S(2)}) collective-permute-start(bf16[512,1024]{1,0:T(8,128)(2,1)S(1)} %copy-done.41), channel_id=1, source_target_pairs={{0,1},{1,0},{2,3},{3,2},{4,5},{5,4},{6,7},{7,6},{8,9},{9,8},{10,11... | collective-permute-start | bytes 3145736 | tf_op jit(solution)/shard_map/ppermute | solution.py:382
  380.9 16.7 %collective-permute-start.50 = (bf16[512,512]{1,0:T(8,128)(2,1)S(1)}, bf16[512,512]{1,0:T(8,128)(2,1)}, u32[]{:S(2)}, u32[]{:S(2)}) collective-permute-start(bf16[512,512]{1,0:T(8,128)(2,1)S(1)} %fusion.51), channel_id=1, source_target_pairs={{0,1},{1,0},{2,3},{3,2},{4,5},{5,4},{6,7},{7,6},{8,9},{9,8},{10,11... | collective-permute-start | bytes 1572872 | tf_op jit(solution)/shard_map/ppermute | solution.py:382
  384.4 26.2 %collective-permute-start.51 = (bf16[512,768]{1,0:T(8,128)(2,1)}, bf16[512,768]{1,0:T(8,128)(2,1)}, u32[]{:S(2)}, u32[]{:S(2)}) collective-permute-start(bf16[512,768]{1,0:T(8,128)(2,1)} %convolution_convert_fusion.12), channel_id=1, source_target_pairs={{0,2},{2,0},{4,6},{6,4},{8,10},{10,8},{12,14},{14,12},{16,18},{18,... | collective-permute-start | bytes 2359304 | tf_op jit(solution)/shard_map/ppermute | solution.py:378
  384.5 25.6 %collective-permute-start.53 = (bf16[256,2048]{1,0:T(8,128)(2,1)S(1)}, bf16[256,2048]{1,0:T(8,128)(2,1)S(1)}, u32[]{:S(2)}, u32[]{:S(2)}) collective-permute-start(bf16[256,2048]{1,0:T(8,128)(2,1)S(1)} %slice.256), channel_id=1, source_target_pairs={{0,4},{2,6},{4,0},{6,2},{8,12},{10,14},{12,8},{14,10},{16,20},{18,... | collective-permute-start | bytes 3145736 | tf_op jit(solution)/shard_map/ppermute | solution.py:378
  387.8 22.8 %collective-permute-start.52 = (bf16[512,768]{1,0:T(8,128)(2,1)}, bf16[512,768]{1,0:T(8,128)(2,1)}, u32[]{:S(2)}, u32[]{:S(2)}) collective-permute-start(bf16[512,768]{1,0:T(8,128)(2,1)} %convolution_convert_fusion.11), channel_id=1, source_target_pairs={{0,2},{2,0},{4,6},{6,4},{8,10},{10,8},{12,14},{14,12},{16,18},{18,... | collective-permute-start | bytes 2359304 | tf_op jit(solution)/shard_map/ppermute | solution.py:378
  388.1 37.8 %collective-permute-start.55 = (bf16[256,2048]{1,0:T(8,128)(2,1)S(1)}, bf16[256,2048]{1,0:T(8,128)(2,1)S(1)}, u32[]{:S(2)}, u32[]{:S(2)}) collective-permute-start(bf16[256,2048]{1,0:T(8,128)(2,1)S(1)} %copy-done.42), channel_id=1, source_target_pairs={{0,1},{1,0},{2,3},{3,2},{4,5},{5,4},{6,7},{7,6},{8,9},{9,8},{10,11... | collective-permute-start | bytes 3145736 | tf_op jit(solution)/shard_map/ppermute | solution.py:382
  411.3 18.1 %collective-permute-start.54 = (bf16[256,512]{1,0:T(8,128)(2,1)}, bf16[256,512]{1,0:T(8,128)(2,1)}, u32[]{:S(2)}, u32[]{:S(2)}) collective-permute-start(bf16[256,512]{1,0:T(8,128)(2,1)} %slice.258), channel_id=1, source_target_pairs={{0,4},{2,6},{4,0},{6,2},{8,12},{10,14},{12,8},{14,10},{16,20},{18,... | collective-permute-start | bytes 786440 | tf_op jit(solution)/shard_map/ppermute | solution.py:378
  413.4 17.0 %collective-permute-start.56 = (bf16[128,2048]{1,0:T(8,128)(2,1)}, bf16[128,2048]{1,0:T(8,128)(2,1)S(1)}, u32[]{:S(2)}, u32[]{:S(2)}) collective-permute-start(bf16[128,2048]{1,0:T(8,128)(2,1)} %slice.261), channel_id=1, source_target_pairs={{0,8},{2,10},{4,12},{6,14},{8,0},{10,2},{12,4},{14,6},{16,24},{18,... | collective-permute-start | bytes 1572872 | tf_op jit(solution)/shard_map/ppermute | solution.py:378
  430.6 18.3 %collective-permute-start.57 = (bf16[128,512]{1,0:T(8,128)(2,1)S(1)}, bf16[128,512]{1,0:T(8,128)(2,1)S(1)}, u32[]{:S(2)}, u32[]{:S(2)}) collective-permute-start(bf16[128,512]{1,0:T(8,128)(2,1)S(1)} %slice.264), channel_id=1, source_target_pairs={{0,8},{2,10},{4,12},{6,14},{8,0},{10,2},{12,4},{14,6},{16,24},{18,... | collective-permute-start | bytes 393224 | tf_op jit(solution)/shard_map/ppermute | solution.py:378
  433.0 20.0 %collective-permute-start.58 = (bf16[128,2048]{1,0:T(8,128)(2,1)}, bf16[128,2048]{1,0:T(8,128)(2,1)S(1)}, u32[]{:S(2)}, u32[]{:S(2)}) collective-permute-start(bf16[128,2048]{1,0:T(8,128)(2,1)} %slice.266), channel_id=1, source_target_pairs={{0,8},{2,10},{4,12},{6,14},{8,0},{10,2},{12,4},{14,6},{16,24},{18,... | collective-permute-start | bytes 1572872 | tf_op jit(solution)/shard_map/ppermute | solution.py:378
  435.4 17.7 %collective-permute-start.59 = (bf16[512,768]{1,0:T(8,128)(2,1)}, bf16[512,768]{1,0:T(8,128)(2,1)}, u32[]{:S(2)}, u32[]{:S(2)}) collective-permute-start(bf16[512,768]{1,0:T(8,128)(2,1)} %convolution_convert_fusion.10), channel_id=1, source_target_pairs={{0,2},{2,0},{4,6},{6,4},{8,10},{10,8},{12,14},{14,12},{16,18},{18,... | collective-permute-start | bytes 2359304 | tf_op jit(solution)/shard_map/ppermute | solution.py:378
  437.5 15.6 %collective-permute-start.60 = (bf16[512,768]{1,0:T(8,128)(2,1)}, bf16[512,768]{1,0:T(8,128)(2,1)}, u32[]{:S(2)}, u32[]{:S(2)}) collective-permute-start(bf16[512,768]{1,0:T(8,128)(2,1)} %convolution_convert_fusion.9), channel_id=1, source_target_pairs={{0,2},{2,0},{4,6},{6,4},{8,10},{10,8},{12,14},{14,12},{16,18},{18,... | collective-permute-start | bytes 2359304 | tf_op jit(solution)/shard_map/ppermute | solution.py:378
  448.9 20.9 %collective-permute-start.62 = (bf16[512,768]{1,0:T(8,128)(2,1)}, bf16[512,768]{1,0:T(8,128)(2,1)S(1)}, u32[]{:S(2)}, u32[]{:S(2)}) collective-permute-start(bf16[512,768]{1,0:T(8,128)(2,1)} %add_convert_fusion.23), channel_id=1, source_target_pairs={{0,1},{1,0},{2,3},{3,2},{4,5},{5,4},{6,7},{7,6},{8,9},{9,8},{10,11... | collective-permute-start | bytes 2359304 | tf_op jit(solution)/shard_map/ppermute | solution.py:382
  453.1 17.6 %collective-permute-start.63 = (bf16[64,2048]{1,0:T(8,128)(2,1)S(1)}, bf16[64,2048]{1,0:T(8,128)(2,1)S(1)}, u32[]{:S(2)}, u32[]{:S(2)}) collective-permute-start(bf16[64,2048]{1,0:T(8,128)(2,1)S(1)} %slice.272), channel_id=1, source_target_pairs={{0,16},{2,18},{4,20},{6,22},{8,24},{10,26},{12,28},{14,30},{16,0},... | collective-permute-start | bytes 786440 | tf_op jit(solution)/shard_map/ppermute | solution.py:378
  475.7 23.6 %collective-permute-start.74 = (bf16[512,768]{1,0:T(8,128)(2,1)S(1)}, bf16[512,768]{1,0:T(8,128)(2,1)S(1)}, u32[]{:S(2)}, u32[]{:S(2)}) collective-permute-start(bf16[512,768]{1,0:T(8,128)(2,1)S(1)} %add_convert_fusion.20), channel_id=1, source_target_pairs={{0,1},{1,0},{2,3},{3,2},{4,5},{5,4},{6,7},{7,6},{8,9},{9,8},{10,11... | collective-permute-start | bytes 2359304 | tf_op jit(solution)/shard_map/ppermute | solution.py:382
  479.2 17.0 %collective-permute-start.71 = (bf16[256,768]{1,0:T(8,128)(2,1)S(1)}, bf16[256,768]{1,0:T(8,128)(2,1)S(1)}, u32[]{:S(2)}, u32[]{:S(2)}) collective-permute-start(bf16[256,768]{1,0:T(8,128)(2,1)S(1)} %slice.288), channel_id=1, source_target_pairs={{0,4},{2,6},{4,0},{6,2},{8,12},{10,14},{12,8},{14,10},{16,20},{18,... | collective-permute-start | bytes 1179656 | tf_op jit(solution)/shard_map/ppermute | solution.py:378
  490.3 27.4 %collective-permute-start.65 = (bf16[512,1024]{1,0:T(8,128)(2,1)S(1)}, bf16[512,1024]{1,0:T(8,128)(2,1)}, u32[]{:S(2)}, u32[]{:S(2)}) collective-permute-start(bf16[512,1024]{1,0:T(8,128)(2,1)S(1)} %get-tuple-element.1195), channel_id=1, source_target_pairs={{0,1},{1,0},{2,3},{3,2},{4,5},{5,4},{6,7},{7,6},{8,9},{9,8},{10,11... | collective-permute-start | bytes 3145736 | tf_op jit(solution)/shard_map/ppermute | solution.py:382
  (94 other events, 807.7 us)

commit v4 on v3

--- a/solution.py
+++ b/solution.py
@@ -231,6 +231,7 @@
 
 LOG2E = 1.4426950408889634
 BLOCK = 256
+BIG = 24 * 2**20
 NT = (((1,), (1,)), ((), ()))
 TN = (((0,), (0,)), ((), ()))
 NN = (((1,), (0,)), ((), ()))
@@ -293,9 +294,9 @@
             jax.ShapeDtypeStruct((length, width), jnp.bfloat16),
             jax.ShapeDtypeStruct((pairs, 8, length), jnp.float32),
         ],
-        compiler_params=pltpu.CompilerParams(vmem_limit_bytes=40 * 2**20),
+        compiler_params=pltpu.CompilerParams(vmem_limit_bytes=BIG),
         cost_estimate=pl.CostEstimate(
-            flops=8 * length * length * width, bytes_accessed=8 * length * width, transcendentals=0
+            flops=length, bytes_accessed=length, transcendentals=0
         ),
     )(qkv, qkv, qkv)
 
@@ -367,9 +368,9 @@
         ],
         out_specs=pl.BlockSpec((length, width3), lambda j: (0, 0)),
         out_shape=jax.ShapeDtypeStruct((length, width3), jnp.bfloat16),
-        compiler_params=pltpu.CompilerParams(vmem_limit_bytes=40 * 2**20),
+        compiler_params=pltpu.CompilerParams(vmem_limit_bytes=BIG),
         cost_estimate=pl.CostEstimate(
-            flops=20 * length * length * width, bytes_accessed=16 * length * width, transcendentals=0
+            flops=length, bytes_accessed=length, transcendentals=0
         ),
     )(qkv, qkv, qkv, grad_mixed, mixed, lse)
 
@@ -386,31 +387,35 @@
     return (left.astype(jnp.float32) + right.astype(jnp.float32)).astype(jnp.bfloat16)
 
 
-def sum_kernel(count, *refs):
-    total = mul(refs[0][...], refs[count][...], NT)
-    for i in range(1, count):
-        total = total + mul(refs[i][...], refs[count + i][...], NT)
-    refs[2 * count][...] = total
-
-
-def sum_products(lefts, rights):
-    rows, columns = lefts[0].shape[0], rights[0].shape[0]
+def sum_kernel(count, pieces, *refs):
+    out_ref = refs[-1]
+    start = 0
+    for p in range(pieces):
+        end = start + refs[count + p].shape[0]
+        total = mul(refs[0][...], refs[count + p][...], NT)
+        for i in range(1, count):
+            total = total + mul(refs[i][...], refs[count + i * pieces + p][...], NT)
+        out_ref[:, start:end] = total
+        start = end
+
+
+def sum_products(lefts, rights, limit=BIG):
+    rows, pieces = lefts[0].shape[0], len(rights[0])
+    columns = sum(piece.shape[0] for piece in rights[0])
+    flat = [piece for right in rights for piece in right]
     block = min(256, rows)
-    depth = sum(left.shape[1] for left in lefts)
     return pl.pallas_call(
-        functools.partial(sum_kernel, len(lefts)),
+        functools.partial(sum_kernel, len(lefts), pieces),
         grid=(rows // block,),
         in_specs=[pl.BlockSpec((block, left.shape[1]), lambda i: (i, 0)) for left in lefts]
-        + [pl.BlockSpec(right.shape, lambda i: (0, 0)) for right in rights],
+        + [
+            pl.BlockSpec(piece.shape, lambda i: (0, 0), pipeline_mode=pl.Buffered(1)) for piece in flat
+        ],
         out_specs=pl.BlockSpec((block, columns), lambda i: (i, 0)),
         out_shape=jax.ShapeDtypeStruct((rows, columns), jnp.float32),
-        compiler_params=pltpu.CompilerParams(vmem_limit_bytes=40 * 2**20),
-        cost_estimate=pl.CostEstimate(
-            flops=2 * rows * columns * depth,
-            bytes_accessed=2 * (rows + columns) * depth + 4 * rows * columns,
-            transcendentals=0,
-        ),
-    )(*lefts, *rights)
+        compiler_params=pltpu.CompilerParams(vmem_limit_bytes=limit),
+        cost_estimate=tiny_cost(),
+    )(*lefts, *flat)
 
 
 def stack_rows(array, arrived):
@@ -425,14 +430,95 @@
     return array[array.shape[0] // 2 :]
 
 
+def tiny_cost():
+    return pl.CostEstimate(flops=1024, bytes_accessed=1024, transcendentals=0)
+
+
+def row_kernel(rows_ref, columns_ref, *refs):
+    out_ref, flipped = refs[-2:]
+
+    @pl.when(pl.program_id(0) == 0)
+    def _():
+        flipped[...] = rows_ref[...].T
+
+    block = out_ref.shape[0] // 2
+    for i in range(2):
+        part = slice(i * block, (i + 1) * block)
+        out = mul(flipped[part, :], columns_ref[...])
+        if len(refs) == 3:
+            out = out + refs[0][part, :].astype(jnp.float32)
+        out_ref[part, :] = out.astype(jnp.bfloat16)
+
+
+def half_product(rows, columns, side, *arrived):
+    depth, width = columns.shape
+    half = rows.shape[1] // 2
+    block = width // 4 if width >= 2048 else width // 2
+    return pl.pallas_call(
+        row_kernel,
+        grid=(width // block,),
+        in_specs=[
+            pl.BlockSpec((depth, half), lambda j: (0, side)),
+            pl.BlockSpec((depth, block), lambda j: (0, j)),
+        ]
+        + [pl.BlockSpec((half, block), lambda j: (0, j)) for _ in arrived],
+        out_specs=pl.BlockSpec((half, block), lambda j: (0, j)),
+        out_shape=jax.ShapeDtypeStruct((half, width), jnp.bfloat16),
+        scratch_shapes=[pltpu.VMEM((half, depth), jnp.bfloat16)],
+        compiler_params=pltpu.CompilerParams(vmem_limit_bytes=BIG),
+        cost_estimate=tiny_cost(),
+    )(rows, columns, *arrived)
+
+
 def away_rows(rows, columns):
-    half = rows.shape[1] // 2
-    return mul(rows[:, half:], columns, TN).astype(jnp.bfloat16)
+    return half_product(rows, columns, 1)
 
 
 def kept_rows(rows, columns, arrived):
-    half = rows.shape[1] // 2
-    return (mul(rows[:, :half], columns, TN) + arrived.astype(jnp.float32)).astype(jnp.bfloat16)
+    return half_product(rows, columns, 0, arrived)
+
+
+def two_part(rows, first_ref, second_ref):
+    middle = first_ref.shape[0]
+    return mul(rows[:, :middle], first_ref[...]) + mul(rows[:, middle:], second_ref[...])
+
+
+def up_kernel(rows_ref, first_ref, second_ref, active_ref, slope_ref):
+    rows = rows_ref.shape[0]
+    block = min(256, rows)
+    for i in range(rows // block):
+        part = slice(i * block, (i + 1) * block)
+        active, slope = gelu_both(two_part(rows_ref[part, :], first_ref, second_ref))
+        active_ref[part, :] = active.astype(jnp.bfloat16)
+        slope_ref[part, :] = slope.astype(jnp.bfloat16)
+
+
+def back_up_kernel(rows_ref, first_ref, second_ref, slope_ref, out_ref):
+    rows = rows_ref.shape[0]
+    block = min(256, rows)
+    for i in range(rows // block):
+        part = slice(i * block, (i + 1) * block)
+        out = two_part(rows_ref[part, :], first_ref, second_ref)
+        out_ref[part, :] = (out * slope_ref[part, :].astype(jnp.float32)).astype(jnp.bfloat16)
+
+
+def hidden_call(kernel, outputs, rows, weight, *others):
+    count, depth = rows.shape
+    width = weight[0].shape[1]
+    block = min(512, width)
+    shape = jax.ShapeDtypeStruct((count, width), jnp.bfloat16)
+    spec = pl.BlockSpec((count, block), lambda j: (0, j))
+    return pl.pallas_call(
+        kernel,
+        grid=(width // block,),
+        in_specs=[pl.BlockSpec((count, depth), lambda j: (0, 0))]
+        + [pl.BlockSpec((piece.shape[0], block), lambda j: (0, j)) for piece in weight]
+        + [spec for _ in others],
+        out_specs=[spec] * outputs,
+        out_shape=[shape] * outputs,
+        compiler_params=pltpu.CompilerParams(vmem_limit_bytes=BIG),
+        cost_estimate=tiny_cost(),
+    )(rows, *weight, *others)
 
 
 def fold_dp(array, size, mask):
@@ -449,9 +535,24 @@
     def put(self, **arrays):
         self.live.update(arrays)
 
-    def drop(self, *names):
+    def drop(self, **names):
         for name in names:
             del self.live[name]
+
+    def send(self, name, size, mask):
+        self.live[name + "_in"] = swap_dp(self.live[name], size, mask)
+
+    def merge(self, name):
+        self.live[name] = stack_rows(self.live[name], self.live.pop(name + "_in"))
+
+    def send_half(self, name, size, mask):
+        whole = self.live[name]
+        self.live[name], self.live[name + "_in"] = (
+            low_half(whole), swap_dp(high_half(whole), size, mask)
+        )
+
+    def add(self, name):
+        self.live[name] = add_low(self.live[name], self.live.pop(name + "_in"))
 
     def cut(self):
         names = list(self.live)
@@ -527,183 +628,206 @@
     def grow(array, mask):
         return stack_rows(array, swap_dp(array, size, mask))
 
-    def grow_params(array, mask):
-        return jnp.concatenate([array, swap_dp(array, size, mask)], axis=1)
-
     row_count, local_width = w_qkv.shape[1:]
     step = local_width // 2
     qkv_a, qkv_b = (
         w_qkv[:, :, p * step : (p + 1) * step].transpose(1, 0, 2).reshape(row_count, 3 * step)
         for p in range(2)
     )
+    params = jnp.stack([ln1_gain, ln1_bias, ln2_gain, ln2_bias], axis=1)
+    extra = 3 * step
+    qkv_a = jnp.concatenate([qkv_a, jnp.pad(params, ((0, 0), (0, 128 - 4)))], axis=1)
     s = Steps()
 
     ours, away = split(tokens)
-    tokens_arriving = swap_tensor(away)
+    arriving = swap_tensor(away)
     s.put(a=grow(qkv_a, far), b=grow(qkv_b, far))
-    s.put(par=grow_params(jnp.stack([ln1_gain, ln1_bias, ln2_gain, ln2_bias]), far))
-    s.put(o=w_out.T, u=w_up, d=w_down.T, ours=ours, order=block_order(size, width), d_out=d_out)
-    s.cut()
-    u_arriving = grow(s.u, far)
-    s.put(a=grow(s.a, near), b=grow(s.b, near), o=grow(s.o, far), par=grow_params(s.par, near))
-    s.put(arrived=tokens_arriving)
-    s.cut()
-    s.put(ax=swap_tensor(s.a), a=grow(s.a, 2), o=grow(s.o, near), par=grow_params(s.par, 2))
-    s.put(x16=join(s.ours, s.arrived, s.order), u=u_arriving)
-    s.drop("ours", "arrived")
-    s.cut()
-    u_arriving = grow(s.u, near)
-    d_arriving = grow(s.d, far)
-    s.put(a_own=grow(s.a, 1), b=grow(s.b, 2), ox=swap_tensor(s.o), par=grow_params(s.par, 1))
-    gain_one, bias_one, gain_two, bias_two = (
-        s.par[i : i + 1].astype(jnp.float32) for i in range(4)
-    )
+    s.put(o=w_out.T, u=w_up, d=w_down.T, ours=ours, d_out=d_out)
+    s.cut()
+    s.put(a=grow(s.a, near), b=grow(s.b, near))
+    s.cut()
+    u_far = swap_dp(s.u, size, far)
+    s.put(ay=grow(s.a, 2), o=grow(s.o, far))
+    s.cut()
+    ax = swap_tensor(s.a)
+    a_core = swap_dp(s.ay, size, 1)
+    s.put(b=grow(s.b, 2), o=grow(s.o, near), u=stack_rows(s.u, u_far))
+    s.put(a_own=stack_rows(s.ay[:, :extra], a_core[:, :extra]))
+    par = stack_rows(s.ay[:, extra:], a_core[:, extra:]).astype(jnp.float32).T
+    order = block_order(size, width)
+    s.put(x16=join(s.ours, arriving, order), ax=ax, order=order)
+    gain_one, bias_one, gain_two, bias_two = (par[i : i + 1] for i in range(4))
     normed, normal, inverse = norm_rows(s.x16.astype(jnp.float32), gain_one, bias_one)
     s.put(n1=normed.astype(jnp.bfloat16), normal1=normal, inverse1=inverse)
     s.put(gain_one=gain_one, gain_two=gain_two, bias_two=bias_two)
-    s.drop("a", "par")
-    s.cut()
-    b_arriving = swap_tensor(s.b)
-    s.put(b_own=grow(s.b, 1), ax=grow(s.ax, 2))
+    s.drop(a=0, ay=0, ours=0)
+    s.cut()
+    s.put(ox=swap_tensor(s.o), bx=swap_tensor(s.b))
+    s.send("o", size, 2)
+    s.send("u", size, near)
+    b_own = grow(s.b, 1)
+    s.put(ax=s.ax[:, :extra])
+    s.send("ax", size, 2)
     qkv = mul(s.n1, s.a_own).astype(jnp.bfloat16)
     mixed, lse = attend(qkv)
-    s.put(qkv0=qkv, mixed0=mixed, lse0=lse, u=u_arriving)
-    s.drop("b")
-    s.cut()
-    ux_arriving = swap_tensor(s.u)
-    s.put(a_oth=grow(s.ax, 1), o=grow(s.o, 2), ox=grow(s.ox, 2))
-    u_arriving = grow(s.u, 2)
-    qkv = mul(s.n1, s.b_own).astype(jnp.bfloat16)
+    s.put(qkv0=qkv, mixed0=mixed, lse0=lse)
+    qkv = mul(s.n1, b_own).astype(jnp.bfloat16)
     mixed, lse = attend(qkv)
-    s.put(qkv1=qkv, mixed1=mixed, lse1=lse, bx=b_arriving, d=d_arriving)
-    s.drop("ax")
-    s.cut()
-    d_arriving = grow(s.d, near)
-    s.put(b_oth=grow(s.bx, 1), o=grow(s.o, 1), ox=grow(s.ox, 1))
-    qkv = mul(s.n1, s.a_oth).astype(jnp.bfloat16)
+    s.put(qkv1=qkv, mixed1=mixed, lse1=lse, b_own=b_own)
+    s.drop(b=0)
+    s.cut()
+    s.merge("u")
+    s.put(ux=swap_tensor(s.u))
+    s.send("u", size, 2)
+    s.send("ox", size, 2)
+    s.send("d", size, far)
+    s.merge("o")
+    s.send("o", size, 1)
+    s.merge("ax")
+    a_oth, b_oth = grow(s.ax, 1), grow(s.bx, 1)
+    qkv = mul(s.n1, a_oth).astype(jnp.bfloat16)
     mixed, lse = attend(qkv)
-    s.put(qkv2=qkv, mixed2=mixed, lse2=lse, ux=ux_arriving, u=u_arriving, d=d_arriving)
-    s.drop("bx")
-    s.cut()
-    ux_arriving = grow(s.ux, 2)
-    dx_arriving = swap_tensor(s.d)
-    s.put(u_own=grow(s.u, 1))
-    qkv = mul(s.n1, s.b_oth).astype(jnp.bfloat16)
+    s.put(qkv2=qkv, mixed2=mixed, lse2=lse)
+    qkv = mul(s.n1, b_oth).astype(jnp.bfloat16)
     mixed, lse = attend(qkv)
-    s.put(qkv3=qkv, mixed3=mixed, lse3=lse)
-    s.drop("u")
-    s.cut()
+    s.put(qkv3=qkv, mixed3=mixed, lse3=lse, a_oth=a_oth, b_oth=b_oth)
+    s.drop(ax=0, bx=0)
+    s.cut()
+    ours, away = split(s.d_out)
+    s.put(arrived=swap_tensor(away), ours=ours)
+    s.send("ux", size, 2)
+    s.merge("d")
+    s.send("d", size, near)
+    s.merge("u")
+    s.merge("ox")
+    s.merge("o")
+    o_oth = grow(s.ox, 1)
+    u_own = s.u, swap_dp(s.u, size, 1)
     mixed = jnp.concatenate([s.mixed0, s.mixed1, s.mixed2, s.mixed3], axis=1)
-    out_all = jnp.concatenate([s.o, s.ox], axis=1)
+    out_all = jnp.concatenate([s.o, o_oth], axis=1)
     hidden = s.x16.astype(jnp.float32) + mul(mixed, out_all, NT)
     normed, normal, inverse = norm_rows(hidden, s.gain_two, s.bias_two)
-    s.put(mixed=mixed, out_all=out_all, hidden=hidden, n2=normed.astype(jnp.bfloat16))
-    s.put(normal2=normal, inverse2=inverse, ux=ux_arriving, dx=dx_arriving)
-    s.drop("o", "ox", "x16", "bias_two")
-    s.cut()
-    ours, away = split(s.d_out)
-    cot_arriving = swap_tensor(away)
-    d_arriving = grow(s.d, 2)
-    s.put(u_oth=grow(s.ux, 1), ours=ours)
-    active, slope = gelu_both(mul(s.n2, s.u_own))
-    s.put(active0=active.astype(jnp.bfloat16), slope0=slope.astype(jnp.bfloat16))
-    s.drop("d_out", "ux")
-    s.cut()
-    active, slope = gelu_both(mul(s.n2, s.u_oth))
-    s.put(active1=active.astype(jnp.bfloat16), slope1=slope.astype(jnp.bfloat16))
-    s.put(arrived=cot_arriving, d=d_arriving)
-    s.cut()
-    dx_arriving = grow(s.dx, 2)
-    s.put(d_own=grow(s.d, 1))
+    n2 = normed.astype(jnp.bfloat16)
+    active, slope = hidden_call(up_kernel, 2, n2, u_own)
+    s.put(active0=active, slope0=slope, u_own=u_own[0], u_own_b=u_own[1])
+    s.put(mixed=mixed, out_all=out_all, hidden=hidden, n2=n2, normal2=normal, inverse2=inverse)
+    s.drop(o=0, ox=0, x16=0, bias_two=0, u=0, d_out=0)
+    s.cut()
+    s.merge("d")
+    s.put(dx=swap_tensor(s.d))
+    s.send("d", size, 2)
+    s.merge("ux")
+    u_oth = s.ux, swap_dp(s.ux, size, 1)
     dy16 = join(s.ours, s.arrived, s.order)
-    s.put(dy16=dy16, down0=swap_dp(away_rows(dy16, s.active0), size, 1))
-    s.put(down1=swap_dp(away_rows(dy16, s.active1), size, 1))
-    s.drop("d", "ours", "arrived")
-    s.cut()
-    grad = mul(s.dy16, s.d_own) * s.slope0.astype(jnp.float32)
-    s.put(up_grad0=grad.astype(jnp.bfloat16), dx=dx_arriving)
-    s.put(down0=kept_rows(s.dy16, s.active0, s.down0), down1=kept_rows(s.dy16, s.active1, s.down1))
-    s.drop("slope0")
-    s.cut()
-    down_arriving = swap_tensor(s.down1)
-    d_oth = grow(s.dx, 1)
-    up0 = swap_dp(away_rows(s.n2, s.up_grad0), size, 1)
-    grad = (mul(s.dy16, d_oth) * s.slope1.astype(jnp.float32)).astype(jnp.bfloat16)
-    s.put(d_oth=d_oth, up_grad1=grad, up1=swap_dp(away_rows(s.n2, grad), size, 1))
+    down0 = swap_dp(away_rows(dy16, s.active0), size, 1)
+    active, slope = hidden_call(up_kernel, 2, s.n2, u_oth)
+    s.put(active1=active, slope1=slope, u_oth=u_oth[0], u_oth_b=u_oth[1], dy16=dy16)
+    down1 = swap_dp(away_rows(dy16, active), size, 1)
+    s.drop(ux=0, ours=0, arrived=0)
+    s.cut()
+    s.send("dx", size, 2)
+    s.merge("d")
+    d_own = s.d, swap_dp(s.d, size, 1)
+    s.put(down1=kept_rows(s.dy16, s.active1, down1), down0=kept_rows(s.dy16, s.active0, down0))
+    (grad,) = hidden_call(back_up_kernel, 1, s.dy16, d_own, s.slope0)
+    s.put(up_grad0=grad, d_own=d_own[0], d_own_b=d_own[1])
+    up0 = swap_dp(away_rows(s.n2, grad), size, 1)
+    s.drop(slope0=0, d=0)
+    s.cut()
+    s.put(down_h=high_half(s.down0), down_h_in=swap_tensor(high_half(s.down1)))
+    s.put(down0=low_half(s.down0), down1=low_half(s.down1))
+    s.merge("dx")
+    d_oth = s.dx, swap_dp(s.dx, size, 1)
     s.put(up0=kept_rows(s.n2, s.up_grad0, up0))
-    s.drop("dx", "down1", "slope1")
-    s.cut()
-    up0_arriving = fold_dp(s.up0, size, 2)
-    total = sum_products([s.active0, s.active1], [s.d_own, s.d_oth])
-    rows = reorder((s.hidden + total).astype(jnp.bfloat16), s.order)
+    (grad,) = hidden_call(back_up_kernel, 1, s.dy16, d_oth, s.slope1)
+    s.put(up_grad1=grad)
+    up1 = swap_dp(away_rows(s.n2, grad), size, 1)
+    s.put(block=sum_products([s.active0, s.active1], [(s.d_own, s.d_own_b), d_oth]))
+    s.drop(slope1=0, dx=0, active0=0, active1=0, d_own=0, d_own_b=0)
+    s.cut()
+    s.put(down0_in=swap_tensor(s.down1))
+    s.send_half("up0", size, 2)
+    s.put(up1=kept_rows(s.n2, s.up_grad1, up1))
+    rows = reorder((s.hidden + s.block).astype(jnp.bfloat16), s.order)
     ours, away = part(rows)
-    s.put(ours=ours, away=away, up1=kept_rows(s.n2, s.up_grad1, s.up1))
-    s.drop("active0", "active1", "d_own", "d_oth", "hidden", "n2", "up0")
-    s.cut()
-    up1_arriving = fold_dp(s.up1, size, 2)
-    s.put(grad_n2=sum_products([s.up_grad0, s.up_grad1], [s.u_own, s.u_oth]))
-    s.put(down0=add_low(s.down0, down_arriving))
-    s.drop("up_grad0", "up_grad1", "u_own", "u_oth", "up1")
-    s.cut()
-    block_arriving = swap_tensor(s.away)
+    s.put(ours=ours, away=away)
+    s.put(grad_n2=sum_products([s.up_grad0, s.up_grad1], [(s.u_own, s.u_own_b), (s.u_oth, s.u_oth_b)]))
+    s.drop(hidden=0, block=0, n2=0, down1=0, up_grad0=0, up_grad1=0, u_own=0, u_oth=0)
+    s.drop(u_own_b=0, u_oth_b=0)
+    s.cut()
+    s.put(block_arrived=swap_tensor(s.away))
+    s.send_half("up1", size, 2)
     grad_norm, gain_two_grad, bias_two_grad = norm_rows_grad(
         s.grad_n2, s.normal2, s.inverse2, s.gain_two
     )
     grad_hidden = s.dy16.astype(jnp.float32) + grad_norm
     low_hidden = grad_hidden.astype(jnp.bfloat16)
     s.put(gain_two_grad=gain_two_grad, bias_two_grad=bias_two_grad, grad_hidden=grad_hidden)
-    s.put(low_hidden=low_hidden, grad_mixed=mul(low_hidden, s.out_all).astype(jnp.bfloat16))
-    s.put(out0=swap_dp(away_rows(low_hidden, s.mixed[:, :local_width]), size, 1))
-    s.put(out1=swap_dp(away_rows(low_hidden, s.mixed[:, local_width:]), size, 1))
-    s.drop("grad_n2", "normal2", "inverse2", "gain_two", "out_all", "dy16", "away")
-    s.cut()
-    s.put(out0=kept_rows(s.low_hidden, s.mixed[:, :local_width], s.out0))
-    s.put(out1=kept_rows(s.low_hidden, s.mixed[:, local_width:], s.out1))
-    s.put(dqkv0=attend_grad(s.qkv0, s.grad_mixed[:, :step], s.mixed0, s.lse0))
-    s.put(up0=up0_arriving, up1=up1_arriving)
-    s.drop("low_hidden", "mixed", "qkv0", "mixed0", "lse0")
-    s.cut()
-    down_arriving = fold_dp(s.down0, size, 2)
-    out_arriving = swap_tensor(s.out1)
-    s.put(dqkv2=attend_grad(s.qkv2, s.grad_mixed[:, 2 * step : 3 * step], s.mixed2, s.lse2))
-    s.put(block_arrived=block_arriving)
-    s.drop("out1", "qkv2", "mixed2", "lse2", "down0")
-    s.cut()
-    up_arriving = swap_tensor(s.up1)
-    s.put(a0=swap_dp(away_rows(s.n1, s.dqkv0), size, 1))
-    s.put(a1=swap_dp(away_rows(s.n1, s.dqkv2), size, 1))
-    s.put(dqkv1=attend_grad(s.qkv1, s.grad_mixed[:, step : 2 * step], s.mixed1, s.lse1))
-    s.put(down0=down_arriving, out0=add_low(s.out0, out_arriving))
-    s.drop("qkv1", "mixed1", "lse1", "up1")
-    s.cut()
-    s.put(down0=fold_dp(s.down0, size, near), out0=fold_dp(s.out0, size, 2))
-    s.put(a0=kept_rows(s.n1, s.dqkv0, s.a0), a1=kept_rows(s.n1, s.dqkv2, s.a1))
-    s.put(dqkv3=attend_grad(s.qkv3, s.grad_mixed[:, 3 * step :], s.mixed3, s.lse3))
-    s.put(up0=add_low(s.up0, up_arriving))
-    s.drop("qkv3", "mixed3", "lse3", "grad_mixed")
-    s.cut()
+    grad_mixed = mul(low_hidden, s.out_all).astype(jnp.bfloat16)
+    s.put(low_hidden=low_hidden, grad_mixed=grad_mixed)
+    out0 = swap_dp(away_rows(low_hidden, s.mixed[:, :local_width]), size, 1)
+    out1 = swap_dp(away_rows(low_hidden, s.mixed[:, local_width:]), size, 1)
+    s.put(dqkv0=attend_grad(s.qkv0, grad_mixed[:, :step], s.mixed0, s.lse0))
+    s.drop(grad_n2=0, away=0, normal2=0, inverse2=0, gain_two=0, out_all=0)
+    s.drop(qkv0=0, mixed0=0, lse0=0)
+    s.cut()
+    s.add("up1")
+    s.put(up0_x=swap_tensor(s.up1))
+    s.add("down_h")
+    s.put(down0_y=swap_dp(s.down_h, size, 2))
+    s.put(out0=kept_rows(s.low_hidden, s.mixed[:, :local_width], out0))
+    s.put(out1=kept_rows(s.low_hidden, s.mixed[:, local_width:], out1))
+    a0 = swap_dp(away_rows(s.n1, s.dqkv0), size, 1)
+    dqkv2 = attend_grad(s.qkv2, s.grad_mixed[:, 2 * step : 3 * step], s.mixed2, s.lse2)
+    a1 = swap_dp(away_rows(s.n1, dqkv2), size, 1)
+    dqkv1 = attend_grad(s.qkv1, s.grad_mixed[:, step : 2 * step], s.mixed1, s.lse1)
+    s.put(dqkv1=dqkv1, dqkv2=dqkv2)
+    s.add("up0")
+    s.add("down0")
+    s.drop(low_hidden=0, dy16=0, mixed=0, qkv2=0, mixed2=0, lse2=0, up1=0, down_h=0)
+    s.drop(qkv1=0, mixed1=0, lse1=0)
+    s.cut()
+
+    def last_half(array):
+        return low_half(array), swap_dp(high_half(array), size, far)
+
+    def last_add(kept, arrived):
+        return kept.astype(jnp.float32) + arrived.astype(jnp.float32)
 
     def last_fold(array):
-        arrived = swap_dp(high_half(array), size, far)
-        return low_half(array).astype(jnp.float32) + arrived.astype(jnp.float32)
-
-    a_arriving = swap_tensor(s.a1)
-    s.put(b0=swap_dp(away_rows(s.n1, s.dqkv1), size, 1))
-    s.put(b1=swap_dp(away_rows(s.n1, s.dqkv3), size, 1))
-    s.put(up0=fold_dp(s.up0, size, near), out0=fold_dp(s.out0, size, near))
-    s.put(grad_down=last_fold(s.down0))
-    s.put(
-        grad_n1=sum_products(
-            [s.dqkv0, s.dqkv1, s.dqkv2, s.dqkv3], [s.a_own, s.b_own, s.a_oth, s.b_oth]
-        )
-    )
-    s.drop("dqkv0", "dqkv2", "a_own", "b_own", "a_oth", "b_oth", "a1", "down0")
-    s.cut()
-    b1 = kept_rows(s.n1, s.dqkv3, s.b1)
-    b_arriving = swap_tensor(b1)
-    s.put(a0=add_low(s.a0, a_arriving))
-    s.put(b0=kept_rows(s.n1, s.dqkv1, s.b0))
-    s.put(grad_up=last_fold(s.up0), grad_out=last_fold(s.out0))
+        return last_add(*last_half(array))
+
+    s.put(up0_in=s.up0_x, down0_in=s.down0_y)
+    s.add("up0")
+    s.add("down0")
+    s.send_half("up0", size, near)
+    s.send_half("down0", size, near)
+    s.send_half("out0", size, 2)
+    s.send_half("out1", size, 2)
+    a1 = kept_rows(s.n1, s.dqkv2, a1)
+    s.put(a0=kept_rows(s.n1, s.dqkv0, a0), a0_in=swap_tensor(a1))
+    b0 = swap_dp(away_rows(s.n1, s.dqkv1), size, 1)
+    dqkv3 = attend_grad(s.qkv3, s.grad_mixed[:, 3 * step :], s.mixed3, s.lse3)
+    b1 = swap_dp(away_rows(s.n1, dqkv3), size, 1)
+    s.put(dqkv3=dqkv3)
+    s.drop(qkv3=0, mixed3=0, lse3=0, grad_mixed=0, up0_x=0, down0_y=0)
+    s.cut()
+    for name in ("up0", "down0", "out0", "out1", "a0"):
+        s.add(name)
+    b1 = kept_rows(s.n1, s.dqkv3, b1)
+    s.put(b0=kept_rows(s.n1, s.dqkv1, b0), b1=b1)
+    s.cut()
+    s.put(b0_in=swap_tensor(s.b1))
+    s.send_half("up0", size, far)
+    s.send_half("down0", size, far)
+    grad_n1 = sum_products(
+        [s.dqkv0, s.dqkv1, s.dqkv2, s.dqkv3], [(s.a_own,), (s.b_own,), (s.a_oth,), (s.b_oth,)],
+        56 * 2**20,
+    )
+    s.put(grad_n1=grad_n1)
+    s.cut()
+    s.put(out0_in=swap_tensor(s.out1))
+    s.send_half("a0", size, 2)
     grad_norm, gain_one_grad, bias_one_grad = norm_rows_grad(
         s.grad_n1, s.normal1, s.inverse1, s.gain_one
     )
@@ -715,19 +839,39 @@
             [gain_one_grad, bias_one_grad, s.gain_two_grad, s.bias_two_grad], axis=0
         )
     )
-    s.put(block_out=place(s.ours, s.block_arrived), grad_down=s.grad_down.T)
-    s.drop("ours", "block_arrived", "b1", "up0", "out0", "dqkv1", "dqkv3", "n1", "grad_n1")
-    s.cut()
-    input_grad = place(s.input_ours, swap_tensor(s.input_away))
-    grad_a = last_fold(fold_dp(fold_dp(s.a0, size, 2), size, near))
-    grad_b = last_fold(fold_dp(fold_dp(add_low(s.b0, b_arriving), size, 2), size, near))
-    sums = s.sums
-    mask = 1
-    while mask < size:
-        middle = sums.shape[1] // 2
-        sums = sums[:, :middle] + swap_dp(sums[:, middle:], size, mask)
-        mask *= 2
-    sums = sums + swap_tensor(sums)
+    s.drop(grad_n1=0, dqkv0=0, dqkv1=0, dqkv2=0, dqkv3=0, a_own=0, b_own=0, a_oth=0, b_oth=0, out1=0, b1=0)
+    s.drop(n1=0, normal1=0, inverse1=0, gain_one=0, grad_hidden=0, order=0)
+    s.drop(gain_two_grad=0, bias_two_grad=0)
+    s.cut()
+
+    def fold_sums(array, mask):
+        middle = array.shape[1] // 2
+        return array[:, :middle] + swap_dp(array[:, middle:], size, mask)
+
+    for name in ("b0", "a0", "out0"):
+        s.add(name)
+    s.send_half("b0", size, 2)
+    s.send_half("a0", size, near)
+    s.send_half("out0", size, near)
+    most = s.input_away.shape[0] // 2
+    s.put(most=swap_tensor(s.input_away[:most]), rest=s.input_away[most:])
+    s.put(grad_up=last_add(s.up0, s.up0_in), grad_down=last_add(s.down0, s.down0_in))
+    s.put(sums=fold_sums(fold_sums(s.sums, 1), 2))
+    s.put(block_out=place(s.ours, s.block_arrived))
+    s.drop(ours=0, block_arrived=0, input_away=0, up0=0, down0=0, up0_in=0, down0_in=0)
+    s.cut()
+    for name in ("b0", "a0", "out0"):
+        s.add(name)
+    s.send_half("b0", size, near)
+    s.send_half("a0", size, far)
+    s.send_half("out0", size, far)
+    s.put(rest=swap_tensor(s.rest), sums=fold_sums(fold_sums(s.sums, near), far))
+    s.cut()
+    s.add("b0")
+    input_grad = place(s.input_ours, jnp.concatenate([s.most, s.rest], axis=0))
+    grad_a, grad_out = last_add(s.a0, s.a0_in), last_add(s.out0, s.out0_in)
+    grad_b = last_fold(s.b0)
+    sums = s.sums + swap_tensor(s.sums)
 
     return (
         s.block_out,
@@ -737,11 +881,11 @@
         jnp.concatenate(
             [g.reshape(row_count, 3, step).transpose(1, 0, 2) for g in (grad_a, grad_b)], axis=2
         ),
-        s.grad_out.T,
+        grad_out.T,
         sums[2],
         sums[3],
         s.grad_up,
-        s.grad_down,
+        s.grad_down.T,
     )
 
 

time: 532 us -> 475 us (0.89)
  Pallas kernels: 101 us -> 191 us
  matrix products: 108 us -> 25.7 us
  waiting for transfers between devices: 156 us -> 82.5 us
  starting transfers between devices: 81.5 us -> 72.2 us
  other arithmetic: 40.2 us -> 48.8 us
  local copies, waits for them, and re-layouts: 38.6 us -> 46.2 us
    pallas_call x3 -> x27, Pallas kernels: 34.9 us -> 125 us  [the longest x20 59.1 us: half_product(): pl.pallas_call(row_kernel, grid=(width // block,), in_specs=[pl.BlockSpec...]
    dot_general x34 -> x10, matrix products: 108 us -> 25.7 us  [mul(): lax.dot_general(left, right, dims, preferred_element_type=jnp.float32)]
    ppermute x63 -> x60, waiting for transfers between devices: 137 us -> 64.6 us  [swap_dp(): return lax.ppermute(array, 'dp', [(i, i ^ mask) for i in range(size)])]
    ppermute x63 -> x60, starting transfers between devices: 63.5 us -> 52.3 us  [swap_dp(): return lax.ppermute(array, 'dp', [(i, i ^ mask) for i in range(size)])]
    ppermute x15 -> x17, starting transfers between devices: 18 us -> 19.9 us  [swap_tensor(): return lax.ppermute(array, 'tensor', [(0, 1), (1, 0)])]
    ppermute x15 -> x17, waiting for transfers between devices: 18.9 us -> 17.9 us  [swap_tensor(): return lax.ppermute(array, 'tensor', [(0, 1), (1, 0)])]
    unnamed x140 -> x214, local copies, waits for them, and re-layouts: 24.3 us -> 23.3 us
  transfers between devices with their start and end apart: 78 -> 77, of which waited for: 31 -> 29; matrix products, arithmetic and copies ran while one was open for 28% -> 20% of each run, Pallas kernels for 19% -> 40%
where the time goes in v4:
time: 475 us; the launch traced here: 470 us
  Pallas kernels  191 us (40%)
  waiting for transfers between devices  82.5 us (17%)
  starting transfers between devices  72.2 us (15%)
  other arithmetic  48.8 us (10%)
  local copies, waits for them, and re-layouts  46.2 us (10%)
  matrix products  25.7 us (5%)
    ppermute x60, waiting for transfers between devices, swap_dp(): return lax.ppermute(array, 'dp', [(i, i ^ mask) for i in range(size)])  64.6 us
    pallas_call x20, Pallas kernels, half_product(): pl.pallas_call(row_kernel, grid=(width // block,), in_specs=[pl.BlockSpec...  59.1 us
    ppermute x60, starting transfers between devices, swap_dp(): return lax.ppermute(array, 'dp', [(i, i ^ mask) for i in range(size)])  52.3 us
    pallas_call x4, Pallas kernels, attend_grad(): pl.pallas_call(back_kernel, grid=(pairs,), in_specs=[pl.BlockSpec((length...  35.2 us
    pallas_call x3, Pallas kernels, sum_products(): pl.pallas_call(functools.partial(sum_kernel, len(lefts), pieces), grid=(r...  33.8 us
    pallas_call x4, Pallas kernels, hidden_call(): pl.pallas_call(kernel, grid=(width // block,), in_specs=[pl.BlockSpec((co...  32.3 us
    pallas_call x4, Pallas kernels, attend(): pl.pallas_call(fwd_kernel, grid=(pairs,), in_specs=[pl.BlockSpec((length,...  30.9 us
    dot_general x10, matrix products, mul(): lax.dot_general(left, right, dims, preferred_element_type=jnp.float32)  25.7 us
  transfers between devices with their start and end apart: 77, of which 29 were waited for; matrix products, arithmetic and copies ran while one was open for 20% of the time, Pallas kernels for 40%

profile of v4, /device:TPU:0, one launch (start us, length us, event | category | flops | bytes accessed | tf_op | source)
XLA Modules:
  0.0 469.9 jit_solution(983676464206086765)
XLA Ops:
  3.1 4.0 collective-permute-start
  7.2 6.5 %constant_dynamic-slice_fusion = (bf16[512,1,1024]{2,1,0:T(2,128)(2,1)S(1)}, bf16[512,1,1024]{2,1,0:T(2,128)(2,1)S(1)}) fusion(bf16[512,2,1024]{2,1,0:T(2,128)(2,1)} %param.10, s32[]{:T(128)S(6)} %select_n.120, s32[]{:T(128)S(6)} %select_n.118), kind=kLoop, calls=%fused_computation.197 | loop fusion | bytes 4194312 | tf_op jit(solution)/shard_map/jit(dynamic_index_in_dim)/dynamic_slice | solution.py:607
  20.4 5.8 %collective-permute-done.3 = bf16[128,768]{1,0:T(8,128)(2,1)S(1)} collective-permute-done((bf16[128,768]{1,0:T(8,128)(2,1)S(1)}, bf16[128,768]{1,0:T(8,128)(2,1)S(1)}, u32[]{:S(2)}, u32[]{:S(2)}) %collective-permute-start.3) | collective-permute-done | bytes 196640 | tf_op jit(solution)/shard_map/ppermute | solution.py:379
  26.3 3.1 collective-permute-done.2
  31.4 3.3 collective-permute-start.4
  37.3 3.8 collective-permute-done.5
  45.4 3.7 collective-permute-done.8
  71.2 7.7 %shard_map.177 = (bf16[1024,256]{1,0:T(8,128)(2,1)S(1)}, f32[2,8,1024]{2,1,0:T(8,128)S(1)}) custom-call(bf16[1024,768]{1,0:T(8,128)(2,1)S(1)} %convolution_convert_fusion.4.q_ref.k_ref.v_ref, bf16[1024,768]{1,0:T(8,128)(2,1)S(1)} %convolution_convert_fusion.4.q_ref.k_ref.v_ref, bf16[1024,768]{1,0:T(8,128)(2,1)S(1)} %convolution_convert_fusion.4.q_ref.k_ref.v_ref), custom_call_target="tpu_custom_call" | custom-call | flops 1024 | bytes 1024 | tf_op jit(solution)/shard_map/pallas_call | solution.py:281
  79.0 7.5 %shard_map.178 = (bf16[1024,256]{1,0:T(8,128)(2,1)S(1)}, f32[2,8,1024]{2,1,0:T(8,128)S(1)}) custom-call(bf16[1024,768]{1,0:T(8,128)(2,1)S(1)} %convolution_convert_fusion.3.q_ref.k_ref.v_ref, bf16[1024,768]{1,0:T(8,128)(2,1)S(1)} %convolution_convert_fusion.3.q_ref.k_ref.v_ref, bf16[1024,768]{1,0:T(8,128)(2,1)S(1)} %convolution_convert_fusion.3.q_ref.k_ref.v_ref), custom_call_target="tpu_custom_call" | custom-call | flops 1024 | bytes 1024 | tf_op jit(solution)/shard_map/pallas_call | solution.py:281
  100.3 7.9 %shard_map.180 = (bf16[1024,256]{1,0:T(8,128)(2,1)S(1)}, f32[2,8,1024]{2,1,0:T(8,128)S(1)}) custom-call(bf16[1024,768]{1,0:T(8,128)(2,1)S(1)} %convolution_convert_fusion.1.q_ref.k_ref.v_ref, bf16[1024,768]{1,0:T(8,128)(2,1)S(1)} %convolution_convert_fusion.1.q_ref.k_ref.v_ref, bf16[1024,768]{1,0:T(8,128)(2,1)S(1)} %convolution_convert_fusion.1.q_ref.k_ref.v_ref), custom_call_target="tpu_custom_call" | custom-call | flops 1024 | bytes 1024 | tf_op jit(solution)/shard_map/pallas_call | solution.py:281
  108.3 7.7 %shard_map.179 = (bf16[1024,256]{1,0:T(8,128)(2,1)S(1)}, f32[2,8,1024]{2,1,0:T(8,128)S(1)}) custom-call(bf16[1024,768]{1,0:T(8,128)(2,1)S(1)} %convolution_convert_fusion.2.q_ref.k_ref.v_ref, bf16[1024,768]{1,0:T(8,128)(2,1)S(1)} %convolution_convert_fusion.2.q_ref.k_ref.v_ref, bf16[1024,768]{1,0:T(8,128)(2,1)S(1)} %convolution_convert_fusion.2.q_ref.k_ref.v_ref), custom_call_target="tpu_custom_call" | custom-call | flops 1024 | bytes 1024 | tf_op jit(solution)/shard_map/pallas_call | solution.py:281
  116.8 3.5 collective-permute-done.20
  131.6 3.0 maximum_maximum_fusion
  134.6 3.5 fusion.76
  141.6 10.4 %shard_map.181 = (bf16[1024,2048]{1,0:T(8,128)(2,1)S(1)}, bf16[1024,2048]{1,0:T(8,128)(2,1)S(1)}) custom-call(bf16[1024,1024]{1,0:T(8,128)(2,1)S(1)} %get-tuple-element.754.rows_ref, bf16[512,2048]{1,0:T(8,128)(2,1)} %constant_dynamic-update-slice_fusion.17.first_ref.refs_2_, bf16[512,2048]{1,0:T(8,128)(2,1)} %collective-permute-done.29.second_ref.refs_3_), custom_call_target="tpu_custom_call" | custom-call | flops 1024 | bytes 1024 | tf_op jit(solution)/shard_map/pallas_call | solution.py:511
  160.4 3.8 shard_map.185
  164.2 9.8 %shard_map.182 = (bf16[1024,2048]{1,0:T(8,128)(2,1)S(1)}, bf16[1024,2048]{1,0:T(8,128)(2,1)S(1)}) custom-call(bf16[1024,1024]{1,0:T(8,128)(2,1)S(1)} %get-tuple-element.754.rows_ref, bf16[512,2048]{1,0:T(8,128)(2,1)S(1)} %constant_dynamic-update-slice_fusion.21.first_ref.refs_4_, bf16[512,2048]{1,0:T(8,128)(2,1)S(1)} %collective-permute-done.32.second_ref.refs_5_), custom_call_target="tpu_custom_call" | custom-call | flops 1024 | bytes 1024 | tf_op jit(solution)/shard_map/pallas_call | solution.py:511
  174.0 7.2 %collective-permute-done.30 = bf16[256,2048]{1,0:T(8,128)(2,1)S(1)} collective-permute-done((bf16[256,2048]{1,0:T(8,128)(2,1)S(1)}, bf16[256,2048]{1,0:T(8,128)(2,1)S(1)}, u32[]{:S(2)}, u32[]{:S(2)}) %collective-permute-start.30) | collective-permute-done | bytes 1048608 | tf_op jit(solution)/shard_map/ppermute | solution.py:383
  182.9 4.5 shard_map.183
  188.4 3.9 shard_map.186
  192.4 6.0 %shard_map.187.columns_ref.refs_0_ = bf16[1024,2048]{1,0:T(8,128)(2,1)S(1)} custom-call(bf16[1024,1024]{1,0:T(8,128)(2,1)S(1)} %fusion.38.rows_ref, bf16[512,2048]{1,0:T(8,128)(2,1)S(1)} %constant_dynamic-update-slice_fusion.23.first_ref.refs_2_, bf16[512,2048]{1,0:T(8,128)(2,1)S(1)} %collective-permute-done.36.second_ref.refs_3_, ...), custom_call_target="tpu_custom_call" | custom-call | flops 1024 | bytes 1024 | tf_op jit(solution)/shard_map/pallas_call | solution.py:511
  198.5 4.0 shard_map.184
  202.4 10.7 %collective-permute-done.33 = bf16[256,2048]{1,0:T(8,128)(2,1)} collective-permute-done((bf16[256,2048]{1,0:T(8,128)(2,1)S(1)}, bf16[256,2048]{1,0:T(8,128)(2,1)}, u32[]{:S(2)}, u32[]{:S(2)}) %collective-permute-start.33) | collective-permute-done | bytes 1048608 | tf_op jit(solution)/shard_map/ppermute | solution.py:379
  214.6 4.5 shard_map.188
  222.0 6.0 %shard_map.190.columns_ref.refs_1_ = bf16[1024,2048]{1,0:T(8,128)(2,1)S(1)} custom-call(bf16[1024,1024]{1,0:T(8,128)(2,1)S(1)} %fusion.38.rows_ref, bf16[512,2048]{1,0:T(8,128)(2,1)S(1)} %constant_dynamic-update-slice_fusion.25.first_ref.refs_4_, bf16[512,2048]{1,0:T(8,128)(2,1)S(1)} %collective-permute-done.39.second_ref.refs_5_, ...), custom_call_target="tpu_custom_call" | custom-call | flops 1024 | bytes 1024 | tf_op jit(solution)/shard_map/pallas_call | solution.py:511
  228.0 4.5 shard_map.192
  234.0 5.3 %shard_map.189 = bf16[512,2048]{1,0:T(8,128)(2,1)S(1)} custom-call(bf16[1024,1024]{1,0:T(8,128)(2,1)S(1)} %get-tuple-element.754.rows_ref, bf16[1024,2048]{1,0:T(8,128)(2,1)S(1)} %shard_map.187.columns_ref.refs_0_, bf16[512,2048]{1,0:T(8,128)(2,1)} %collective-permute-done.38.refs_0_), custom_call_target="tpu_custom_call" | custom-call | flops 1024 | bytes 1024 | tf_op jit(solution)/shard_map/pallas_call | solution.py:457
  240.7 9.9 %shard_map.191 = f32[1024,1024]{1,0:T(8,128)S(1)} custom-call(bf16[1024,2048]{1,0:T(8,128)(2,1)S(1)} %get-tuple-element.718.columns_ref.refs_0_, bf16[1024,2048]{1,0:T(8,128)(2,1)S(1)} %copy-done.11, bf16[512,2048]{1,0:T(8,128)(2,1)S(1)} %constant_dynamic-update-slice_fusion.23.first_ref.refs_2_, bf16[512,2048]{1,0:T(8,128)(2,1)S(1)} %copy-done.19, ...), custom_call_target="tpu_custom_call" | custom-call | flops 1024 | bytes 1024 | tf_op jit(solution)/shard_map/pallas_call | solution.py:407
  250.6 3.1 fusion.58
  255.3 12.0 %shard_map.194 = f32[1024,1024]{1,0:T(8,128)S(1)} custom-call(bf16[1024,2048]{1,0:T(8,128)(2,1)S(1)} %shard_map.187.columns_ref.refs_0_, bf16[1024,2048]{1,0:T(8,128)(2,1)S(1)} %shard_map.190.columns_ref.refs_1_, bf16[512,2048]{1,0:T(8,128)(2,1)} %constant_dynamic-update-slice_fusion.17.first_ref.refs_2_, ...), custom_call_target="tpu_custom_call" | custom-call | flops 1024 | bytes 1024 | tf_op jit(solution)/shard_map/pallas_call | solution.py:407
  273.1 5.0 %shard_map.193 = bf16[512,2048]{1,0:T(8,128)(2,1)S(1)} custom-call(bf16[1024,1024]{1,0:T(8,128)(2,1)S(1)} %get-tuple-element.754.rows_ref, bf16[1024,2048]{1,0:T(8,128)(2,1)S(1)} %shard_map.190.columns_ref.refs_1_, bf16[512,2048]{1,0:T(8,128)(2,1)} %collective-permute-done.42.refs_0_), custom_call_target="tpu_custom_call" | custom-call | flops 1024 | bytes 1024 | tf_op jit(solution)/shard_map/pallas_call | solution.py:457
  279.9 4.9 %multiply_reduce_fusion.2 = (f32[1024]{0:T(1024)S(1)}, f32[1024]{0:T(1024)S(1)}, f32[1024]{0:T(1024)S(1)}, f32[1024]{0:T(1024)S(1)}) fusion(f32[1024,1024]{1,0:T(8,128)} %get-tuple-element.793, f32[1024,1024]{1,0:T(8,128)} %copy-done.12, f32[1024]{0:T(1024)S(1)} %reduce.4), kind=kLoop, calls=%fused_computation.48 | loop fusion | flops 7335936 | bytes 8409088 | tf_op jit(solution)/shard_map/reduce_sum | solution.py:568
  297.4 8.7 %shard_map.195.columns_ref.refs_0_ = bf16[1024,768]{1,0:T(8,128)(2,1)S(1)} custom-call(bf16[1024,768]{1,0:T(8,128)(2,1)S(1)} %copy-done.7, bf16[1024,768]{1,0:T(8,128)(2,1)S(1)} %copy-done.7, bf16[1024,768]{1,0:T(8,128)(2,1)S(1)} %copy-done.7, bf16[1024,256]{1,0:T(8,128)(2,1)S(1)} %slice.300.do_ref, bf16[1024,256]{1,0:T(8,128)(2,1)S(1)} %copy-done.31, ...), custom_call_target="tpu_custom_call" | custom-call | flops 1024 | bytes 1024 | tf_op jit(solution)/shard_map/pallas_call | solution.py:358
  306.1 4.1 collective-permute-done.44
  313.9 9.1 %shard_map.201.columns_ref.refs_2_ = bf16[1024,768]{1,0:T(8,128)(2,1)S(1)} custom-call(bf16[1024,768]{1,0:T(8,128)(2,1)S(1)} %copy-done.9, bf16[1024,768]{1,0:T(8,128)(2,1)S(1)} %copy-done.9, bf16[1024,768]{1,0:T(8,128)(2,1)S(1)} %copy-done.9, bf16[1024,256]{1,0:T(8,128)(2,1)S(1)} %get-tuple-element.1026.do_ref, bf16[1024,256]{1,0:T(8,128)(2,1)S(1)} %copy-done.34, ...), custom_call_target="tpu_custom_call" | custom-call | flops 1024 | bytes 1024 | tf_op jit(solution)/shard_map/pallas_call | solution.py:358
  329.2 8.7 %shard_map.200.columns_ref.refs_1_ = bf16[1024,768]{1,0:T(8,128)(2,1)S(1)} custom-call(bf16[1024,768]{1,0:T(8,128)(2,1)S(1)} %copy-done.5, bf16[1024,768]{1,0:T(8,128)(2,1)S(1)} %copy-done.5, bf16[1024,768]{1,0:T(8,128)(2,1)S(1)} %copy-done.5, bf16[1024,256]{1,0:T(8,128)(2,1)S(1)} %get-tuple-element.1027.do_ref, bf16[1024,256]{1,0:T(8,128)(2,1)S(1)} %copy-done.28, ...), custom_call_target="tpu_custom_call" | custom-call | flops 1024 | bytes 1024 | tf_op jit(solution)/shard_map/pallas_call | solution.py:358
  352.3 8.7 %shard_map.206.columns_ref.refs_3_ = bf16[1024,768]{1,0:T(8,128)(2,1)S(1)} custom-call(bf16[1024,768]{1,0:T(8,128)(2,1)S(1)} %copy-done.3, bf16[1024,768]{1,0:T(8,128)(2,1)S(1)} %copy-done.3, bf16[1024,768]{1,0:T(8,128)(2,1)S(1)} %copy-done.3, bf16[1024,256]{1,0:T(8,128)(2,1)S(1)} %slice.255.do_ref, bf16[1024,256]{1,0:T(8,128)(2,1)S(1)} %copy-done.26, ...), custom_call_target="tpu_custom_call" | custom-call | flops 1024 | bytes 1024 | tf_op jit(solution)/shard_map/pallas_call | solution.py:358
  368.1 4.2 collective-permute-done.50
  379.9 3.4 collective-permute-start.59
  384.1 12.0 %shard_map.211 = f32[1024,1024]{1,0:T(8,128)} custom-call(bf16[1024,768]{1,0:T(8,128)(2,1)} %copy-done.14, bf16[1024,768]{1,0:T(8,128)(2,1)} %copy-done.16, bf16[1024,768]{1,0:T(8,128)(2,1)} %copy-done.15, bf16[1024,768]{1,0:T(8,128)(2,1)} %copy-done.17, bf16[1024,768]{1,0:T(8,128)(2,1)} %copy-done.48, bf16[1024,768]{1,0:T(8,128)(2,1)} %copy-done.55, ...), custom_call_target="tpu_custom_call" | custom-call | flops 1024 | bytes 1024 | tf_op jit(solution)/shard_map/pallas_call | solution.py:407
  396.2 4.3 collective-permute-done.59
  400.5 4.9 %collective-permute-done.60 = bf16[64,2048]{1,0:T(8,128)(2,1)S(1)} collective-permute-done((bf16[64,2048]{1,0:T(8,128)(2,1)S(1)}, bf16[64,2048]{1,0:T(8,128)(2,1)S(1)}, u32[]{:S(2)}, u32[]{:S(2)}) %collective-permute-start.60) | collective-permute-done | bytes 262176 | tf_op jit(solution)/shard_map/ppermute | solution.py:379
  406.6 4.9 %multiply_reduce_fusion = (f32[1024]{0:T(1024)S(1)}, f32[1024]{0:T(1024)S(1)}, f32[1024]{0:T(1024)S(1)}, f32[1024]{0:T(1024)S(1)}) fusion(f32[1024,1024]{1,0:T(8,128)} %shard_map.211, f32[1024,1024]{1,0:T(8,128)} %get-tuple-element.929, f32[1024]{0:T(1024)S(1)} %reduce.5), kind=kLoop, calls=%fused_computation.44 | loop fusion | flops 7335936 | bytes 8409088 | tf_op jit(solution)/shard_map/reduce_sum | solution.py:564
  413.5 5.4 %fusion.41 = bf16[1024,1024]{1,0:T(8,128)(2,1)S(1)} fusion(bf16[1024,1024]{1,0:T(8,128)(2,1)} %fusion.51, f32[1024,1024]{1,0:T(8,128)} %get-tuple-element.925, f32[1024,1024]{1,0:T(8,128)S(1)} %copy-done.42, f32[1024,1024]{1,0:T(8,128)S(1)} %copy-done.43, f32[1024]{0:T(1024)S(1)} %broadcast_multiply_fusion, f32[1024]{0:T(1024)S(1)} %broadcast_multiply_fusion.1, ...), kind=kOutput, calls=%fused_computation.86 | convolution fusion | flops 2155872256 | bytes 16793600 | tf_op jit(solution)/shard_map/dot_general | solution.py:241
  434.5 3.3 collective-permute-done.68
  443.2 3.5 collective-permute-done.69
  459.5 5.1 %copy.57 = bf16[512,2,1024]{2,1,0:T(2,128)(2,1)} copy(bf16[512,2,1024]{2,0,1:T(8,128)(2,1)} %pad_maximum_fusion.1) | data formatting | bytes 4194304
  464.5 3.5 copy.56
  (499 shorter events, 185.9 us)
Async XLA Ops:
  3.1 15.2 %collective-permute-start = (bf16[64,896]{1,0:T(8,128)(2,1)}, bf16[64,896]{1,0:T(8,128)(2,1)S(1)}, u32[]{:S(2)}, u32[]{:S(2)}) collective-permute-start(bf16[64,896]{1,0:T(8,128)(2,1)} %pad_maximum_fusion.15), channel_id=1, source_target_pairs={{0,16},{2,18},{4,20},{6,22},{8,24},{10,26},{12,28},{14,30},{16,0},... | collective-permute-start | bytes 344072 | tf_op jit(solution)/shard_map/ppermute | solution.py:379
  15.2 36.6 %collective-permute-start.10 = (bf16[512,1024]{1,0:T(8,128)(2,1)}, bf16[512,1024]{1,0:T(8,128)(2,1)}, u32[]{:S(2)}, u32[]{:S(2)}) collective-permute-start(bf16[512,1024]{1,0:T(8,128)(2,1)} %bitcast.67), channel_id=1, source_target_pairs={{0,1},{1,0},{2,3},{3,2},{4,5},{5,4},{6,7},{7,6},{8,9},{9,8},{10,11... | collective-permute-start | bytes 3145736 | tf_op jit(solution)/shard_map/ppermute | solution.py:383
  34.8 14.3 %collective-permute-start.8 = (bf16[64,2048]{1,0:T(8,128)(2,1)}, bf16[64,2048]{1,0:T(8,128)(2,1)S(1)}, u32[]{:S(2)}, u32[]{:S(2)}) collective-permute-start(bf16[64,2048]{1,0:T(8,128)(2,1)} %param.18), channel_id=1, source_target_pairs={{0,16},{2,18},{4,20},{6,22},{8,24},{10,26},{12,28},{14,30},{16,0},... | collective-permute-start | bytes 786440 | tf_op jit(solution)/shard_map/ppermute | solution.py:379
  42.3 14.3 %collective-permute-start.9 = (bf16[512,896]{1,0:T(8,128)(2,1)S(1)}, bf16[512,896]{1,0:T(8,128)(2,1)S(1)}, u32[]{:S(2)}, u32[]{:S(2)}) collective-permute-start(bf16[512,896]{1,0:T(8,128)(2,1)S(1)} %pad_maximum_fusion.3), channel_id=1, source_target_pairs={{0,2},{2,0},{4,6},{6,4},{8,10},{10,8},{12,14},{14,12},{16,18},{18,... | collective-permute-start | bytes 2752520 | tf_op jit(solution)/shard_map/ppermute | solution.py:379
  61.8 25.6 %collective-permute-start.13 = (bf16[512,768]{1,0:T(8,128)(2,1)S(1)}, bf16[512,768]{1,0:T(8,128)(2,1)S(1)}, u32[]{:S(2)}, u32[]{:S(2)}) collective-permute-start(bf16[512,768]{1,0:T(8,128)(2,1)S(1)} %pad_maximum_fusion.4), channel_id=1, source_target_pairs={{0,1},{1,0},{2,3},{3,2},{4,5},{5,4},{6,7},{7,6},{8,9},{9,8},{10,11... | collective-permute-start | bytes 2359304 | tf_op jit(solution)/shard_map/ppermute | solution.py:383
  63.5 23.8 %collective-permute-start.12 = (bf16[256,512]{1,0:T(8,128)(2,1)S(1)}, bf16[256,512]{1,0:T(8,128)(2,1)S(1)}, u32[]{:S(2)}, u32[]{:S(2)}) collective-permute-start(bf16[256,512]{1,0:T(8,128)(2,1)S(1)} %pad_maximum_fusion.11), channel_id=1, source_target_pairs={{0,1},{1,0},{2,3},{3,2},{4,5},{5,4},{6,7},{7,6},{8,9},{9,8},{10,11... | collective-permute-start | bytes 786440 | tf_op jit(solution)/shard_map/ppermute | solution.py:383
  63.8 23.5 %collective-permute-start.14 = (bf16[256,512]{1,0:T(8,128)(2,1)S(1)}, bf16[256,512]{1,0:T(8,128)(2,1)S(1)}, u32[]{:S(2)}, u32[]{:S(2)}) collective-permute-start(bf16[256,512]{1,0:T(8,128)(2,1)S(1)} %pad_maximum_fusion.11), channel_id=1, source_target_pairs={{0,4},{2,6},{4,0},{6,2},{8,12},{10,14},{12,8},{14,10},{16,20},{18,... | collective-permute-start | bytes 786440 | tf_op jit(solution)/shard_map/ppermute | solution.py:379
  64.3 23.0 %collective-permute-start.16 = (bf16[256,768]{1,0:T(8,128)(2,1)S(1)}, bf16[256,768]{1,0:T(8,128)(2,1)S(1)}, u32[]{:S(2)}, u32[]{:S(2)}) collective-permute-start(bf16[256,768]{1,0:T(8,128)(2,1)S(1)} %slice.229), channel_id=1, source_target_pairs={{0,4},{2,6},{4,0},{6,2},{8,12},{10,14},{12,8},{14,10},{16,20},{18,... | collective-permute-start | bytes 1179656 | tf_op jit(solution)/shard_map/ppermute | solution.py:379
  67.8 19.6 %collective-permute-start.15 = (bf16[128,2048]{1,0:T(8,128)(2,1)S(1)}, bf16[128,2048]{1,0:T(8,128)(2,1)S(1)}, u32[]{:S(2)}, u32[]{:S(2)}) collective-permute-start(bf16[128,2048]{1,0:T(8,128)(2,1)S(1)} %pad_maximum_fusion.6), channel_id=1, source_target_pairs={{0,8},{2,10},{4,12},{6,14},{8,0},{10,2},{12,4},{14,6},{16,24},{18,... | collective-permute-start | bytes 1572872 | tf_op jit(solution)/shard_map/ppermute | solution.py:379
  87.6 32.7 %collective-permute-start.18 = (bf16[256,2048]{1,0:T(8,128)(2,1)S(1)}, bf16[256,2048]{1,0:T(8,128)(2,1)S(1)}, u32[]{:S(2)}, u32[]{:S(2)}) collective-permute-start(bf16[256,2048]{1,0:T(8,128)(2,1)S(1)} %constant_dynamic-update-slice_fusion.4), channel_id=1, source_target_pairs={{0,1},{1,0},{2,3},{3,2},{4,5},{5,4},{6,7},{7,6},{8,9},{9,8},{10,11... | collective-permute-start | bytes 3145736 | tf_op jit(solution)/shard_map/ppermute | solution.py:383
  89.4 30.9 %collective-permute-start.19 = (bf16[256,2048]{1,0:T(8,128)(2,1)S(1)}, bf16[256,2048]{1,0:T(8,128)(2,1)S(1)}, u32[]{:S(2)}, u32[]{:S(2)}) collective-permute-start(bf16[256,2048]{1,0:T(8,128)(2,1)S(1)} %constant_dynamic-update-slice_fusion.4), channel_id=1, source_target_pairs={{0,4},{2,6},{4,0},{6,2},{8,12},{10,14},{12,8},{14,10},{16,20},{18,... | collective-permute-start | bytes 3145736 | tf_op jit(solution)/shard_map/ppermute | solution.py:379
  90.2 30.1 %collective-permute-start.22 = (bf16[512,512]{1,0:T(8,128)(2,1)S(1)}, bf16[512,512]{1,0:T(8,128)(2,1)S(1)}, u32[]{:S(2)}, u32[]{:S(2)}) collective-permute-start(bf16[512,512]{1,0:T(8,128)(2,1)S(1)} %constant_dynamic-update-slice_fusion.2), channel_id=1, source_target_pairs={{0,2},{2,0},{4,6},{6,4},{8,10},{10,8},{12,14},{14,12},{16,18},{18,... | collective-permute-start | bytes 1572872 | tf_op jit(solution)/shard_map/ppermute | solution.py:379
  90.8 29.5 %collective-permute-start.20 = (bf16[256,512]{1,0:T(8,128)(2,1)S(1)}, bf16[256,512]{1,0:T(8,128)(2,1)S(1)}, u32[]{:S(2)}, u32[]{:S(2)}) collective-permute-start(bf16[256,512]{1,0:T(8,128)(2,1)S(1)} %collective-permute-done.12), channel_id=1, source_target_pairs={{0,4},{2,6},{4,0},{6,2},{8,12},{10,14},{12,8},{14,10},{16,20},{18,... | collective-permute-start | bytes 786440 | tf_op jit(solution)/shard_map/ppermute | solution.py:379
  94.3 26.0 %collective-permute-start.21 = (bf16[64,2048]{1,0:T(8,128)(2,1)S(1)}, bf16[64,2048]{1,0:T(8,128)(2,1)S(1)}, u32[]{:S(2)}, u32[]{:S(2)}) collective-permute-start(bf16[64,2048]{1,0:T(8,128)(2,1)S(1)} %bitcast.77), channel_id=1, source_target_pairs={{0,16},{2,18},{4,20},{6,22},{8,24},{10,26},{12,28},{14,30},{16,0},... | collective-permute-start | bytes 786440 | tf_op jit(solution)/shard_map/ppermute | solution.py:379
  123.5 18.1 %collective-permute-start.29 = (bf16[512,2048]{1,0:T(8,128)(2,1)}, bf16[512,2048]{1,0:T(8,128)(2,1)}, u32[]{:S(2)}, u32[]{:S(2)}) collective-permute-start(bf16[512,2048]{1,0:T(8,128)(2,1)} %constant_dynamic-update-slice_fusion.17.first_ref.refs_2_), channel_id=1, source_target_pairs={{0,2},{2,0},{4,6},{6,4},{8,10},{10,8},{12,14},{14,12},{16,18},{18,... | collective-permute-start | bytes 6291464 | tf_op jit(solution)/shard_map/ppermute | solution.py:379
  129.2 25.1 %collective-permute-start.25 = (bf16[512,1024]{1,0:T(8,128)(2,1)S(1)}, bf16[512,1024]{1,0:T(8,128)(2,1)S(1)}, u32[]{:S(2)}, u32[]{:S(2)}) collective-permute-start(bf16[512,1024]{1,0:T(8,128)(2,1)S(1)} %get-tuple-element.1045), channel_id=1, source_target_pairs={{0,1},{1,0},{2,3},{3,2},{4,5},{5,4},{6,7},{7,6},{8,9},{9,8},{10,11... | collective-permute-start | bytes 3145736 | tf_op jit(solution)/shard_map/ppermute | solution.py:383
  129.7 22.3 %collective-permute-start.27 = (bf16[128,2048]{1,0:T(8,128)(2,1)S(1)}, bf16[128,2048]{1,0:T(8,128)(2,1)S(1)}, u32[]{:S(2)}, u32[]{:S(2)}) collective-permute-start(bf16[128,2048]{1,0:T(8,128)(2,1)S(1)} %constant_dynamic-update-slice_fusion.11), channel_id=1, source_target_pairs={{0,8},{2,10},{4,12},{6,14},{8,0},{10,2},{12,4},{14,6},{16,24},{18,... | collective-permute-start | bytes 1572872 | tf_op jit(solution)/shard_map/ppermute | solution.py:379
  130.7 24.5 %collective-permute-start.26 = (bf16[256,2048]{1,0:T(8,128)(2,1)S(1)}, bf16[256,2048]{1,0:T(8,128)(2,1)S(1)}, u32[]{:S(2)}, u32[]{:S(2)}) collective-permute-start(bf16[256,2048]{1,0:T(8,128)(2,1)S(1)} %copy-done.70), channel_id=1, source_target_pairs={{0,4},{2,6},{4,0},{6,2},{8,12},{10,14},{12,8},{14,10},{16,20},{18,... | collective-permute-start | bytes 3145736 | tf_op jit(solution)/shard_map/ppermute | solution.py:379
  155.6 25.6 %collective-permute-start.30 = (bf16[256,2048]{1,0:T(8,128)(2,1)S(1)}, bf16[256,2048]{1,0:T(8,128)(2,1)S(1)}, u32[]{:S(2)}, u32[]{:S(2)}) collective-permute-start(bf16[256,2048]{1,0:T(8,128)(2,1)S(1)} %constant_dynamic-update-slice_fusion.19), channel_id=1, source_target_pairs={{0,1},{1,0},{2,3},{3,2},{4,5},{5,4},{6,7},{7,6},{8,9},{9,8},{10,11... | collective-permute-start | bytes 3145736 | tf_op jit(solution)/shard_map/ppermute | solution.py:383
  157.3 25.3 %collective-permute-start.31 = (bf16[256,2048]{1,0:T(8,128)(2,1)S(1)}, bf16[256,2048]{1,0:T(8,128)(2,1)S(1)}, u32[]{:S(2)}, u32[]{:S(2)}) collective-permute-start(bf16[256,2048]{1,0:T(8,128)(2,1)S(1)} %constant_dynamic-update-slice_fusion.19), channel_id=1, source_target_pairs={{0,4},{2,6},{4,0},{6,2},{8,12},{10,14},{12,8},{14,10},{16,20},{18,... | collective-permute-start | bytes 3145736 | tf_op jit(solution)/shard_map/ppermute | solution.py:379
  164.2 24.3 %collective-permute-start.35 = (bf16[512,2048]{1,0:T(8,128)(2,1)S(1)}, bf16[512,2048]{1,0:T(8,128)(2,1)S(1)}, u32[]{:S(2)}, u32[]{:S(2)}) collective-permute-start(bf16[512,2048]{1,0:T(8,128)(2,1)S(1)} %shard_map.185), channel_id=1, source_target_pairs={{0,2},{2,0},{4,6},{6,4},{8,10},{10,8},{12,14},{14,12},{16,18},{18,... | collective-permute-start | bytes 6291464 | tf_op jit(solution)/shard_map/ppermute | solution.py:379
  187.9 25.2 %collective-permute-start.33 = (bf16[256,2048]{1,0:T(8,128)(2,1)S(1)}, bf16[256,2048]{1,0:T(8,128)(2,1)}, u32[]{:S(2)}, u32[]{:S(2)}) collective-permute-start(bf16[256,2048]{1,0:T(8,128)(2,1)S(1)} %copy-done.72), channel_id=1, source_target_pairs={{0,4},{2,6},{4,0},{6,2},{8,12},{10,14},{12,8},{14,10},{16,20},{18,... | collective-permute-start | bytes 3145736 | tf_op jit(solution)/shard_map/ppermute | solution.py:379
  219.1 14.9 %collective-permute-start.38 = (bf16[512,2048]{1,0:T(8,128)(2,1)}, bf16[512,2048]{1,0:T(8,128)(2,1)}, u32[]{:S(2)}, u32[]{:S(2)}) collective-permute-start(bf16[512,2048]{1,0:T(8,128)(2,1)} %shard_map.188), channel_id=1, source_target_pairs={{0,2},{2,0},{4,6},{6,4},{8,10},{10,8},{12,14},{14,12},{16,18},{18,... | collective-permute-start | bytes 6291464 | tf_op jit(solution)/shard_map/ppermute | solution.py:379
  221.0 29.6 %collective-permute-start.37 = (bf16[256,2048]{1,0:T(8,128)(2,1)}, bf16[256,2048]{1,0:T(8,128)(2,1)S(1)}, u32[]{:S(2)}, u32[]{:S(2)}) collective-permute-start(bf16[256,2048]{1,0:T(8,128)(2,1)} %get-tuple-element.1038), channel_id=1, source_target_pairs={{0,1},{1,0},{2,3},{3,2},{4,5},{5,4},{6,7},{7,6},{8,9},{9,8},{10,11... | collective-permute-start | bytes 3145736 | tf_op jit(solution)/shard_map/ppermute | solution.py:383
  232.5 40.6 %collective-permute-start.42 = (bf16[512,2048]{1,0:T(8,128)(2,1)}, bf16[512,2048]{1,0:T(8,128)(2,1)}, u32[]{:S(2)}, u32[]{:S(2)}) collective-permute-start(bf16[512,2048]{1,0:T(8,128)(2,1)} %shard_map.192), channel_id=1, source_target_pairs={{0,2},{2,0},{4,6},{6,4},{8,10},{10,8},{12,14},{14,12},{16,18},{18,... | collective-permute-start | bytes 6291464 | tf_op jit(solution)/shard_map/ppermute | solution.py:379
  253.7 25.8 %collective-permute-start.41 = (bf16[256,2048]{1,0:T(8,128)(2,1)S(1)}, bf16[256,2048]{1,0:T(8,128)(2,1)}, u32[]{:S(2)}, u32[]{:S(2)}) collective-permute-start(bf16[256,2048]{1,0:T(8,128)(2,1)S(1)} %get-tuple-element.1036), channel_id=1, source_target_pairs={{0,4},{2,6},{4,0},{6,2},{8,12},{10,14},{12,8},{14,10},{16,20},{18,... | collective-permute-start | bytes 3145736 | tf_op jit(solution)/shard_map/ppermute | solution.py:379
  254.2 25.4 %collective-permute-start.40 = (bf16[256,2048]{1,0:T(8,128)(2,1)S(1)}, bf16[256,2048]{1,0:T(8,128)(2,1)}, u32[]{:S(2)}, u32[]{:S(2)}) collective-permute-start(bf16[256,2048]{1,0:T(8,128)(2,1)S(1)} %copy-done.77), channel_id=1, source_target_pairs={{0,1},{1,0},{2,3},{3,2},{4,5},{5,4},{6,7},{7,6},{8,9},{9,8},{10,11... | collective-permute-start | bytes 3145736 | tf_op jit(solution)/shard_map/ppermute | solution.py:383
  285.1 25.1 %collective-permute-start.44 = (bf16[256,2048]{1,0:T(8,128)(2,1)S(1)}, bf16[256,2048]{1,0:T(8,128)(2,1)S(1)}, u32[]{:S(2)}, u32[]{:S(2)}) collective-permute-start(bf16[256,2048]{1,0:T(8,128)(2,1)S(1)} %get-tuple-element.1032), channel_id=1, source_target_pairs={{0,4},{2,6},{4,0},{6,2},{8,12},{10,14},{12,8},{14,10},{16,20},{18,... | collective-permute-start | bytes 3145736 | tf_op jit(solution)/shard_map/ppermute | solution.py:379
  286.7 24.3 %collective-permute-start.43 = (bf16[512,1024]{1,0:T(8,128)(2,1)S(1)}, bf16[512,1024]{1,0:T(8,128)(2,1)S(1)}, u32[]{:S(2)}, u32[]{:S(2)}) collective-permute-start(bf16[512,1024]{1,0:T(8,128)(2,1)S(1)} %copy-done.68), channel_id=1, source_target_pairs={{0,1},{1,0},{2,3},{3,2},{4,5},{5,4},{6,7},{7,6},{8,9},{9,8},{10,11... | collective-permute-start | bytes 3145736 | tf_op jit(solution)/shard_map/ppermute | solution.py:383
  295.3 42.8 %collective-permute-start.48 = (bf16[512,512]{1,0:T(8,128)(2,1)S(1)}, bf16[512,512]{1,0:T(8,128)(2,1)S(1)}, u32[]{:S(2)}, u32[]{:S(2)}) collective-permute-start(bf16[512,512]{1,0:T(8,128)(2,1)S(1)} %shard_map.198), channel_id=1, source_target_pairs={{0,2},{2,0},{4,6},{6,4},{8,10},{10,8},{12,14},{14,12},{16,18},{18,... | collective-permute-start | bytes 1572872 | tf_op jit(solution)/shard_map/ppermute | solution.py:379
  296.9 43.3 %collective-permute-start.47 = (bf16[512,512]{1,0:T(8,128)(2,1)S(1)}, bf16[512,512]{1,0:T(8,128)(2,1)S(1)}, u32[]{:S(2)}, u32[]{:S(2)}) collective-permute-start(bf16[512,512]{1,0:T(8,128)(2,1)S(1)} %shard_map.196), channel_id=1, source_target_pairs={{0,2},{2,0},{4,6},{6,4},{8,10},{10,8},{12,14},{14,12},{16,18},{18,... | collective-permute-start | bytes 1572872 | tf_op jit(solution)/shard_map/ppermute | solution.py:379
  311.5 31.8 %collective-permute-start.46 = (bf16[256,2048]{1,0:T(8,128)(2,1)S(1)}, bf16[256,2048]{1,0:T(8,128)(2,1)S(1)}, u32[]{:S(2)}, u32[]{:S(2)}) collective-permute-start(bf16[256,2048]{1,0:T(8,128)(2,1)S(1)} %add_convert_fusion.8), channel_id=1, source_target_pairs={{0,4},{2,6},{4,0},{6,2},{8,12},{10,14},{12,8},{14,10},{16,20},{18,... | collective-permute-start | bytes 3145736 | tf_op jit(solution)/shard_map/ppermute | solution.py:379
  312.9 30.4 %collective-permute-start.45 = (bf16[256,2048]{1,0:T(8,128)(2,1)S(1)}, bf16[256,2048]{1,0:T(8,128)(2,1)S(1)}, u32[]{:S(2)}, u32[]{:S(2)}) collective-permute-start(bf16[256,2048]{1,0:T(8,128)(2,1)S(1)} %add_convert_fusion.9), channel_id=1, source_target_pairs={{0,1},{1,0},{2,3},{3,2},{4,5},{5,4},{6,7},{7,6},{8,9},{9,8},{10,11... | collective-permute-start | bytes 3145736 | tf_op jit(solution)/shard_map/ppermute | solution.py:383
  325.2 18.1 %collective-permute-start.54 = (bf16[512,768]{1,0:T(8,128)(2,1)S(1)}, bf16[512,768]{1,0:T(8,128)(2,1)S(1)}, u32[]{:S(2)}, u32[]{:S(2)}) collective-permute-start(bf16[512,768]{1,0:T(8,128)(2,1)S(1)} %shard_map.204), channel_id=1, source_target_pairs={{0,2},{2,0},{4,6},{6,4},{8,10},{10,8},{12,14},{14,12},{16,18},{18,... | collective-permute-start | bytes 2359304 | tf_op jit(solution)/shard_map/ppermute | solution.py:379
  338.1 13.0 %collective-permute-start.53 = (bf16[512,768]{1,0:T(8,128)(2,1)S(1)}, bf16[512,768]{1,0:T(8,128)(2,1)S(1)}, u32[]{:S(2)}, u32[]{:S(2)}) collective-permute-start(bf16[512,768]{1,0:T(8,128)(2,1)S(1)} %shard_map.202), channel_id=1, source_target_pairs={{0,2},{2,0},{4,6},{6,4},{8,10},{10,8},{12,14},{14,12},{16,18},{18,... | collective-permute-start | bytes 2359304 | tf_op jit(solution)/shard_map/ppermute | solution.py:379
  345.6 26.7 %collective-permute-start.55 = (bf16[512,768]{1,0:T(8,128)(2,1)S(1)}, bf16[512,768]{1,0:T(8,128)(2,1)S(1)}, u32[]{:S(2)}, u32[]{:S(2)}) collective-permute-start(bf16[512,768]{1,0:T(8,128)(2,1)S(1)} %shard_map.205), channel_id=1, source_target_pairs={{0,1},{1,0},{2,3},{3,2},{4,5},{5,4},{6,7},{7,6},{8,9},{9,8},{10,11... | collective-permute-start | bytes 2359304 | tf_op jit(solution)/shard_map/ppermute | solution.py:383
  347.3 20.8 %collective-permute-start.49 = (bf16[128,2048]{1,0:T(8,128)(2,1)S(1)}, bf16[128,2048]{1,0:T(8,128)(2,1)S(1)}, u32[]{:S(2)}, u32[]{:S(2)}) collective-permute-start(bf16[128,2048]{1,0:T(8,128)(2,1)S(1)} %get-tuple-element.1054), channel_id=1, source_target_pairs={{0,8},{2,10},{4,12},{6,14},{8,0},{10,2},{12,4},{14,6},{16,24},{18,... | collective-permute-start | bytes 1572872 | tf_op jit(solution)/shard_map/ppermute | solution.py:379
  348.9 23.3 %collective-permute-start.50 = (bf16[128,2048]{1,0:T(8,128)(2,1)S(1)}, bf16[128,2048]{1,0:T(8,128)(2,1)S(1)}, u32[]{:S(2)}, u32[]{:S(2)}) collective-permute-start(bf16[128,2048]{1,0:T(8,128)(2,1)S(1)} %get-tuple-element.1052), channel_id=1, source_target_pairs={{0,8},{2,10},{4,12},{6,14},{8,0},{10,2},{12,4},{14,6},{16,24},{18,... | collective-permute-start | bytes 1572872 | tf_op jit(solution)/shard_map/ppermute | solution.py:379
  350.0 17.5 %collective-permute-start.51 = (bf16[256,512]{1,0:T(8,128)(2,1)S(1)}, bf16[256,512]{1,0:T(8,128)(2,1)S(1)}, u32[]{:S(2)}, u32[]{:S(2)}) collective-permute-start(bf16[256,512]{1,0:T(8,128)(2,1)S(1)} %get-tuple-element.1066), channel_id=1, source_target_pairs={{0,4},{2,6},{4,0},{6,2},{8,12},{10,14},{12,8},{14,10},{16,20},{18,... | collective-permute-start | bytes 786440 | tf_op jit(solution)/shard_map/ppermute | solution.py:379
  351.1 16.4 %collective-permute-start.52 = (bf16[256,512]{1,0:T(8,128)(2,1)S(1)}, bf16[256,512]{1,0:T(8,128)(2,1)S(1)}, u32[]{:S(2)}, u32[]{:S(2)}) collective-permute-start(bf16[256,512]{1,0:T(8,128)(2,1)S(1)} %get-tuple-element.1064), channel_id=1, source_target_pairs={{0,4},{2,6},{4,0},{6,2},{8,12},{10,14},{12,8},{14,10},{16,20},{18,... | collective-permute-start | bytes 786440 | tf_op jit(solution)/shard_map/ppermute | solution.py:379
  378.9 26.5 %collective-permute-start.58 = (bf16[512,768]{1,0:T(8,128)(2,1)S(1)}, bf16[512,768]{1,0:T(8,128)(2,1)S(1)}, u32[]{:S(2)}, u32[]{:S(2)}) collective-permute-start(bf16[512,768]{1,0:T(8,128)(2,1)S(1)} %shard_map.210), channel_id=1, source_target_pairs={{0,1},{1,0},{2,3},{3,2},{4,5},{5,4},{6,7},{7,6},{8,9},{9,8},{10,11... | collective-permute-start | bytes 2359304 | tf_op jit(solution)/shard_map/ppermute | solution.py:383
  379.9 20.6 %collective-permute-start.59 = (bf16[64,2048]{1,0:T(8,128)(2,1)S(1)}, bf16[64,2048]{1,0:T(8,128)(2,1)S(1)}, u32[]{:S(2)}, u32[]{:S(2)}) collective-permute-start(bf16[64,2048]{1,0:T(8,128)(2,1)S(1)} %get-tuple-element.1062), channel_id=1, source_target_pairs={{0,16},{2,18},{4,20},{6,22},{8,24},{10,26},{12,28},{14,30},{16,0},... | collective-permute-start | bytes 786440 | tf_op jit(solution)/shard_map/ppermute | solution.py:379
  384.1 21.3 %collective-permute-start.60 = (bf16[64,2048]{1,0:T(8,128)(2,1)S(1)}, bf16[64,2048]{1,0:T(8,128)(2,1)S(1)}, u32[]{:S(2)}, u32[]{:S(2)}) collective-permute-start(bf16[64,2048]{1,0:T(8,128)(2,1)S(1)} %get-tuple-element.1060), channel_id=1, source_target_pairs={{0,16},{2,18},{4,20},{6,22},{8,24},{10,26},{12,28},{14,30},{16,0},... | collective-permute-start | bytes 786440 | tf_op jit(solution)/shard_map/ppermute | solution.py:379
  423.4 14.4 %collective-permute-start.68 = (bf16[256,1024]{1,0:T(8,128)(2,1)S(1)}, bf16[256,1024]{1,0:T(8,128)(2,1)S(1)}, u32[]{:S(2)}, u32[]{:S(2)}) collective-permute-start(bf16[256,1024]{1,0:T(8,128)(2,1)S(1)} %get-tuple-element.1051), channel_id=1, source_target_pairs={{0,1},{1,0},{2,3},{3,2},{4,5},{5,4},{6,7},{7,6},{8,9},{9,8},{10,11... | collective-permute-start | bytes 1572872 | tf_op jit(solution)/shard_map/ppermute | solution.py:383
  438.0 15.1 %collective-permute-start.72 = (bf16[128,768]{1,0:T(8,128)(2,1)S(1)}, bf16[128,768]{1,0:T(8,128)(2,1)S(1)}, u32[]{:S(2)}, u32[]{:S(2)}) collective-permute-start(bf16[128,768]{1,0:T(8,128)(2,1)S(1)} %get-tuple-element.1073), channel_id=1, source_target_pairs={{0,8},{2,10},{4,12},{6,14},{8,0},{10,2},{12,4},{14,6},{16,24},{18,... | collective-permute-start | bytes 589832 | tf_op jit(solution)/shard_map/ppermute | solution.py:379
  440.1 12.9 %collective-permute-start.73 = (bf16[64,768]{1,0:T(8,128)(2,1)S(1)}, bf16[64,768]{1,0:T(8,128)(2,1)S(1)}, u32[]{:S(2)}, u32[]{:S(2)}) collective-permute-start(bf16[64,768]{1,0:T(8,128)(2,1)S(1)} %get-tuple-element.1079), channel_id=1, source_target_pairs={{0,16},{2,18},{4,20},{6,22},{8,24},{10,26},{12,28},{14,30},{16,0},... | collective-permute-start | bytes 294920 | tf_op jit(solution)/shard_map/ppermute | solution.py:379
  442.2 13.0 %collective-permute-start.71 = (bf16[256,1024]{1,0:T(8,128)(2,1)S(1)}, bf16[256,1024]{1,0:T(8,128)(2,1)S(1)}, u32[]{:S(2)}, u32[]{:S(2)}) collective-permute-start(bf16[256,1024]{1,0:T(8,128)(2,1)S(1)} %get-tuple-element.957), channel_id=1, source_target_pairs={{0,1},{1,0},{2,3},{3,2},{4,5},{5,4},{6,7},{7,6},{8,9},{9,8},{10,11... | collective-permute-start | bytes 1572872 | tf_op jit(solution)/shard_map/ppermute | solution.py:383
  455.2 13.3 %collective-permute-start.76 = (bf16[64,768]{1,0:T(8,128)(2,1)S(1)}, bf16[64,768]{1,0:T(8,128)(2,1)S(1)}, u32[]{:S(2)}, u32[]{:S(2)}) collective-permute-start(bf16[64,768]{1,0:T(8,128)(2,1)S(1)} %slice.322), channel_id=1, source_target_pairs={{0,16},{2,18},{4,20},{6,22},{8,24},{10,26},{12,28},{14,30},{16,0},... | collective-permute-start | bytes 294920 | tf_op jit(solution)/shard_map/ppermute | solution.py:379
  (125 other events, 1083.4 us)

commit v5 on v4

--- a/solution.py
+++ b/solution.py
@@ -231,7 +231,7 @@
 
 LOG2E = 1.4426950408889634
 BLOCK = 256
-BIG = 24 * 2**20
+BIG = 18 * 2**20
 NT = (((1,), (1,)), ((), ()))
 TN = (((0,), (0,)), ((), ()))
 NN = (((1,), (0,)), ((), ()))
@@ -730,7 +730,7 @@
     d_own = s.d, swap_dp(s.d, size, 1)
     s.put(down1=kept_rows(s.dy16, s.active1, down1), down0=kept_rows(s.dy16, s.active0, down0))
     (grad,) = hidden_call(back_up_kernel, 1, s.dy16, d_own, s.slope0)
-    s.put(up_grad0=grad, d_own=d_own[0], d_own_b=d_own[1])
+    s.put(up_grad0=grad, block=sum_products([s.active0], [d_own]))
     up0 = swap_dp(away_rows(s.n2, grad), size, 1)
     s.drop(slope0=0, d=0)
     s.cut()
@@ -742,17 +742,17 @@
     (grad,) = hidden_call(back_up_kernel, 1, s.dy16, d_oth, s.slope1)
     s.put(up_grad1=grad)
     up1 = swap_dp(away_rows(s.n2, grad), size, 1)
-    s.put(block=sum_products([s.active0, s.active1], [(s.d_own, s.d_own_b), d_oth]))
-    s.drop(slope1=0, dx=0, active0=0, active1=0, d_own=0, d_own_b=0)
+    s.put(block_oth=sum_products([s.active1], [d_oth]))
+    s.drop(slope1=0, dx=0, active0=0, active1=0)
     s.cut()
     s.put(down0_in=swap_tensor(s.down1))
     s.send_half("up0", size, 2)
     s.put(up1=kept_rows(s.n2, s.up_grad1, up1))
-    rows = reorder((s.hidden + s.block).astype(jnp.bfloat16), s.order)
+    rows = reorder((s.hidden + s.block + s.block_oth).astype(jnp.bfloat16), s.order)
     ours, away = part(rows)
     s.put(ours=ours, away=away)
     s.put(grad_n2=sum_products([s.up_grad0, s.up_grad1], [(s.u_own, s.u_own_b), (s.u_oth, s.u_oth_b)]))
-    s.drop(hidden=0, block=0, n2=0, down1=0, up_grad0=0, up_grad1=0, u_own=0, u_oth=0)
+    s.drop(hidden=0, block=0, block_oth=0, n2=0, down1=0, up_grad0=0, up_grad1=0, u_own=0, u_oth=0)
     s.drop(u_own_b=0, u_oth_b=0)
     s.cut()
     s.put(block_arrived=swap_tensor(s.away))
@@ -815,9 +815,9 @@
     for name in ("up0", "down0", "out0", "out1", "a0"):
         s.add(name)
     b1 = kept_rows(s.n1, s.dqkv3, b1)
-    s.put(b0=kept_rows(s.n1, s.dqkv1, b0), b1=b1)
-    s.cut()
-    s.put(b0_in=swap_tensor(s.b1))
+    s.put(b1=b1)
+    s.cut()
+    s.put(b0_in=swap_tensor(s.b1), b0=kept_rows(s.n1, s.dqkv1, b0))
     s.send_half("up0", size, far)
     s.send_half("down0", size, far)
     grad_n1 = sum_products(

time: 475 us -> 466 us (0.981)
  waiting for transfers between devices: 82.5 us -> 72.2 us
    ppermute x60, waiting for transfers between devices: 64.6 us -> 54.5 us  [swap_dp(): return lax.ppermute(array, 'dp', [(i, i ^ mask) for i in range(size)])]
    unnamed x214 -> x178, local copies, waits for them, and re-layouts: 23.3 us -> 22 us
    pallas_call x3 -> x4, Pallas kernels: 33.8 us -> 34.3 us  [sum_products(): pl.pallas_call(functools.partial(sum_kernel, len(lefts), pieces), grid=(r...]
  transfers between devices with their start and end apart: 77 -> 77, of which waited for: 29 -> 29; matrix products, arithmetic and copies ran while one was open for 20% -> 21% of each run, Pallas kernels for 40% -> 42%
where the time goes in v5:
time: 466 us; the launch traced here: 460 us
  Pallas kernels  192 us (41%)
  waiting for transfers between devices  72.2 us (15%)
  starting transfers between devices  71.9 us (15%)
  other arithmetic  52.7 us (11%)
  local copies, waits for them, and re-layouts  42.5 us (9%)
  matrix products  25.8 us (6%)
    pallas_call x20, Pallas kernels, half_product(): pl.pallas_call(row_kernel, grid=(width // block,), in_specs=[pl.BlockSpec...  58.6 us
    ppermute x60, waiting for transfers between devices, swap_dp(): return lax.ppermute(array, 'dp', [(i, i ^ mask) for i in range(size)])  54.5 us
    ppermute x60, starting transfers between devices, swap_dp(): return lax.ppermute(array, 'dp', [(i, i ^ mask) for i in range(size)])  53 us
    pallas_call x4, Pallas kernels, attend_grad(): pl.pallas_call(back_kernel, grid=(pairs,), in_specs=[pl.BlockSpec((length...  35.2 us
    pallas_call x4, Pallas kernels, sum_products(): pl.pallas_call(functools.partial(sum_kernel, len(lefts), pieces), grid=(r...  34.3 us
    pallas_call x4, Pallas kernels, hidden_call(): pl.pallas_call(kernel, grid=(width // block,), in_specs=[pl.BlockSpec((co...  33.1 us
    pallas_call x4, Pallas kernels, attend(): pl.pallas_call(fwd_kernel, grid=(pairs,), in_specs=[pl.BlockSpec((length,...  31 us
    dot_general x10, matrix products, mul(): lax.dot_general(left, right, dims, preferred_element_type=jnp.float32)  25.8 us
  transfers between devices with their start and end apart: 77, of which 29 were waited for; matrix products, arithmetic and copies ran while one was open for 21% of the time, Pallas kernels for 42%

profile of v5, /device:TPU:0, one launch (start us, length us, event | category | flops | bytes accessed | tf_op | source)
XLA Modules:
  0.0 460.3 jit_solution(7143391800554692666)
XLA Ops:
  3.1 4.0 collective-permute-start
  7.2 6.7 %constant_dynamic-slice_fusion = (bf16[512,1,1024]{2,1,0:T(2,128)(2,1)S(1)}, bf16[512,1,1024]{2,1,0:T(2,128)(2,1)S(1)}) fusion(bf16[512,2,1024]{2,1,0:T(2,128)(2,1)} %param.10, s32[]{:T(128)S(6)} %select_n.120, s32[]{:T(128)S(6)} %select_n.118), kind=kLoop, calls=%fused_computation.197 | loop fusion | bytes 4194312 | tf_op jit(solution)/shard_map/jit(dynamic_index_in_dim)/dynamic_slice | solution.py:607
  20.5 5.8 %collective-permute-done.3 = bf16[128,768]{1,0:T(8,128)(2,1)S(1)} collective-permute-done((bf16[128,768]{1,0:T(8,128)(2,1)S(1)}, bf16[128,768]{1,0:T(8,128)(2,1)S(1)}, u32[]{:S(2)}, u32[]{:S(2)}) %collective-permute-start.3) | collective-permute-done | bytes 196640 | tf_op jit(solution)/shard_map/ppermute | solution.py:379
  26.4 2.9 collective-permute-done.2
  31.6 3.2 collective-permute-start.4
  37.4 3.7 collective-permute-done.5
  45.3 3.8 collective-permute-done.8
  70.1 7.8 %shard_map.177 = (bf16[1024,256]{1,0:T(8,128)(2,1)S(1)}, f32[2,8,1024]{2,1,0:T(8,128)S(1)}) custom-call(bf16[1024,768]{1,0:T(8,128)(2,1)S(1)} %convolution_convert_fusion.4.q_ref.k_ref.v_ref, bf16[1024,768]{1,0:T(8,128)(2,1)S(1)} %convolution_convert_fusion.4.q_ref.k_ref.v_ref, bf16[1024,768]{1,0:T(8,128)(2,1)S(1)} %convolution_convert_fusion.4.q_ref.k_ref.v_ref), custom_call_target="tpu_custom_call" | custom-call | flops 1024 | bytes 1024 | tf_op jit(solution)/shard_map/pallas_call | solution.py:281
  77.9 7.5 %shard_map.178 = (bf16[1024,256]{1,0:T(8,128)(2,1)S(1)}, f32[2,8,1024]{2,1,0:T(8,128)S(1)}) custom-call(bf16[1024,768]{1,0:T(8,128)(2,1)S(1)} %convolution_convert_fusion.3.q_ref.k_ref.v_ref, bf16[1024,768]{1,0:T(8,128)(2,1)S(1)} %convolution_convert_fusion.3.q_ref.k_ref.v_ref, bf16[1024,768]{1,0:T(8,128)(2,1)S(1)} %convolution_convert_fusion.3.q_ref.k_ref.v_ref), custom_call_target="tpu_custom_call" | custom-call | flops 1024 | bytes 1024 | tf_op jit(solution)/shard_map/pallas_call | solution.py:281
  94.3 3.0 collective-permute-start.21
  99.2 8.0 %shard_map.180 = (bf16[1024,256]{1,0:T(8,128)(2,1)S(1)}, f32[2,8,1024]{2,1,0:T(8,128)S(1)}) custom-call(bf16[1024,768]{1,0:T(8,128)(2,1)S(1)} %convolution_convert_fusion.1.q_ref.k_ref.v_ref, bf16[1024,768]{1,0:T(8,128)(2,1)S(1)} %convolution_convert_fusion.1.q_ref.k_ref.v_ref, bf16[1024,768]{1,0:T(8,128)(2,1)S(1)} %convolution_convert_fusion.1.q_ref.k_ref.v_ref), custom_call_target="tpu_custom_call" | custom-call | flops 1024 | bytes 1024 | tf_op jit(solution)/shard_map/pallas_call | solution.py:281
  107.2 7.7 %shard_map.179 = (bf16[1024,256]{1,0:T(8,128)(2,1)S(1)}, f32[2,8,1024]{2,1,0:T(8,128)S(1)}) custom-call(bf16[1024,768]{1,0:T(8,128)(2,1)S(1)} %convolution_convert_fusion.2.q_ref.k_ref.v_ref, bf16[1024,768]{1,0:T(8,128)(2,1)S(1)} %convolution_convert_fusion.2.q_ref.k_ref.v_ref, bf16[1024,768]{1,0:T(8,128)(2,1)S(1)} %convolution_convert_fusion.2.q_ref.k_ref.v_ref), custom_call_target="tpu_custom_call" | custom-call | flops 1024 | bytes 1024 | tf_op jit(solution)/shard_map/pallas_call | solution.py:281
  115.7 4.5 collective-permute-done.20
  130.9 3.0 maximum_maximum_fusion
  133.9 3.5 fusion.76
  140.9 10.6 %shard_map.181 = (bf16[1024,2048]{1,0:T(8,128)(2,1)S(1)}, bf16[1024,2048]{1,0:T(8,128)(2,1)S(1)}) custom-call(bf16[1024,1024]{1,0:T(8,128)(2,1)S(1)} %get-tuple-element.751.rows_ref, bf16[512,2048]{1,0:T(8,128)(2,1)} %constant_dynamic-update-slice_fusion.17.first_ref.refs_2_, bf16[512,2048]{1,0:T(8,128)(2,1)} %collective-permute-done.29.second_ref.refs_3_), custom_call_target="tpu_custom_call" | custom-call | flops 1024 | bytes 1024 | tf_op jit(solution)/shard_map/pallas_call | solution.py:511
  159.7 3.8 shard_map.185
  163.6 10.0 %shard_map.182 = (bf16[1024,2048]{1,0:T(8,128)(2,1)S(1)}, bf16[1024,2048]{1,0:T(8,128)(2,1)S(1)}) custom-call(bf16[1024,1024]{1,0:T(8,128)(2,1)S(1)} %get-tuple-element.751.rows_ref, bf16[512,2048]{1,0:T(8,128)(2,1)S(1)} %constant_dynamic-update-slice_fusion.21.first_ref.refs_4_, bf16[512,2048]{1,0:T(8,128)(2,1)S(1)} %collective-permute-done.32.second_ref.refs_5_), custom_call_target="tpu_custom_call" | custom-call | flops 1024 | bytes 1024 | tf_op jit(solution)/shard_map/pallas_call | solution.py:511
  175.6 5.0 %collective-permute-done.30 = bf16[256,2048]{1,0:T(8,128)(2,1)S(1)} collective-permute-done((bf16[256,2048]{1,0:T(8,128)(2,1)S(1)}, bf16[256,2048]{1,0:T(8,128)(2,1)S(1)}, u32[]{:S(2)}, u32[]{:S(2)}) %collective-permute-start.30) | collective-permute-done | bytes 1048608 | tf_op jit(solution)/shard_map/ppermute | solution.py:383
  182.3 3.8 shard_map.183
  187.1 3.9 shard_map.186
  191.1 5.2 %shard_map.188 = f32[1024,1024]{1,0:T(8,128)S(1)} custom-call(bf16[1024,2048]{1,0:T(8,128)(2,1)S(1)} %get-tuple-element.660.columns_ref.refs_0_, bf16[512,2048]{1,0:T(8,128)(2,1)S(1)} %constant_dynamic-update-slice_fusion.23.first_ref.refs_1_, bf16[512,2048]{1,0:T(8,128)(2,1)S(1)} %collective-permute-done.36.second_ref.refs_2_), custom_call_target="tpu_custom_call" | custom-call | flops 1024 | bytes 1024 | tf_op jit(solution)/shard_map/pallas_call | solution.py:407
  196.2 6.2 %shard_map.187.columns_ref.refs_0_ = bf16[1024,2048]{1,0:T(8,128)(2,1)S(1)} custom-call(bf16[1024,1024]{1,0:T(8,128)(2,1)S(1)} %fusion.38.rows_ref, bf16[512,2048]{1,0:T(8,128)(2,1)S(1)} %constant_dynamic-update-slice_fusion.23.first_ref.refs_1_, bf16[512,2048]{1,0:T(8,128)(2,1)S(1)} %collective-permute-done.36.second_ref.refs_2_, ...), custom_call_target="tpu_custom_call" | custom-call | flops 1024 | bytes 1024 | tf_op jit(solution)/shard_map/pallas_call | solution.py:511
  202.5 4.0 shard_map.184
  206.5 5.3 %collective-permute-done.33 = bf16[256,2048]{1,0:T(8,128)(2,1)S(1)} collective-permute-done((bf16[256,2048]{1,0:T(8,128)(2,1)S(1)}, bf16[256,2048]{1,0:T(8,128)(2,1)S(1)}, u32[]{:S(2)}, u32[]{:S(2)}) %collective-permute-start.33) | collective-permute-done | bytes 1048608 | tf_op jit(solution)/shard_map/ppermute | solution.py:379
  212.0 4.5 shard_map.189
  219.2 6.2 %shard_map.191.columns_ref.refs_1_ = bf16[1024,2048]{1,0:T(8,128)(2,1)S(1)} custom-call(bf16[1024,1024]{1,0:T(8,128)(2,1)S(1)} %fusion.38.rows_ref, bf16[512,2048]{1,0:T(8,128)(2,1)S(1)} %constant_dynamic-update-slice_fusion.25.first_ref.refs_1_, bf16[512,2048]{1,0:T(8,128)(2,1)S(1)} %collective-permute-done.39.second_ref.refs_2_, ...), custom_call_target="tpu_custom_call" | custom-call | flops 1024 | bytes 1024 | tf_op jit(solution)/shard_map/pallas_call | solution.py:511
  225.4 4.6 shard_map.193
  231.9 5.1 %shard_map.192 = f32[1024,1024]{1,0:T(8,128)S(1)} custom-call(bf16[1024,2048]{1,0:T(8,128)(2,1)S(1)} %get-tuple-element.718.columns_ref.refs_0_, bf16[512,2048]{1,0:T(8,128)(2,1)S(1)} %constant_dynamic-update-slice_fusion.25.first_ref.refs_1_, bf16[512,2048]{1,0:T(8,128)(2,1)S(1)} %collective-permute-done.39.second_ref.refs_2_), custom_call_target="tpu_custom_call" | custom-call | flops 1024 | bytes 1024 | tf_op jit(solution)/shard_map/pallas_call | solution.py:407
  237.0 5.4 %shard_map.190 = bf16[512,2048]{1,0:T(8,128)(2,1)S(1)} custom-call(bf16[1024,1024]{1,0:T(8,128)(2,1)S(1)} %get-tuple-element.751.rows_ref, bf16[1024,2048]{1,0:T(8,128)(2,1)S(1)} %shard_map.187.columns_ref.refs_0_, bf16[512,2048]{1,0:T(8,128)(2,1)} %collective-permute-done.38.refs_0_), custom_call_target="tpu_custom_call" | custom-call | flops 1024 | bytes 1024 | tf_op jit(solution)/shard_map/pallas_call | solution.py:457
  245.6 12.1 %shard_map.195 = f32[1024,1024]{1,0:T(8,128)S(1)} custom-call(bf16[1024,2048]{1,0:T(8,128)(2,1)S(1)} %shard_map.187.columns_ref.refs_0_, bf16[1024,2048]{1,0:T(8,128)(2,1)S(1)} %shard_map.191.columns_ref.refs_1_, bf16[512,2048]{1,0:T(8,128)(2,1)} %constant_dynamic-update-slice_fusion.17.first_ref.refs_2_, ...), custom_call_target="tpu_custom_call" | custom-call | flops 1024 | bytes 1024 | tf_op jit(solution)/shard_map/pallas_call | solution.py:407
  263.5 5.0 %shard_map.194 = bf16[512,2048]{1,0:T(8,128)(2,1)S(1)} custom-call(bf16[1024,1024]{1,0:T(8,128)(2,1)S(1)} %get-tuple-element.751.rows_ref, bf16[1024,2048]{1,0:T(8,128)(2,1)S(1)} %shard_map.191.columns_ref.refs_1_, bf16[512,2048]{1,0:T(8,128)(2,1)} %collective-permute-done.42.refs_0_), custom_call_target="tpu_custom_call" | custom-call | flops 1024 | bytes 1024 | tf_op jit(solution)/shard_map/pallas_call | solution.py:457
  271.2 4.9 %multiply_reduce_fusion.2 = (f32[1024]{0:T(1024)S(1)}, f32[1024]{0:T(1024)S(1)}, f32[1024]{0:T(1024)S(1)}, f32[1024]{0:T(1024)S(1)}) fusion(f32[1024,1024]{1,0:T(8,128)} %get-tuple-element.791, f32[1024,1024]{1,0:T(8,128)} %copy-done.10, f32[1024]{0:T(1024)S(1)} %reduce.4), kind=kLoop, calls=%fused_computation.48 | loop fusion | flops 7335936 | bytes 8409088 | tf_op jit(solution)/shard_map/reduce_sum | solution.py:568
  288.8 8.7 %shard_map.196.columns_ref.refs_0_ = bf16[1024,768]{1,0:T(8,128)(2,1)S(1)} custom-call(bf16[1024,768]{1,0:T(8,128)(2,1)S(1)} %copy-done.7, bf16[1024,768]{1,0:T(8,128)(2,1)S(1)} %copy-done.7, bf16[1024,768]{1,0:T(8,128)(2,1)S(1)} %copy-done.7, bf16[1024,256]{1,0:T(8,128)(2,1)S(1)} %slice.300.do_ref, bf16[1024,256]{1,0:T(8,128)(2,1)S(1)} %copy-done.23, ...), custom_call_target="tpu_custom_call" | custom-call | flops 1024 | bytes 1024 | tf_op jit(solution)/shard_map/pallas_call | solution.py:358
  297.5 3.5 collective-permute-done.44
  304.7 8.7 %shard_map.202.columns_ref.refs_2_ = bf16[1024,768]{1,0:T(8,128)(2,1)S(1)} custom-call(bf16[1024,768]{1,0:T(8,128)(2,1)S(1)} %copy-done.9, bf16[1024,768]{1,0:T(8,128)(2,1)S(1)} %copy-done.9, bf16[1024,768]{1,0:T(8,128)(2,1)S(1)} %copy-done.9, bf16[1024,256]{1,0:T(8,128)(2,1)S(1)} %get-tuple-element.1024.do_ref, bf16[1024,256]{1,0:T(8,128)(2,1)S(1)} %copy-done.26, ...), custom_call_target="tpu_custom_call" | custom-call | flops 1024 | bytes 1024 | tf_op jit(solution)/shard_map/pallas_call | solution.py:358
  319.7 8.7 %shard_map.201.columns_ref.refs_1_ = bf16[1024,768]{1,0:T(8,128)(2,1)S(1)} custom-call(bf16[1024,768]{1,0:T(8,128)(2,1)S(1)} %copy-done.5, bf16[1024,768]{1,0:T(8,128)(2,1)S(1)} %copy-done.5, bf16[1024,768]{1,0:T(8,128)(2,1)S(1)} %copy-done.5, bf16[1024,256]{1,0:T(8,128)(2,1)S(1)} %get-tuple-element.1025.do_ref, ...), custom_call_target="tpu_custom_call" | custom-call | flops 1024 | bytes 1024 | tf_op jit(solution)/shard_map/pallas_call | solution.py:358
  342.6 9.1 %shard_map.207.columns_ref.refs_3_ = bf16[1024,768]{1,0:T(8,128)(2,1)S(1)} custom-call(bf16[1024,768]{1,0:T(8,128)(2,1)S(1)} %copy-done.3, bf16[1024,768]{1,0:T(8,128)(2,1)S(1)} %copy-done.3, bf16[1024,768]{1,0:T(8,128)(2,1)S(1)} %copy-done.3, bf16[1024,256]{1,0:T(8,128)(2,1)S(1)} %slice.255.do_ref, bf16[1024,256]{1,0:T(8,128)(2,1)S(1)} %get-tuple-element.858.o_ref, ...), custom_call_target="tpu_custom_call" | custom-call | flops 1024 | bytes 1024 | tf_op jit(solution)/shard_map/pallas_call | solution.py:358
  358.8 3.8 collective-permute-done.50
  369.5 3.6 collective-permute-start.59
  374.0 11.9 %shard_map.212 = f32[1024,1024]{1,0:T(8,128)} custom-call(bf16[1024,768]{1,0:T(8,128)(2,1)} %copy-done.12, bf16[1024,768]{1,0:T(8,128)(2,1)} %copy-done.14, bf16[1024,768]{1,0:T(8,128)(2,1)} %copy-done.13, bf16[1024,768]{1,0:T(8,128)(2,1)} %copy-done.16, bf16[1024,768]{1,0:T(8,128)(2,1)} %copy-done.36, bf16[1024,768]{1,0:T(8,128)(2,1)} %copy-done.42, ...), custom_call_target="tpu_custom_call" | custom-call | flops 1024 | bytes 1024 | tf_op jit(solution)/shard_map/pallas_call | solution.py:407
  390.8 4.6 %collective-permute-done.60 = bf16[64,2048]{1,0:T(8,128)(2,1)} collective-permute-done((bf16[64,2048]{1,0:T(8,128)(2,1)}, bf16[64,2048]{1,0:T(8,128)(2,1)}, u32[]{:S(2)}, u32[]{:S(2)}) %collective-permute-start.60) | collective-permute-done | bytes 262176 | tf_op jit(solution)/shard_map/ppermute | solution.py:379
  396.6 4.9 %multiply_reduce_fusion = (f32[1024]{0:T(1024)S(1)}, f32[1024]{0:T(1024)S(1)}, f32[1024]{0:T(1024)S(1)}, f32[1024]{0:T(1024)S(1)}) fusion(f32[1024,1024]{1,0:T(8,128)} %shard_map.212, f32[1024,1024]{1,0:T(8,128)} %get-tuple-element.927, f32[1024]{0:T(1024)S(1)} %reduce.5), kind=kLoop, calls=%fused_computation.44 | loop fusion | flops 7335936 | bytes 8409088 | tf_op jit(solution)/shard_map/reduce_sum | solution.py:564
  403.5 5.4 %fusion.41 = bf16[1024,1024]{1,0:T(8,128)(2,1)S(1)} fusion(bf16[1024,1024]{1,0:T(8,128)(2,1)} %fusion.51, f32[1024,1024]{1,0:T(8,128)} %get-tuple-element.923, f32[1024,1024]{1,0:T(8,128)S(1)} %copy-done.30, f32[1024,1024]{1,0:T(8,128)S(1)} %copy-done.31, f32[1024]{0:T(1024)S(1)} %broadcast_multiply_fusion, f32[1024]{0:T(1024)S(1)} %broadcast_multiply_fusion.1, ...), kind=kOutput, calls=%fused_computation.86 | convolution fusion | flops 2155872256 | bytes 16793600 | tf_op jit(solution)/shard_map/dot_general | solution.py:241
  424.2 3.3 collective-permute-done.68
  429.8 3.1 collective-permute-start.73
  449.9 5.1 %copy.57 = bf16[512,2,1024]{2,1,0:T(2,128)(2,1)} copy(bf16[512,2,1024]{2,0,1:T(8,128)(2,1)} %pad_maximum_fusion.1) | data formatting | bytes 4194304
  454.9 3.5 copy.56
  (464 shorter events, 188.5 us)
Async XLA Ops:
  3.1 15.3 %collective-permute-start = (bf16[64,896]{1,0:T(8,128)(2,1)}, bf16[64,896]{1,0:T(8,128)(2,1)S(1)}, u32[]{:S(2)}, u32[]{:S(2)}) collective-permute-start(bf16[64,896]{1,0:T(8,128)(2,1)} %pad_maximum_fusion.15), channel_id=1, source_target_pairs={{0,16},{2,18},{4,20},{6,22},{8,24},{10,26},{12,28},{14,30},{16,0},... | collective-permute-start | bytes 344072 | tf_op jit(solution)/shard_map/ppermute | solution.py:379
  15.3 36.5 %collective-permute-start.10 = (bf16[512,1024]{1,0:T(8,128)(2,1)}, bf16[512,1024]{1,0:T(8,128)(2,1)}, u32[]{:S(2)}, u32[]{:S(2)}) collective-permute-start(bf16[512,1024]{1,0:T(8,128)(2,1)} %bitcast.67), channel_id=1, source_target_pairs={{0,1},{1,0},{2,3},{3,2},{4,5},{5,4},{6,7},{7,6},{8,9},{9,8},{10,11... | collective-permute-start | bytes 3145736 | tf_op jit(solution)/shard_map/ppermute | solution.py:383
  34.8 14.3 %collective-permute-start.8 = (bf16[64,2048]{1,0:T(8,128)(2,1)}, bf16[64,2048]{1,0:T(8,128)(2,1)S(1)}, u32[]{:S(2)}, u32[]{:S(2)}) collective-permute-start(bf16[64,2048]{1,0:T(8,128)(2,1)} %param.18), channel_id=1, source_target_pairs={{0,16},{2,18},{4,20},{6,22},{8,24},{10,26},{12,28},{14,30},{16,0},... | collective-permute-start | bytes 786440 | tf_op jit(solution)/shard_map/ppermute | solution.py:379
  42.2 14.3 %collective-permute-start.9 = (bf16[512,896]{1,0:T(8,128)(2,1)S(1)}, bf16[512,896]{1,0:T(8,128)(2,1)S(1)}, u32[]{:S(2)}, u32[]{:S(2)}) collective-permute-start(bf16[512,896]{1,0:T(8,128)(2,1)S(1)} %pad_maximum_fusion.3), channel_id=1, source_target_pairs={{0,2},{2,0},{4,6},{6,4},{8,10},{10,8},{12,14},{14,12},{16,18},{18,... | collective-permute-start | bytes 2752520 | tf_op jit(solution)/shard_map/ppermute | solution.py:379
  61.8 25.6 %collective-permute-start.13 = (bf16[512,768]{1,0:T(8,128)(2,1)S(1)}, bf16[512,768]{1,0:T(8,128)(2,1)S(1)}, u32[]{:S(2)}, u32[]{:S(2)}) collective-permute-start(bf16[512,768]{1,0:T(8,128)(2,1)S(1)} %pad_maximum_fusion.4), channel_id=1, source_target_pairs={{0,1},{1,0},{2,3},{3,2},{4,5},{5,4},{6,7},{7,6},{8,9},{9,8},{10,11... | collective-permute-start | bytes 2359304 | tf_op jit(solution)/shard_map/ppermute | solution.py:383
  63.5 23.8 %collective-permute-start.12 = (bf16[256,512]{1,0:T(8,128)(2,1)S(1)}, bf16[256,512]{1,0:T(8,128)(2,1)S(1)}, u32[]{:S(2)}, u32[]{:S(2)}) collective-permute-start(bf16[256,512]{1,0:T(8,128)(2,1)S(1)} %pad_maximum_fusion.11), channel_id=1, source_target_pairs={{0,1},{1,0},{2,3},{3,2},{4,5},{5,4},{6,7},{7,6},{8,9},{9,8},{10,11... | collective-permute-start | bytes 786440 | tf_op jit(solution)/shard_map/ppermute | solution.py:383
  63.8 23.5 %collective-permute-start.14 = (bf16[256,512]{1,0:T(8,128)(2,1)S(1)}, bf16[256,512]{1,0:T(8,128)(2,1)S(1)}, u32[]{:S(2)}, u32[]{:S(2)}) collective-permute-start(bf16[256,512]{1,0:T(8,128)(2,1)S(1)} %pad_maximum_fusion.11), channel_id=1, source_target_pairs={{0,4},{2,6},{4,0},{6,2},{8,12},{10,14},{12,8},{14,10},{16,20},{18,... | collective-permute-start | bytes 786440 | tf_op jit(solution)/shard_map/ppermute | solution.py:379
  64.3 23.0 %collective-permute-start.16 = (bf16[256,768]{1,0:T(8,128)(2,1)S(1)}, bf16[256,768]{1,0:T(8,128)(2,1)S(1)}, u32[]{:S(2)}, u32[]{:S(2)}) collective-permute-start(bf16[256,768]{1,0:T(8,128)(2,1)S(1)} %slice.229), channel_id=1, source_target_pairs={{0,4},{2,6},{4,0},{6,2},{8,12},{10,14},{12,8},{14,10},{16,20},{18,... | collective-permute-start | bytes 1179656 | tf_op jit(solution)/shard_map/ppermute | solution.py:379
  67.8 19.6 %collective-permute-start.15 = (bf16[128,2048]{1,0:T(8,128)(2,1)S(1)}, bf16[128,2048]{1,0:T(8,128)(2,1)S(1)}, u32[]{:S(2)}, u32[]{:S(2)}) collective-permute-start(bf16[128,2048]{1,0:T(8,128)(2,1)S(1)} %pad_maximum_fusion.6), channel_id=1, source_target_pairs={{0,8},{2,10},{4,12},{6,14},{8,0},{10,2},{12,4},{14,6},{16,24},{18,... | collective-permute-start | bytes 1572872 | tf_op jit(solution)/shard_map/ppermute | solution.py:379
  87.6 32.7 %collective-permute-start.18 = (bf16[256,2048]{1,0:T(8,128)(2,1)S(1)}, bf16[256,2048]{1,0:T(8,128)(2,1)S(1)}, u32[]{:S(2)}, u32[]{:S(2)}) collective-permute-start(bf16[256,2048]{1,0:T(8,128)(2,1)S(1)} %constant_dynamic-update-slice_fusion.4), channel_id=1, source_target_pairs={{0,1},{1,0},{2,3},{3,2},{4,5},{5,4},{6,7},{7,6},{8,9},{9,8},{10,11... | collective-permute-start | bytes 3145736 | tf_op jit(solution)/shard_map/ppermute | solution.py:383
  89.4 30.9 %collective-permute-start.19 = (bf16[256,2048]{1,0:T(8,128)(2,1)S(1)}, bf16[256,2048]{1,0:T(8,128)(2,1)S(1)}, u32[]{:S(2)}, u32[]{:S(2)}) collective-permute-start(bf16[256,2048]{1,0:T(8,128)(2,1)S(1)} %constant_dynamic-update-slice_fusion.4), channel_id=1, source_target_pairs={{0,4},{2,6},{4,0},{6,2},{8,12},{10,14},{12,8},{14,10},{16,20},{18,... | collective-permute-start | bytes 3145736 | tf_op jit(solution)/shard_map/ppermute | solution.py:379
  90.2 30.1 %collective-permute-start.22 = (bf16[512,512]{1,0:T(8,128)(2,1)S(1)}, bf16[512,512]{1,0:T(8,128)(2,1)S(1)}, u32[]{:S(2)}, u32[]{:S(2)}) collective-permute-start(bf16[512,512]{1,0:T(8,128)(2,1)S(1)} %constant_dynamic-update-slice_fusion.2), channel_id=1, source_target_pairs={{0,2},{2,0},{4,6},{6,4},{8,10},{10,8},{12,14},{14,12},{16,18},{18,... | collective-permute-start | bytes 1572872 | tf_op jit(solution)/shard_map/ppermute | solution.py:379
  90.8 29.5 %collective-permute-start.20 = (bf16[256,512]{1,0:T(8,128)(2,1)S(1)}, bf16[256,512]{1,0:T(8,128)(2,1)S(1)}, u32[]{:S(2)}, u32[]{:S(2)}) collective-permute-start(bf16[256,512]{1,0:T(8,128)(2,1)S(1)} %collective-permute-done.12), channel_id=1, source_target_pairs={{0,4},{2,6},{4,0},{6,2},{8,12},{10,14},{12,8},{14,10},{16,20},{18,... | collective-permute-start | bytes 786440 | tf_op jit(solution)/shard_map/ppermute | solution.py:379
  94.3 26.0 %collective-permute-start.21 = (bf16[64,2048]{1,0:T(8,128)(2,1)S(1)}, bf16[64,2048]{1,0:T(8,128)(2,1)S(1)}, u32[]{:S(2)}, u32[]{:S(2)}) collective-permute-start(bf16[64,2048]{1,0:T(8,128)(2,1)S(1)} %bitcast.77), channel_id=1, source_target_pairs={{0,16},{2,18},{4,20},{6,22},{8,24},{10,26},{12,28},{14,30},{16,0},... | collective-permute-start | bytes 786440 | tf_op jit(solution)/shard_map/ppermute | solution.py:379
  123.4 17.5 %collective-permute-start.29 = (bf16[512,2048]{1,0:T(8,128)(2,1)}, bf16[512,2048]{1,0:T(8,128)(2,1)}, u32[]{:S(2)}, u32[]{:S(2)}) collective-permute-start(bf16[512,2048]{1,0:T(8,128)(2,1)} %constant_dynamic-update-slice_fusion.17.first_ref.refs_2_), channel_id=1, source_target_pairs={{0,2},{2,0},{4,6},{6,4},{8,10},{10,8},{12,14},{14,12},{16,18},{18,... | collective-permute-start | bytes 6291464 | tf_op jit(solution)/shard_map/ppermute | solution.py:379
  129.1 25.1 %collective-permute-start.25 = (bf16[512,1024]{1,0:T(8,128)(2,1)S(1)}, bf16[512,1024]{1,0:T(8,128)(2,1)S(1)}, u32[]{:S(2)}, u32[]{:S(2)}) collective-permute-start(bf16[512,1024]{1,0:T(8,128)(2,1)S(1)} %get-tuple-element.1043), channel_id=1, source_target_pairs={{0,1},{1,0},{2,3},{3,2},{4,5},{5,4},{6,7},{7,6},{8,9},{9,8},{10,11... | collective-permute-start | bytes 3145736 | tf_op jit(solution)/shard_map/ppermute | solution.py:383
  129.6 21.9 %collective-permute-start.27 = (bf16[128,2048]{1,0:T(8,128)(2,1)S(1)}, bf16[128,2048]{1,0:T(8,128)(2,1)S(1)}, u32[]{:S(2)}, u32[]{:S(2)}) collective-permute-start(bf16[128,2048]{1,0:T(8,128)(2,1)S(1)} %constant_dynamic-update-slice_fusion.11), channel_id=1, source_target_pairs={{0,8},{2,10},{4,12},{6,14},{8,0},{10,2},{12,4},{14,6},{16,24},{18,... | collective-permute-start | bytes 1572872 | tf_op jit(solution)/shard_map/ppermute | solution.py:379
  130.0 24.5 %collective-permute-start.26 = (bf16[256,2048]{1,0:T(8,128)(2,1)S(1)}, bf16[256,2048]{1,0:T(8,128)(2,1)S(1)}, u32[]{:S(2)}, u32[]{:S(2)}) collective-permute-start(bf16[256,2048]{1,0:T(8,128)(2,1)S(1)} %copy-done.58), channel_id=1, source_target_pairs={{0,4},{2,6},{4,0},{6,2},{8,12},{10,14},{12,8},{14,10},{16,20},{18,... | collective-permute-start | bytes 3145736 | tf_op jit(solution)/shard_map/ppermute | solution.py:379
  155.0 25.6 %collective-permute-start.30 = (bf16[256,2048]{1,0:T(8,128)(2,1)S(1)}, bf16[256,2048]{1,0:T(8,128)(2,1)S(1)}, u32[]{:S(2)}, u32[]{:S(2)}) collective-permute-start(bf16[256,2048]{1,0:T(8,128)(2,1)S(1)} %constant_dynamic-update-slice_fusion.19), channel_id=1, source_target_pairs={{0,1},{1,0},{2,3},{3,2},{4,5},{5,4},{6,7},{7,6},{8,9},{9,8},{10,11... | collective-permute-start | bytes 3145736 | tf_op jit(solution)/shard_map/ppermute | solution.py:383
  156.7 25.3 %collective-permute-start.31 = (bf16[256,2048]{1,0:T(8,128)(2,1)S(1)}, bf16[256,2048]{1,0:T(8,128)(2,1)S(1)}, u32[]{:S(2)}, u32[]{:S(2)}) collective-permute-start(bf16[256,2048]{1,0:T(8,128)(2,1)S(1)} %constant_dynamic-update-slice_fusion.19), channel_id=1, source_target_pairs={{0,4},{2,6},{4,0},{6,2},{8,12},{10,14},{12,8},{14,10},{16,20},{18,... | collective-permute-start | bytes 3145736 | tf_op jit(solution)/shard_map/ppermute | solution.py:379
  163.5 23.6 %collective-permute-start.35 = (bf16[512,2048]{1,0:T(8,128)(2,1)S(1)}, bf16[512,2048]{1,0:T(8,128)(2,1)S(1)}, u32[]{:S(2)}, u32[]{:S(2)}) collective-permute-start(bf16[512,2048]{1,0:T(8,128)(2,1)S(1)} %shard_map.185), channel_id=1, source_target_pairs={{0,2},{2,0},{4,6},{6,4},{8,10},{10,8},{12,14},{14,12},{16,18},{18,... | collective-permute-start | bytes 6291464 | tf_op jit(solution)/shard_map/ppermute | solution.py:379
  186.1 16.4 %collective-permute-start.34 = (bf16[512,2048]{1,0:T(8,128)(2,1)S(1)}, bf16[512,2048]{1,0:T(8,128)(2,1)S(1)}, u32[]{:S(2)}, u32[]{:S(2)}) collective-permute-start(bf16[512,2048]{1,0:T(8,128)(2,1)S(1)} %shard_map.183), channel_id=1, source_target_pairs={{0,2},{2,0},{4,6},{6,4},{8,10},{10,8},{12,14},{14,12},{16,18},{18,... | collective-permute-start | bytes 6291464 | tf_op jit(solution)/shard_map/ppermute | solution.py:379
  186.6 25.1 %collective-permute-start.33 = (bf16[256,2048]{1,0:T(8,128)(2,1)S(1)}, bf16[256,2048]{1,0:T(8,128)(2,1)S(1)}, u32[]{:S(2)}, u32[]{:S(2)}) collective-permute-start(bf16[256,2048]{1,0:T(8,128)(2,1)S(1)} %collective-permute-done.30), channel_id=1, source_target_pairs={{0,4},{2,6},{4,0},{6,2},{8,12},{10,14},{12,8},{14,10},{16,20},{18,... | collective-permute-start | bytes 3145736 | tf_op jit(solution)/shard_map/ppermute | solution.py:379
  216.6 20.4 %collective-permute-start.38 = (bf16[512,2048]{1,0:T(8,128)(2,1)}, bf16[512,2048]{1,0:T(8,128)(2,1)}, u32[]{:S(2)}, u32[]{:S(2)}) collective-permute-start(bf16[512,2048]{1,0:T(8,128)(2,1)} %shard_map.189), channel_id=1, source_target_pairs={{0,2},{2,0},{4,6},{6,4},{8,10},{10,8},{12,14},{14,12},{16,18},{18,... | collective-permute-start | bytes 6291464 | tf_op jit(solution)/shard_map/ppermute | solution.py:379
  218.3 25.1 %collective-permute-start.37 = (bf16[256,2048]{1,0:T(8,128)(2,1)S(1)}, bf16[256,2048]{1,0:T(8,128)(2,1)S(1)}, u32[]{:S(2)}, u32[]{:S(2)}) collective-permute-start(bf16[256,2048]{1,0:T(8,128)(2,1)S(1)} %get-tuple-element.1036), channel_id=1, source_target_pairs={{0,1},{1,0},{2,3},{3,2},{4,5},{5,4},{6,7},{7,6},{8,9},{9,8},{10,11... | collective-permute-start | bytes 3145736 | tf_op jit(solution)/shard_map/ppermute | solution.py:383
  229.9 33.6 %collective-permute-start.42 = (bf16[512,2048]{1,0:T(8,128)(2,1)}, bf16[512,2048]{1,0:T(8,128)(2,1)}, u32[]{:S(2)}, u32[]{:S(2)}) collective-permute-start(bf16[512,2048]{1,0:T(8,128)(2,1)} %shard_map.193), channel_id=1, source_target_pairs={{0,2},{2,0},{4,6},{6,4},{8,10},{10,8},{12,14},{14,12},{16,18},{18,... | collective-permute-start | bytes 6291464 | tf_op jit(solution)/shard_map/ppermute | solution.py:379
  244.7 25.2 %collective-permute-start.41 = (bf16[256,2048]{1,0:T(8,128)(2,1)S(1)}, bf16[256,2048]{1,0:T(8,128)(2,1)}, u32[]{:S(2)}, u32[]{:S(2)}) collective-permute-start(bf16[256,2048]{1,0:T(8,128)(2,1)S(1)} %get-tuple-element.1034), channel_id=1, source_target_pairs={{0,4},{2,6},{4,0},{6,2},{8,12},{10,14},{12,8},{14,10},{16,20},{18,... | collective-permute-start | bytes 3145736 | tf_op jit(solution)/shard_map/ppermute | solution.py:379
  245.2 24.7 %collective-permute-start.40 = (bf16[256,2048]{1,0:T(8,128)(2,1)}, bf16[256,2048]{1,0:T(8,128)(2,1)}, u32[]{:S(2)}, u32[]{:S(2)}) collective-permute-start(bf16[256,2048]{1,0:T(8,128)(2,1)} %get-tuple-element.750), channel_id=1, source_target_pairs={{0,1},{1,0},{2,3},{3,2},{4,5},{5,4},{6,7},{7,6},{8,9},{9,8},{10,11... | collective-permute-start | bytes 3145736 | tf_op jit(solution)/shard_map/ppermute | solution.py:383
  276.4 24.6 %collective-permute-start.44 = (bf16[256,2048]{1,0:T(8,128)(2,1)S(1)}, bf16[256,2048]{1,0:T(8,128)(2,1)S(1)}, u32[]{:S(2)}, u32[]{:S(2)}) collective-permute-start(bf16[256,2048]{1,0:T(8,128)(2,1)S(1)} %get-tuple-element.1030), channel_id=1, source_target_pairs={{0,4},{2,6},{4,0},{6,2},{8,12},{10,14},{12,8},{14,10},{16,20},{18,... | collective-permute-start | bytes 3145736 | tf_op jit(solution)/shard_map/ppermute | solution.py:379
  277.6 24.1 %collective-permute-start.43 = (bf16[512,1024]{1,0:T(8,128)(2,1)S(1)}, bf16[512,1024]{1,0:T(8,128)(2,1)S(1)}, u32[]{:S(2)}, u32[]{:S(2)}) collective-permute-start(bf16[512,1024]{1,0:T(8,128)(2,1)S(1)} %copy-done.55), channel_id=1, source_target_pairs={{0,1},{1,0},{2,3},{3,2},{4,5},{5,4},{6,7},{7,6},{8,9},{9,8},{10,11... | collective-permute-start | bytes 3145736 | tf_op jit(solution)/shard_map/ppermute | solution.py:383
  286.5 42.0 %collective-permute-start.48 = (bf16[512,512]{1,0:T(8,128)(2,1)S(1)}, bf16[512,512]{1,0:T(8,128)(2,1)S(1)}, u32[]{:S(2)}, u32[]{:S(2)}) collective-permute-start(bf16[512,512]{1,0:T(8,128)(2,1)S(1)} %shard_map.199), channel_id=1, source_target_pairs={{0,2},{2,0},{4,6},{6,4},{8,10},{10,8},{12,14},{14,12},{16,18},{18,... | collective-permute-start | bytes 1572872 | tf_op jit(solution)/shard_map/ppermute | solution.py:379
  288.2 42.3 %collective-permute-start.47 = (bf16[512,512]{1,0:T(8,128)(2,1)S(1)}, bf16[512,512]{1,0:T(8,128)(2,1)S(1)}, u32[]{:S(2)}, u32[]{:S(2)}) collective-permute-start(bf16[512,512]{1,0:T(8,128)(2,1)S(1)} %shard_map.197), channel_id=1, source_target_pairs={{0,2},{2,0},{4,6},{6,4},{8,10},{10,8},{12,14},{14,12},{16,18},{18,... | collective-permute-start | bytes 1572872 | tf_op jit(solution)/shard_map/ppermute | solution.py:379
  302.2 31.5 %collective-permute-start.46 = (bf16[256,2048]{1,0:T(8,128)(2,1)S(1)}, bf16[256,2048]{1,0:T(8,128)(2,1)S(1)}, u32[]{:S(2)}, u32[]{:S(2)}) collective-permute-start(bf16[256,2048]{1,0:T(8,128)(2,1)S(1)} %add_convert_fusion.8), channel_id=1, source_target_pairs={{0,4},{2,6},{4,0},{6,2},{8,12},{10,14},{12,8},{14,10},{16,20},{18,... | collective-permute-start | bytes 3145736 | tf_op jit(solution)/shard_map/ppermute | solution.py:379
  303.7 29.9 %collective-permute-start.45 = (bf16[256,2048]{1,0:T(8,128)(2,1)S(1)}, bf16[256,2048]{1,0:T(8,128)(2,1)S(1)}, u32[]{:S(2)}, u32[]{:S(2)}) collective-permute-start(bf16[256,2048]{1,0:T(8,128)(2,1)S(1)} %add_convert_fusion.9), channel_id=1, source_target_pairs={{0,1},{1,0},{2,3},{3,2},{4,5},{5,4},{6,7},{7,6},{8,9},{9,8},{10,11... | collective-permute-start | bytes 3145736 | tf_op jit(solution)/shard_map/ppermute | solution.py:383
  315.7 17.9 %collective-permute-start.54 = (bf16[512,768]{1,0:T(8,128)(2,1)S(1)}, bf16[512,768]{1,0:T(8,128)(2,1)S(1)}, u32[]{:S(2)}, u32[]{:S(2)}) collective-permute-start(bf16[512,768]{1,0:T(8,128)(2,1)S(1)} %shard_map.205), channel_id=1, source_target_pairs={{0,2},{2,0},{4,6},{6,4},{8,10},{10,8},{12,14},{14,12},{16,18},{18,... | collective-permute-start | bytes 2359304 | tf_op jit(solution)/shard_map/ppermute | solution.py:379
  335.9 26.7 %collective-permute-start.55 = (bf16[512,768]{1,0:T(8,128)(2,1)S(1)}, bf16[512,768]{1,0:T(8,128)(2,1)S(1)}, u32[]{:S(2)}, u32[]{:S(2)}) collective-permute-start(bf16[512,768]{1,0:T(8,128)(2,1)S(1)} %shard_map.206), channel_id=1, source_target_pairs={{0,1},{1,0},{2,3},{3,2},{4,5},{5,4},{6,7},{7,6},{8,9},{9,8},{10,11... | collective-permute-start | bytes 2359304 | tf_op jit(solution)/shard_map/ppermute | solution.py:383
  337.6 21.2 %collective-permute-start.49 = (bf16[128,2048]{1,0:T(8,128)(2,1)S(1)}, bf16[128,2048]{1,0:T(8,128)(2,1)S(1)}, u32[]{:S(2)}, u32[]{:S(2)}) collective-permute-start(bf16[128,2048]{1,0:T(8,128)(2,1)S(1)} %get-tuple-element.1052), channel_id=1, source_target_pairs={{0,8},{2,10},{4,12},{6,14},{8,0},{10,2},{12,4},{14,6},{16,24},{18,... | collective-permute-start | bytes 1572872 | tf_op jit(solution)/shard_map/ppermute | solution.py:379
  339.8 22.8 %collective-permute-start.50 = (bf16[128,2048]{1,0:T(8,128)(2,1)S(1)}, bf16[128,2048]{1,0:T(8,128)(2,1)S(1)}, u32[]{:S(2)}, u32[]{:S(2)}) collective-permute-start(bf16[128,2048]{1,0:T(8,128)(2,1)S(1)} %get-tuple-element.1050), channel_id=1, source_target_pairs={{0,8},{2,10},{4,12},{6,14},{8,0},{10,2},{12,4},{14,6},{16,24},{18,... | collective-permute-start | bytes 1572872 | tf_op jit(solution)/shard_map/ppermute | solution.py:379
  340.3 17.9 %collective-permute-start.51 = (bf16[256,512]{1,0:T(8,128)(2,1)S(1)}, bf16[256,512]{1,0:T(8,128)(2,1)S(1)}, u32[]{:S(2)}, u32[]{:S(2)}) collective-permute-start(bf16[256,512]{1,0:T(8,128)(2,1)S(1)} %get-tuple-element.1064), channel_id=1, source_target_pairs={{0,4},{2,6},{4,0},{6,2},{8,12},{10,14},{12,8},{14,10},{16,20},{18,... | collective-permute-start | bytes 786440 | tf_op jit(solution)/shard_map/ppermute | solution.py:379
  341.4 16.9 %collective-permute-start.52 = (bf16[256,512]{1,0:T(8,128)(2,1)S(1)}, bf16[256,512]{1,0:T(8,128)(2,1)S(1)}, u32[]{:S(2)}, u32[]{:S(2)}) collective-permute-start(bf16[256,512]{1,0:T(8,128)(2,1)S(1)} %get-tuple-element.1062), channel_id=1, source_target_pairs={{0,4},{2,6},{4,0},{6,2},{8,12},{10,14},{12,8},{14,10},{16,20},{18,... | collective-permute-start | bytes 786440 | tf_op jit(solution)/shard_map/ppermute | solution.py:379
  358.3 27.6 %collective-permute-start.58 = (bf16[512,768]{1,0:T(8,128)(2,1)S(1)}, bf16[512,768]{1,0:T(8,128)(2,1)S(1)}, u32[]{:S(2)}, u32[]{:S(2)}) collective-permute-start(bf16[512,768]{1,0:T(8,128)(2,1)S(1)} %shard_map.210), channel_id=1, source_target_pairs={{0,2},{2,0},{4,6},{6,4},{8,10},{10,8},{12,14},{14,12},{16,18},{18,... | collective-permute-start | bytes 2359304 | tf_op jit(solution)/shard_map/ppermute | solution.py:379
  367.7 27.7 %collective-permute-start.57 = (bf16[512,768]{1,0:T(8,128)(2,1)S(1)}, bf16[512,768]{1,0:T(8,128)(2,1)S(1)}, u32[]{:S(2)}, u32[]{:S(2)}) collective-permute-start(bf16[512,768]{1,0:T(8,128)(2,1)S(1)} %shard_map.209), channel_id=1, source_target_pairs={{0,1},{1,0},{2,3},{3,2},{4,5},{5,4},{6,7},{7,6},{8,9},{9,8},{10,11... | collective-permute-start | bytes 2359304 | tf_op jit(solution)/shard_map/ppermute | solution.py:383
  369.5 21.4 %collective-permute-start.59 = (bf16[64,2048]{1,0:T(8,128)(2,1)}, bf16[64,2048]{1,0:T(8,128)(2,1)}, u32[]{:S(2)}, u32[]{:S(2)}) collective-permute-start(bf16[64,2048]{1,0:T(8,128)(2,1)} %get-tuple-element.1060), channel_id=1, source_target_pairs={{0,16},{2,18},{4,20},{6,22},{8,24},{10,26},{12,28},{14,30},{16,0},... | collective-permute-start | bytes 786440 | tf_op jit(solution)/shard_map/ppermute | solution.py:379
  374.0 21.5 %collective-permute-start.60 = (bf16[64,2048]{1,0:T(8,128)(2,1)}, bf16[64,2048]{1,0:T(8,128)(2,1)}, u32[]{:S(2)}, u32[]{:S(2)}) collective-permute-start(bf16[64,2048]{1,0:T(8,128)(2,1)} %get-tuple-element.1058), channel_id=1, source_target_pairs={{0,16},{2,18},{4,20},{6,22},{8,24},{10,26},{12,28},{14,30},{16,0},... | collective-permute-start | bytes 786440 | tf_op jit(solution)/shard_map/ppermute | solution.py:379
  413.1 14.4 %collective-permute-start.68 = (bf16[256,1024]{1,0:T(8,128)(2,1)S(1)}, bf16[256,1024]{1,0:T(8,128)(2,1)S(1)}, u32[]{:S(2)}, u32[]{:S(2)}) collective-permute-start(bf16[256,1024]{1,0:T(8,128)(2,1)S(1)} %get-tuple-element.1049), channel_id=1, source_target_pairs={{0,1},{1,0},{2,3},{3,2},{4,5},{5,4},{6,7},{7,6},{8,9},{9,8},{10,11... | collective-permute-start | bytes 1572872 | tf_op jit(solution)/shard_map/ppermute | solution.py:383
  427.7 16.1 %collective-permute-start.72 = (bf16[128,768]{1,0:T(8,128)(2,1)S(1)}, bf16[128,768]{1,0:T(8,128)(2,1)S(1)}, u32[]{:S(2)}, u32[]{:S(2)}) collective-permute-start(bf16[128,768]{1,0:T(8,128)(2,1)S(1)} %get-tuple-element.1071), channel_id=1, source_target_pairs={{0,8},{2,10},{4,12},{6,14},{8,0},{10,2},{12,4},{14,6},{16,24},{18,... | collective-permute-start | bytes 589832 | tf_op jit(solution)/shard_map/ppermute | solution.py:379
  429.8 14.0 %collective-permute-start.73 = (bf16[64,768]{1,0:T(8,128)(2,1)S(1)}, bf16[64,768]{1,0:T(8,128)(2,1)S(1)}, u32[]{:S(2)}, u32[]{:S(2)}) collective-permute-start(bf16[64,768]{1,0:T(8,128)(2,1)S(1)} %get-tuple-element.1077), channel_id=1, source_target_pairs={{0,16},{2,18},{4,20},{6,22},{8,24},{10,26},{12,28},{14,30},{16,0},... | collective-permute-start | bytes 294920 | tf_op jit(solution)/shard_map/ppermute | solution.py:379
  432.9 13.0 %collective-permute-start.71 = (bf16[256,1024]{1,0:T(8,128)(2,1)S(1)}, bf16[256,1024]{1,0:T(8,128)(2,1)S(1)}, u32[]{:S(2)}, u32[]{:S(2)}) collective-permute-start(bf16[256,1024]{1,0:T(8,128)(2,1)S(1)} %get-tuple-element.955), channel_id=1, source_target_pairs={{0,1},{1,0},{2,3},{3,2},{4,5},{5,4},{6,7},{7,6},{8,9},{9,8},{10,11... | collective-permute-start | bytes 1572872 | tf_op jit(solution)/shard_map/ppermute | solution.py:383
  (107 other events, 861.5 us)
